TPU v7x, 32 devices: a whole 2x2x4 slice. The times are simulated.
32 devices in a mesh: ctx: 8 (over y, x, core), head: 4 (over z).
Axes of the slice: x: 2, y: 2, z: 4, core: 2. Of those that a mesh axis runs over, the one named last changes fastest.
Arguments:
- inputs: bfloat16 [4096, 2048], P('ctx'), may hold values from -6 to 6
- query_key_weight: bfloat16 [2, 2048, 2048], P(None, None, 'head'), may hold values from -0.125 to 0.125
- value_gate_weight: bfloat16 [2, 2048, 4096], P(None, None, 'head'), may hold values from -0.125 to 0.125
- decay_beta_weight: bfloat16 [2, 2048, 32], P(None, None, 'head'), may hold values from -0.125 to 0.125
- beta_bias: float32 [32], P('head'), may hold values from -5 to -3
- decay_scale: float32 [32], P('head'), may hold values from 0.0001 to 0.1
- norm_gain: float32 [128], replicated, may hold values from 0.1 to 1.9
- out_weight: bfloat16 [4096, 2048], P('head'), may hold values from -0.09375 to 0.09375
- boundaries: int32 [4096], P('ctx'), may hold values 0 or 1
- grad_mixed: bfloat16 [4096, 2048], P('ctx'), may hold values from -6 to 6
Outputs:
- mixed: bfloat16 [4096, 2048], P('ctx', 'head')
- grad_inputs: bfloat16 [4096, 2048], P('ctx', 'head')
- grad_query_key: float32 [2, 2048, 2048], P(None, 'ctx', 'head')
- grad_value_gate: float32 [2, 2048, 4096], P(None, 'ctx', 'head')
- grad_decay_beta: float32 [2, 2048, 32], P(None, 'ctx', 'head')
- grad_out_weight: float32 [4096, 2048], P('head', 'ctx')
All inputs are finite; a program needn't handle non-finite values. No bound on the sum of `boundaries` on one device may be relied on, other than what follows from the above.
Results may differ from a plain program's by a relative error of at most 0.02.
Values may be sent and summed in bfloat16 or wider, within the bound.
No kernel may reach another device: no remote copies, remote signals or barrier semaphores. Data moves between devices by JAX's collectives and lax.ppermute only.
A program may use at most 192 MiB of HBM per device.

v0:
```python
import jax
import jax.numpy as jnp
from jax import lax
from jax.sharding import PartitionSpec as P

DK = 128
DV = 128
SPAN = 64


EPS = 1e-06
PRECISE_MODE = lax.Precision.HIGHEST


def shifted(block, axis, distance):
    devices = range(lax.axis_size(axis))
    route = [(i - distance, i) for i in devices if i - distance in devices]
    return lax.ppermute(block, axis, route)


def head_inputs(proj_query_key, proj_value_gate, proj_decay_beta, beta_bias, decay_scale):
    tok_count = proj_query_key.shape[1]
    key_heads = proj_query_key.shape[2] // DK
    value_heads = proj_value_gate.shape[2] // DV
    repeat_count = value_heads // key_heads
    query_rows = proj_query_key[0].reshape(tok_count, key_heads, DK)
    key_rows = proj_query_key[1].reshape(tok_count, key_heads, DK)
    query_rows = query_rows * lax.rsqrt(
        jnp.sum(query_rows * query_rows, axis=-1, keepdims=True) + EPS
    )
    key_rows = key_rows * lax.rsqrt(jnp.sum(key_rows * key_rows, axis=-1, keepdims=True) + EPS)
    query_rows = jnp.repeat(query_rows, repeat_count, axis=1) * DK ** (-0.5)
    key_rows = jnp.repeat(key_rows, repeat_count, axis=1)
    value_rows = proj_value_gate[0].reshape(tok_count, value_heads, DV)
    gate_rows = proj_value_gate[1].reshape(tok_count, value_heads, DV)
    beta_rows = jax.nn.sigmoid(proj_decay_beta[1] + beta_bias)
    log_decay = -decay_scale * jax.nn.softplus(proj_decay_beta[0])
    return (query_rows, key_rows, value_rows, gate_rows, beta_rows, log_decay)


def to_spans(array_in, spans):
    head_count = array_in.shape[1]
    shaped = array_in.reshape(spans, SPAN, head_count, -1)
    return jnp.transpose(shaped, (2, 0, 1, 3))


def span_terms(query_rows, key_rows, value_rows, beta_rows, log_decay, resets):
    spans = beta_rows.shape[0] // SPAN
    query_blocks = to_spans(query_rows, spans)
    key_blocks = to_spans(key_rows, spans)
    value_blocks = to_spans(value_rows, spans)
    beta_blocks = to_spans(beta_rows[:, :, None], spans)[..., 0]
    cumulative = jnp.cumsum(to_spans(log_decay[:, :, None], spans)[..., 0], axis=-1)
    doc_index = jnp.cumsum(resets.reshape(spans, SPAN), axis=-1)[None]
    positions = jnp.arange(SPAN)
    lower_incl = positions[:, None] >= positions[None, :]
    lower_strict = (positions[:, None] > positions[None, :]).astype(jnp.float32)
    same_doc = (doc_index[..., :, None] == doc_index[..., None, :]) & lower_incl
    log_gap = jnp.minimum(cumulative[..., :, None] - cumulative[..., None, :], 0.0)
    pair_decay = jnp.where(same_doc, jnp.exp(log_gap), 0.0)
    start_keep = jnp.where(doc_index == 0, jnp.exp(cumulative), 0.0)
    end_keep = jnp.where(
        doc_index == doc_index[..., -1:],
        jnp.exp(jnp.minimum(cumulative[..., -1:] - cumulative, 0.0)),
        0.0,
    )
    total_keep = start_keep[..., -1]
    key_gram = jnp.einsum("hnck,hnjk->hncj", key_blocks, key_blocks, precision=PRECISE_MODE)
    system = (
        jnp.eye(SPAN, dtype=jnp.float32)
        + beta_blocks[..., :, None] * pair_decay * lower_strict * key_gram
    )
    right_side = jnp.concatenate(
        [beta_blocks[..., None] * value_blocks, (beta_blocks * start_keep)[..., None] * key_blocks],
        axis=-1,
    )
    solved = jax.scipy.linalg.solve_triangular(system, right_side, lower=True, unit_diagonal=True)
    pseudo_base = solved[..., :DV]
    key_weights = solved[..., DV:]
    end_keys = end_keep[..., None] * key_blocks
    scores = pair_decay * jnp.einsum(
        "hnck,hnjk->hncj", query_blocks, key_blocks, precision=PRECISE_MODE
    )
    start_queries = start_keep[..., None] * query_blocks
    return (start_queries, scores, pseudo_base, key_weights, end_keys, total_keep)


def run_spans(terms, state_in):

    def advance(carried_state, block_terms):
        (
            block_query_rows,
            block_score_matrix,
            block_starting_offset,
            block_weight_matrix,
            block_final_keys,
            block_retained_decay,
        ) = block_terms
        surrogate_values = block_starting_offset - jnp.einsum(
            "xuy,xyf->xuf", block_weight_matrix, carried_state, precision=PRECISE_MODE
        )
        produced_output = jnp.einsum(
            "xuy,xyf->xuf", block_query_rows, carried_state, precision=PRECISE_MODE
        ) + jnp.einsum("adx,axo->ado", block_score_matrix, surrogate_values, precision=PRECISE_MODE)
        updated_state = block_retained_decay[:, None, None] * carried_state + jnp.einsum(
            "gzy,gzq->gyq", block_final_keys, surrogate_values, precision=PRECISE_MODE
        )
        return (updated_state, produced_output)

    moved = tuple([jnp.moveaxis(member, 1, 0) for member in terms])
    final, produced_output = lax.scan(advance, state_in, moved)
    spans, head_count = (produced_output.shape[0], produced_output.shape[1])
    produced_output = jnp.transpose(produced_output, (0, 2, 1, 3)).reshape(
        spans * SPAN, head_count, DV
    )
    return (produced_output, final)


def transition_totals(terms):
    start_queries, scores, pseudo_base, key_weights, end_keys, total_keep = terms
    head_count = total_keep.shape[0]
    identity = jnp.eye(DK, dtype=jnp.float32)
    maps_a = total_keep[..., None, None] * identity - jnp.einsum(
        "hnck,hncj->hnkj", end_keys, key_weights, precision=PRECISE_MODE
    )
    maps_b = jnp.einsum("hnck,hncv->hnkv", end_keys, pseudo_base, precision=PRECISE_MODE)

    def compose(carried_state, block_maps):
        first_span, second_span = block_maps
        return (
            (
                jnp.einsum("hkj,hjm->hkm", first_span, carried_state[0], precision=PRECISE_MODE),
                jnp.einsum("azf,afg->azg", first_span, carried_state[1], precision=PRECISE_MODE)
                + second_span,
            ),
            None,
        )

    start = (
        jnp.broadcast_to(identity, (head_count, DK, DK)),
        jnp.zeros((head_count, DK, DV), jnp.float32),
    )
    totals, unused = lax.scan(
        compose, start, (jnp.moveaxis(maps_a, 1, 0), jnp.moveaxis(maps_b, 1, 0))
    )
    return totals


def mixer(
    proj_query_key,
    proj_value_gate,
    proj_decay_beta,
    beta_bias,
    decay_scale,
    norm_gain,
    resets,
    state_in,
):
    query_rows, key_rows, value_rows, gate_rows, beta_rows, log_decay = head_inputs(
        proj_query_key, proj_value_gate, proj_decay_beta, beta_bias, decay_scale
    )
    terms = span_terms(query_rows, key_rows, value_rows, beta_rows, log_decay, resets)
    produced_output, final = run_spans(terms, state_in)
    scale_rows = lax.rsqrt(
        jnp.mean(produced_output * produced_output, axis=-1, keepdims=True) + EPS
    )
    normed = produced_output * scale_rows * norm_gain * jax.nn.silu(gate_rows)
    return (normed.reshape(normed.shape[0], -1), final)


def mixer_totals(proj_query_key, proj_value_gate, proj_decay_beta, beta_bias, decay_scale, resets):
    query_rows, key_rows, value_rows, gate_rows, beta_rows, log_decay = head_inputs(
        proj_query_key, proj_value_gate, proj_decay_beta, beta_bias, decay_scale
    )
    return transition_totals(
        span_terms(query_rows, key_rows, value_rows, beta_rows, log_decay, resets)
    )


def body(
    inputs,
    query_key_weight,
    value_gate_weight,
    decay_beta_weight,
    beta_bias,
    decay_scale,
    norm_gain,
    out_weight,
    boundaries,
    grad_mixed,
):
    proj_query_key = jnp.einsum(
        "td,sdf->stf", inputs, query_key_weight, preferred_element_type=jnp.float32
    )
    proj_value_gate = jnp.einsum(
        "td,sdf->stf", inputs, value_gate_weight, preferred_element_type=jnp.float32
    )
    proj_decay_beta = jnp.einsum(
        "td,sdf->stf", inputs, decay_beta_weight, preferred_element_type=jnp.float32
    )
    head_count = beta_bias.shape[0]
    first_total, second_total = mixer_totals(
        proj_query_key, proj_value_gate, proj_decay_beta, beta_bias, decay_scale, boundaries
    )
    zero_state = jnp.zeros((head_count, DK, DV), jnp.float32)

    def hand_forward(position, incoming_state):
        outgoing_state = (
            jnp.einsum("azf,afg->azg", first_total, incoming_state, precision=PRECISE_MODE)
            + second_total
        )
        return shifted(outgoing_state.astype(jnp.bfloat16), "ctx", 1).astype(outgoing_state.dtype)

    state_in = lax.fori_loop(0, lax.axis_size("ctx") - 1, hand_forward, zero_state)

    def local_mixer(part_query_key, part_value_gate, part_decay_beta, carried_in):
        return mixer(
            part_query_key,
            part_value_gate,
            part_decay_beta,
            beta_bias,
            decay_scale,
            norm_gain,
            boundaries,
            carried_in,
        )

    (normed, state_out), pullback = jax.vjp(
        local_mixer, proj_query_key, proj_value_gate, proj_decay_beta, state_in
    )
    hidden = normed.astype(jnp.bfloat16)
    partial_out = jnp.dot(hidden, out_weight, preferred_element_type=jnp.float32)
    mixed = lax.psum_scatter(
        partial_out.astype(jnp.bfloat16), "head", scatter_dimension=1, tiled=True
    )
    delta_hidden = jnp.einsum(
        "td,fd->tf", grad_mixed, out_weight, preferred_element_type=jnp.float32
    )
    own_pull = pullback((delta_hidden, jnp.zeros_like(state_out)))
    local_state = own_pull[3]

    def hand_backward(position, incoming_state):
        outgoing_state = (
            jnp.einsum("lfg,lfb->lgb", first_total, incoming_state, precision=PRECISE_MODE)
            + local_state
        )
        return shifted(outgoing_state.astype(jnp.bfloat16), "ctx", -1).astype(outgoing_state.dtype)

    grad_state_out = lax.fori_loop(0, lax.axis_size("ctx") - 1, hand_backward, zero_state)
    far_pull = pullback((jnp.zeros_like(delta_hidden), grad_state_out))
    delta_query_key = (own_pull[0] + far_pull[0]).astype(jnp.bfloat16)
    delta_value_gate = (own_pull[1] + far_pull[1]).astype(jnp.bfloat16)
    delta_decay_beta = (own_pull[2] + far_pull[2]).astype(jnp.bfloat16)
    grad_rows = jnp.einsum(
        "stf,sdf->td", delta_query_key, query_key_weight, preferred_element_type=jnp.float32
    )
    grad_rows = grad_rows + jnp.einsum(
        "stf,sdf->td", delta_value_gate, value_gate_weight, preferred_element_type=jnp.float32
    )
    grad_rows = grad_rows + jnp.einsum(
        "stf,sdf->td", delta_decay_beta, decay_beta_weight, preferred_element_type=jnp.float32
    )
    grad_inputs = lax.psum_scatter(
        grad_rows.astype(jnp.bfloat16), "head", scatter_dimension=1, tiled=True
    )
    term_query_key = jnp.einsum(
        "td,stf->sdf", inputs, delta_query_key, preferred_element_type=jnp.float32
    )
    term_value_gate = jnp.einsum(
        "td,stf->sdf", inputs, delta_value_gate, preferred_element_type=jnp.float32
    )
    term_decay_beta = jnp.einsum(
        "td,stf->sdf", inputs, delta_decay_beta, preferred_element_type=jnp.float32
    )
    term_out = jnp.einsum("tf,td->fd", hidden, grad_mixed, preferred_element_type=jnp.float32)
    grad_query_key, grad_value_gate, grad_decay_beta, grad_out_weight = (
        lax.psum_scatter(
            term_query_key.astype(jnp.bfloat16), "ctx", scatter_dimension=1, tiled=True
        ).astype(jnp.float32),
        lax.psum_scatter(
            term_value_gate.astype(jnp.bfloat16), "ctx", scatter_dimension=1, tiled=True
        ).astype(jnp.float32),
        lax.psum_scatter(
            term_decay_beta.astype(jnp.bfloat16), "ctx", scatter_dimension=1, tiled=True
        ).astype(jnp.float32),
        lax.psum_scatter(
            term_out.astype(jnp.bfloat16), "ctx", scatter_dimension=1, tiled=True
        ).astype(jnp.float32),
    )
    return (mixed, grad_inputs, grad_query_key, grad_value_gate, grad_decay_beta, grad_out_weight)


def solution(mesh):
    in_specs = (
        P("ctx", None),
        P(None, None, "head"),
        P(None, None, "head"),
        P(None, None, "head"),
        P("head"),
        P("head"),
        P(),
        P("head", None),
        P("ctx"),
        P("ctx", None),
    )
    out_specs = (
        P("ctx", "head"),
        P("ctx", "head"),
        P(None, "ctx", "head"),
        P(None, "ctx", "head"),
        P(None, "ctx", "head"),
        P("head", "ctx"),
    )
    return jax.shard_map(body, mesh=mesh, in_specs=in_specs, out_specs=out_specs, check_vma=False)
```

profile of v0, /device:TPU:0, one launch (start us, length us, event | category | flops | bytes accessed | tf_op | source)
XLA Modules:
  0.0 1583.2 jit_solution(7287726930890809916)
XLA Ops:
  40.1 316.0 %custom-call.13 = f32[8,8,1,64,64]{3,4,2,1,0:T(8,128)} custom-call(f32[8,8,1,64,64]{4,3,2,1,0:T(8,128)} %get-tuple-element.1313), custom_call_target="InvertDiagBlocksLowerTriangular" | custom-call | tf_op jit(solution)/shard_map/jit(_solve_triangular)/vmap(vmap())/triangular_solve/custom-call.1 | solution.py:77
  359.6 7.2 convolution_bitcast_fusion.9
  388.1 8.8 convolution_bitcast_fusion.8
  396.9 9.7 bitcast_subtract_fusion
  407.4 50.4 %while.108 = (s32[]{:T(128)}, f32[8,128,128]{2,1,0:T(8,128)}, f32[8,128,128]{2,1,0:T(8,128)}, f32[8,8,128,128]{3,2,0,1:T(8,128)}, f32[8,8,128,128]{3,2,0,1:T(8,128)}, /*index=5*/s32[]{:T(128)}, s32[]{:T(128)}) while((s32[]{:T(128)}, f32[8,128,128]{2,1,0:T(8,128)}, f32[8,128,128]{2,1,0:T(8,128)}, f32[8,8,128,128]{3,2,0,1:T(8,128)}, ...), condition=%wide.region_4.6_spmd.clone, body=%wide.region_3.5_spmd.clone.sunk | while | flops 402915328 | bytes 7865971 | solution.py:143
  471.1 75.9 %while.109 = (s32[]{:T(128)}, f32[8,128,128]{2,1,0:T(8,128)}, f32[8,128,128]{2,1,0:T(8,128)}, f32[8,128,128]{2,1,0:T(8,128)}, s32[]{:T(128)}, /*index=5*/s32[]{:T(128)}) while((s32[]{:T(128)}, f32[8,128,128]{2,1,0:T(8,128)}, f32[8,128,128]{2,1,0:T(8,128)}, f32[8,128,128]{2,1,0:T(8,128)}, s32[]{:T(128)}, /*index=5*/s32[]{:T(128)}) %tuple.242), condition=%wide.region_6.8_spmd.clone, body=%wide.region_5.7_spmd.clone.sunk | while | flops 201850880 | bytes 3670135 | solution.py:214
  480.9 6.8 collective-permute-start
  504.0 6.5 collective-permute-start
  548.6 104.9 %while.106 = (s32[]{:T(128)}, f32[8,128,128]{2,1,0:T(8,128)}, f32[8,8,64,128]{3,1,2,0:T(8,128)}, f32[8,8,128,128]{3,2,1,0:T(8,128)}, f32[8,8,64,128]{3,2,1,0:T(8...) while((s32[]{:T(128)}, f32[8,128,128]{2,1,0:T(8,128)}, ...), condition=%wide.region_9.11_spmd, body=%wide.region_8.10_spmd.sunk | while | flops 352714752 | bytes 6821089 | solution.py:111
  693.5 178.9 %while.110 = (s32[]{:T(128)}, f32[8,128,128]{2,1,0:T(8,128)S(1)}, f32[8,8,64,128]{3,2,0,1:T(8,128)}, f32[8,8,64,64]{3,2,0,1:T(8,128)}, f32[8,8,64,128]{3,2,1,0:T...) while((s32[]{:T(128)}, f32[8,128,128]{2,1,0:T(8,128)S(1)}, ...), condition=%wide.region_15.17_spmd.clone, body=%wide.region_13.16_spmd.clone.sunk | while | flops 706019328 | bytes 11016097 | solution.py:111
  872.4 9.2 fusion.119
  887.2 77.0 %while.111 = (s32[]{:T(128)}, f32[8,128,128]{2,1,0:T(8,128)S(1)}, f32[8,128,128]{1,2,0:T(8,128)}, f32[8,128,128]{2,1,0:T(8,128)S(1)}, s32[]{:T(128)}, /*index=5*/s32[]{:T(128)}) while((s32[]{:T(128)}, f32[8,128,128]{2,1,0:T(8,128)S(1)}, f32[8,128,128]{1,2,0:T(8,128)}, f32[8,128,128]{2,1,0:T(8,128)S(1)}, s32[]{:T(128)}, ...), condition=%wide.region_21.24_spmd.clone, body=%wide.region_20.23_spmd.clone.sunk | while | flops 201850880 | bytes 3670135 | solution.py:249
  901.1 7.2 collective-permute-done.1
  912.1 6.6 collective-permute-done.1
  922.4 8.0 collective-permute-done.1
  934.2 7.5 collective-permute-done.1
  945.4 7.5 collective-permute-done.1
  956.7 7.5 collective-permute-done.1
  972.2 168.8 %while.107 = (s32[]{:T(128)}, f32[8,128,128]{2,1,0:T(8,128)S(1)}, f32[8,8,64,128]{3,2,0,1:T(8,128)}, f32[8,8,64,64]{3,2,0,1:T(8,128)}, f32[8,8,64,128]{3,2,1,0:T...) while((s32[]{:T(128)}, f32[8,128,128]{2,1,0:T(8,128)S(1)}, ...), condition=%wide.region_25.28_spmd, body=%wide.region_23.27_spmd.sunk | while | flops 705495040 | bytes 11015573 | solution.py:111
  1141.0 8.2 fusion.115
  1157.9 9.4 fusion.145
  1167.3 6.8 multiply_reduce_fusion
  1201.3 7.4 fusion.157
  1243.9 8.8 fusion.231
  1252.7 7.0 fusion.161
  1262.5 7.6 fusion.169
  1339.2 6.8 convert_bitcast_fusion
  1351.0 7.2 fusion.300
  1371.3 37.1 %reduce-scatter.17.cloned.1.call-done = bf16[1024,256]{1,0:T(8,128)(2,1)} async-done(((bf16[1024,2048]{1,0:T(8,128)(2,1)}), bf16[1024,256]{1,0:T(8,128)(2,1)}) %reduce-scatter.17.cloned.1.call-update) | async-done | bytes 524304 | tf_op jit(solution)/shard_map/reduce_scatter | solution.py:286
  1410.6 72.9 %reduce-scatter.13.cloned.1.call-done = bf16[2,256,1024]{1,2,0:T(8,128)(2,1)} async-done(((bf16[2,2048,1024]{1,2,0:T(8,128)(2,1)}), bf16[2,256,1024]{1,2,0:T(8,128)(2,1)}) %reduce-scatter.13.cloned.1.call-update) | async-done | bytes 1048592 | tf_op jit(solution)/shard_map/reduce_scatter | solution.py:280
  1486.1 44.0 %reduce-scatter.9.cloned.1.call-done = bf16[512,512]{1,0:T(8,128)(2,1)} async-done(((bf16[512,2048]{1,0:T(8,128)(2,1)}), bf16[512,512]{1,0:T(8,128)(2,1)}) %reduce-scatter.9.cloned.1.call-update) | async-done | bytes 524304 | tf_op jit(solution)/shard_map/reduce_scatter | solution.py:263
  1530.1 46.1 %reduce-scatter.7.cloned.1.call-done = bf16[512,512]{1,0:T(8,128)(2,1)} async-done(((bf16[512,2048]{1,0:T(8,128)(2,1)}), bf16[512,512]{1,0:T(8,128)(2,1)}) %reduce-scatter.7.cloned.1.call-update) | async-done | bytes 524304 | tf_op jit(solution)/shard_map/reduce_scatter | solution.py:233
  (733 shorter events, 888.5 us)
Async XLA Ops:
  7.2 1360.6 %reduce-scatter.15.cloned.1.call-start = ((), (), s32[]{:S(2)}) async-start(), calls=%async_computation.10 | async-start | bytes 73728 | tf_op jit(solution)/shard_map/reduce_scatter | solution.py:283
  15.1 11.8 copy-start.79
  19.7 16.8 %copy-start.54 = (f32[64,64]{1,0:T(8,128)}, f32[64,64]{1,0:T(8,128)S(1)}, u32[]{:S(2)}) copy-start(f32[64,64]{1,0:T(8,128)S(1)} %fusion.263) | copy-start | bytes 49156
  36.5 319.5 %copy-start.73 = (f32[8,8,64]{2,0,1:T(8,128)S(1)}, f32[8,8,64]{2,0,1:T(8,128)}, u32[]{:S(2)}) copy-start(f32[8,8,64]{2,0,1:T(8,128)} %fusion.241) | copy-start | bytes 49156
  381.2 15.7 copy-start.58
  385.0 11.9 copy-start.7
  473.7 3.7 collective-permute-start
  480.9 8.1 collective-permute-start
  492.6 7.9 collective-permute-start
  504.0 7.9 collective-permute-start
  515.4 7.9 collective-permute-start
  526.9 7.9 collective-permute-start
  538.3 7.9 collective-permute-start
  872.4 9.2 copy-start.29
  872.4 9.2 copy-start.30
  889.6 7.8 collective-permute-start.1
  899.8 8.5 collective-permute-start.1
  910.8 7.9 collective-permute-start.1
  921.1 9.3 collective-permute-start.1
  932.9 8.8 collective-permute-start.1
  944.1 8.8 collective-permute-start.1
  955.4 8.8 collective-permute-start.1
  1153.5 13.8 copy-start.24
  1157.0 10.3 copy-start.15
  1157.9 9.4 copy-start.4
  1157.9 9.4 copy-start.23
  1157.9 9.4 copy-start.34
  1201.0 168.1 %reduce-scatter.11.cloned.1.call-start = ((), (), s32[]{:S(2)}) async-start(), calls=%async_computation.8 | async-start | bytes 4718592 | tf_op jit(solution)/shard_map/reduce_scatter | solution.py:277
  1290.0 118.4 %reduce-scatter.17.cloned.1.call-start = ((), (), s32[]{:S(2)}) async-start(), calls=%async_computation.11 | async-start | bytes 4718592 | tf_op jit(solution)/shard_map/reduce_scatter | solution.py:286
  1305.6 177.9 %reduce-scatter.13.cloned.1.call-start = ((), (), s32[]{:S(2)}) async-start(), calls=%async_computation.9 | async-start | bytes 9437184 | tf_op jit(solution)/shard_map/reduce_scatter | solution.py:280
  1346.0 184.1 %reduce-scatter.9.cloned.1.call-start = ((), (), s32[]{:S(2)}) async-start(), calls=%async_computation.7 | async-start | bytes 2621440 | tf_op jit(solution)/shard_map/reduce_scatter | solution.py:263
  1360.3 215.9 %reduce-scatter.7.cloned.1.call-start = ((), (), s32[]{:S(2)}) async-start(), calls=%async_computation.6 | async-start | bytes 2621440 | tf_op jit(solution)/shard_map/reduce_scatter | solution.py:233
  (96 other events, 416.0 us)
Sparse Core Ops, SparseCore 0:
  1201.1 43.6 reduce-scatter.14
  1290.2 63.5 reduce-scatter.10
  1357.2 51.2 reduce-scatter.16
  1412.2 71.2 reduce-scatter.12
  1486.2 43.8 reduce-scatter.8
  1532.9 43.1 reduce-scatter.6
where the time goes:
time: 1600 us; the launch traced here: 1580 us
  matrix products  611 us (38%)
  other arithmetic  427 us (27%)
  waiting for transfers between devices  260 us (16%)
  local copies, waits for them, and re-layouts  216 us (14%)
  starting transfers between devices  51.4 us (3%)
    another operation x4, other arithmetic, span_terms(): jax.scipy.linalg.solve_triangular(system, right_side, lower=True, unit_di...  317 us
    dot_general x40, matrix products, advance(): jnp.einsum('xuy,xyf->xuf', block_weight_matrix, carried_state, precision=...  96.8 us
    dot_general x40, matrix products, advance(): jnp.einsum('gzy,gzq->gyq', block_final_keys, surrogate_values, precision=...  92.5 us
    dot_general x40, matrix products, advance(): jnp.einsum('xuy,xyf->xuf', block_query_rows, carried_state, precision=PRE...  90.8 us
    dot_general x40, matrix products, advance(): jnp.einsum('adx,axo->ado', block_score_matrix, surrogate_values, precisio...  78.8 us
    reduce_scatter x1, waiting for transfers between devices, body(): lax.psum_scatter(term_value_gate.astype(jnp.bfloat16), 'ctx', scatter_dim...  72.9 us
    ppermute x14, waiting for transfers between devices, shifted(): return lax.ppermute(block, axis, route)  60.2 us
    ppermute x14, starting transfers between devices, shifted(): return lax.ppermute(block, axis, route)  50.8 us
  transfers between devices with their start and end apart: 20, of which 18 were waited for; matrix products, arithmetic and copies ran while one was open for 11% of the time, Pallas kernels for 0%

commit v1 on v0

v1 whole, which is shorter than its diff:
```python
import functools

import jax
import jax.numpy as jnp
from jax import lax
from jax.experimental import pallas as pl
from jax.experimental.pallas import tpu as pltpu
from jax.sharding import PartitionSpec as P

DK = 128
DV = 128
CHUNK = 128
EPS = 1e-06
QUERY_SCALE = DK ** (-0.5)

F32 = jnp.float32
BF16 = jnp.bfloat16
NN = ((1,), (0,))
NT = ((1,), (1,))
TN = ((0,), (0,))


def dot(a, b, dims=NN):
    return lax.dot_general(
        a.astype(BF16), b.astype(BF16), (dims, ((), ())), preferred_element_type=F32
    )


def exact(a, b, dims=NN):
    return lax.dot_general(
        a, b, (dims, ((), ())), precision=lax.Precision.HIGHEST, preferred_element_type=F32
    )


def softplus(x):
    return jnp.maximum(x, 0.0) + jnp.log1p(jnp.exp(-jnp.abs(x)))


def sigmoid(x):
    return 1.0 / (1.0 + jnp.exp(-x))


def row_sum(x):
    return jnp.sum(x, axis=-1, keepdims=True)


def grid_of(size):
    row = lax.broadcasted_iota(jnp.int32, (size, size), 0)
    col = lax.broadcasted_iota(jnp.int32, (size, size), 1)
    return row, col


def decays(decay_beta_ref, bias_ref, scale_ref, resets_ref):
    row, col = grid_of(CHUNK)
    lower = (row >= col).astype(F32)
    decay_logit = decay_beta_ref[0]
    beta = sigmoid(decay_beta_ref[1] + bias_ref[...])
    log_decay = -scale_ref[...] * softplus(decay_logit)
    resets = jnp.broadcast_to(resets_ref[0].astype(F32), (8, CHUNK))
    doc_row = dot(resets, lower, NT)[0:1]
    doc_col = dot(lower, resets, NT)[:, 0:1]
    cum_col = exact(lower, log_decay)
    cum_row = exact(log_decay, lower, ((0,), (1,)))
    same = (doc_col == doc_row) & (row >= col)
    start = jnp.where(doc_col == 0.0, jnp.exp(cum_col), 0.0)
    last = CHUNK - 1
    end = jnp.where(
        doc_col == doc_col[last:],
        jnp.exp(jnp.minimum(cum_col[last:] - cum_col, 0.0)),
        0.0,
    )
    return beta, cum_col, cum_row, same, start, end, start[last:], resets


def pair_decay(cum_col, cum_row, same, h):
    gap = jnp.minimum(cum_col[:, h : h + 1] - cum_row[h : h + 1, :], 0.0)
    return jnp.where(same, jnp.exp(gap), 0.0)


def head(ref, index, h):
    return ref[index][:, h * DK : (h + 1) * DK]


def unit_rows(x):
    inverse = lax.rsqrt(row_sum(x * x) + EPS)
    return x * inverse, inverse


def forward_kernel(
    query_key_ref,
    value_ref,
    decay_beta_ref,
    bias_ref,
    scale_ref,
    resets_ref,
    solve_ref,
    start_ref,
    map_ref,
    local_ref,
    total_ref,
    state_ref,
):
    heads = state_ref.shape[0]
    key_heads = query_key_ref.shape[2] // DK
    repeat = heads // key_heads
    row, col = grid_of(CHUNK)

    @pl.when(pl.program_id(0) == 0)
    def _():
        first = jnp.concatenate([(row == col).astype(F32), jnp.zeros((DK, DV), F32)], axis=1)
        for h in range(heads):
            state_ref[h] = first

    beta, cum_col, cum_row, same, start, end, total, _ = decays(
        decay_beta_ref, bias_ref, scale_ref, resets_ref
    )
    strict = row > col
    differ = row ^ col
    keys, queries, systems, scores = [], [], [], []
    for g in range(key_heads):
        q = unit_rows(head(query_key_ref, 0, g))[0] * QUERY_SCALE
        k = unit_rows(head(query_key_ref, 1, g))[0]
        queries.append(q)
        keys.append(k)
        key_gram = dot(k, k, NT)
        query_gram = dot(q, k, NT)
        for h in range(g * repeat, (g + 1) * repeat):
            decay = pair_decay(cum_col, cum_row, same, h)
            scores.append((decay * query_gram).astype(BF16))
            systems.append(jnp.where(strict, beta[:, h : h + 1] * decay * key_gram, 0.0))
    identity = (row == col).astype(F32)
    inverse = [
        (identity - jnp.where(differ == 1, system, 0.0)).astype(BF16) for system in systems
    ]
    level = 1
    while (1 << level) < CHUNK:
        here = (differ >> level) == 1
        inner = [
            dot(jnp.where(here, system, 0.0), x).astype(BF16)
            for system, x in zip(systems, inverse)
        ]
        inverse = [x - dot(x, y).astype(BF16) for x, y in zip(inverse, inner)]
        level += 1
    weights = []
    for h in range(heads):
        k = keys[h // repeat]
        v = value_ref[0][:, h * DV : (h + 1) * DV]
        b = beta[:, h : h + 1]
        right = jnp.concatenate([(b * start[:, h : h + 1]) * k, b * v], axis=1)
        weights.append(dot(inverse[h], right))
        solve_ref[0, h] = inverse[h]
    values = []
    for h in range(heads):
        state = state_ref[h].astype(BF16)
        start_ref[0, h] = state
        solved = weights[h]
        base = jnp.concatenate([jnp.zeros((CHUNK, DK), F32), solved[:, DK:]], axis=1)
        values.append((base - dot(solved[:, :DK], state)).astype(BF16))
    for h in range(heads):
        k, q = keys[h // repeat], queries[h // repeat]
        state = state_ref[h]
        out = dot(start[:, h : h + 1] * q, state) + dot(scores[h], values[h])
        map_ref[:, h * DK : (h + 1) * DK] = out[:, :DK].astype(BF16)
        local_ref[:, h * DV : (h + 1) * DV] = out[:, DK:]
        state = total[:, h : h + 1] * state + dot(end[:, h : h + 1] * k, values[h], TN)
        state_ref[h] = state
        total_ref[h] = state.astype(BF16)


def output_kernel(
    local_ref,
    map_ref,
    gate_ref,
    delta_ref,
    state_ref,
    gain_ref,
    hidden_ref,
    delta_gate_ref,
    delta_out_ref,
    delta_state_ref,
    total_ref,
):
    heads = state_ref.shape[0]
    step = pl.program_id(0)
    gain = gain_ref[...]
    for h in range(heads):
        cols = slice(h * DV, (h + 1) * DV)
        reach = map_ref[:, cols]
        out = local_ref[:, cols] + dot(reach, state_ref[h])
        gate = gate_ref[0][:, cols]
        delta = delta_ref[:, cols]
        scale = lax.rsqrt(row_sum(out * out) * (1.0 / DV) + EPS)
        normed = out * scale
        share = sigmoid(gate)
        silu = gate * share
        scaled = normed * gain
        hidden_ref[:, cols] = (scaled * silu).astype(BF16)
        delta_gate_ref[:, cols] = (
            delta * scaled * (share * (1.0 + gate * (1.0 - share)))
        ).astype(BF16)
        delta_normed = delta * gain * silu
        delta_out = scale * (
            delta_normed - normed * (row_sum(normed * delta_normed) * (1.0 / DV))
        )
        delta_out = delta_out.astype(BF16)
        delta_out_ref[:, cols] = delta_out
        part = dot(reach, delta_out, TN)

        @pl.when(step == 0)
        def _():
            total_ref[h] = part

        @pl.when(step > 0)
        def _():
            total_ref[h] += part

        delta_state_ref[h] = total_ref[h].astype(BF16)


def backward_kernel(
    query_key_ref,
    value_ref,
    decay_beta_ref,
    bias_ref,
    scale_ref,
    resets_ref,
    solve_ref,
    start_ref,
    state_in_ref,
    delta_out_ref,
    delta_final_ref,
    delta_query_key_ref,
    delta_value_ref,
    delta_decay_beta_ref,
    carry_ref,
):
    heads = carry_ref.shape[0]
    key_heads = query_key_ref.shape[2] // DK
    repeat = heads // key_heads
    row, col = grid_of(CHUNK)

    @pl.when(pl.program_id(0) == 0)
    def _():
        carry_ref[...] = delta_final_ref[...].astype(F32)

    beta, cum_col, cum_row, same, start, end, total, resets = decays(
        decay_beta_ref, bias_ref, scale_ref, resets_ref
    )
    strict = row > col
    lane = lax.broadcasted_iota(jnp.int32, (CHUNK, heads), 1)
    lane_one = lax.broadcasted_iota(jnp.int32, (1, heads), 1)
    state_of, value_of, right_of = [], [], []
    qs, ks, q_inv, k_inv, grams = [], [], [], [], []
    for g in range(key_heads):
        q, qi = unit_rows(head(query_key_ref, 0, g))
        k, ki = unit_rows(head(query_key_ref, 1, g))
        q = q * QUERY_SCALE
        qs.append(q)
        ks.append(k)
        q_inv.append(qi)
        k_inv.append(ki)
        grams.append((dot(k, k, NT), dot(q, k, NT)))
    for h in range(heads):
        before = start_ref[0, h]
        state = dot(before[:, :DK], state_in_ref[h]) + before[:, DK:].astype(F32)
        state_of.append(state.astype(BF16))
    for h in range(heads):
        k = ks[h // repeat]
        v = value_ref[0][:, h * DV : (h + 1) * DV]
        seen = dot(k, state_of[h])
        right_of.append(beta[:, h : h + 1] * (v - start[:, h : h + 1] * seen))
    for h in range(heads):
        value_of.append(dot(solve_ref[0, h], right_of[h]).astype(BF16))
    decay_of, delta_value_of, delta_right_of = [], [], []
    for h in range(heads):
        decay = pair_decay(cum_col, cum_row, same, h)
        decay_of.append(decay)
        k = ks[h // repeat]
        delta_out = delta_out_ref[:, h * DV : (h + 1) * DV]
        carry = carry_ref[h].astype(BF16)
        delta_value_of.append(
            dot(decay * grams[h // repeat][1], delta_out, TN)
            + dot(end[:, h : h + 1] * k, carry)
        )
    for h in range(heads):
        delta_right_of.append(dot(solve_ref[0, h], delta_value_of[h], TN))
    sums = jnp.zeros((CHUNK, heads), F32)
    logits = jnp.zeros((CHUNK, heads), F32)
    tail = jnp.zeros((1, heads), F32)
    lower_rows = []
    for g in range(key_heads):
        q, k = qs[g], ks[g]
        key_gram, query_gram = grams[g]
        delta_q = jnp.zeros((CHUNK, DK), F32)
        delta_k = jnp.zeros((CHUNK, DK), F32)
        for h in range(g * repeat, (g + 1) * repeat):
            cols = slice(h * DV, (h + 1) * DV)
            b, s, e = beta[:, h : h + 1], start[:, h : h + 1], end[:, h : h + 1]
            delta_out = delta_out_ref[:, cols]
            delta_right = delta_right_of[h]
            delta_value_ref[:, cols] = (b * delta_right).astype(BF16)
            pseudo = value_of[h]
            both = jnp.concatenate([delta_out, delta_right.astype(BF16)], axis=0)
            carry = carry_ref[h]
            pairs = dot(both, pseudo, NT)
            states = dot(both, state_of[h], NT)
            decay = decay_of[h]
            pair_q = decay * pairs[:CHUNK]
            pair_k = jnp.where(strict, (-b) * decay * pairs[CHUNK:], 0.0)
            cross = pair_q * query_gram + pair_k * key_gram
            state_q = s * states[:CHUNK]
            state_k = (b * s) * states[CHUNK:]
            end_k = e * dot(pseudo, carry, NT)
            delta_q += dot(pair_q, k) + state_q
            delta_k += (
                dot(pair_k, k)
                + dot(
                    jnp.concatenate([pair_q, pair_k], axis=0),
                    jnp.concatenate([q, k], axis=0),
                    TN,
                )
                + end_k
                - state_k
            )
            ends = row_sum(end_k * k)
            column = row_sum(cross + state_q * q - state_k * k) - ends
            sums = jnp.where(lane == h, column, sums)
            lower_rows.append(jnp.sum(cross, axis=0, keepdims=True))
            held = total[:, h : h + 1] * jnp.sum(
                state_of[h].astype(F32) * carry, axis=(0, 1), keepdims=True
            )
            tail = jnp.where(lane_one == h, held + jnp.sum(ends, axis=0, keepdims=True), tail)
            logits = jnp.where(lane == h, row_sum(delta_right * pseudo.astype(F32)), logits)
            carry_ref[h] = total[:, h : h + 1] * carry + dot(
                jnp.concatenate([s * q, (-b * s) * k], axis=0), both, TN
            )
        delta_q = delta_q * QUERY_SCALE
        unit = q * (1.0 / QUERY_SCALE)
        delta_q = q_inv[g] * (delta_q - unit * row_sum(unit * delta_q))
        delta_k = k_inv[g] * (delta_k - k * row_sum(k * delta_k))
        delta_query_key_ref[0, :, g * DK : (g + 1) * DK] = delta_q.astype(BF16)
        delta_query_key_ref[1, :, g * DK : (g + 1) * DK] = delta_k.astype(BF16)
    upper = (row <= col).astype(F32)
    reset_col = dot((row == col).astype(F32), resets, NT)[:, 0:1]
    pad = -heads % 8
    if pad:
        lower_rows.append(jnp.zeros((pad, CHUNK), F32))
    below = jnp.concatenate(lower_rows, axis=0)
    delta_log = exact(upper, sums) - exact(upper, below, NT)[:, :heads] + tail
    delta_log = jnp.where(reset_col == 0.0, delta_log, 0.0)
    delta_decay_beta_ref[0] = (
        delta_log * (-scale_ref[...]) * sigmoid(decay_beta_ref[0])
    ).astype(BF16)
    delta_decay_beta_ref[1] = (logits * (1.0 - beta)).astype(BF16)


def chain_forward_kernel(totals_ref, states_ref):
    devices, heads = totals_ref.shape[0], totals_ref.shape[1]
    for h in range(heads):
        state = jnp.zeros(states_ref.shape[2:], F32)
        for i in range(devices):
            states_ref[i, h] = state.astype(BF16)
            if i < devices - 1:
                step = totals_ref[i, h]
                high = state.astype(BF16)
                low = state - high.astype(F32)
                state = (
                    dot(step[:, :DK], high) + dot(step[:, :DK], low) + step[:, DK:].astype(F32)
                )


def chain_backward_kernel(totals_ref, deltas_ref, states_ref):
    devices, heads = totals_ref.shape[0], totals_ref.shape[1]
    for h in range(heads):
        state = jnp.zeros(states_ref.shape[2:], F32)
        for i in reversed(range(devices)):
            states_ref[i, h] = state.astype(BF16)
            if i > 0:
                step = totals_ref[i, h]
                high = state.astype(BF16)
                low = state - high.astype(F32)
                state = (
                    dot(step[:, :DK], high, TN)
                    + dot(step[:, :DK], low, TN)
                    + deltas_ref[i, h].astype(F32)
                )


PARAMS = pltpu.CompilerParams(
    dimension_semantics=("arbitrary",), vmem_limit_bytes=56 * 1024 * 1024
)
INTERPRET = False


def whole(shape):
    return pl.BlockSpec(shape, lambda c: (0,) * len(shape))


def run_forward(query_key, value_gate, decay_beta, bias, scale, resets):
    tokens, heads = query_key.shape[1], decay_beta.shape[2]
    chunks = tokens // CHUNK
    key_width, value_width = query_key.shape[2], heads * DV
    return pl.pallas_call(
        forward_kernel,
        grid=(chunks,),
        in_specs=[
            pl.BlockSpec((2, CHUNK, key_width), lambda c: (0, c, 0)),
            pl.BlockSpec((1, CHUNK, value_width), lambda c: (0, c, 0)),
            pl.BlockSpec((2, CHUNK, heads), lambda c: (0, c, 0)),
            whole((1, heads)),
            whole((1, heads)),
            pl.BlockSpec((1, 1, CHUNK), lambda c: (c, 0, 0)),
        ],
        out_specs=[
            pl.BlockSpec((1, heads, CHUNK, CHUNK), lambda c: (c, 0, 0, 0)),
            pl.BlockSpec((1, heads, DK, DK + DV), lambda c: (c, 0, 0, 0)),
            pl.BlockSpec((CHUNK, value_width), lambda c: (c, 0)),
            pl.BlockSpec((CHUNK, value_width), lambda c: (c, 0)),
            whole((heads, DK, DK + DV)),
        ],
        out_shape=[
            jax.ShapeDtypeStruct((chunks, heads, CHUNK, CHUNK), BF16),
            jax.ShapeDtypeStruct((chunks, heads, DK, DK + DV), BF16),
            jax.ShapeDtypeStruct((tokens, value_width), BF16),
            jax.ShapeDtypeStruct((tokens, value_width), F32),
            jax.ShapeDtypeStruct((heads, DK, DK + DV), BF16),
        ],
        scratch_shapes=[pltpu.VMEM((heads, DK, DK + DV), F32)],
        compiler_params=PARAMS,
        interpret=INTERPRET,
        name="forward_blocks",
    )(query_key, value_gate, decay_beta, bias, scale, resets)


def run_output(local, reach, value_gate, delta_hidden, state_in, gain):
    tokens, value_width = local.shape
    heads = value_width // DV
    chunks = tokens // CHUNK
    block = pl.BlockSpec((CHUNK, value_width), lambda c: (c, 0))
    return pl.pallas_call(
        output_kernel,
        grid=(chunks,),
        in_specs=[
            block,
            block,
            pl.BlockSpec((1, CHUNK, value_width), lambda c: (1, c, 0)),
            block,
            whole((heads, DK, DV)),
            whole((1, DV)),
        ],
        out_specs=[block, block, block, whole((heads, DK, DV))],
        out_shape=[
            jax.ShapeDtypeStruct((tokens, value_width), BF16),
            jax.ShapeDtypeStruct((tokens, value_width), BF16),
            jax.ShapeDtypeStruct((tokens, value_width), BF16),
            jax.ShapeDtypeStruct((heads, DK, DV), BF16),
        ],
        scratch_shapes=[pltpu.VMEM((heads, DK, DV), F32)],
        compiler_params=PARAMS,
        interpret=INTERPRET,
        name="gated_norm",
    )(local, reach, value_gate, delta_hidden, state_in, gain)


def run_backward(
    query_key, value_gate, decay_beta, bias, scale, resets, solve, starts, state_in, delta_out, final
):
    tokens, heads = query_key.shape[1], decay_beta.shape[2]
    chunks = tokens // CHUNK
    key_width, value_width = query_key.shape[2], heads * DV
    last = chunks - 1
    return pl.pallas_call(
        backward_kernel,
        grid=(chunks,),
        in_specs=[
            pl.BlockSpec((2, CHUNK, key_width), lambda c: (0, last - c, 0)),
            pl.BlockSpec((1, CHUNK, value_width), lambda c: (0, last - c, 0)),
            pl.BlockSpec((2, CHUNK, heads), lambda c: (0, last - c, 0)),
            whole((1, heads)),
            whole((1, heads)),
            pl.BlockSpec((1, 1, CHUNK), lambda c: (last - c, 0, 0)),
            pl.BlockSpec((1, heads, CHUNK, CHUNK), lambda c: (last - c, 0, 0, 0)),
            pl.BlockSpec((1, heads, DK, DK + DV), lambda c: (last - c, 0, 0, 0)),
            whole((heads, DK, DV)),
            pl.BlockSpec((CHUNK, value_width), lambda c: (last - c, 0)),
            whole((heads, DK, DV)),
        ],
        out_specs=[
            pl.BlockSpec((2, CHUNK, key_width), lambda c: (0, last - c, 0)),
            pl.BlockSpec((CHUNK, value_width), lambda c: (last - c, 0)),
            pl.BlockSpec((2, CHUNK, heads), lambda c: (0, last - c, 0)),
        ],
        out_shape=[
            jax.ShapeDtypeStruct(query_key.shape, BF16),
            jax.ShapeDtypeStruct((tokens, value_width), BF16),
            jax.ShapeDtypeStruct(decay_beta.shape, BF16),
        ],
        scratch_shapes=[pltpu.VMEM((heads, DK, DV), F32)],
        compiler_params=PARAMS,
        interpret=INTERPRET,
        name="backward_blocks",
    )(query_key, value_gate, decay_beta, bias, scale, resets, solve, starts, state_in, delta_out, final)


def spread(array, devices):
    heads, depth, width = array.shape
    if heads >= devices:
        return array.reshape(devices, heads // devices, depth, width)
    cuts = devices // heads
    parts = array.reshape(heads, depth, cuts, width // cuts)
    return jnp.transpose(parts, (0, 2, 1, 3)).reshape(devices, 1, depth, width // cuts)


def gather_parts(parts, heads):
    devices, each, depth, width = parts.shape
    if heads >= devices:
        return parts.reshape(heads, depth, width)
    cuts = devices // heads
    parts = parts.reshape(heads, cuts, depth, width)
    return jnp.transpose(parts, (0, 2, 1, 3)).reshape(heads, depth, cuts * width)


def swap(parts):
    return lax.all_to_all(parts, "ctx", split_axis=0, concat_axis=0, tiled=True)


def chain_forward(totals):
    devices, heads = lax.axis_size("ctx"), totals.shape[0]
    if heads >= devices:
        parts = spread(totals, devices)
    else:
        maps = jnp.repeat(totals[:, :, :DK], devices // heads, axis=0)[:, None]
        parts = jnp.concatenate([maps, spread(totals[:, :, DK:], devices)], axis=-1)
    held = swap(parts)
    states = pl.pallas_call(
        chain_forward_kernel,
        out_shape=jax.ShapeDtypeStruct((*held.shape[:3], held.shape[3] - DK), BF16),
        interpret=INTERPRET,
        name="chain_forward",
    )(held)
    return gather_parts(swap(states), heads), held


def chain_backward(held, deltas):
    devices, heads = lax.axis_size("ctx"), deltas.shape[0]
    parts = swap(spread(deltas, devices))
    states = pl.pallas_call(
        chain_backward_kernel,
        out_shape=jax.ShapeDtypeStruct(parts.shape, BF16),
        interpret=INTERPRET,
        name="chain_backward",
    )(held, parts)
    return gather_parts(swap(states), heads)


def product(spec, a, b):
    return jnp.einsum(spec, a, b, preferred_element_type=F32)


def scatter(partial, axis, dimension):
    return lax.psum_scatter(partial.astype(BF16), axis, scatter_dimension=dimension, tiled=True)


def body(
    inputs,
    query_key_weight,
    value_gate_weight,
    decay_beta_weight,
    beta_bias,
    decay_scale,
    norm_gain,
    out_weight,
    boundaries,
    grad_mixed,
):
    tokens, heads = inputs.shape[0], beta_bias.shape[0]
    query_key = product("td,sdf->stf", inputs, query_key_weight)
    value_gate = product("td,sdf->stf", inputs, value_gate_weight)
    decay_beta = product("td,sdf->stf", inputs, decay_beta_weight)
    bias, scale = beta_bias.reshape(1, heads), decay_scale.reshape(1, heads)
    resets = boundaries.reshape(tokens // CHUNK, 1, CHUNK)
    solve, starts, reach, local, totals = run_forward(
        query_key, value_gate, decay_beta, bias, scale, resets
    )
    state_in, held = chain_forward(totals)
    delta_hidden = product("td,fd->tf", grad_mixed, out_weight)
    hidden, delta_gate, delta_out, delta_state = run_output(
        local, reach, value_gate, delta_hidden, state_in, norm_gain.reshape(1, DV)
    )
    mixed = scatter(product("tf,fd->td", hidden, out_weight), "head", 1)
    grad_out_weight = scatter(product("tf,td->fd", hidden, grad_mixed), "ctx", 1)
    grad_gate = scatter(product("td,tf->df", inputs, delta_gate), "ctx", 0)
    delta_final = chain_backward(held, delta_state)
    delta_query_key, delta_value, delta_decay_beta = run_backward(
        query_key,
        value_gate,
        decay_beta,
        bias,
        scale,
        resets,
        solve,
        starts,
        state_in,
        delta_out,
        delta_final,
    )
    grad_value = scatter(product("td,tf->df", inputs, delta_value), "ctx", 0)
    grad_query_key = scatter(product("td,stf->sdf", inputs, delta_query_key), "ctx", 1)
    grad_decay_beta = scatter(product("td,stf->sdf", inputs, delta_decay_beta), "ctx", 1)
    grad_rows = (
        product("tf,df->td", delta_gate, value_gate_weight[1])
        + product("stf,sdf->td", delta_query_key, query_key_weight)
        + product("tf,df->td", delta_value, value_gate_weight[0])
        + product("stf,sdf->td", delta_decay_beta, decay_beta_weight)
    )
    grad_inputs = scatter(grad_rows, "head", 1)
    return (
        mixed,
        grad_inputs,
        grad_query_key.astype(F32),
        jnp.stack([grad_value, grad_gate]).astype(F32),
        grad_decay_beta.astype(F32),
        grad_out_weight.astype(F32),
    )


def solution(mesh):
    in_specs = (
        P("ctx", None),
        P(None, None, "head"),
        P(None, None, "head"),
        P(None, None, "head"),
        P("head"),
        P("head"),
        P(),
        P("head", None),
        P("ctx"),
        P("ctx", None),
    )
    out_specs = (
        P("ctx", "head"),
        P("ctx", "head"),
        P(None, "ctx", "head"),
        P(None, "ctx", "head"),
        P(None, "ctx", "head"),
        P("head", "ctx"),
    )
    return jax.shard_map(body, mesh=mesh, in_specs=in_specs, out_specs=out_specs, check_vma=False)
```

time: 1600 us -> 487 us (0.30)
  matrix products: 611 us -> 64.8 us
  other arithmetic: 427 us -> 6.07 us
  local copies, waits for them, and re-layouts: 216 us -> 8.57 us
  Pallas kernels: 0 us -> 61.8 us
  starting transfers between devices: 51.4 us -> 3.93 us
  blocking collectives: 0 us -> 37 us
  waiting for transfers between devices: 260 us -> 289 us
    dot_general x216 -> x14, matrix products: 585 us -> 64.8 us  [product(): return jnp.einsum(spec, a, b, preferred_element_type=F32)]
    another operation x11 -> x0, other arithmetic: 329 us -> none  [the longest x4 317 us: span_terms(): jax.scipy.linalg.solve_triangular(system, right_side, lower=True, unit_di...]
    reduce_scatter x6 -> x7, waiting for transfers between devices: 200 us -> 289 us  [scatter(): lax.psum_scatter(partial.astype(BF16), axis, scatter_dimension=dimension,...]
    pallas_call x0 -> x5, Pallas kernels: none -> 61.8 us  [the longest x1 23.4 us: run_backward(): pl.pallas_call(backward_kernel, grid=(chunks,), in_specs=[pl.BlockSpec((2...]
    ppermute x14 -> x0, waiting for transfers between devices: 60.2 us -> none  [shifted(): return lax.ppermute(block, axis, route)]
    reduce_sum x29 -> x0, other arithmetic: 53.1 us -> none  [the longest x16 19.3 us: advance(): block_retained_decay[:, None, None] * carried_state]
    ppermute x14 -> x0, starting transfers between devices: 50.8 us -> none  [shifted(): return lax.ppermute(block, axis, route)]
    dynamic_update_slice x40 -> x0, local copies, waits for them, and re-layouts: 42.3 us -> none  [run_spans(): final, produced_output = lax.scan(advance, state_in, moved)]
  transfers between devices with their start and end apart: 20 -> 8, of which waited for: 18 -> 7; matrix products, arithmetic and copies ran while one was open for 11% -> 12% of each run, Pallas kernels for 0% -> 0%
where the time goes in v1:
time: 487 us; the launch traced here: 486 us
  waiting for transfers between devices  289 us (59%)
  matrix products  64.8 us (13%)
  Pallas kernels  61.8 us (13%)
  blocking collectives  37 us (8%)
  between operations  14.3 us (3%)
  local copies, waits for them, and re-layouts  8.57 us (2%)
  other arithmetic  6.07 us (1%)
    reduce_scatter x7, waiting for transfers between devices, scatter(): lax.psum_scatter(partial.astype(BF16), axis, scatter_dimension=dimension,...  289 us
    dot_general x14, matrix products, product(): return jnp.einsum(spec, a, b, preferred_element_type=F32)  64.8 us
    all_to_all x3, blocking collectives, swap(): return lax.all_to_all(parts, 'ctx', split_axis=0, concat_axis=0, tiled=True)  37 us
    pallas_call x1, Pallas kernels, run_backward(): pl.pallas_call(backward_kernel, grid=(chunks,), in_specs=[pl.BlockSpec((2...  23.4 us
    pallas_call x1, Pallas kernels, run_output(): pl.pallas_call(output_kernel, grid=(chunks,), in_specs=[block, block, pl....  17.3 us
    pallas_call x1, Pallas kernels, run_forward(): pl.pallas_call(forward_kernel, grid=(chunks,), in_specs=[pl.BlockSpec((2,...  15.3 us
  transfers between devices with their start and end apart: 8, of which 7 were waited for; matrix products, arithmetic and copies ran while one was open for 12% of the time, Pallas kernels for 0%

profile of v1, /device:TPU:0, one launch (start us, length us, event | category | flops | bytes accessed | tf_op | source)
XLA Modules:
  0.0 485.6 jit_solution(1287033093946713151)
XLA Ops:
  8.8 9.6 %convolution_bitcast_fusion.value_ref.gate_ref = f32[2,512,1024]{2,1,0:T(8,128)} fusion(bf16[2,2048,1024]{2,1,0:T(8,128)(2,1)} %param.12, bf16[512,2048]{1,0:T(8,128)(2,1)S(1)} %copy-done), kind=kOutput, calls=%fused_computation.17 | convolution fusion | flops 4294967296 | bytes 14680064 | tf_op jit(solution)/shard_map/td,sdf->stf/dot_general | solution.py:557
  18.4 3.6 fusion.16.query_key_ref
  23.6 15.3 %forward_blocks.1 = (bf16[4,8,128,128]{3,2,1,0:T(8,128)(2,1)}, bf16[4,8,128,256]{3,2,1,0:T(8,128)(2,1)}, bf16[512,1024]{1,0:T(8,128)(2,1)}, f32[512,1024]{1,0:T(8,128)}, bf16[8,128,256]{2,1,0:T(8,128)(2,1)}) custom-call(f32[2,512,512]{2,1,0:T(8,128)} %fusion.16.query_key_ref, f32[2,512,1024]{2,1,0:T(8,128)} %convolution_bitcast_fusion.value_ref.gate_ref, ...), custom_call_target="tpu_custom_call" | custom-call | tf_op jit(solution)/shard_map/forward_blocks/pallas_call | solution.py:403
  38.9 15.0 %all_to_all.20.totals_ref = bf16[8,1,128,256]{3,2,1,0:T(8,128)(2,1)} all-to-all(bf16[8,1,128,256]{3,2,1,0:T(8,128)(2,1)} %bitcast.79), channel_id=1, replica_groups=mesh['ctx'=8,'head'=4] {'ctx'}, dimensions={0} | all-to-all | bytes 1048576 | tf_op jit(solution)/shard_map/all_to_all | solution.py:524
  53.9 2.8 chain_forward.1
  56.7 3.4 all-to-all-start.1
  60.2 6.6 %fusion.22.delta_ref = f32[512,1024]{1,0:T(8,128)} fusion(bf16[512,2048]{1,0:T(8,128)(2,1)} %param.19, bf16[1024,2048]{1,0:T(8,128)(2,1)} %param.17), kind=kOutput, calls=%fused_computation.28 | convolution fusion | flops 2147483648 | bytes 8388608 | tf_op jit(solution)/shard_map/td,fd->tf/dot_general | solution.py:557
  67.7 17.3 %gated_norm.1 = (bf16[512,1024]{1,0:T(8,128)(2,1)}, bf16[512,1024]{1,0:T(8,128)(2,1)}, bf16[512,1024]{1,0:T(8,128)(2,1)}, bf16[8,128,128]{2,1,0:T(8,128)(2,1)}) custom-call(f32[512,1024]{1,0:T(8,128)} %get-tuple-element.18.local_ref, bf16[512,1024]{1,0:T(8,128)(2,1)} %get-tuple-element.19.map_ref, ...), custom_call_target="tpu_custom_call" | custom-call | tf_op jit(solution)/shard_map/gated_norm/pallas_call | solution.py:440
  85.0 11.0 %all_to_all.21.deltas_ref = bf16[8,1,128,128]{3,2,1,0:T(8,128)(2,1)} all-to-all(bf16[8,1,128,128]{3,2,1,0:T(8,128)(2,1)} %bitcast.82), channel_id=1, replica_groups=mesh['ctx'=8,'head'=4] {'ctx'}, dimensions={0} | all-to-all | bytes 524288 | tf_op jit(solution)/shard_map/all_to_all | solution.py:524
  96.0 2.9 chain_backward.1
  99.0 11.0 %all_to_all.22 = bf16[8,1,128,128]{3,2,1,0:T(8,128)(2,1)} all-to-all(bf16[8,1,128,128]{3,2,1,0:T(8,128)(2,1)} %chain_backward.1), channel_id=1, replica_groups=mesh['ctx'=8,'head'=4] {'ctx'}, dimensions={0} | all-to-all | bytes 524288 | tf_op jit(solution)/shard_map/all_to_all | solution.py:524
  109.9 23.4 %backward_blocks.1 = (bf16[2,512,512]{2,1,0:T(8,128)(2,1)}, bf16[512,1024]{1,0:T(8,128)(2,1)}, bf16[2,512,8]{2,1,0:T(8,128)(2,1)}) custom-call(f32[2,512,512]{2,1,0:T(8,128)} %fusion.16.query_key_ref, f32[2,512,1024]{2,1,0:T(8,128)} %convolution_bitcast_fusion.value_ref.gate_ref, f32[2,512,8]{2,1,0:T(8,128)} %fusion.19.decay_beta_ref, f32[1,8]{1,0:T(1,128)} %bitcast.86, ...), custom_call_target="tpu_custom_call" | custom-call | tf_op jit(solution)/shard_map/backward_blocks/pallas_call | solution.py:472
  133.3 2.0 fusion.8
  135.4 5.9 %convolution_convert_fusion = bf16[1024,2048]{1,0:T(8,128)(2,1)} fusion(bf16[512,1024]{1,0:T(8,128)(2,1)S(1)} %copy-done.8, bf16[512,2048]{1,0:T(8,128)(2,1)} %param.19), kind=kOutput, calls=%fused_computation.13 | convolution fusion | flops 2149580800 | bytes 7340032 | tf_op jit(solution)/shard_map/tf,td->fd/dot_general | solution.py:557
  142.6 4.3 convert_bitcast_fusion
  147.0 5.5 %convert_bitcast_fusion.1 = bf16[2048,1024]{0,1:T(8,128)(2,1)} fusion(bf16[512,1024]{1,0:T(8,128)(2,1)} %get-tuple-element.28, bf16[512,2048]{1,0:T(8,128)(2,1)S(1)} %copy-done), kind=kOutput, calls=%fused_computation.9 | convolution fusion | flops 2149580800 | bytes 7340032 | tf_op jit(solution)/shard_map/td,tf->df/dot_general | solution.py:557
  152.8 5.6 %convert_bitcast_fusion.2 = bf16[2,2048,512]{1,2,0:T(8,128)(2,1)} fusion(bf16[2,512,512]{2,1,0:T(8,128)(2,1)} %get-tuple-element.27, bf16[512,2048]{1,0:T(8,128)(2,1)S(1)} %copy-done), kind=kOutput, calls=%fused_computation.10 | convolution fusion | flops 2149580800 | bytes 7340032 | tf_op jit(solution)/shard_map/td,stf->sdf/dot_general | solution.py:557
  158.5 6.2 %convolution_convert_fusion.1 = bf16[512,2048]{1,0:T(8,128)(2,1)} fusion(bf16[512,1024]{1,0:T(8,128)(2,1)} %get-tuple-element.21, bf16[1024,2048]{1,0:T(8,128)(2,1)} %param.17), kind=kOutput, calls=%fused_computation.14 | convolution fusion | flops 2148532224 | bytes 7340032 | tf_op jit(solution)/shard_map/tf,fd->td/dot_general | solution.py:557
  164.7 4.7 fusion.4
  169.4 4.7 fusion.1
  174.2 2.4 fusion.23
  176.6 2.1 fusion
  180.1 41.6 %reduce-scatter.20.cloned.1.call-done = bf16[1024,256]{1,0:T(8,128)(2,1)} async-done(((bf16[1024,2048]{1,0:T(8,128)(2,1)}), bf16[1024,256]{1,0:T(8,128)(2,1)}) %reduce-scatter.20.cloned.1.call-update) | async-done | bytes 524304 | tf_op jit(solution)/shard_map/reduce_scatter | solution.py:561
  221.7 2.1 convert_element_type.59
  223.8 52.6 %reduce-scatter.16.cloned.1.call-done = bf16[256,1024]{0,1:T(8,128)(2,1)} async-done(((bf16[2048,1024]{0,1:T(8,128)(2,1)}), bf16[256,1024]{0,1:T(8,128)(2,1)}) %reduce-scatter.16.cloned.1.call-update) | async-done | bytes 524304 | tf_op jit(solution)/shard_map/reduce_scatter | solution.py:561
  276.4 55.0 %reduce-scatter.14.cloned.1.call-done = bf16[256,1024]{0,1:T(8,128)(2,1)} async-done(((bf16[2048,1024]{0,1:T(8,128)(2,1)}), bf16[256,1024]{0,1:T(8,128)(2,1)}) %reduce-scatter.14.cloned.1.call-update) | async-done | bytes 524304 | tf_op jit(solution)/shard_map/reduce_scatter | solution.py:561
  331.3 2.7 maximum_convert_fusion
  334.0 2.9 copy.37
  336.9 49.0 %reduce-scatter.12.cloned.1.call-done = bf16[2,256,512]{1,2,0:T(8,128)(2,1)} async-done(((bf16[2,2048,512]{1,2,0:T(8,128)(2,1)}), bf16[2,256,512]{1,2,0:T(8,128)(2,1)}) %reduce-scatter.12.cloned.1.call-update) | async-done | bytes 524304 | tf_op jit(solution)/shard_map/reduce_scatter | solution.py:561
  385.9 2.2 copy.36
  388.1 44.5 %reduce-scatter.8.cloned.1.call-done = bf16[512,512]{1,0:T(8,128)(2,1)} async-done(((bf16[512,2048]{1,0:T(8,128)(2,1)}), bf16[512,512]{1,0:T(8,128)(2,1)}) %reduce-scatter.8.cloned.1.call-update) | async-done | bytes 524304 | tf_op jit(solution)/shard_map/reduce_scatter | solution.py:561
  432.6 46.1 %reduce-scatter.10.cloned.1.call-done = bf16[512,512]{1,0:T(8,128)(2,1)} async-done(((bf16[512,2048]{1,0:T(8,128)(2,1)}), bf16[512,512]{1,0:T(8,128)(2,1)}) %reduce-scatter.10.cloned.1.call-update) | async-done | bytes 524304 | tf_op jit(solution)/shard_map/reduce_scatter | solution.py:561
  (38 shorter events, 7.2 us)
Async XLA Ops:
  7.2 1.6 copy-start
  7.2 11.2 %copy-start.4 = (bf16[2,2048,512]{2,1,0:T(8,128)(2,1)S(1)}, bf16[2,2048,512]{2,1,0:T(8,128)(2,1)}, u32[]{:S(2)}) copy-start(bf16[2,2048,512]{2,1,0:T(8,128)(2,1)} %param.11) | copy-start | bytes 12582916
  18.4 3.7 copy-start.3
  56.7 10.3 %all-to-all-start.1 = ((bf16[8,1,128,128]{3,2,1,0:T(8,128)(2,1)}), bf16[8,1,128,128]{3,2,1,0:T(8,128)(2,1)S(1)}, u32[]{:S(2)}, u32[]{:S(2)}) async-start(bf16[8,1,128,128]{3,2,1,0:T(8,128)(2,1)} %chain_forward.1), calls=%async_computation.1 | async-start | bytes 524288 | tf_op jit(solution)/shard_map/all_to_all | solution.py:524
  60.2 118.6 %reduce-scatter.18.cloned.1.call-start = ((), (), s32[]{:S(2)}) async-start(), calls=%async_computation.16 | async-start | bytes 73728 | tf_op jit(solution)/shard_map/reduce_scatter | solution.py:561
  67.0 0.7 copy-start.1
  109.9 25.5 %copy-start.8 = (bf16[512,1024]{1,0:T(8,128)(2,1)S(1)}, bf16[512,1024]{1,0:T(8,128)(2,1)}, u32[]{:S(2)}) copy-start(bf16[512,1024]{1,0:T(8,128)(2,1)} %get-tuple-element.21) | copy-start | bytes 3145732
  135.3 86.3 %reduce-scatter.20.cloned.1.call-start = ((), (), s32[]{:S(2)}) async-start(), calls=%async_computation.17 | async-start | bytes 4718592 | tf_op jit(solution)/shard_map/reduce_scatter | solution.py:561
  141.3 1.2 copy-start.6
  141.4 135.0 %reduce-scatter.16.cloned.1.call-start = ((), (), s32[]{:S(2)}) async-start(), calls=%async_computation.15 | async-start | bytes 4718592 | tf_op jit(solution)/shard_map/reduce_scatter | solution.py:561
  147.0 184.4 %reduce-scatter.14.cloned.1.call-start = ((), (), s32[]{:S(2)}) async-start(), calls=%async_computation.14 | async-start | bytes 4718592 | tf_op jit(solution)/shard_map/reduce_scatter | solution.py:561
  152.6 233.3 %reduce-scatter.12.cloned.1.call-start = ((), (), s32[]{:S(2)}) async-start(), calls=%async_computation.13 | async-start | bytes 4718592 | tf_op jit(solution)/shard_map/reduce_scatter | solution.py:561
  158.4 274.2 %reduce-scatter.8.cloned.1.call-start = ((), (), s32[]{:S(2)}) async-start(), calls=%async_computation.11 | async-start | bytes 2621440 | tf_op jit(solution)/shard_map/reduce_scatter | solution.py:561
  164.7 314.0 %reduce-scatter.10.cloned.1.call-start = ((), (), s32[]{:S(2)}) async-start(), calls=%async_computation.12 | async-start | bytes 2621440 | tf_op jit(solution)/shard_map/reduce_scatter | solution.py:561
  164.7 4.7 copy-start.9
  169.4 4.7 copy-start.5
  169.4 4.7 copy-start.7
  174.2 2.4 copy-start.2
Sparse Core Ops, SparseCore 0:
  135.5 31.0 reduce-scatter.17
  170.3 51.3 reduce-scatter.19
  225.0 51.2 reduce-scatter.15
  280.0 51.3 reduce-scatter.13
  334.5 51.3 reduce-scatter.11
  388.7 43.8 reduce-scatter.7
  435.5 43.1 reduce-scatter.9

commit v2 on v1

--- a/solution.py
+++ b/solution.py
@@ -12,6 +12,7 @@
 CHUNK = 128
 EPS = 1e-06
 QUERY_SCALE = DK ** (-0.5)
+LANES = 128
 
 F32 = jnp.float32
 BF16 = jnp.bfloat16
@@ -144,7 +145,7 @@
     weights = []
     for h in range(heads):
         k = keys[h // repeat]
-        v = value_ref[0][:, h * DV : (h + 1) * DV]
+        v = value_ref[:, h * DV : (h + 1) * DV]
         b = beta[:, h : h + 1]
         right = jnp.concatenate([(b * start[:, h : h + 1]) * k, b * v], axis=1)
         weights.append(dot(inverse[h], right))
@@ -181,13 +182,17 @@
     total_ref,
 ):
     heads = state_ref.shape[0]
-    step = pl.program_id(0)
     gain = gain_ref[...]
+
+    @pl.when(pl.program_id(0) == 0)
+    def _():
+        total_ref[...] = jnp.zeros_like(total_ref)
+
     for h in range(heads):
         cols = slice(h * DV, (h + 1) * DV)
         reach = map_ref[:, cols]
         out = local_ref[:, cols] + dot(reach, state_ref[h])
-        gate = gate_ref[0][:, cols]
+        gate = gate_ref[:, cols]
         delta = delta_ref[:, cols]
         scale = lax.rsqrt(row_sum(out * out) * (1.0 / DV) + EPS)
         normed = out * scale
@@ -204,17 +209,9 @@
         )
         delta_out = delta_out.astype(BF16)
         delta_out_ref[:, cols] = delta_out
-        part = dot(reach, delta_out, TN)
-
-        @pl.when(step == 0)
-        def _():
-            total_ref[h] = part
-
-        @pl.when(step > 0)
-        def _():
-            total_ref[h] += part
-
-        delta_state_ref[h] = total_ref[h].astype(BF16)
+        part = total_ref[h] + dot(reach, delta_out, TN)
+        total_ref[h] = part
+        delta_state_ref[h] = part.astype(BF16)
 
 
 def backward_kernel(
@@ -231,7 +228,6 @@
     delta_final_ref,
     delta_query_key_ref,
     delta_value_ref,
-    delta_decay_beta_ref,
     carry_ref,
 ):
     heads = carry_ref.shape[0]
@@ -266,7 +262,7 @@
         state_of.append(state.astype(BF16))
     for h in range(heads):
         k = ks[h // repeat]
-        v = value_ref[0][:, h * DV : (h + 1) * DV]
+        v = value_ref[:, h * DV : (h + 1) * DV]
         seen = dot(k, state_of[h])
         right_of.append(beta[:, h : h + 1] * (v - start[:, h : h + 1] * seen))
     for h in range(heads):
@@ -338,8 +334,10 @@
         unit = q * (1.0 / QUERY_SCALE)
         delta_q = q_inv[g] * (delta_q - unit * row_sum(unit * delta_q))
         delta_k = k_inv[g] * (delta_k - k * row_sum(k * delta_k))
-        delta_query_key_ref[0, :, g * DK : (g + 1) * DK] = delta_q.astype(BF16)
-        delta_query_key_ref[1, :, g * DK : (g + 1) * DK] = delta_k.astype(BF16)
+        delta_query_key_ref[:, g * DK : (g + 1) * DK] = delta_q.astype(BF16)
+        delta_query_key_ref[:, (key_heads + g) * DK : (key_heads + g + 1) * DK] = (
+            delta_k.astype(BF16)
+        )
     upper = (row <= col).astype(F32)
     reset_col = dot((row == col).astype(F32), resets, NT)[:, 0:1]
     pad = -heads % 8
@@ -348,10 +346,12 @@
     below = jnp.concatenate(lower_rows, axis=0)
     delta_log = exact(upper, sums) - exact(upper, below, NT)[:, :heads] + tail
     delta_log = jnp.where(reset_col == 0.0, delta_log, 0.0)
-    delta_decay_beta_ref[0] = (
-        delta_log * (-scale_ref[...]) * sigmoid(decay_beta_ref[0])
+    delta_decay = delta_log * (-scale_ref[...]) * sigmoid(decay_beta_ref[0])
+    delta_beta = logits * (1.0 - beta)
+    rest = jnp.zeros((CHUNK, LANES - 2 * heads), F32)
+    delta_query_key_ref[:, 2 * key_heads * DK :] = jnp.concatenate(
+        [delta_decay, delta_beta, rest], axis=1
     ).astype(BF16)
-    delta_decay_beta_ref[1] = (logits * (1.0 - beta)).astype(BF16)
 
 
 def chain_forward_kernel(totals_ref, states_ref):
@@ -396,7 +396,7 @@
     return pl.BlockSpec(shape, lambda c: (0,) * len(shape))
 
 
-def run_forward(query_key, value_gate, decay_beta, bias, scale, resets):
+def run_forward(query_key, value, decay_beta, bias, scale, resets):
     tokens, heads = query_key.shape[1], decay_beta.shape[2]
     chunks = tokens // CHUNK
     key_width, value_width = query_key.shape[2], heads * DV
@@ -405,7 +405,7 @@
         grid=(chunks,),
         in_specs=[
             pl.BlockSpec((2, CHUNK, key_width), lambda c: (0, c, 0)),
-            pl.BlockSpec((1, CHUNK, value_width), lambda c: (0, c, 0)),
+            pl.BlockSpec((CHUNK, value_width), lambda c: (c, 0)),
             pl.BlockSpec((2, CHUNK, heads), lambda c: (0, c, 0)),
             whole((1, heads)),
             whole((1, heads)),
@@ -429,10 +429,10 @@
         compiler_params=PARAMS,
         interpret=INTERPRET,
         name="forward_blocks",
-    )(query_key, value_gate, decay_beta, bias, scale, resets)
-
-
-def run_output(local, reach, value_gate, delta_hidden, state_in, gain):
+    )(query_key, value, decay_beta, bias, scale, resets)
+
+
+def run_output(local, reach, gate, delta_hidden, state_in, gain):
     tokens, value_width = local.shape
     heads = value_width // DV
     chunks = tokens // CHUNK
@@ -443,7 +443,7 @@
         in_specs=[
             block,
             block,
-            pl.BlockSpec((1, CHUNK, value_width), lambda c: (1, c, 0)),
+            block,
             block,
             whole((heads, DK, DV)),
             whole((1, DV)),
@@ -459,11 +459,11 @@
         compiler_params=PARAMS,
         interpret=INTERPRET,
         name="gated_norm",
-    )(local, reach, value_gate, delta_hidden, state_in, gain)
+    )(local, reach, gate, delta_hidden, state_in, gain)
 
 
 def run_backward(
-    query_key, value_gate, decay_beta, bias, scale, resets, solve, starts, state_in, delta_out, final
+    query_key, value, decay_beta, bias, scale, resets, solve, starts, state_in, delta_out, final
 ):
     tokens, heads = query_key.shape[1], decay_beta.shape[2]
     chunks = tokens // CHUNK
@@ -474,7 +474,7 @@
         grid=(chunks,),
         in_specs=[
             pl.BlockSpec((2, CHUNK, key_width), lambda c: (0, last - c, 0)),
-            pl.BlockSpec((1, CHUNK, value_width), lambda c: (0, last - c, 0)),
+            pl.BlockSpec((CHUNK, value_width), lambda c: (last - c, 0)),
             pl.BlockSpec((2, CHUNK, heads), lambda c: (0, last - c, 0)),
             whole((1, heads)),
             whole((1, heads)),
@@ -486,20 +486,18 @@
             whole((heads, DK, DV)),
         ],
         out_specs=[
-            pl.BlockSpec((2, CHUNK, key_width), lambda c: (0, last - c, 0)),
+            pl.BlockSpec((CHUNK, 2 * key_width + LANES), lambda c: (last - c, 0)),
             pl.BlockSpec((CHUNK, value_width), lambda c: (last - c, 0)),
-            pl.BlockSpec((2, CHUNK, heads), lambda c: (0, last - c, 0)),
         ],
         out_shape=[
-            jax.ShapeDtypeStruct(query_key.shape, BF16),
+            jax.ShapeDtypeStruct((tokens, 2 * key_width + LANES), BF16),
             jax.ShapeDtypeStruct((tokens, value_width), BF16),
-            jax.ShapeDtypeStruct(decay_beta.shape, BF16),
         ],
         scratch_shapes=[pltpu.VMEM((heads, DK, DV), F32)],
         compiler_params=PARAMS,
         interpret=INTERPRET,
         name="backward_blocks",
-    )(query_key, value_gate, decay_beta, bias, scale, resets, solve, starts, state_in, delta_out, final)
+    )(query_key, value, decay_beta, bias, scale, resets, solve, starts, state_in, delta_out, final)
 
 
 def spread(array, devices):
@@ -524,37 +522,256 @@
     return lax.all_to_all(parts, "ctx", split_axis=0, concat_axis=0, tiled=True)
 
 
-def chain_forward(totals):
+def spread_totals(totals):
     devices, heads = lax.axis_size("ctx"), totals.shape[0]
     if heads >= devices:
-        parts = spread(totals, devices)
-    else:
-        maps = jnp.repeat(totals[:, :, :DK], devices // heads, axis=0)[:, None]
-        parts = jnp.concatenate([maps, spread(totals[:, :, DK:], devices)], axis=-1)
-    held = swap(parts)
-    states = pl.pallas_call(
+        return spread(totals, devices)
+    maps = jnp.repeat(totals[:, :, :DK], devices // heads, axis=0)[:, None]
+    return jnp.concatenate([maps, spread(totals[:, :, DK:], devices)], axis=-1)
+
+
+def run_chain_forward(held):
+    return pl.pallas_call(
         chain_forward_kernel,
         out_shape=jax.ShapeDtypeStruct((*held.shape[:3], held.shape[3] - DK), BF16),
         interpret=INTERPRET,
         name="chain_forward",
     )(held)
-    return gather_parts(swap(states), heads), held
-
-
-def chain_backward(held, deltas):
-    devices, heads = lax.axis_size("ctx"), deltas.shape[0]
-    parts = swap(spread(deltas, devices))
-    states = pl.pallas_call(
+
+
+def run_chain_backward(held, deltas):
+    return pl.pallas_call(
         chain_backward_kernel,
-        out_shape=jax.ShapeDtypeStruct(parts.shape, BF16),
+        out_shape=jax.ShapeDtypeStruct(deltas.shape, BF16),
         interpret=INTERPRET,
         name="chain_backward",
-    )(held, parts)
-    return gather_parts(swap(states), heads)
+    )(held, deltas)
 
 
 def product(spec, a, b):
     return jnp.einsum(spec, a, b, preferred_element_type=F32)
+
+
+def projection_kernel(
+    inputs_ref,
+    query_key_weight_ref,
+    value_weight_ref,
+    decay_beta_weight_ref,
+    query_key_ref,
+    value_ref,
+    decay_beta_ref,
+):
+    inputs = inputs_ref[...]
+    query_key_ref[0] = dot(inputs, query_key_weight_ref[0])
+    query_key_ref[1] = dot(inputs, query_key_weight_ref[1])
+    value_ref[...] = dot(inputs, value_weight_ref[0])
+
+    @pl.when(pl.program_id(0) == 0)
+    def _():
+        decay_beta_ref[0] = dot(inputs, decay_beta_weight_ref[0])
+        decay_beta_ref[1] = dot(inputs, decay_beta_weight_ref[1])
+
+
+def run_projection(inputs, query_key_weight, value_gate_weight, decay_beta_weight):
+    tokens, model = inputs.shape
+    key_width, value_width = query_key_weight.shape[2], value_gate_weight.shape[2]
+    heads = decay_beta_weight.shape[2]
+    steps = 2
+    keys, values = key_width // steps, value_width // steps
+    return pl.pallas_call(
+        projection_kernel,
+        grid=(steps,),
+        in_specs=[
+            whole((tokens, model)),
+            pl.BlockSpec((2, model, keys), lambda j: (0, 0, j)),
+            pl.BlockSpec((1, model, values), lambda j: (0, 0, j)),
+            whole((2, model, heads)),
+        ],
+        out_specs=[
+            pl.BlockSpec((2, tokens, keys), lambda j: (0, 0, j)),
+            pl.BlockSpec((tokens, values), lambda j: (0, j)),
+            whole((2, tokens, heads)),
+        ],
+        out_shape=[
+            jax.ShapeDtypeStruct((2, tokens, key_width), F32),
+            jax.ShapeDtypeStruct((tokens, value_width), F32),
+            jax.ShapeDtypeStruct((2, tokens, heads), F32),
+        ],
+        compiler_params=PARAMS,
+        interpret=INTERPRET,
+        name="projection",
+    )(inputs, query_key_weight, value_gate_weight, decay_beta_weight)
+
+
+def input_gradient_kernel(
+    delta_query_key_ref,
+    delta_value_ref,
+    delta_gate_ref,
+    query_key_weight_ref,
+    value_gate_weight_ref,
+    decay_beta_weight_ref,
+    out_ref,
+):
+    rows = decay_beta_weight_ref.shape[1]
+    heads = decay_beta_weight_ref.shape[2]
+    packed = jnp.concatenate(
+        [
+            query_key_weight_ref[0],
+            query_key_weight_ref[1],
+            decay_beta_weight_ref[0],
+            decay_beta_weight_ref[1],
+            jnp.zeros((rows, LANES - 2 * heads), BF16),
+        ],
+        axis=1,
+    )
+    total = dot(delta_gate_ref[...], value_gate_weight_ref[1], NT)
+    total += dot(delta_value_ref[...], value_gate_weight_ref[0], NT)
+    total += dot(delta_query_key_ref[...], packed, NT)
+    out_ref[...] = total.astype(BF16)
+
+
+def run_input_gradient(
+    delta_query_key, delta_value, delta_gate, query_key_weight, value_gate_weight, decay_beta_weight
+):
+    tokens, model = delta_value.shape[0], query_key_weight.shape[1]
+    cut = 256
+
+    def weight(array):
+        return pl.BlockSpec((2, cut, array.shape[2]), lambda j: (0, j, 0))
+
+    return pl.pallas_call(
+        input_gradient_kernel,
+        grid=(model // cut,),
+        in_specs=[
+            whole(delta_query_key.shape),
+            whole(delta_value.shape),
+            whole(delta_gate.shape),
+            weight(query_key_weight),
+            weight(value_gate_weight),
+            weight(decay_beta_weight),
+        ],
+        out_specs=pl.BlockSpec((tokens, cut), lambda j: (0, j)),
+        out_shape=jax.ShapeDtypeStruct((tokens, model), BF16),
+        compiler_params=PARAMS,
+        interpret=INTERPRET,
+        name="input_gradient",
+    )(delta_query_key, delta_value, delta_gate, query_key_weight, value_gate_weight, decay_beta_weight)
+
+
+def together(*arrays):
+    return lax.optimization_barrier(arrays)
+
+
+def exchange(array, distance):
+    devices = range(lax.axis_size("ctx"))
+    return lax.ppermute(array, "ctx", [(i, i ^ distance) for i in devices])
+
+
+def block_of(step, place, flip):
+    x, y = (place // 2) % 2, place // 4
+    core = lax.rem(place + flip, 2)
+    across_x, across_y = 1 - step // 2, 1 - lax.rem(step, 2)
+    target_x, target_y = lax.rem(x + across_x, 2), lax.rem(y + across_y, 2)
+    return target_y * 4 + target_x * 2 + core
+
+
+def send_kernel(place_ref, left_ref, delta_ref, out_ref):
+    out_ref[...] = dot(left_ref[...], delta_ref[...], TN).astype(BF16)
+
+
+def keep_kernel(
+    place_ref, left_ref, delta_ref, arrived_ref, x_send_ref, x_keep_ref, y_send_ref, y_keep_ref
+):
+    step = pl.program_id(0)
+    cut = x_send_ref.shape[2]
+    total = dot(left_ref[...], delta_ref[...], TN) + arrived_ref[...].astype(F32)
+    total = total.astype(BF16)
+
+    @pl.when(step < 2)
+    def _():
+        x_send_ref[0] = total[:, :cut]
+
+    @pl.when(step >= 2)
+    def _():
+        x_keep_ref[0] = total[:, :cut]
+
+    @pl.when(lax.rem(step, 2) == 0)
+    def _():
+        y_send_ref[0] = total[:, cut:]
+
+    @pl.when(lax.rem(step, 2) == 1)
+    def _():
+        y_keep_ref[0] = total[:, cut:]
+
+
+def halving_start(place, left, delta):
+    tokens, width = delta.shape
+    rows = left.shape[1] // 8
+    send = pl.pallas_call(
+        send_kernel,
+        grid_spec=pltpu.PrefetchScalarGridSpec(
+            num_scalar_prefetch=1,
+            grid=(4,),
+            in_specs=[
+                pl.BlockSpec((tokens, rows), lambda i, place: (0, block_of(i, place[0], 1))),
+                pl.BlockSpec((tokens, width), lambda i, place: (0, 0)),
+            ],
+            out_specs=pl.BlockSpec((rows, width), lambda i, place: (i, 0)),
+        ),
+        out_shape=jax.ShapeDtypeStruct((4 * rows, width), BF16),
+        compiler_params=PARAMS,
+        interpret=INTERPRET,
+        name="send_rows",
+    )(place, left, delta)
+    return exchange(send, 1)
+
+
+def halving_keep(place, left, delta, arrived):
+    tokens, width = delta.shape
+    rows = left.shape[1] // 8
+    cut = -(-(width // 2) // LANES) * LANES
+    return pl.pallas_call(
+        keep_kernel,
+        grid_spec=pltpu.PrefetchScalarGridSpec(
+            num_scalar_prefetch=1,
+            grid=(4,),
+            in_specs=[
+                pl.BlockSpec((tokens, rows), lambda i, place: (0, block_of(i, place[0], 0))),
+                pl.BlockSpec((tokens, width), lambda i, place: (0, 0)),
+                pl.BlockSpec((rows, width), lambda i, place: (i, 0)),
+            ],
+            out_specs=[
+                pl.BlockSpec((1, rows, cut), lambda i, place: (jnp.minimum(i, 1), 0, 0)),
+                pl.BlockSpec((1, rows, cut), lambda i, place: (jnp.maximum(i - 2, 0), 0, 0)),
+                pl.BlockSpec((1, rows, width - cut), lambda i, place: (i // 2, 0, 0)),
+                pl.BlockSpec((1, rows, width - cut), lambda i, place: (i // 2, 0, 0)),
+            ],
+        ),
+        out_shape=[
+            jax.ShapeDtypeStruct((2, rows, cut), BF16),
+            jax.ShapeDtypeStruct((2, rows, cut), BF16),
+            jax.ShapeDtypeStruct((2, rows, width - cut), BF16),
+            jax.ShapeDtypeStruct((2, rows, width - cut), BF16),
+        ],
+        compiler_params=PARAMS,
+        interpret=INTERPRET,
+        name="keep_rows",
+    )(place, left, delta, arrived)
+
+
+def halving_cross(x_send, x_keep, y_send, y_keep):
+    return x_keep, exchange(x_send, 2), y_keep, exchange(y_send, 4)
+
+
+def halving_last(a, a_arrived, b, b_arrived):
+    a_send = (a[0].astype(F32) + a_arrived[0].astype(F32)).astype(BF16)
+    b_send = (b[0].astype(F32) + b_arrived[0].astype(F32)).astype(BF16)
+    return a[1], a_arrived[1], exchange(a_send, 4), b[1], b_arrived[1], exchange(b_send, 2)
+
+
+def halving_sum(*pieces):
+    a, a_near, a_far, b, b_near, b_far = [piece.astype(F32) for piece in pieces]
+    return jnp.concatenate([a + a_near + a_far, b + b_near + b_far], axis=1)
 
 
 def scatter(partial, axis, dimension):
@@ -574,26 +791,46 @@
     grad_mixed,
 ):
     tokens, heads = inputs.shape[0], beta_bias.shape[0]
-    query_key = product("td,sdf->stf", inputs, query_key_weight)
-    value_gate = product("td,sdf->stf", inputs, value_gate_weight)
-    decay_beta = product("td,sdf->stf", inputs, decay_beta_weight)
+    key_width = query_key_weight.shape[2]
+    cubic = lax.axis_size("ctx") == 8
+    query_key, value, decay_beta = run_projection(
+        inputs, query_key_weight, value_gate_weight, decay_beta_weight
+    )
     bias, scale = beta_bias.reshape(1, heads), decay_scale.reshape(1, heads)
     resets = boundaries.reshape(tokens // CHUNK, 1, CHUNK)
     solve, starts, reach, local, totals = run_forward(
-        query_key, value_gate, decay_beta, bias, scale, resets
-    )
-    state_in, held = chain_forward(totals)
+        query_key, value, decay_beta, bias, scale, resets
+    )
+
+    held = swap(spread_totals(totals))
+    gate = product("td,df->tf", inputs, value_gate_weight[1])
+    held, gate = together(held, gate)
+    states = swap(run_chain_forward(held))
     delta_hidden = product("td,fd->tf", grad_mixed, out_weight)
+    states, delta_hidden = together(states, delta_hidden)
+    state_in = gather_parts(states, heads)
     hidden, delta_gate, delta_out, delta_state = run_output(
-        local, reach, value_gate, delta_hidden, state_in, norm_gain.reshape(1, DV)
-    )
-    mixed = scatter(product("tf,fd->td", hidden, out_weight), "head", 1)
-    grad_out_weight = scatter(product("tf,td->fd", hidden, grad_mixed), "ctx", 1)
-    grad_gate = scatter(product("td,tf->df", inputs, delta_gate), "ctx", 0)
-    delta_final = chain_backward(held, delta_state)
-    delta_query_key, delta_value, delta_decay_beta = run_backward(
+        local, reach, gate, delta_hidden, state_in, norm_gain.reshape(1, DV)
+    )
+
+    deltas = swap(spread(delta_state, lax.axis_size("ctx")))
+    partial_out = product("tf,fd->td", hidden, out_weight).astype(BF16)
+    deltas, partial_out = together(deltas, partial_out)
+    mixed = scatter(partial_out, "head", 1)
+    finals = swap(run_chain_backward(held, deltas))
+    if cubic:
+        place = lax.axis_index("ctx").astype(jnp.int32).reshape(1)
+        place, deltas = together(place, deltas)
+        gate_sent = halving_start(place, inputs, delta_gate)
+        out_sent = halving_start(place, grad_mixed, hidden)
+        gate_cut = halving_keep(place, inputs, delta_gate, gate_sent)
+        out_cut = halving_keep(place, grad_mixed, hidden, out_sent)
+        finals, gate_cut, out_cut = together(finals, gate_cut, out_cut)
+        gate_next, out_next = halving_cross(*gate_cut), halving_cross(*out_cut)
+    delta_final = gather_parts(finals, heads)
+    delta_query_key, delta_value = run_backward(
         query_key,
-        value_gate,
+        value,
         decay_beta,
         bias,
         scale,
@@ -604,23 +841,40 @@
         delta_out,
         delta_final,
     )
-    grad_value = scatter(product("td,tf->df", inputs, delta_value), "ctx", 0)
-    grad_query_key = scatter(product("td,stf->sdf", inputs, delta_query_key), "ctx", 1)
-    grad_decay_beta = scatter(product("td,stf->sdf", inputs, delta_decay_beta), "ctx", 1)
-    grad_rows = (
-        product("tf,df->td", delta_gate, value_gate_weight[1])
-        + product("stf,sdf->td", delta_query_key, query_key_weight)
-        + product("tf,df->td", delta_value, value_gate_weight[0])
-        + product("stf,sdf->td", delta_decay_beta, decay_beta_weight)
+    if cubic:
+        value_sent = halving_start(place, inputs, delta_value)
+        query_key_sent = halving_start(place, inputs, delta_query_key)
+        value_next = halving_cross(*halving_keep(place, inputs, delta_value, value_sent))
+        query_key_next = halving_cross(
+            *halving_keep(place, inputs, delta_query_key, query_key_sent)
+        )
+    grad_rows = run_input_gradient(
+        delta_query_key,
+        delta_value,
+        delta_gate,
+        query_key_weight,
+        value_gate_weight,
+        decay_beta_weight,
     )
     grad_inputs = scatter(grad_rows, "head", 1)
+    if cubic:
+        grad_gate = halving_sum(*halving_last(*gate_next))
+        grad_out = halving_sum(*halving_last(*out_next)).T
+        grad_value = halving_sum(*halving_last(*value_next))
+        packed = halving_sum(*halving_last(*query_key_next))
+    else:
+        grad_gate = scatter(product("td,tf->df", inputs, delta_gate), "ctx", 0).astype(F32)
+        grad_out = scatter(product("tf,td->fd", hidden, grad_mixed), "ctx", 1).astype(F32)
+        grad_value = scatter(product("td,tf->df", inputs, delta_value), "ctx", 0).astype(F32)
+        packed = scatter(product("td,tf->df", inputs, delta_query_key), "ctx", 0).astype(F32)
+    rest = packed[:, 2 * key_width :]
     return (
         mixed,
         grad_inputs,
-        grad_query_key.astype(F32),
-        jnp.stack([grad_value, grad_gate]).astype(F32),
-        grad_decay_beta.astype(F32),
-        grad_out_weight.astype(F32),
+        jnp.stack([packed[:, :key_width], packed[:, key_width : 2 * key_width]]),
+        jnp.stack([grad_value, grad_gate]),
+        jnp.stack([rest[:, :heads], rest[:, heads : 2 * heads]]),
+        grad_out,
     )
 
 

time: 487 us -> 254 us (0.52)
  waiting for transfers between devices: 289 us -> 42.3 us
  Pallas kernels: 61.8 us -> 118 us
  matrix products: 64.8 us -> 18.5 us
  blocking collectives: 37 us -> 0 us
  starting transfers between devices: 3.93 us -> 34.1 us
  other arithmetic: 6.07 us -> 17.3 us
    reduce_scatter x7 -> x2, waiting for transfers between devices: 289 us -> 0.01 us  [scatter(): lax.psum_scatter(partial.astype(BF16), axis, scatter_dimension=dimension,...]
    pallas_call x3 -> x13, Pallas kernels: 23.1 us -> 78.9 us  [the longest x4 22.7 us: halving_keep(): pl.pallas_call(keep_kernel, grid_spec=pltpu.PrefetchScalarGridSpec(num_sc...]
    dot_general x14 -> x3, matrix products: 64.8 us -> 18.5 us  [product(): return jnp.einsum(spec, a, b, preferred_element_type=F32)]
    ppermute x0 -> x20, waiting for transfers between devices: none -> 37.4 us  [exchange(): return lax.ppermute(array, 'ctx', [(i, i ^ distance) for i in devices])]
    all_to_all x3 -> x0, blocking collectives: 37 us -> none  [swap(): return lax.all_to_all(parts, 'ctx', split_axis=0, concat_axis=0, tiled=True)]
    ppermute x0 -> x20, starting transfers between devices: none -> 18.1 us  [exchange(): return lax.ppermute(array, 'ctx', [(i, i ^ distance) for i in devices])]
    all_to_all x1 -> x4, starting transfers between devices: 3.41 us -> 15.8 us  [swap(): return lax.all_to_all(parts, 'ctx', split_axis=0, concat_axis=0, tiled=True)]
    add x0 -> x8, other arithmetic: none -> 6.45 us  [halving_sum(): return jnp.concatenate([a + a_near + a_far, b + b_near + b_far], axis=1)]
  transfers between devices with their start and end apart: 8 -> 26, of which waited for: 7 -> 10; matrix products, arithmetic and copies ran while one was open for 12% -> 15% of each run, Pallas kernels for 0% -> 33%
where the time goes in v2:
time: 254 us; the launch traced here: 253 us
  Pallas kernels  118 us (46%)
  waiting for transfers between devices  42.3 us (17%)
  starting transfers between devices  34.1 us (13%)
  matrix products  18.5 us (7%)
  other arithmetic  17.3 us (7%)
  between operations  14.3 us (6%)
  local copies, waits for them, and re-layouts  7.88 us (3%)
    ppermute x20, waiting for transfers between devices, exchange(): return lax.ppermute(array, 'ctx', [(i, i ^ distance) for i in devices])  37.4 us
    pallas_call x1, Pallas kernels, run_backward(): pl.pallas_call(backward_kernel, grid=(chunks,), in_specs=[pl.BlockSpec((2...  23.8 us
    pallas_call x4, Pallas kernels, halving_keep(): pl.pallas_call(keep_kernel, grid_spec=pltpu.PrefetchScalarGridSpec(num_sc...  22.7 us
    pallas_call x4, Pallas kernels, halving_start(): pl.pallas_call(send_kernel, grid_spec=pltpu.PrefetchScalarGridSpec(num_sc...  19.7 us
    dot_general x3, matrix products, product(): return jnp.einsum(spec, a, b, preferred_element_type=F32)  18.5 us
    ppermute x20, starting transfers between devices, exchange(): return lax.ppermute(array, 'ctx', [(i, i ^ distance) for i in devices])  18.1 us
    all_to_all x4, starting transfers between devices, swap(): return lax.all_to_all(parts, 'ctx', split_axis=0, concat_axis=0, tiled=True)  15.8 us
    pallas_call x1, Pallas kernels, run_forward(): pl.pallas_call(forward_kernel, grid=(chunks,), in_specs=[pl.BlockSpec((2,...  15.5 us
  transfers between devices with their start and end apart: 26, of which 10 were waited for; matrix products, arithmetic and copies ran while one was open for 15% of the time, Pallas kernels for 33%

profile of v2, /device:TPU:0, one launch (start us, length us, event | category | flops | bytes accessed | tf_op | source)
XLA Modules:
  0.0 252.6 jit_solution(1784944637756414807)
XLA Ops:
  7.2 2.2 copy.22.decay_beta_weight_ref
  9.3 10.6 %projection.1 = (f32[2,512,512]{2,1,0:T(8,128)}, f32[512,1024]{1,0:T(8,128)}, f32[2,512,8]{2,1,0:T(8,128)}) custom-call(bf16[512,2048]{1,0:T(8,128)(2,1)} %left_ref.15, bf16[2,2048,512]{2,1,0:T(8,128)(2,1)} %query_key_weight_ref.3, bf16[2,2048,1024]{2,1,0:T(8,128)(2,1)} %value_gate_weight_ref.1, bf16[2,2048,8]{2,1,0:T(8,128)(2,1)} %copy.22.decay_beta_weight_ref), custom_call_target="tpu_custom_call" | custom-call | tf_op jit(solution)/shard_map/projection/pallas_call | solution.py:581
  19.9 15.5 %forward_blocks.1 = (bf16[4,8,128,128]{3,2,1,0:T(8,128)(2,1)}, bf16[4,8,128,256]{3,2,1,0:T(8,128)(2,1)}, bf16[512,1024]{1,0:T(8,128)(2,1)}, f32[512,1024]{1,0:T(8,128)}, bf16[8,128,256]{2,1,0:T(8,128)(2,1)}) custom-call(f32[2,512,512]{2,1,0:T(8,128)} %get-tuple-element.52.query_key_ref, f32[512,1024]{1,0:T(8,128)} %get-tuple-element.53.value_ref, ...), custom_call_target="tpu_custom_call" | custom-call | tf_op jit(solution)/shard_map/forward_blocks/pallas_call | solution.py:403
  35.4 5.2 %all-to-all-start = ((bf16[8,1,128,256]{3,2,1,0:T(8,128)(2,1)}), bf16[8,1,128,256]{3,2,1,0:T(8,128)(2,1)S(1)}, u32[]{:S(2)}, u32[]{:S(2)}) async-start(bf16[8,1,128,256]{3,2,1,0:T(8,128)(2,1)} %bitcast.66), calls=%async_computation | async-start | bytes 1048576 | tf_op jit(solution)/shard_map/all_to_all | solution.py:522
  40.6 5.8 %fusion.gate_ref = f32[512,1024]{1,0:T(8,128)} fusion(bf16[512,2048]{1,0:T(8,128)(2,1)S(1)} %copy-done, bf16[2,2048,1024]{2,1,0:T(8,128)(2,1)} %value_gate_weight_ref.1), kind=kOutput, calls=%fused_computation | convolution fusion | flops 2147483648 | bytes 8388608 | tf_op jit(solution)/shard_map/td,df->tf/dot_general | solution.py:552
  46.4 3.9 %all-to-all-done.totals_ref = bf16[8,1,128,256]{3,2,1,0:T(8,128)(2,1)S(1)} async-done(((bf16[8,1,128,256]{3,2,1,0:T(8,128)(2,1)}), bf16[8,1,128,256]{3,2,1,0:T(8,128)(2,1)S(1)}, u32[]{:S(2)}, u32[]{:S(2)}) %all-to-all-start) | async-done | bytes 524320 | tf_op jit(solution)/shard_map/all_to_all | solution.py:522
  51.1 2.8 %chain_forward.1 = bf16[8,1,128,128]{3,2,1,0:T(8,128)(2,1)} custom-call(bf16[8,1,128,256]{3,2,1,0:T(8,128)(2,1)} %copy-done.1), custom_call_target="tpu_custom_call" | custom-call | tf_op jit(solution)/shard_map/chain_forward/pallas_call | solution.py:534
  54.0 3.4 %all-to-all-start.1 = ((bf16[8,1,128,128]{3,2,1,0:T(8,128)(2,1)}), bf16[8,1,128,128]{3,2,1,0:T(8,128)(2,1)S(1)}, u32[]{:S(2)}, u32[]{:S(2)}) async-start(bf16[8,1,128,128]{3,2,1,0:T(8,128)(2,1)} %chain_forward.1), calls=%async_computation.1 | async-start | bytes 524288 | tf_op jit(solution)/shard_map/all_to_all | solution.py:522
  57.4 6.5 %fusion.12.delta_ref = f32[512,1024]{1,0:T(8,128)} fusion(bf16[512,2048]{1,0:T(8,128)(2,1)} %left_ref.11, bf16[1024,2048]{1,0:T(8,128)(2,1)} %param.17), kind=kOutput, calls=%fused_computation.39 | convolution fusion | flops 2147483648 | bytes 8388608 | tf_op jit(solution)/shard_map/td,fd->tf/dot_general | solution.py:552
  65.0 6.8 %gated_norm.1 = (bf16[512,1024]{1,0:T(8,128)(2,1)}, bf16[512,1024]{1,0:T(8,128)(2,1)}, bf16[512,1024]{1,0:T(8,128)(2,1)}, bf16[8,128,128]{2,1,0:T(8,128)(2,1)}) custom-call(f32[512,1024]{1,0:T(8,128)} %get-tuple-element.55.local_ref, bf16[512,1024]{1,0:T(8,128)(2,1)} %get-tuple-element.56.map_ref, f32[512,1024]{1,0:T(8,128)} %fusion.gate_ref, ...), custom_call_target="tpu_custom_call" | custom-call | tf_op jit(solution)/shard_map/gated_norm/pallas_call | solution.py:440
  71.8 3.8 %all-to-all-start.2 = ((bf16[8,1,128,128]{3,2,1,0:T(8,128)(2,1)}), bf16[8,1,128,128]{3,2,1,0:T(8,128)(2,1)S(1)}, u32[]{:S(2)}, u32[]{:S(2)}) async-start(bf16[8,1,128,128]{3,2,1,0:T(8,128)(2,1)} %bitcast.67), calls=%async_computation.2 | async-start | bytes 524288 | tf_op jit(solution)/shard_map/all_to_all | solution.py:522
  75.8 6.2 %convolution_convert_fusion = bf16[512,2048]{1,0:T(8,128)(2,1)} fusion(bf16[512,1024]{1,0:T(8,128)(2,1)} %get-tuple-element.63.delta_ref, bf16[1024,2048]{1,0:T(8,128)(2,1)} %param.17), kind=kOutput, calls=%fused_computation.3 | convolution fusion | flops 2148532224 | bytes 7340032 | tf_op jit(solution)/shard_map/tf,fd->td/dot_general | solution.py:552
  82.5 4.9 %send_rows.4 = bf16[1024,1024]{1,0:T(8,128)(2,1)} custom-call(s32[1]{0:T(128)} %bitcast.8.place_ref, bf16[512,2048]{1,0:T(8,128)(2,1)} %left_ref.15, bf16[512,1024]{1,0:T(8,128)(2,1)} %get-tuple-element.70.delta_ref.delta_gate_ref), custom_call_target="tpu_custom_call" | custom-call | tf_op jit(solution)/shard_map/send_rows/pallas_call | solution.py:710
  87.4 4.9 %send_rows.5 = bf16[1024,1024]{1,0:T(8,128)(2,1)} custom-call(s32[1]{0:T(128)} %bitcast.8.place_ref, bf16[512,2048]{1,0:T(8,128)(2,1)} %left_ref.11, bf16[512,1024]{1,0:T(8,128)(2,1)} %get-tuple-element.63.delta_ref), custom_call_target="tpu_custom_call" | custom-call | tf_op jit(solution)/shard_map/send_rows/pallas_call | solution.py:710
  92.7 2.9 %chain_backward.1 = bf16[8,1,128,128]{3,2,1,0:T(8,128)(2,1)} custom-call(bf16[8,1,128,256]{3,2,1,0:T(8,128)(2,1)} %copy-done.1, bf16[8,1,128,128]{3,2,1,0:T(8,128)(2,1)} %copy-done.6), custom_call_target="tpu_custom_call" | custom-call | tf_op jit(solution)/shard_map/chain_backward/pallas_call | solution.py:543
  95.7 3.5 %all-to-all-start.3 = ((bf16[8,1,128,128]{3,2,1,0:T(8,128)(2,1)}), bf16[8,1,128,128]{3,2,1,0:T(8,128)(2,1)S(1)}, u32[]{:S(2)}, u32[]{:S(2)}) async-start(bf16[8,1,128,128]{3,2,1,0:T(8,128)(2,1)} %chain_backward.1), calls=%async_computation.4 | async-start | bytes 524288 | tf_op jit(solution)/shard_map/all_to_all | solution.py:522
  99.2 5.7 %keep_rows.4 = (bf16[2,256,512]{2,1,0:T(8,128)(2,1)}, bf16[2,256,512]{2,1,0:T(8,128)(2,1)}, bf16[2,256,512]{2,1,0:T(8,128)(2,1)}, bf16[2,256,512]{2,1,0:T(8,128)(2,1)}) custom-call(s32[1]{0:T(128)} %bitcast.8.place_ref, bf16[512,2048]{1,0:T(8,128)(2,1)} %left_ref.15, bf16[512,1024]{1,0:T(8,128)(2,1)} %get-tuple-element.70.delta_ref.delta_gate_ref, ...), custom_call_target="tpu_custom_call" | custom-call | tf_op jit(solution)/shard_map/keep_rows/pallas_call | solution.py:733
  106.1 5.5 %keep_rows.5 = (bf16[2,256,512]{2,1,0:T(8,128)(2,1)}, bf16[2,256,512]{2,1,0:T(8,128)(2,1)}, bf16[2,256,512]{2,1,0:T(8,128)(2,1)}, bf16[2,256,512]{2,1,0:T(8,128)(2,1)}) custom-call(s32[1]{0:T(128)} %bitcast.8.place_ref, bf16[512,2048]{1,0:T(8,128)(2,1)} %left_ref.11, bf16[512,1024]{1,0:T(8,128)(2,1)} %get-tuple-element.63.delta_ref, bf16[1024,1024]{1,0:T(8,128)(2,1)} %copy-done.4), custom_call_target="tpu_custom_call" | custom-call | tf_op jit(solution)/shard_map/keep_rows/pallas_call | solution.py:733
  111.7 2.1 collective-permute-start.14
  113.8 23.8 %backward_blocks.1 = (bf16[512,1152]{1,0:T(8,128)(2,1)}, bf16[512,1024]{1,0:T(8,128)(2,1)}) custom-call(f32[2,512,512]{2,1,0:T(8,128)} %get-tuple-element.52.query_key_ref, f32[512,1024]{1,0:T(8,128)} %get-tuple-element.53.value_ref, f32[2,512,8]{2,1,0:T(8,128)} %get-tuple-element.54.decay_beta_ref, f32[1,8]{1,0:T(1,128)} %bitcast.71, f32[1,8]{1,0:T(1,128)} %bitcast.73, ...), custom_call_target="tpu_custom_call" | custom-call | tf_op jit(solution)/shard_map/backward_blocks/pallas_call | solution.py:472
  137.5 4.8 %send_rows.7 = bf16[1024,1024]{1,0:T(8,128)(2,1)} custom-call(s32[1]{0:T(128)} %bitcast.8.place_ref, bf16[512,2048]{1,0:T(8,128)(2,1)} %left_ref.15, bf16[512,1024]{1,0:T(8,128)(2,1)} %get-tuple-element.81.delta_value_ref.delta_ref), custom_call_target="tpu_custom_call" | custom-call | tf_op jit(solution)/shard_map/send_rows/pallas_call | solution.py:710
  143.8 5.1 %send_rows.6 = bf16[1024,1152]{1,0:T(8,128)(2,1)} custom-call(s32[1]{0:T(128)} %bitcast.8.place_ref, bf16[512,2048]{1,0:T(8,128)(2,1)} %left_ref.15, bf16[512,1152]{1,0:T(8,128)(2,1)} %get-tuple-element.80.delta_query_key_ref.delta_ref), custom_call_target="tpu_custom_call" | custom-call | tf_op jit(solution)/shard_map/send_rows/pallas_call | solution.py:710
  149.8 13.4 %input_gradient.1 = bf16[512,2048]{1,0:T(8,128)(2,1)} custom-call(bf16[512,1152]{1,0:T(8,128)(2,1)} %get-tuple-element.80.delta_query_key_ref.delta_ref, bf16[512,1024]{1,0:T(8,128)(2,1)} %get-tuple-element.81.delta_value_ref.delta_ref, bf16[512,1024]{1,0:T(8,128)(2,1)} %get-tuple-element.70.delta_ref.delta_gate_ref, ...), custom_call_target="tpu_custom_call" | custom-call | tf_op jit(solution)/shard_map/input_gradient/pallas_call | solution.py:642
  165.0 1.5 collective-permute-start.15
  170.2 8.1 %collective-permute-done.16 = bf16[2,256,512]{2,1,0:T(8,128)(2,1)S(1)} collective-permute-done((bf16[2,256,512]{2,1,0:T(8,128)(2,1)}, bf16[2,256,512]{2,1,0:T(8,128)(2,1)S(1)}, u32[]{:S(2)}, u32[]{:S(2)}) %collective-permute-start.16) | collective-permute-done | bytes 524320 | tf_op jit(solution)/shard_map/ppermute | solution.py:667
  178.9 5.0 %collective-permute-done.15 = bf16[256,512]{1,0:T(8,128)(2,1)S(1)} collective-permute-done((bf16[256,512]{1,0:T(8,128)(2,1)S(1)}, bf16[256,512]{1,0:T(8,128)(2,1)S(1)}, u32[]{:S(2)}, u32[]{:S(2)}) %collective-permute-start.15) | collective-permute-done | bytes 262176 | tf_op jit(solution)/shard_map/ppermute | solution.py:667
  191.1 5.6 %keep_rows.7 = (bf16[2,256,512]{2,1,0:T(8,128)(2,1)}, bf16[2,256,512]{2,1,0:T(8,128)(2,1)}, bf16[2,256,512]{2,1,0:T(8,128)(2,1)}, bf16[2,256,512]{2,1,0:T(8,128)(2,1)}) custom-call(s32[1]{0:T(128)} %bitcast.8.place_ref, bf16[512,2048]{1,0:T(8,128)(2,1)} %left_ref.15, bf16[512,1024]{1,0:T(8,128)(2,1)} %get-tuple-element.81.delta_value_ref.delta_ref, ...), custom_call_target="tpu_custom_call" | custom-call | tf_op jit(solution)/shard_map/keep_rows/pallas_call | solution.py:733
  198.7 6.0 %keep_rows.6 = (bf16[2,256,640]{2,1,0:T(8,128)(2,1)}, bf16[2,256,640]{2,1,0:T(8,128)(2,1)}, bf16[2,256,512]{2,1,0:T(8,128)(2,1)}, bf16[2,256,512]{2,1,0:T(8,128)(2,1)}) custom-call(s32[1]{0:T(128)} %bitcast.8.place_ref, bf16[512,2048]{1,0:T(8,128)(2,1)} %left_ref.15, bf16[512,1152]{1,0:T(8,128)(2,1)} %get-tuple-element.80.delta_query_key_ref.delta_ref, ...), custom_call_target="tpu_custom_call" | custom-call | tf_op jit(solution)/shard_map/keep_rows/pallas_call | solution.py:733
  208.4 3.4 %collective-permute-done.10 = bf16[2,256,512]{2,1,0:T(8,128)(2,1)} collective-permute-done((bf16[2,256,512]{2,1,0:T(8,128)(2,1)}, bf16[2,256,512]{2,1,0:T(8,128)(2,1)}, u32[]{:S(2)}, u32[]{:S(2)}) %collective-permute-start.10) | collective-permute-done | bytes 524320 | tf_op jit(solution)/shard_map/ppermute | solution.py:667
  215.9 7.2 %collective-permute-done.5 = bf16[2,256,512]{2,1,0:T(8,128)(2,1)} collective-permute-done((bf16[2,256,512]{2,1,0:T(8,128)(2,1)}, bf16[2,256,512]{2,1,0:T(8,128)(2,1)}, u32[]{:S(2)}, u32[]{:S(2)}) %collective-permute-start.5) | collective-permute-done | bytes 524320 | tf_op jit(solution)/shard_map/ppermute | solution.py:667
  224.8 7.8 %collective-permute-done.11 = bf16[256,512]{1,0:T(8,128)(2,1)S(1)} collective-permute-done((bf16[256,512]{1,0:T(8,128)(2,1)S(1)}, bf16[256,512]{1,0:T(8,128)(2,1)S(1)}, u32[]{:S(2)}, u32[]{:S(2)}) %collective-permute-start.11) | collective-permute-done | bytes 262176 | tf_op jit(solution)/shard_map/ppermute | solution.py:667
  239.9 4.6 %collective-permute-done.4 = bf16[256,640]{1,0:T(8,128)(2,1)S(1)} collective-permute-done((bf16[256,640]{1,0:T(8,128)(2,1)}, bf16[256,640]{1,0:T(8,128)(2,1)S(1)}, u32[]{:S(2)}, u32[]{:S(2)}) %collective-permute-start.4) | collective-permute-done | bytes 327712 | tf_op jit(solution)/shard_map/ppermute | solution.py:667
  (98 shorter events, 40.1 us)
Async XLA Ops:
  19.9 20.7 %copy-start = (bf16[512,2048]{1,0:T(8,128)(2,1)S(1)}, bf16[512,2048]{1,0:T(8,128)(2,1)}, u32[]{:S(2)}) copy-start(bf16[512,2048]{1,0:T(8,128)(2,1)} %left_ref.15) | copy-start | bytes 6291460
  35.4 14.9 %all-to-all-start = ((bf16[8,1,128,256]{3,2,1,0:T(8,128)(2,1)}), bf16[8,1,128,256]{3,2,1,0:T(8,128)(2,1)S(1)}, u32[]{:S(2)}, u32[]{:S(2)}) async-start(bf16[8,1,128,256]{3,2,1,0:T(8,128)(2,1)} %bitcast.66), calls=%async_computation | async-start | bytes 1048576 | tf_op jit(solution)/shard_map/all_to_all | solution.py:522
  54.0 10.3 %all-to-all-start.1 = ((bf16[8,1,128,128]{3,2,1,0:T(8,128)(2,1)}), bf16[8,1,128,128]{3,2,1,0:T(8,128)(2,1)S(1)}, u32[]{:S(2)}, u32[]{:S(2)}) async-start(bf16[8,1,128,128]{3,2,1,0:T(8,128)(2,1)} %chain_forward.1), calls=%async_computation.1 | async-start | bytes 524288 | tf_op jit(solution)/shard_map/all_to_all | solution.py:522
  71.8 10.7 %all-to-all-start.2 = ((bf16[8,1,128,128]{3,2,1,0:T(8,128)(2,1)}), bf16[8,1,128,128]{3,2,1,0:T(8,128)(2,1)S(1)}, u32[]{:S(2)}, u32[]{:S(2)}) async-start(bf16[8,1,128,128]{3,2,1,0:T(8,128)(2,1)} %bitcast.67), calls=%async_computation.2 | async-start | bytes 524288 | tf_op jit(solution)/shard_map/all_to_all | solution.py:522
  75.5 170.2 %reduce-scatter.3.cloned.1.call-start = ((), (), s32[]{:S(2)}) async-start(), calls=%async_computation.6 | async-start | bytes 2621440 | tf_op jit(solution)/shard_map/reduce_scatter | solution.py:778
  87.4 11.8 %collective-permute-start = (bf16[1024,1024]{1,0:T(8,128)(2,1)}, bf16[1024,1024]{1,0:T(8,128)(2,1)}, u32[]{:S(2)}, u32[]{:S(2)}) collective-permute-start(bf16[1024,1024]{1,0:T(8,128)(2,1)} %send_rows.4), channel_id=1, source_target_pairs={{0,4},{4,0},{8,12},{12,8},{16,20},{20,16},{24,28},{28,24},{1,5},{5... | collective-permute-start | bytes 6291464 | tf_op jit(solution)/shard_map/ppermute | solution.py:667
  92.3 12.6 %collective-permute-start.1 = (bf16[1024,1024]{1,0:T(8,128)(2,1)}, bf16[1024,1024]{1,0:T(8,128)(2,1)S(1)}, u32[]{:S(2)}, u32[]{:S(2)}) collective-permute-start(bf16[1024,1024]{1,0:T(8,128)(2,1)} %send_rows.5), channel_id=1, source_target_pairs={{0,4},{4,0},{8,12},{12,8},{16,20},{20,16},{24,28},{28,24},{1,5},{5... | collective-permute-start | bytes 6291464 | tf_op jit(solution)/shard_map/ppermute | solution.py:667
  95.7 16.0 %all-to-all-start.3 = ((bf16[8,1,128,128]{3,2,1,0:T(8,128)(2,1)}), bf16[8,1,128,128]{3,2,1,0:T(8,128)(2,1)S(1)}, u32[]{:S(2)}, u32[]{:S(2)}) async-start(bf16[8,1,128,128]{3,2,1,0:T(8,128)(2,1)} %chain_backward.1), calls=%async_computation.4 | async-start | bytes 524288 | tf_op jit(solution)/shard_map/all_to_all | solution.py:522
  99.1 146.6 %reduce-scatter.5.cloned.1.call-start = ((), (), s32[]{:S(2)}) async-start(), calls=%async_computation.7 | async-start | bytes 2621440 | tf_op jit(solution)/shard_map/reduce_scatter | solution.py:778
  111.7 51.5 %collective-permute-start.14 = (bf16[2,256,512]{2,1,0:T(8,128)(2,1)}, bf16[2,256,512]{2,1,0:T(8,128)(2,1)}, u32[]{:S(2)}, u32[]{:S(2)}) collective-permute-start(bf16[2,256,512]{2,1,0:T(8,128)(2,1)} %get-tuple-element.93), channel_id=1, source_target_pairs={{0,16},{4,20},{8,24},{12,28},{16,0},{20,4},{24,8},{28,12},{1,17},{... | collective-permute-start | bytes 1572872 | tf_op jit(solution)/shard_map/ppermute | solution.py:667
  142.4 47.4 %collective-permute-start.7 = (bf16[1024,1024]{1,0:T(8,128)(2,1)}, bf16[1024,1024]{1,0:T(8,128)(2,1)S(1)}, u32[]{:S(2)}, u32[]{:S(2)}) collective-permute-start(bf16[1024,1024]{1,0:T(8,128)(2,1)} %send_rows.7), channel_id=1, source_target_pairs={{0,4},{4,0},{8,12},{12,8},{16,20},{20,16},{24,28},{28,24},{1,5},{5... | collective-permute-start | bytes 6291464 | tf_op jit(solution)/shard_map/ppermute | solution.py:667
  142.4 22.6 %collective-permute-start.12 = (bf16[2,256,512]{2,1,0:T(8,128)(2,1)}, bf16[2,256,512]{2,1,0:T(8,128)(2,1)}, u32[]{:S(2)}, u32[]{:S(2)}) collective-permute-start(bf16[2,256,512]{2,1,0:T(8,128)(2,1)} %get-tuple-element.91), channel_id=1, source_target_pairs={{0,8},{4,12},{8,0},{12,4},{16,24},{20,28},{24,16},{28,20},{1,9},{5... | collective-permute-start | bytes 1572872 | tf_op jit(solution)/shard_map/ppermute | solution.py:667
  148.9 49.8 %collective-permute-start.2 = (bf16[1024,1152]{1,0:T(8,128)(2,1)}, bf16[1024,1152]{1,0:T(8,128)(2,1)}, u32[]{:S(2)}, u32[]{:S(2)}) collective-permute-start(bf16[1024,1152]{1,0:T(8,128)(2,1)} %send_rows.6), channel_id=1, source_target_pairs={{0,4},{4,0},{8,12},{12,8},{16,20},{20,16},{24,28},{28,24},{1,5},{5... | collective-permute-start | bytes 7077896 | tf_op jit(solution)/shard_map/ppermute | solution.py:667
  149.2 18.4 %collective-permute-start.18 = (bf16[2,256,512]{2,1,0:T(8,128)(2,1)}, bf16[2,256,512]{2,1,0:T(8,128)(2,1)}, u32[]{:S(2)}, u32[]{:S(2)}) collective-permute-start(bf16[2,256,512]{2,1,0:T(8,128)(2,1)} %get-tuple-element.97), channel_id=1, source_target_pairs={{0,16},{4,20},{8,24},{12,28},{16,0},{20,4},{24,8},{28,12},{1,17},{... | collective-permute-start | bytes 1572872 | tf_op jit(solution)/shard_map/ppermute | solution.py:667
  163.2 15.7 %copy-start.8 = (bf16[2,256,512]{2,1,0:T(8,128)(2,1)S(1)}, bf16[2,256,512]{2,1,0:T(8,128)(2,1)}, u32[]{:S(2)}) copy-start(bf16[2,256,512]{2,1,0:T(8,128)(2,1)} %get-tuple-element.94) | copy-start | bytes 1572868
  163.2 22.1 %copy-start.11 = (bf16[2,256,512]{2,1,0:T(8,128)(2,1)S(1)}, bf16[2,256,512]{2,1,0:T(8,128)(2,1)}, u32[]{:S(2)}) copy-start(bf16[2,256,512]{2,1,0:T(8,128)(2,1)} %get-tuple-element.92) | copy-start | bytes 1572868
  163.2 15.0 %collective-permute-start.16 = (bf16[2,256,512]{2,1,0:T(8,128)(2,1)}, bf16[2,256,512]{2,1,0:T(8,128)(2,1)S(1)}, u32[]{:S(2)}, u32[]{:S(2)}) collective-permute-start(bf16[2,256,512]{2,1,0:T(8,128)(2,1)} %get-tuple-element.95), channel_id=1, source_target_pairs={{0,8},{4,12},{8,0},{12,4},{16,24},{20,28},{24,16},{28,20},{1,9},{5... | collective-permute-start | bytes 1572872 | tf_op jit(solution)/shard_map/ppermute | solution.py:667
  165.0 18.9 %collective-permute-start.15 = (bf16[256,512]{1,0:T(8,128)(2,1)S(1)}, bf16[256,512]{1,0:T(8,128)(2,1)S(1)}, u32[]{:S(2)}, u32[]{:S(2)}) collective-permute-start(bf16[256,512]{1,0:T(8,128)(2,1)S(1)} %fusion.9), channel_id=1, source_target_pairs={{0,8},{4,12},{8,0},{12,4},{16,24},{20,28},{24,16},{28,20},{1,9},{5... | collective-permute-start | bytes 786440 | tf_op jit(solution)/shard_map/ppermute | solution.py:667
  167.5 21.2 %copy-start.10 = (bf16[2,256,512]{2,1,0:T(8,128)(2,1)S(1)}, bf16[2,256,512]{2,1,0:T(8,128)(2,1)}, u32[]{:S(2)}) copy-start(bf16[2,256,512]{2,1,0:T(8,128)(2,1)} %get-tuple-element.96) | copy-start | bytes 1572868
  167.5 18.8 %collective-permute-start.13 = (bf16[256,512]{1,0:T(8,128)(2,1)S(1)}, bf16[256,512]{1,0:T(8,128)(2,1)S(1)}, u32[]{:S(2)}, u32[]{:S(2)}) collective-permute-start(bf16[256,512]{1,0:T(8,128)(2,1)S(1)} %fusion.8), channel_id=1, source_target_pairs={{0,16},{4,20},{8,24},{12,28},{16,0},{20,4},{24,8},{28,12},{1,17},{... | collective-permute-start | bytes 786440 | tf_op jit(solution)/shard_map/ppermute | solution.py:667
  178.3 10.5 %collective-permute-start.19 = (bf16[256,512]{1,0:T(8,128)(2,1)S(1)}, bf16[256,512]{1,0:T(8,128)(2,1)S(1)}, u32[]{:S(2)}, u32[]{:S(2)}) collective-permute-start(bf16[256,512]{1,0:T(8,128)(2,1)S(1)} %fusion.11), channel_id=1, source_target_pairs={{0,8},{4,12},{8,0},{12,4},{16,24},{20,28},{24,16},{28,20},{1,9},{5... | collective-permute-start | bytes 786440 | tf_op jit(solution)/shard_map/ppermute | solution.py:667
  183.9 14.6 %collective-permute-start.17 = (bf16[256,512]{1,0:T(8,128)(2,1)S(1)}, bf16[256,512]{1,0:T(8,128)(2,1)S(1)}, u32[]{:S(2)}, u32[]{:S(2)}) collective-permute-start(bf16[256,512]{1,0:T(8,128)(2,1)S(1)} %fusion.10), channel_id=1, source_target_pairs={{0,16},{4,20},{8,24},{12,28},{16,0},{20,4},{24,8},{28,12},{1,17},{... | collective-permute-start | bytes 786440 | tf_op jit(solution)/shard_map/ppermute | solution.py:667
  196.7 15.2 %collective-permute-start.10 = (bf16[2,256,512]{2,1,0:T(8,128)(2,1)}, bf16[2,256,512]{2,1,0:T(8,128)(2,1)}, u32[]{:S(2)}, u32[]{:S(2)}) collective-permute-start(bf16[2,256,512]{2,1,0:T(8,128)(2,1)} %get-tuple-element.89), channel_id=1, source_target_pairs={{0,16},{4,20},{8,24},{12,28},{16,0},{20,4},{24,8},{28,12},{1,17},{... | collective-permute-start | bytes 1572872 | tf_op jit(solution)/shard_map/ppermute | solution.py:667
  197.9 15.8 %collective-permute-start.8 = (bf16[2,256,512]{2,1,0:T(8,128)(2,1)}, bf16[2,256,512]{2,1,0:T(8,128)(2,1)}, u32[]{:S(2)}, u32[]{:S(2)}) collective-permute-start(bf16[2,256,512]{2,1,0:T(8,128)(2,1)} %get-tuple-element.87), channel_id=1, source_target_pairs={{0,8},{4,12},{8,0},{12,4},{16,24},{20,28},{24,16},{28,20},{1,9},{5... | collective-permute-start | bytes 1572872 | tf_op jit(solution)/shard_map/ppermute | solution.py:667
  204.7 18.4 %collective-permute-start.5 = (bf16[2,256,512]{2,1,0:T(8,128)(2,1)}, bf16[2,256,512]{2,1,0:T(8,128)(2,1)}, u32[]{:S(2)}, u32[]{:S(2)}) collective-permute-start(bf16[2,256,512]{2,1,0:T(8,128)(2,1)} %get-tuple-element.85), channel_id=1, source_target_pairs={{0,16},{4,20},{8,24},{12,28},{16,0},{20,4},{24,8},{28,12},{1,17},{... | collective-permute-start | bytes 1572872 | tf_op jit(solution)/shard_map/ppermute | solution.py:667
  205.7 17.4 %copy-start.13 = (bf16[2,256,512]{2,1,0:T(8,128)(2,1)S(1)}, bf16[2,256,512]{2,1,0:T(8,128)(2,1)}, u32[]{:S(2)}) copy-start(bf16[2,256,512]{2,1,0:T(8,128)(2,1)} %get-tuple-element.84) | copy-start | bytes 1572868
  207.0 25.6 %copy-start.14 = (bf16[2,256,512]{2,1,0:T(8,128)(2,1)S(1)}, bf16[2,256,512]{2,1,0:T(8,128)(2,1)}, u32[]{:S(2)}) copy-start(bf16[2,256,512]{2,1,0:T(8,128)(2,1)} %get-tuple-element.88) | copy-start | bytes 1572868
  207.0 29.3 %collective-permute-start.3 = (bf16[2,256,640]{2,1,0:T(8,128)(2,1)}, bf16[2,256,640]{2,1,0:T(8,128)(2,1)S(1)}, u32[]{:S(2)}, u32[]{:S(2)}) collective-permute-start(bf16[2,256,640]{2,1,0:T(8,128)(2,1)} %get-tuple-element.83), channel_id=1, source_target_pairs={{0,8},{4,12},{8,0},{12,4},{16,24},{20,28},{24,16},{28,20},{1,9},{5... | collective-permute-start | bytes 1966088 | tf_op jit(solution)/shard_map/ppermute | solution.py:667
  212.9 19.7 %collective-permute-start.11 = (bf16[256,512]{1,0:T(8,128)(2,1)S(1)}, bf16[256,512]{1,0:T(8,128)(2,1)S(1)}, u32[]{:S(2)}, u32[]{:S(2)}) collective-permute-start(bf16[256,512]{1,0:T(8,128)(2,1)S(1)} %fusion.7), channel_id=1, source_target_pairs={{0,8},{4,12},{8,0},{12,4},{16,24},{20,28},{24,16},{28,20},{1,9},{5... | collective-permute-start | bytes 786440 | tf_op jit(solution)/shard_map/ppermute | solution.py:667
  214.6 19.0 %collective-permute-start.9 = (bf16[256,512]{1,0:T(8,128)(2,1)S(1)}, bf16[256,512]{1,0:T(8,128)(2,1)S(1)}, u32[]{:S(2)}, u32[]{:S(2)}) collective-permute-start(bf16[256,512]{1,0:T(8,128)(2,1)S(1)} %fusion.6), channel_id=1, source_target_pairs={{0,16},{4,20},{8,24},{12,28},{16,0},{20,4},{24,8},{28,12},{1,17},{... | collective-permute-start | bytes 786440 | tf_op jit(solution)/shard_map/ppermute | solution.py:667
  224.1 13.9 %collective-permute-start.6 = (bf16[256,512]{1,0:T(8,128)(2,1)S(1)}, bf16[256,512]{1,0:T(8,128)(2,1)S(1)}, u32[]{:S(2)}, u32[]{:S(2)}) collective-permute-start(bf16[256,512]{1,0:T(8,128)(2,1)S(1)} %fusion.5), channel_id=1, source_target_pairs={{0,8},{4,12},{8,0},{12,4},{16,24},{20,28},{24,16},{28,20},{1,9},{5... | collective-permute-start | bytes 786440 | tf_op jit(solution)/shard_map/ppermute | solution.py:667
  237.1 7.3 %collective-permute-start.4 = (bf16[256,640]{1,0:T(8,128)(2,1)}, bf16[256,640]{1,0:T(8,128)(2,1)S(1)}, u32[]{:S(2)}, u32[]{:S(2)}) collective-permute-start(bf16[256,640]{1,0:T(8,128)(2,1)} %fusion.4), channel_id=1, source_target_pairs={{0,16},{4,20},{8,24},{12,28},{16,0},{20,4},{24,8},{28,12},{1,17},{... | collective-permute-start | bytes 983048 | tf_op jit(solution)/shard_map/ppermute | solution.py:667
  (9 other events, 25.0 us)
Sparse Core Ops, SparseCore 0:
  82.6 44.8 reduce-scatter.2
  163.3 44.0 reduce-scatter.4

commit v3 on v2

--- a/solution.py
+++ b/solution.py
@@ -54,8 +54,9 @@
 def decays(decay_beta_ref, bias_ref, scale_ref, resets_ref):
     row, col = grid_of(CHUNK)
     lower = (row >= col).astype(F32)
-    decay_logit = decay_beta_ref[0]
-    beta = sigmoid(decay_beta_ref[1] + bias_ref[...])
+    heads = bias_ref.shape[1]
+    decay_logit = decay_beta_ref[:, :heads]
+    beta = sigmoid(decay_beta_ref[:, heads:] + bias_ref[...])
     log_decay = -scale_ref[...] * softplus(decay_logit)
     resets = jnp.broadcast_to(resets_ref[0].astype(F32), (8, CHUNK))
     doc_row = dot(resets, lower, NT)[0:1]
@@ -346,7 +347,7 @@
     below = jnp.concatenate(lower_rows, axis=0)
     delta_log = exact(upper, sums) - exact(upper, below, NT)[:, :heads] + tail
     delta_log = jnp.where(reset_col == 0.0, delta_log, 0.0)
-    delta_decay = delta_log * (-scale_ref[...]) * sigmoid(decay_beta_ref[0])
+    delta_decay = delta_log * (-scale_ref[...]) * sigmoid(decay_beta_ref[:, :heads])
     delta_beta = logits * (1.0 - beta)
     rest = jnp.zeros((CHUNK, LANES - 2 * heads), F32)
     delta_query_key_ref[:, 2 * key_heads * DK :] = jnp.concatenate(
@@ -397,7 +398,7 @@
 
 
 def run_forward(query_key, value, decay_beta, bias, scale, resets):
-    tokens, heads = query_key.shape[1], decay_beta.shape[2]
+    tokens, heads = query_key.shape[1], bias.shape[1]
     chunks = tokens // CHUNK
     key_width, value_width = query_key.shape[2], heads * DV
     return pl.pallas_call(
@@ -406,7 +407,7 @@
         in_specs=[
             pl.BlockSpec((2, CHUNK, key_width), lambda c: (0, c, 0)),
             pl.BlockSpec((CHUNK, value_width), lambda c: (c, 0)),
-            pl.BlockSpec((2, CHUNK, heads), lambda c: (0, c, 0)),
+            pl.BlockSpec((CHUNK, 2 * heads), lambda c: (c, 0)),
             whole((1, heads)),
             whole((1, heads)),
             pl.BlockSpec((1, 1, CHUNK), lambda c: (c, 0, 0)),
@@ -465,7 +466,7 @@
 def run_backward(
     query_key, value, decay_beta, bias, scale, resets, solve, starts, state_in, delta_out, final
 ):
-    tokens, heads = query_key.shape[1], decay_beta.shape[2]
+    tokens, heads = query_key.shape[1], bias.shape[1]
     chunks = tokens // CHUNK
     key_width, value_width = query_key.shape[2], heads * DV
     last = chunks - 1
@@ -475,7 +476,7 @@
         in_specs=[
             pl.BlockSpec((2, CHUNK, key_width), lambda c: (0, last - c, 0)),
             pl.BlockSpec((CHUNK, value_width), lambda c: (last - c, 0)),
-            pl.BlockSpec((2, CHUNK, heads), lambda c: (0, last - c, 0)),
+            pl.BlockSpec((CHUNK, 2 * heads), lambda c: (last - c, 0)),
             whole((1, heads)),
             whole((1, heads)),
             pl.BlockSpec((1, 1, CHUNK), lambda c: (last - c, 0, 0)),
@@ -550,6 +551,10 @@
 
 def product(spec, a, b):
     return jnp.einsum(spec, a, b, preferred_element_type=F32)
+
+
+def rows_of(small_weight_ref):
+    return jnp.concatenate([small_weight_ref[0].astype(F32), small_weight_ref[1].astype(F32)], axis=0)
 
 
 def projection_kernel(
@@ -563,39 +568,37 @@
 ):
     inputs = inputs_ref[...]
     query_key_ref[0] = dot(inputs, query_key_weight_ref[0])
-    query_key_ref[1] = dot(inputs, query_key_weight_ref[1])
     value_ref[...] = dot(inputs, value_weight_ref[0])
 
     @pl.when(pl.program_id(0) == 0)
     def _():
-        decay_beta_ref[0] = dot(inputs, decay_beta_weight_ref[0])
-        decay_beta_ref[1] = dot(inputs, decay_beta_weight_ref[1])
+        decay_beta_ref[...] = dot(inputs, rows_of(decay_beta_weight_ref), NT)
 
 
 def run_projection(inputs, query_key_weight, value_gate_weight, decay_beta_weight):
     tokens, model = inputs.shape
     key_width, value_width = query_key_weight.shape[2], value_gate_weight.shape[2]
-    heads = decay_beta_weight.shape[2]
-    steps = 2
-    keys, values = key_width // steps, value_width // steps
+    heads = decay_beta_weight.shape[1]
+    steps = 4
+    keys, values = 2 * key_width // steps, value_width // steps
     return pl.pallas_call(
         projection_kernel,
         grid=(steps,),
         in_specs=[
             whole((tokens, model)),
-            pl.BlockSpec((2, model, keys), lambda j: (0, 0, j)),
+            pl.BlockSpec((1, model, keys), lambda j: (j // 2, 0, j % 2)),
             pl.BlockSpec((1, model, values), lambda j: (0, 0, j)),
-            whole((2, model, heads)),
+            whole((2, heads, model)),
         ],
         out_specs=[
-            pl.BlockSpec((2, tokens, keys), lambda j: (0, 0, j)),
+            pl.BlockSpec((1, tokens, keys), lambda j: (j // 2, 0, j % 2)),
             pl.BlockSpec((tokens, values), lambda j: (0, j)),
-            whole((2, tokens, heads)),
+            whole((tokens, 2 * heads)),
         ],
         out_shape=[
             jax.ShapeDtypeStruct((2, tokens, key_width), F32),
             jax.ShapeDtypeStruct((tokens, value_width), F32),
-            jax.ShapeDtypeStruct((2, tokens, heads), F32),
+            jax.ShapeDtypeStruct((tokens, 2 * heads), F32),
         ],
         compiler_params=PARAMS,
         interpret=INTERPRET,
@@ -612,21 +615,14 @@
     decay_beta_weight_ref,
     out_ref,
 ):
-    rows = decay_beta_weight_ref.shape[1]
-    heads = decay_beta_weight_ref.shape[2]
-    packed = jnp.concatenate(
-        [
-            query_key_weight_ref[0],
-            query_key_weight_ref[1],
-            decay_beta_weight_ref[0],
-            decay_beta_weight_ref[1],
-            jnp.zeros((rows, LANES - 2 * heads), BF16),
-        ],
-        axis=1,
-    )
+    width = query_key_weight_ref.shape[2]
+    heads = decay_beta_weight_ref.shape[1]
+    keys = jnp.concatenate([query_key_weight_ref[0], query_key_weight_ref[1]], axis=1)
+    small = delta_query_key_ref[:, 2 * width : 2 * width + 2 * heads]
     total = dot(delta_gate_ref[...], value_gate_weight_ref[1], NT)
     total += dot(delta_value_ref[...], value_gate_weight_ref[0], NT)
-    total += dot(delta_query_key_ref[...], packed, NT)
+    total += dot(delta_query_key_ref[:, : 2 * width], keys, NT)
+    total += dot(small, rows_of(decay_beta_weight_ref))
     out_ref[...] = total.astype(BF16)
 
 
@@ -634,7 +630,7 @@
     delta_query_key, delta_value, delta_gate, query_key_weight, value_gate_weight, decay_beta_weight
 ):
     tokens, model = delta_value.shape[0], query_key_weight.shape[1]
-    cut = 256
+    cut = 512
 
     def weight(array):
         return pl.BlockSpec((2, cut, array.shape[2]), lambda j: (0, j, 0))
@@ -648,7 +644,7 @@
             whole(delta_gate.shape),
             weight(query_key_weight),
             weight(value_gate_weight),
-            weight(decay_beta_weight),
+            pl.BlockSpec((2, decay_beta_weight.shape[1], cut), lambda j: (0, 0, j)),
         ],
         out_specs=pl.BlockSpec((tokens, cut), lambda j: (0, j)),
         out_shape=jax.ShapeDtypeStruct((tokens, model), BF16),
@@ -675,103 +671,103 @@
     return target_y * 4 + target_x * 2 + core
 
 
-def send_kernel(place_ref, left_ref, delta_ref, out_ref):
-    out_ref[...] = dot(left_ref[...], delta_ref[...], TN).astype(BF16)
+def send_kernel(place_ref, left_a_ref, a_ref, left_b_ref, b_ref, a_out_ref, b_out_ref):
+    a_out_ref[...] = dot(left_a_ref[...], a_ref[...], TN).astype(BF16)
+    b_out_ref[...] = dot(left_b_ref[...], b_ref[...], TN).astype(BF16)
 
 
 def keep_kernel(
-    place_ref, left_ref, delta_ref, arrived_ref, x_send_ref, x_keep_ref, y_send_ref, y_keep_ref
+    place_ref, left_a_ref, a_ref, left_b_ref, b_ref, a_arrived_ref, b_arrived_ref, *out_refs
 ):
     step = pl.program_id(0)
-    cut = x_send_ref.shape[2]
-    total = dot(left_ref[...], delta_ref[...], TN) + arrived_ref[...].astype(F32)
-    total = total.astype(BF16)
-
-    @pl.when(step < 2)
-    def _():
-        x_send_ref[0] = total[:, :cut]
-
-    @pl.when(step >= 2)
-    def _():
-        x_keep_ref[0] = total[:, :cut]
-
-    @pl.when(lax.rem(step, 2) == 0)
-    def _():
-        y_send_ref[0] = total[:, cut:]
-
-    @pl.when(lax.rem(step, 2) == 1)
-    def _():
-        y_keep_ref[0] = total[:, cut:]
-
-
-def halving_start(place, left, delta):
-    tokens, width = delta.shape
-    rows = left.shape[1] // 8
-    send = pl.pallas_call(
+    a = dot(left_a_ref[...], a_ref[...], TN) + a_arrived_ref[...].astype(F32)
+    b = dot(left_b_ref[...], b_ref[...], TN) + b_arrived_ref[...].astype(F32)
+    for i in range(4):
+
+        @pl.when(step == i)
+        def _():
+            out_refs[i][...] = a.astype(BF16)
+            out_refs[4 + i][...] = b.astype(BF16)
+
+
+def pair_specs(left_a, a, left_b, b, flip):
+    def rows(left):
+        return pl.BlockSpec(
+            (left.shape[0], left.shape[1] // 8), lambda i, place: (0, block_of(i, place[0], flip))
+        )
+
+    def full(delta):
+        return pl.BlockSpec(delta.shape, lambda i, place: (0, 0))
+
+    return [rows(left_a), full(a), rows(left_b), full(b)]
+
+
+def halving_start(place, left_a, a, left_b, b):
+    rows = left_a.shape[1] // 8
+    return pl.pallas_call(
         send_kernel,
         grid_spec=pltpu.PrefetchScalarGridSpec(
             num_scalar_prefetch=1,
             grid=(4,),
-            in_specs=[
-                pl.BlockSpec((tokens, rows), lambda i, place: (0, block_of(i, place[0], 1))),
-                pl.BlockSpec((tokens, width), lambda i, place: (0, 0)),
+            in_specs=pair_specs(left_a, a, left_b, b, 1),
+            out_specs=[
+                pl.BlockSpec((rows, delta.shape[1]), lambda i, place: (i, 0)) for delta in (a, b)
             ],
-            out_specs=pl.BlockSpec((rows, width), lambda i, place: (i, 0)),
         ),
-        out_shape=jax.ShapeDtypeStruct((4 * rows, width), BF16),
+        out_shape=[
+            jax.ShapeDtypeStruct((4 * rows, delta.shape[1]), BF16) for delta in (a, b)
+        ],
         compiler_params=PARAMS,
         interpret=INTERPRET,
         name="send_rows",
-    )(place, left, delta)
-    return exchange(send, 1)
-
-
-def halving_keep(place, left, delta, arrived):
-    tokens, width = delta.shape
-    rows = left.shape[1] // 8
-    cut = -(-(width // 2) // LANES) * LANES
+    )(place, left_a, a, left_b, b)
+
+
+def halving_keep(place, left_a, a, left_b, b, a_arrived, b_arrived):
+    rows = left_a.shape[1] // 8
     return pl.pallas_call(
         keep_kernel,
         grid_spec=pltpu.PrefetchScalarGridSpec(
             num_scalar_prefetch=1,
             grid=(4,),
-            in_specs=[
-                pl.BlockSpec((tokens, rows), lambda i, place: (0, block_of(i, place[0], 0))),
-                pl.BlockSpec((tokens, width), lambda i, place: (0, 0)),
-                pl.BlockSpec((rows, width), lambda i, place: (i, 0)),
-            ],
+            in_specs=pair_specs(left_a, a, left_b, b, 0)
+            + [pl.BlockSpec((rows, delta.shape[1]), lambda i, place: (i, 0)) for delta in (a, b)],
             out_specs=[
-                pl.BlockSpec((1, rows, cut), lambda i, place: (jnp.minimum(i, 1), 0, 0)),
-                pl.BlockSpec((1, rows, cut), lambda i, place: (jnp.maximum(i - 2, 0), 0, 0)),
-                pl.BlockSpec((1, rows, width - cut), lambda i, place: (i // 2, 0, 0)),
-                pl.BlockSpec((1, rows, width - cut), lambda i, place: (i // 2, 0, 0)),
+                pl.BlockSpec((rows, delta.shape[1]), lambda i, place: (0, 0))
+                for delta in (a, b)
+                for _ in range(4)
             ],
         ),
         out_shape=[
-            jax.ShapeDtypeStruct((2, rows, cut), BF16),
-            jax.ShapeDtypeStruct((2, rows, cut), BF16),
-            jax.ShapeDtypeStruct((2, rows, width - cut), BF16),
-            jax.ShapeDtypeStruct((2, rows, width - cut), BF16),
+            jax.ShapeDtypeStruct((rows, delta.shape[1]), BF16)
+            for delta in (a, b)
+            for _ in range(4)
         ],
         compiler_params=PARAMS,
         interpret=INTERPRET,
         name="keep_rows",
-    )(place, left, delta, arrived)
-
-
-def halving_cross(x_send, x_keep, y_send, y_keep):
-    return x_keep, exchange(x_send, 2), y_keep, exchange(y_send, 4)
-
-
-def halving_last(a, a_arrived, b, b_arrived):
-    a_send = (a[0].astype(F32) + a_arrived[0].astype(F32)).astype(BF16)
-    b_send = (b[0].astype(F32) + b_arrived[0].astype(F32)).astype(BF16)
-    return a[1], a_arrived[1], exchange(a_send, 4), b[1], b_arrived[1], exchange(b_send, 2)
-
-
-def halving_sum(*pieces):
-    a, a_near, a_far, b, b_near, b_far = [piece.astype(F32) for piece in pieces]
-    return jnp.concatenate([a + a_near + a_far, b + b_near + b_far], axis=1)
+    )(place, left_a, a, left_b, b, a_arrived, b_arrived)
+
+
+def summed(a, b):
+    return (a.astype(F32) + b.astype(F32)).astype(BF16)
+
+
+def halving_cross(pieces):
+    a, b = pieces[:4], pieces[4:]
+    return exchange(a[0], 2), exchange(b[0], 4), exchange(a[1], 2), exchange(b[2], 4)
+
+
+def halving_last(pieces, arrived):
+    a, b = pieces[:4], pieces[4:]
+    return exchange(summed(a[2], arrived[0]), 4), exchange(summed(b[1], arrived[1]), 2)
+
+
+def halving_sum(pieces, arrived, last):
+    def total(own, near, far):
+        return own.astype(F32) + near.astype(F32) + far.astype(F32)
+
+    return total(pieces[3], arrived[2], last[0]), total(pieces[7], arrived[3], last[1])
 
 
 def scatter(partial, axis, dimension):
@@ -793,8 +789,9 @@
     tokens, heads = inputs.shape[0], beta_bias.shape[0]
     key_width = query_key_weight.shape[2]
     cubic = lax.axis_size("ctx") == 8
+    small_weight = jnp.swapaxes(decay_beta_weight, 1, 2)
     query_key, value, decay_beta = run_projection(
-        inputs, query_key_weight, value_gate_weight, decay_beta_weight
+        inputs, query_key_weight, value_gate_weight, small_weight
     )
     bias, scale = beta_bias.reshape(1, heads), decay_scale.reshape(1, heads)
     resets = boundaries.reshape(tokens // CHUNK, 1, CHUNK)
@@ -820,13 +817,12 @@
     finals = swap(run_chain_backward(held, deltas))
     if cubic:
         place = lax.axis_index("ctx").astype(jnp.int32).reshape(1)
-        place, deltas = together(place, deltas)
-        gate_sent = halving_start(place, inputs, delta_gate)
-        out_sent = halving_start(place, grad_mixed, hidden)
-        gate_cut = halving_keep(place, inputs, delta_gate, gate_sent)
-        out_cut = halving_keep(place, grad_mixed, hidden, out_sent)
-        finals, gate_cut, out_cut = together(finals, gate_cut, out_cut)
-        gate_next, out_next = halving_cross(*gate_cut), halving_cross(*out_cut)
+        early = (place, inputs, delta_gate, grad_mixed, hidden)
+        sent = halving_start(*early)
+        arrived = [exchange(part, 1) for part in sent]
+        early_pieces = halving_keep(*early, *arrived)
+        finals, early_pieces = together(finals, early_pieces)
+        early_arrived = halving_cross(early_pieces)
     delta_final = gather_parts(finals, heads)
     delta_query_key, delta_value = run_backward(
         query_key,
@@ -842,26 +838,29 @@
         delta_final,
     )
     if cubic:
-        value_sent = halving_start(place, inputs, delta_value)
-        query_key_sent = halving_start(place, inputs, delta_query_key)
-        value_next = halving_cross(*halving_keep(place, inputs, delta_value, value_sent))
-        query_key_next = halving_cross(
-            *halving_keep(place, inputs, delta_query_key, query_key_sent)
-        )
+        late = (place, inputs, delta_value, inputs, delta_query_key)
+        sent = halving_start(*late)
+        arrived = [exchange(part, 1) for part in sent]
     grad_rows = run_input_gradient(
         delta_query_key,
         delta_value,
         delta_gate,
         query_key_weight,
         value_gate_weight,
-        decay_beta_weight,
-    )
+        small_weight,
+    )
+    if cubic:
+        grad_rows, arrived = together(grad_rows, arrived)
     grad_inputs = scatter(grad_rows, "head", 1)
     if cubic:
-        grad_gate = halving_sum(*halving_last(*gate_next))
-        grad_out = halving_sum(*halving_last(*out_next)).T
-        grad_value = halving_sum(*halving_last(*value_next))
-        packed = halving_sum(*halving_last(*query_key_next))
+        late_pieces = halving_keep(*late, *arrived)
+        late_pieces, early_arrived = together(late_pieces, early_arrived)
+        late_arrived = halving_cross(late_pieces)
+        early_last = halving_last(early_pieces, early_arrived)
+        late_last = halving_last(late_pieces, late_arrived)
+        grad_gate, grad_out = halving_sum(early_pieces, early_arrived, early_last)
+        grad_out = grad_out.T
+        grad_value, packed = halving_sum(late_pieces, late_arrived, late_last)
     else:
         grad_gate = scatter(product("td,tf->df", inputs, delta_gate), "ctx", 0).astype(F32)
         grad_out = scatter(product("tf,td->fd", hidden, grad_mixed), "ctx", 1).astype(F32)

time: 254 us -> 236 us (0.929)
  Pallas kernels: 118 us -> 106 us
  other arithmetic: 17.3 us -> 11.2 us
  waiting for transfers between devices: 42.3 us -> 45.1 us
    pallas_call x4 -> x2, Pallas kernels: 19.7 us -> 12.8 us  [halving_start(): pl.pallas_call(send_kernel, grid_spec=pltpu.PrefetchScalarGridSpec(num_sc...]
    pallas_call x4 -> x2, Pallas kernels: 22.7 us -> 17.4 us  [halving_keep(): pl.pallas_call(keep_kernel, grid_spec=pltpu.PrefetchScalarGridSpec(num_sc...]
    add x8 -> x1, other arithmetic: 6.45 us -> 1.26 us  [total(): return own.astype(F32) + near.astype(F32) + far.astype(F32)]
    convert_element_type x8 -> x4, other arithmetic: 7.31 us -> 3.61 us  [summed(): return (a.astype(F32) + b.astype(F32)).astype(BF16)]
    ppermute x20 -> x16, waiting for transfers between devices: 37.4 us -> 40.8 us  [exchange(): return lax.ppermute(array, 'ctx', [(i, i ^ distance) for i in devices])]
    another operation x3, other arithmetic: 1.69 us -> 4.43 us  [body(): jnp.stack([grad_value, grad_gate])]
    ppermute x20 -> x16, starting transfers between devices: 18.1 us -> 16.3 us  [exchange(): return lax.ppermute(array, 'ctx', [(i, i ^ distance) for i in devices])]
    unnamed x32 -> x37, local copies, waits for them, and re-layouts: 7.66 us -> 6.92 us
  transfers between devices with their start and end apart: 26 -> 22, of which waited for: 10 -> 7; matrix products, arithmetic and copies ran while one was open for 15% -> 13% of each run, Pallas kernels for 33% -> 30%
where the time goes in v3:
time: 236 us; the launch traced here: 235 us
  Pallas kernels  106 us (45%)
  waiting for transfers between devices  45.1 us (19%)
  starting transfers between devices  32.9 us (14%)
  matrix products  18.3 us (8%)
  between operations  14.3 us (6%)
  other arithmetic  11.2 us (5%)
  local copies, waits for them, and re-layouts  7.27 us (3%)
    ppermute x16, waiting for transfers between devices, exchange(): return lax.ppermute(array, 'ctx', [(i, i ^ distance) for i in devices])  40.8 us
    pallas_call x1, Pallas kernels, run_backward(): pl.pallas_call(backward_kernel, grid=(chunks,), in_specs=[pl.BlockSpec((2...  25.5 us
    dot_general x3, matrix products, product(): return jnp.einsum(spec, a, b, preferred_element_type=F32)  18.3 us
    pallas_call x2, Pallas kernels, halving_keep(): pl.pallas_call(keep_kernel, grid_spec=pltpu.PrefetchScalarGridSpec(num_sc...  17.4 us
    all_to_all x4, starting transfers between devices, swap(): return lax.all_to_all(parts, 'ctx', split_axis=0, concat_axis=0, tiled=True)  16.3 us
    ppermute x16, starting transfers between devices, exchange(): return lax.ppermute(array, 'ctx', [(i, i ^ distance) for i in devices])  16.3 us
    pallas_call x1, Pallas kernels, run_forward(): pl.pallas_call(forward_kernel, grid=(chunks,), in_specs=[pl.BlockSpec((2,...  16 us
    pallas_call x2, Pallas kernels, halving_start(): pl.pallas_call(send_kernel, grid_spec=pltpu.PrefetchScalarGridSpec(num_sc...  12.8 us
  transfers between devices with their start and end apart: 22, of which 7 were waited for; matrix products, arithmetic and copies ran while one was open for 13% of the time, Pallas kernels for 30%

profile of v3, /device:TPU:0, one launch (start us, length us, event | category | flops | bytes accessed | tf_op | source)
XLA Modules:
  0.0 235.0 jit_solution(3515420235795518753)
XLA Ops:
  7.2 9.9 %projection.1 = (f32[2,512,512]{2,1,0:T(8,128)}, f32[512,1024]{1,0:T(8,128)}, f32[512,16]{1,0:T(8,128)}) custom-call(bf16[512,2048]{1,0:T(8,128)(2,1)} %left_b_ref.7, bf16[2,2048,512]{2,1,0:T(8,128)(2,1)} %query_key_weight_ref.3, bf16[2,2048,1024]{2,1,0:T(8,128)(2,1)} %value_gate_weight_ref.1, bf16[2,8,2048]{2,1,0:T(8,128)(2,1)} %bitcast.36), custom_call_target="tpu_custom_call" | custom-call | tf_op jit(solution)/shard_map/projection/pallas_call | solution.py:584
  17.1 16.0 %forward_blocks.1 = (bf16[4,8,128,128]{3,2,1,0:T(8,128)(2,1)}, bf16[4,8,128,256]{3,2,1,0:T(8,128)(2,1)}, bf16[512,1024]{1,0:T(8,128)(2,1)}, f32[512,1024]{1,0:T(8,128)}, bf16[8,128,256]{2,1,0:T(8,128)(2,1)}) custom-call(f32[2,512,512]{2,1,0:T(8,128)} %get-tuple-element.70.query_key_ref, f32[512,1024]{1,0:T(8,128)} %get-tuple-element.71.value_ref, ...), custom_call_target="tpu_custom_call" | custom-call | tf_op jit(solution)/shard_map/forward_blocks/pallas_call | solution.py:404
  33.1 5.2 %all-to-all-start = ((bf16[8,1,128,256]{3,2,1,0:T(8,128)(2,1)}), bf16[8,1,128,256]{3,2,1,0:T(8,128)(2,1)S(1)}, u32[]{:S(2)}, u32[]{:S(2)}) async-start(bf16[8,1,128,256]{3,2,1,0:T(8,128)(2,1)} %bitcast.35), calls=%async_computation | async-start | bytes 1048576 | tf_op jit(solution)/shard_map/all_to_all | solution.py:523
  38.3 5.9 %fusion.gate_ref = f32[512,1024]{1,0:T(8,128)} fusion(bf16[512,2048]{1,0:T(8,128)(2,1)S(1)} %copy-done, bf16[2,2048,1024]{2,1,0:T(8,128)(2,1)} %value_gate_weight_ref.1), kind=kOutput, calls=%fused_computation | convolution fusion | flops 2147483648 | bytes 8388608 | tf_op jit(solution)/shard_map/td,df->tf/dot_general | solution.py:553
  44.2 3.8 %all-to-all-done.totals_ref = bf16[8,1,128,256]{3,2,1,0:T(8,128)(2,1)S(1)} async-done(((bf16[8,1,128,256]{3,2,1,0:T(8,128)(2,1)}), bf16[8,1,128,256]{3,2,1,0:T(8,128)(2,1)S(1)}, u32[]{:S(2)}, u32[]{:S(2)}) %all-to-all-start) | async-done | bytes 524320 | tf_op jit(solution)/shard_map/all_to_all | solution.py:523
  48.8 2.8 %chain_forward.1 = bf16[8,1,128,128]{3,2,1,0:T(8,128)(2,1)} custom-call(bf16[8,1,128,256]{3,2,1,0:T(8,128)(2,1)} %copy-done.1), custom_call_target="tpu_custom_call" | custom-call | tf_op jit(solution)/shard_map/chain_forward/pallas_call | solution.py:535
  51.6 3.4 %all-to-all-start.1 = ((bf16[8,1,128,128]{3,2,1,0:T(8,128)(2,1)}), bf16[8,1,128,128]{3,2,1,0:T(8,128)(2,1)S(1)}, u32[]{:S(2)}, u32[]{:S(2)}) async-start(bf16[8,1,128,128]{3,2,1,0:T(8,128)(2,1)} %chain_forward.1), calls=%async_computation.1 | async-start | bytes 524288 | tf_op jit(solution)/shard_map/all_to_all | solution.py:523
  55.1 6.5 %fusion.3.delta_ref = f32[512,1024]{1,0:T(8,128)} fusion(bf16[512,2048]{1,0:T(8,128)(2,1)} %left_b_ref.5, bf16[1024,2048]{1,0:T(8,128)(2,1)} %param.17), kind=kOutput, calls=%fused_computation.19 | convolution fusion | flops 2147483648 | bytes 8388608 | tf_op jit(solution)/shard_map/td,fd->tf/dot_general | solution.py:553
  62.7 6.8 %gated_norm.1 = (bf16[512,1024]{1,0:T(8,128)(2,1)}, bf16[512,1024]{1,0:T(8,128)(2,1)}, bf16[512,1024]{1,0:T(8,128)(2,1)}, bf16[8,128,128]{2,1,0:T(8,128)(2,1)}) custom-call(f32[512,1024]{1,0:T(8,128)} %get-tuple-element.73.local_ref, bf16[512,1024]{1,0:T(8,128)(2,1)} %get-tuple-element.74.map_ref, f32[512,1024]{1,0:T(8,128)} %fusion.gate_ref, ...), custom_call_target="tpu_custom_call" | custom-call | tf_op jit(solution)/shard_map/gated_norm/pallas_call | solution.py:441
  69.4 3.8 %all-to-all-start.2 = ((bf16[8,1,128,128]{3,2,1,0:T(8,128)(2,1)}), bf16[8,1,128,128]{3,2,1,0:T(8,128)(2,1)S(1)}, u32[]{:S(2)}, u32[]{:S(2)}) async-start(bf16[8,1,128,128]{3,2,1,0:T(8,128)(2,1)} %bitcast.38), calls=%async_computation.2 | async-start | bytes 524288 | tf_op jit(solution)/shard_map/all_to_all | solution.py:523
  73.4 6.3 %send_rows.2 = (bf16[1024,1024]{1,0:T(8,128)(2,1)}, bf16[1024,1024]{1,0:T(8,128)(2,1)}) custom-call(s32[1]{0:T(128)} %bitcast.9.place_ref, bf16[512,2048]{1,0:T(8,128)(2,1)} %left_b_ref.7, bf16[512,1024]{1,0:T(8,128)(2,1)} %get-tuple-element.87.a_ref.delta_gate_ref, bf16[512,2048]{1,0:T(8,128)(2,1)} %left_b_ref.5, bf16[512,1024]{1,0:T(8,128)(2,1)} %get-tuple-element.81.b_ref), custom_call_target="tpu_custom_call" | custom-call | tf_op jit(solution)/shard_map/send_rows/pallas_call | solution.py:707
  80.2 5.9 %convolution_convert_fusion = bf16[512,2048]{1,0:T(8,128)(2,1)} fusion(bf16[512,1024]{1,0:T(8,128)(2,1)S(1)} %copy-done.2, bf16[1024,2048]{1,0:T(8,128)(2,1)} %param.17), kind=kOutput, calls=%fused_computation.3 | convolution fusion | flops 2148532224 | bytes 7340032 | tf_op jit(solution)/shard_map/tf,fd->td/dot_general | solution.py:553
  86.8 3.0 %chain_backward.1 = bf16[8,1,128,128]{3,2,1,0:T(8,128)(2,1)} custom-call(bf16[8,1,128,256]{3,2,1,0:T(8,128)(2,1)} %copy-done.1, bf16[8,1,128,128]{3,2,1,0:T(8,128)(2,1)} %copy-done.7), custom_call_target="tpu_custom_call" | custom-call | tf_op jit(solution)/shard_map/chain_backward/pallas_call | solution.py:544
  89.8 4.0 %all-to-all-start.3 = ((bf16[8,1,128,128]{3,2,1,0:T(8,128)(2,1)}), bf16[8,1,128,128]{3,2,1,0:T(8,128)(2,1)S(1)}, u32[]{:S(2)}, u32[]{:S(2)}) async-start(bf16[8,1,128,128]{3,2,1,0:T(8,128)(2,1)} %chain_backward.1), calls=%async_computation.4 | async-start | bytes 524288 | tf_op jit(solution)/shard_map/all_to_all | solution.py:523
  95.1 8.4 %keep_rows.2 = (bf16[256,1024]{1,0:T(8,128)(2,1)}, bf16[256,1024]{1,0:T(8,128)(2,1)}, bf16[256,1024]{1,0:T(8,128)(2,1)}, bf16[256,1024]{1,0:T(8,128)(2,1)}, bf16...) custom-call(s32[1]{0:T(128)} %bitcast.9.place_ref, ...), custom_call_target="tpu_custom_call" | custom-call | tf_op jit(solution)/shard_map/keep_rows/pallas_call | solution.py:728
  104.2 25.5 %backward_blocks.1 = (bf16[512,1152]{1,0:T(8,128)(2,1)}, bf16[512,1024]{1,0:T(8,128)(2,1)}) custom-call(f32[2,512,512]{2,1,0:T(8,128)} %get-tuple-element.70.query_key_ref, f32[512,1024]{1,0:T(8,128)} %get-tuple-element.71.value_ref, f32[512,16]{1,0:T(8,128)} %get-tuple-element.72.decay_beta_ref, f32[1,8]{1,0:T(1,128)} %bitcast.42, f32[1,8]{1,0:T(1,128)} %bitcast.44, ...), custom_call_target="tpu_custom_call" | custom-call | tf_op jit(solution)/shard_map/backward_blocks/pallas_call | solution.py:473
  129.7 6.5 %send_rows.3 = (bf16[1024,1024]{1,0:T(8,128)(2,1)}, bf16[1024,1152]{1,0:T(8,128)(2,1)}) custom-call(s32[1]{0:T(128)} %bitcast.9.place_ref, bf16[512,2048]{1,0:T(8,128)(2,1)} %left_b_ref.7, bf16[512,1024]{1,0:T(8,128)(2,1)} %get-tuple-element.100.delta_value_ref.a_ref, bf16[512,2048]{1,0:T(8,128)(2,1)} %left_b_ref.7, ...), custom_call_target="tpu_custom_call" | custom-call | tf_op jit(solution)/shard_map/send_rows/pallas_call | solution.py:707
  136.9 1.9 collective-permute-start.4
  140.8 3.5 %collective-permute-done.2.a_arrived_ref = bf16[1024,1024]{1,0:T(8,128)(2,1)} collective-permute-done((bf16[1024,1024]{1,0:T(8,128)(2,1)}, bf16[1024,1024]{1,0:T(8,128)(2,1)}, u32[]{:S(2)}, u32[]{:S(2)}) %collective-permute-start.2) | collective-permute-done | bytes 2097184 | tf_op jit(solution)/shard_map/ppermute | solution.py:663
  144.3 1.8 collective-permute-start.7
  146.2 11.7 %input_gradient.1 = bf16[512,2048]{1,0:T(8,128)(2,1)} custom-call(bf16[512,1152]{1,0:T(8,128)(2,1)} %get-tuple-element.99.delta_query_key_ref.b_ref, bf16[512,1024]{1,0:T(8,128)(2,1)} %get-tuple-element.100.delta_value_ref.a_ref, bf16[512,1024]{1,0:T(8,128)(2,1)} %get-tuple-element.87.a_ref.delta_gate_ref, bf16[2,2048,512]{2,1,0:T(8,128)(2,1)} %query_key_weight_ref.3, ...), custom_call_target="tpu_custom_call" | custom-call | tf_op jit(solution)/shard_map/input_gradient/pallas_call | solution.py:638
  159.3 9.0 %keep_rows.3 = (bf16[256,1024]{1,0:T(8,128)(2,1)}, bf16[256,1024]{1,0:T(8,128)(2,1)}, bf16[256,1024]{1,0:T(8,128)(2,1)}, bf16[256,1024]{1,0:T(8,128)(2,1)}, bf16...) custom-call(s32[1]{0:T(128)} %bitcast.9.place_ref, ...), custom_call_target="tpu_custom_call" | custom-call | tf_op jit(solution)/shard_map/keep_rows/pallas_call | solution.py:728
  168.4 1.6 collective-permute-start.11
  171.9 2.0 collective-permute-start.9
  175.1 1.6 collective-permute-start.15
  176.7 18.0 %collective-permute-done.12 = bf16[256,1024]{1,0:T(8,128)(2,1)S(1)} collective-permute-done((bf16[256,1024]{1,0:T(8,128)(2,1)}, bf16[256,1024]{1,0:T(8,128)(2,1)S(1)}, u32[]{:S(2)}, u32[]{:S(2)}) %collective-permute-start.12) | collective-permute-done | bytes 524320 | tf_op jit(solution)/shard_map/ppermute | solution.py:663
  195.7 2.0 collective-permute-start.13
  199.5 1.6 collective-permute-start.10
  201.1 4.9 %collective-permute-done.15 = bf16[256,1024]{1,0:T(8,128)(2,1)S(1)} collective-permute-done((bf16[256,1024]{1,0:T(8,128)(2,1)S(1)}, bf16[256,1024]{1,0:T(8,128)(2,1)S(1)}, u32[]{:S(2)}, u32[]{:S(2)}) %collective-permute-start.15) | collective-permute-done | bytes 524320 | tf_op jit(solution)/shard_map/ppermute | solution.py:663
  207.5 14.2 %collective-permute-done.13 = bf16[256,1024]{1,0:T(8,128)(2,1)} collective-permute-done((bf16[256,1024]{1,0:T(8,128)(2,1)}, bf16[256,1024]{1,0:T(8,128)(2,1)}, u32[]{:S(2)}, u32[]{:S(2)}) %collective-permute-start.13) | collective-permute-done | bytes 524320 | tf_op jit(solution)/shard_map/ppermute | solution.py:663
  221.7 1.6 add_bitcast_fusion.2
  223.3 1.5 pad_maximum_fusion
  (80 shorter events, 20.0 us)
Async XLA Ops:
  17.1 21.2 %copy-start = (bf16[512,2048]{1,0:T(8,128)(2,1)S(1)}, bf16[512,2048]{1,0:T(8,128)(2,1)}, u32[]{:S(2)}) copy-start(bf16[512,2048]{1,0:T(8,128)(2,1)} %left_b_ref.7) | copy-start | bytes 6291460
  33.1 14.9 %all-to-all-start = ((bf16[8,1,128,256]{3,2,1,0:T(8,128)(2,1)}), bf16[8,1,128,256]{3,2,1,0:T(8,128)(2,1)S(1)}, u32[]{:S(2)}, u32[]{:S(2)}) async-start(bf16[8,1,128,256]{3,2,1,0:T(8,128)(2,1)} %bitcast.35), calls=%async_computation | async-start | bytes 1048576 | tf_op jit(solution)/shard_map/all_to_all | solution.py:523
  51.6 10.3 %all-to-all-start.1 = ((bf16[8,1,128,128]{3,2,1,0:T(8,128)(2,1)}), bf16[8,1,128,128]{3,2,1,0:T(8,128)(2,1)S(1)}, u32[]{:S(2)}, u32[]{:S(2)}) async-start(bf16[8,1,128,128]{3,2,1,0:T(8,128)(2,1)} %chain_forward.1), calls=%async_computation.1 | async-start | bytes 524288 | tf_op jit(solution)/shard_map/all_to_all | solution.py:523
  69.4 16.7 %all-to-all-start.2 = ((bf16[8,1,128,128]{3,2,1,0:T(8,128)(2,1)}), bf16[8,1,128,128]{3,2,1,0:T(8,128)(2,1)S(1)}, u32[]{:S(2)}, u32[]{:S(2)}) async-start(bf16[8,1,128,128]{3,2,1,0:T(8,128)(2,1)} %bitcast.38), calls=%async_computation.2 | async-start | bytes 524288 | tf_op jit(solution)/shard_map/all_to_all | solution.py:523
  73.2 155.0 %reduce-scatter.3.cloned.1.call-start = ((), (), s32[]{:S(2)}) async-start(), calls=%async_computation.6 | async-start | bytes 2621440 | tf_op jit(solution)/shard_map/reduce_scatter | solution.py:774
  79.7 14.1 %collective-permute-start = (bf16[1024,1024]{1,0:T(8,128)(2,1)}, bf16[1024,1024]{1,0:T(8,128)(2,1)S(1)}, u32[]{:S(2)}, u32[]{:S(2)}) collective-permute-start(bf16[1024,1024]{1,0:T(8,128)(2,1)} %get-tuple-element.88), channel_id=1, source_target_pairs={{0,4},{4,0},{8,12},{12,8},{16,20},{20,16},{24,28},{28,24},{1,5},{5... | collective-permute-start | bytes 6291464 | tf_op jit(solution)/shard_map/ppermute | solution.py:663
  80.0 13.8 %collective-permute-start.1 = (bf16[1024,1024]{1,0:T(8,128)(2,1)}, bf16[1024,1024]{1,0:T(8,128)(2,1)}, u32[]{:S(2)}, u32[]{:S(2)}) collective-permute-start(bf16[1024,1024]{1,0:T(8,128)(2,1)} %get-tuple-element.89), channel_id=1, source_target_pairs={{0,4},{4,0},{8,12},{12,8},{16,20},{20,16},{24,28},{28,24},{1,5},{5... | collective-permute-start | bytes 6291464 | tf_op jit(solution)/shard_map/ppermute | solution.py:663
  89.8 13.7 %all-to-all-start.3 = ((bf16[8,1,128,128]{3,2,1,0:T(8,128)(2,1)}), bf16[8,1,128,128]{3,2,1,0:T(8,128)(2,1)S(1)}, u32[]{:S(2)}, u32[]{:S(2)}) async-start(bf16[8,1,128,128]{3,2,1,0:T(8,128)(2,1)} %chain_backward.1), calls=%async_computation.4 | async-start | bytes 524288 | tf_op jit(solution)/shard_map/all_to_all | solution.py:523
  93.7 134.4 %reduce-scatter.5.cloned.1.call-start = ((), (), s32[]{:S(2)}) async-start(), calls=%async_computation.7 | async-start | bytes 2621440 | tf_op jit(solution)/shard_map/reduce_scatter | solution.py:774
  136.3 21.7 %collective-permute-start.3 = (bf16[1024,1152]{1,0:T(8,128)(2,1)}, bf16[1024,1152]{1,0:T(8,128)(2,1)S(1)}, u32[]{:S(2)}, u32[]{:S(2)}) collective-permute-start(bf16[1024,1152]{1,0:T(8,128)(2,1)} %get-tuple-element.102), channel_id=1, source_target_pairs={{0,4},{4,0},{8,12},{12,8},{16,20},{20,16},{24,28},{28,24},{1,5},{5... | collective-permute-start | bytes 7077896 | tf_op jit(solution)/shard_map/ppermute | solution.py:663
  136.8 7.5 %collective-permute-start.2 = (bf16[1024,1024]{1,0:T(8,128)(2,1)}, bf16[1024,1024]{1,0:T(8,128)(2,1)}, u32[]{:S(2)}, u32[]{:S(2)}) collective-permute-start(bf16[1024,1024]{1,0:T(8,128)(2,1)} %get-tuple-element.101), channel_id=1, source_target_pairs={{0,4},{4,0},{8,12},{12,8},{16,20},{20,16},{24,28},{28,24},{1,5},{5... | collective-permute-start | bytes 6291464 | tf_op jit(solution)/shard_map/ppermute | solution.py:663
  136.9 31.5 %collective-permute-start.4 = (bf16[256,1024]{1,0:T(8,128)(2,1)}, bf16[256,1024]{1,0:T(8,128)(2,1)}, u32[]{:S(2)}, u32[]{:S(2)}) collective-permute-start(bf16[256,1024]{1,0:T(8,128)(2,1)} %get-tuple-element.114), channel_id=1, source_target_pairs={{0,8},{4,12},{8,0},{12,4},{16,24},{20,28},{24,16},{28,20},{1,9},{5... | collective-permute-start | bytes 1572872 | tf_op jit(solution)/shard_map/ppermute | solution.py:663
  138.8 29.6 %collective-permute-start.5 = (bf16[256,1024]{1,0:T(8,128)(2,1)}, bf16[256,1024]{1,0:T(8,128)(2,1)}, u32[]{:S(2)}, u32[]{:S(2)}) collective-permute-start(bf16[256,1024]{1,0:T(8,128)(2,1)} %get-tuple-element.115), channel_id=1, source_target_pairs={{0,16},{4,20},{8,24},{12,28},{16,0},{20,4},{24,8},{28,12},{1,17},{... | collective-permute-start | bytes 1572872 | tf_op jit(solution)/shard_map/ppermute | solution.py:663
  140.3 28.1 %collective-permute-start.6 = (bf16[256,1024]{1,0:T(8,128)(2,1)}, bf16[256,1024]{1,0:T(8,128)(2,1)S(1)}, u32[]{:S(2)}, u32[]{:S(2)}) collective-permute-start(bf16[256,1024]{1,0:T(8,128)(2,1)} %get-tuple-element.116), channel_id=1, source_target_pairs={{0,8},{4,12},{8,0},{12,4},{16,24},{20,28},{24,16},{28,20},{1,9},{5... | collective-permute-start | bytes 1572872 | tf_op jit(solution)/shard_map/ppermute | solution.py:663
  144.3 24.1 %collective-permute-start.7 = (bf16[256,1024]{1,0:T(8,128)(2,1)}, bf16[256,1024]{1,0:T(8,128)(2,1)S(1)}, u32[]{:S(2)}, u32[]{:S(2)}) collective-permute-start(bf16[256,1024]{1,0:T(8,128)(2,1)} %get-tuple-element.117), channel_id=1, source_target_pairs={{0,16},{4,20},{8,24},{12,28},{16,0},{20,4},{24,8},{28,12},{1,17},{... | collective-permute-start | bytes 1572872 | tf_op jit(solution)/shard_map/ppermute | solution.py:663
  159.3 11.2 %copy-start.13 = (bf16[256,1024]{1,0:T(8,128)(2,1)S(1)}, bf16[256,1024]{1,0:T(8,128)(2,1)}, u32[]{:S(2)}) copy-start(bf16[256,1024]{1,0:T(8,128)(2,1)} %get-tuple-element.128) | copy-start | bytes 1572868
  159.3 14.5 %copy-start.12 = (bf16[256,1024]{1,0:T(8,128)(2,1)S(1)}, bf16[256,1024]{1,0:T(8,128)(2,1)}, u32[]{:S(2)}) copy-start(bf16[256,1024]{1,0:T(8,128)(2,1)} %get-tuple-element.132) | copy-start | bytes 1572868
  168.3 26.4 %copy-start.17 = (bf16[256,1024]{1,0:T(8,128)(2,1)S(1)}, bf16[256,1024]{1,0:T(8,128)(2,1)}, u32[]{:S(2)}) copy-start(bf16[256,1024]{1,0:T(8,128)(2,1)} %get-tuple-element.124) | copy-start | bytes 1572868
  168.4 8.3 %copy-start.16 = (bf16[256,1024]{1,0:T(8,128)(2,1)}, bf16[256,1024]{1,0:T(8,128)(2,1)S(1)}, u32[]{:S(2)}) copy-start(bf16[256,1024]{1,0:T(8,128)(2,1)S(1)} %collective-permute-done.6) | copy-start | bytes 1572868
  168.4 8.3 %copy-start.14 = (bf16[256,1024]{1,0:T(8,128)(2,1)}, bf16[256,1024]{1,0:T(8,128)(2,1)S(1)}, u32[]{:S(2)}) copy-start(bf16[256,1024]{1,0:T(8,128)(2,1)S(1)} %collective-permute-done.7) | copy-start | bytes 1572868
  168.4 29.3 %copy-start.11 = (bf16[256,1024]{1,0:T(8,128)(2,1)S(1)}, bf16[256,1024]{1,0:T(8,128)(2,1)}, u32[]{:S(2)}) copy-start(bf16[256,1024]{1,0:T(8,128)(2,1)} %get-tuple-element.126) | copy-start | bytes 1572868
  168.4 39.1 %collective-permute-start.11 = (bf16[256,1024]{1,0:T(8,128)(2,1)}, bf16[256,1024]{1,0:T(8,128)(2,1)}, u32[]{:S(2)}, u32[]{:S(2)}) collective-permute-start(bf16[256,1024]{1,0:T(8,128)(2,1)} %get-tuple-element.123), channel_id=1, source_target_pairs={{0,8},{4,12},{8,0},{12,4},{16,24},{20,28},{24,16},{28,20},{1,9},{5... | collective-permute-start | bytes 1572872 | tf_op jit(solution)/shard_map/ppermute | solution.py:663
  170.0 24.7 %collective-permute-start.12 = (bf16[256,1024]{1,0:T(8,128)(2,1)}, bf16[256,1024]{1,0:T(8,128)(2,1)S(1)}, u32[]{:S(2)}, u32[]{:S(2)}) collective-permute-start(bf16[256,1024]{1,0:T(8,128)(2,1)} %get-tuple-element.125), channel_id=1, source_target_pairs={{0,8},{4,12},{8,0},{12,4},{16,24},{20,28},{24,16},{28,20},{1,9},{5... | collective-permute-start | bytes 1572872 | tf_op jit(solution)/shard_map/ppermute | solution.py:663
  171.8 24.0 %collective-permute-start.14 = (bf16[256,1024]{1,0:T(8,128)(2,1)S(1)}, bf16[256,1024]{1,0:T(8,128)(2,1)S(1)}, u32[]{:S(2)}, u32[]{:S(2)}) collective-permute-start(bf16[256,1024]{1,0:T(8,128)(2,1)S(1)} %add_convert_fusion.2), channel_id=1, source_target_pairs={{0,16},{4,20},{8,24},{12,28},{16,0},{20,4},{24,8},{28,12},{1,17},{... | collective-permute-start | bytes 1572872 | tf_op jit(solution)/shard_map/ppermute | solution.py:663
  171.9 27.5 %collective-permute-start.9 = (bf16[256,1152]{1,0:T(8,128)(2,1)}, bf16[256,1152]{1,0:T(8,128)(2,1)S(1)}, u32[]{:S(2)}, u32[]{:S(2)}) collective-permute-start(bf16[256,1152]{1,0:T(8,128)(2,1)} %get-tuple-element.121), channel_id=1, source_target_pairs={{0,16},{4,20},{8,24},{12,28},{16,0},{20,4},{24,8},{28,12},{1,17},{... | collective-permute-start | bytes 1769480 | tf_op jit(solution)/shard_map/ppermute | solution.py:663
  175.1 24.2 %copy-start.8 = (bf16[256,1152]{1,0:T(8,128)(2,1)S(1)}, bf16[256,1152]{1,0:T(8,128)(2,1)}, u32[]{:S(2)}) copy-start(bf16[256,1152]{1,0:T(8,128)(2,1)} %get-tuple-element.120) | copy-start | bytes 1769476
  175.1 30.8 %collective-permute-start.15 = (bf16[256,1024]{1,0:T(8,128)(2,1)S(1)}, bf16[256,1024]{1,0:T(8,128)(2,1)S(1)}, u32[]{:S(2)}, u32[]{:S(2)}) collective-permute-start(bf16[256,1024]{1,0:T(8,128)(2,1)S(1)} %add_convert_fusion.1), channel_id=1, source_target_pairs={{0,8},{4,12},{8,0},{12,4},{16,24},{20,28},{24,16},{28,20},{1,9},{5... | collective-permute-start | bytes 1572872 | tf_op jit(solution)/shard_map/ppermute | solution.py:663
  194.7 30.1 %collective-permute-start.8 = (bf16[256,1152]{1,0:T(8,128)(2,1)}, bf16[256,1152]{1,0:T(8,128)(2,1)S(1)}, u32[]{:S(2)}, u32[]{:S(2)}) collective-permute-start(bf16[256,1152]{1,0:T(8,128)(2,1)} %get-tuple-element.119), channel_id=1, source_target_pairs={{0,16},{4,20},{8,24},{12,28},{16,0},{20,4},{24,8},{28,12},{1,17},{... | collective-permute-start | bytes 1769480 | tf_op jit(solution)/shard_map/ppermute | solution.py:663
  195.7 10.2 %copy-start.10 = (bf16[256,1024]{1,0:T(8,128)(2,1)S(1)}, bf16[256,1024]{1,0:T(8,128)(2,1)}, u32[]{:S(2)}) copy-start(bf16[256,1024]{1,0:T(8,128)(2,1)} %get-tuple-element.130) | copy-start | bytes 1572868
  195.7 10.2 %copy-start.15 = (bf16[256,1024]{1,0:T(8,128)(2,1)S(1)}, bf16[256,1024]{1,0:T(8,128)(2,1)}, u32[]{:S(2)}) copy-start(bf16[256,1024]{1,0:T(8,128)(2,1)} %copy-done.14) | copy-start | bytes 1572868
  195.7 26.0 %collective-permute-start.13 = (bf16[256,1024]{1,0:T(8,128)(2,1)}, bf16[256,1024]{1,0:T(8,128)(2,1)}, u32[]{:S(2)}, u32[]{:S(2)}) collective-permute-start(bf16[256,1024]{1,0:T(8,128)(2,1)} %add_convert_fusion.3), channel_id=1, source_target_pairs={{0,16},{4,20},{8,24},{12,28},{16,0},{20,4},{24,8},{28,12},{1,17},{... | collective-permute-start | bytes 1572872 | tf_op jit(solution)/shard_map/ppermute | solution.py:663
  199.5 25.4 %collective-permute-start.10 = (bf16[256,1152]{1,0:T(8,128)(2,1)S(1)}, bf16[256,1152]{1,0:T(8,128)(2,1)}, u32[]{:S(2)}, u32[]{:S(2)}) collective-permute-start(bf16[256,1152]{1,0:T(8,128)(2,1)S(1)} %add_convert_fusion), channel_id=1, source_target_pairs={{0,8},{4,12},{8,0},{12,4},{16,24},{20,28},{24,16},{28,20},{1,9},{5... | collective-permute-start | bytes 1769480 | tf_op jit(solution)/shard_map/ppermute | solution.py:663
  (8 other events, 14.0 us)
Sparse Core Ops, SparseCore 0:
  86.2 45.3 reduce-scatter.2
  158.1 43.9 reduce-scatter.4

commit v4 on v3

--- a/solution.py
+++ b/solution.py
@@ -13,6 +13,8 @@
 EPS = 1e-06
 QUERY_SCALE = DK ** (-0.5)
 LANES = 128
+FORWARD_SPANS = 2
+BACKWARD_SPANS = 2
 
 F32 = jnp.float32
 BF16 = jnp.bfloat16
@@ -51,14 +53,14 @@
     return row, col
 
 
-def decays(decay_beta_ref, bias_ref, scale_ref, resets_ref):
+def decays(decay_beta, bias_ref, scale_ref, resets):
     row, col = grid_of(CHUNK)
     lower = (row >= col).astype(F32)
     heads = bias_ref.shape[1]
-    decay_logit = decay_beta_ref[:, :heads]
-    beta = sigmoid(decay_beta_ref[:, heads:] + bias_ref[...])
+    decay_logit = decay_beta[:, :heads]
+    beta = sigmoid(decay_beta[:, heads:] + bias_ref[...])
     log_decay = -scale_ref[...] * softplus(decay_logit)
-    resets = jnp.broadcast_to(resets_ref[0].astype(F32), (8, CHUNK))
+    resets = jnp.broadcast_to(resets.astype(F32), (8, CHUNK))
     doc_row = dot(resets, lower, NT)[0:1]
     doc_col = dot(lower, resets, NT)[:, 0:1]
     cum_col = exact(lower, log_decay)
@@ -75,12 +77,12 @@
 
 
 def pair_decay(cum_col, cum_row, same, h):
-    gap = jnp.minimum(cum_col[:, h : h + 1] - cum_row[h : h + 1, :], 0.0)
+    gap = jnp.minimum(spread_column(cum_col, h) - cum_row[h : h + 1, :], 0.0)
     return jnp.where(same, jnp.exp(gap), 0.0)
 
 
-def head(ref, index, h):
-    return ref[index][:, h * DK : (h + 1) * DK]
+def spread_column(columns, h):
+    return jnp.broadcast_to(columns[:, h : h + 1], (columns.shape[0], LANES))
 
 
 def unit_rows(x):
@@ -105,6 +107,7 @@
     heads = state_ref.shape[0]
     key_heads = query_key_ref.shape[2] // DK
     repeat = heads // key_heads
+    spans = solve_ref.shape[0]
     row, col = grid_of(CHUNK)
 
     @pl.when(pl.program_id(0) == 0)
@@ -113,60 +116,67 @@
         for h in range(heads):
             state_ref[h] = first
 
-    beta, cum_col, cum_row, same, start, end, total, _ = decays(
-        decay_beta_ref, bias_ref, scale_ref, resets_ref
-    )
     strict = row > col
     differ = row ^ col
-    keys, queries, systems, scores = [], [], [], []
-    for g in range(key_heads):
-        q = unit_rows(head(query_key_ref, 0, g))[0] * QUERY_SCALE
-        k = unit_rows(head(query_key_ref, 1, g))[0]
-        queries.append(q)
-        keys.append(k)
-        key_gram = dot(k, k, NT)
-        query_gram = dot(q, k, NT)
-        for h in range(g * repeat, (g + 1) * repeat):
-            decay = pair_decay(cum_col, cum_row, same, h)
-            scores.append((decay * query_gram).astype(BF16))
-            systems.append(jnp.where(strict, beta[:, h : h + 1] * decay * key_gram, 0.0))
+    rows = [slice(c * CHUNK, (c + 1) * CHUNK) for c in range(spans)]
+    each = [(c, h) for c in range(spans) for h in range(heads)]
+    terms = [
+        decays(decay_beta_ref[rows[c]], bias_ref, scale_ref, resets_ref[c]) for c in range(spans)
+    ]
+    keys, queries = {}, {}
+    for c in range(spans):
+        for g in range(key_heads):
+            cols = slice(g * DK, (g + 1) * DK)
+            queries[c, g] = unit_rows(query_key_ref[0, rows[c], cols])[0] * QUERY_SCALE
+            keys[c, g] = unit_rows(query_key_ref[1, rows[c], cols])[0]
+    grams = {p: (dot(keys[p], keys[p], NT), dot(queries[p], keys[p], NT)) for p in keys}
+    scores, systems, betas, starts = {}, {}, {}, {}
+    for c, h in each:
+        beta, cum_col, cum_row, same, start = terms[c][:5]
+        betas[c, h] = spread_column(beta, h)
+        starts[c, h] = spread_column(start, h)
+        decay = pair_decay(cum_col, cum_row, same, h)
+        key_gram, query_gram = grams[c, h // repeat]
+        scores[c, h] = (decay * query_gram).astype(BF16)
+        systems[c, h] = jnp.where(strict, betas[c, h] * decay * key_gram, 0.0)
     identity = (row == col).astype(F32)
-    inverse = [
-        (identity - jnp.where(differ == 1, system, 0.0)).astype(BF16) for system in systems
-    ]
+    inverse = {
+        p: (identity - jnp.where(differ == 1, systems[p], 0.0)).astype(BF16) for p in each
+    }
     level = 1
     while (1 << level) < CHUNK:
         here = (differ >> level) == 1
-        inner = [
-            dot(jnp.where(here, system, 0.0), x).astype(BF16)
-            for system, x in zip(systems, inverse)
-        ]
-        inverse = [x - dot(x, y).astype(BF16) for x, y in zip(inverse, inner)]
+        inner = {
+            p: dot(jnp.where(here, systems[p], 0.0), inverse[p]).astype(BF16) for p in each
+        }
+        inverse = {p: inverse[p] - dot(inverse[p], inner[p]).astype(BF16) for p in each}
         level += 1
-    weights = []
-    for h in range(heads):
-        k = keys[h // repeat]
-        v = value_ref[:, h * DV : (h + 1) * DV]
-        b = beta[:, h : h + 1]
-        right = jnp.concatenate([(b * start[:, h : h + 1]) * k, b * v], axis=1)
-        weights.append(dot(inverse[h], right))
-        solve_ref[0, h] = inverse[h]
-    values = []
-    for h in range(heads):
-        state = state_ref[h].astype(BF16)
-        start_ref[0, h] = state
-        solved = weights[h]
-        base = jnp.concatenate([jnp.zeros((CHUNK, DK), F32), solved[:, DK:]], axis=1)
-        values.append((base - dot(solved[:, :DK], state)).astype(BF16))
-    for h in range(heads):
-        k, q = keys[h // repeat], queries[h // repeat]
-        state = state_ref[h]
-        out = dot(start[:, h : h + 1] * q, state) + dot(scores[h], values[h])
-        map_ref[:, h * DK : (h + 1) * DK] = out[:, :DK].astype(BF16)
-        local_ref[:, h * DV : (h + 1) * DV] = out[:, DK:]
-        state = total[:, h : h + 1] * state + dot(end[:, h : h + 1] * k, values[h], TN)
-        state_ref[h] = state
-        total_ref[h] = state.astype(BF16)
+    weights = {}
+    for c, h in each:
+        k = keys[c, h // repeat]
+        v = value_ref[rows[c], h * DV : (h + 1) * DV]
+        b = betas[c, h]
+        right = jnp.concatenate([(b * starts[c, h]) * k, b * v], axis=1)
+        weights[c, h] = dot(inverse[c, h], right)
+        solve_ref[c, h] = inverse[c, h]
+    for c in range(spans):
+        end, total = terms[c][5:7]
+        values = []
+        for h in range(heads):
+            state = state_ref[h].astype(BF16)
+            start_ref[c, h] = state
+            solved = weights[c, h]
+            base = jnp.concatenate([jnp.zeros((CHUNK, DK), F32), solved[:, DK:]], axis=1)
+            values.append((base - dot(solved[:, :DK], state)).astype(BF16))
+        for h in range(heads):
+            k, q = keys[c, h // repeat], queries[c, h // repeat]
+            state = state_ref[h]
+            out = dot(starts[c, h] * q, state) + dot(scores[c, h], values[h])
+            map_ref[rows[c], h * DK : (h + 1) * DK] = out[:, :DK].astype(BF16)
+            local_ref[rows[c], h * DV : (h + 1) * DV] = out[:, DK:]
+            state = total[:, h : h + 1] * state + dot(spread_column(end, h) * k, values[h], TN)
+            state_ref[h] = state
+            total_ref[h] = state.astype(BF16)
 
 
 def output_kernel(
@@ -189,10 +199,13 @@
     def _():
         total_ref[...] = jnp.zeros_like(total_ref)
 
+    outs, deltas = [], []
     for h in range(heads):
         cols = slice(h * DV, (h + 1) * DV)
-        reach = map_ref[:, cols]
-        out = local_ref[:, cols] + dot(reach, state_ref[h])
+        outs.append(local_ref[:, cols] + dot(map_ref[:, cols], state_ref[h]))
+    for h in range(heads):
+        cols = slice(h * DV, (h + 1) * DV)
+        out = outs[h]
         gate = gate_ref[:, cols]
         delta = delta_ref[:, cols]
         scale = lax.rsqrt(row_sum(out * out) * (1.0 / DV) + EPS)
@@ -210,7 +223,10 @@
         )
         delta_out = delta_out.astype(BF16)
         delta_out_ref[:, cols] = delta_out
-        part = total_ref[h] + dot(reach, delta_out, TN)
+        deltas.append(delta_out)
+    for h in range(heads):
+        cols = slice(h * DV, (h + 1) * DV)
+        part = total_ref[h] + dot(map_ref[:, cols], deltas[h], TN)
         total_ref[h] = part
         delta_state_ref[h] = part.astype(BF16)
 
@@ -234,125 +250,145 @@
     heads = carry_ref.shape[0]
     key_heads = query_key_ref.shape[2] // DK
     repeat = heads // key_heads
+    spans = solve_ref.shape[0]
     row, col = grid_of(CHUNK)
 
     @pl.when(pl.program_id(0) == 0)
     def _():
         carry_ref[...] = delta_final_ref[...].astype(F32)
 
-    beta, cum_col, cum_row, same, start, end, total, resets = decays(
-        decay_beta_ref, bias_ref, scale_ref, resets_ref
-    )
     strict = row > col
-    lane = lax.broadcasted_iota(jnp.int32, (CHUNK, heads), 1)
+    upper = (row <= col).astype(F32)
+    identity = (row == col).astype(F32)
+    rows = [slice(c * CHUNK, (c + 1) * CHUNK) for c in range(spans)]
+    cols = [slice(h * DV, (h + 1) * DV) for h in range(heads)]
+    each = [(c, h) for c in reversed(range(spans)) for h in range(heads)]
+    terms = [
+        decays(decay_beta_ref[rows[c]], bias_ref, scale_ref, resets_ref[c]) for c in range(spans)
+    ]
+    half = lax.broadcasted_iota(jnp.int32, (2 * DK, 2 * heads), 0) // DK
+    lane = lax.broadcasted_iota(jnp.int32, (2 * DK, 2 * heads), 1)
     lane_one = lax.broadcasted_iota(jnp.int32, (1, heads), 1)
-    state_of, value_of, right_of = [], [], []
-    qs, ks, q_inv, k_inv, grams = [], [], [], [], []
-    for g in range(key_heads):
-        q, qi = unit_rows(head(query_key_ref, 0, g))
-        k, ki = unit_rows(head(query_key_ref, 1, g))
-        q = q * QUERY_SCALE
-        qs.append(q)
-        ks.append(k)
-        q_inv.append(qi)
-        k_inv.append(ki)
-        grams.append((dot(k, k, NT), dot(q, k, NT)))
-    for h in range(heads):
-        before = start_ref[0, h]
+    qs, ks, q_inv, k_inv = {}, {}, {}, {}
+    for c in range(spans):
+        for g in range(key_heads):
+            at = slice(g * DK, (g + 1) * DK)
+            q, q_inv[c, g] = unit_rows(query_key_ref[0, rows[c], at])
+            qs[c, g] = q * QUERY_SCALE
+            ks[c, g], k_inv[c, g] = unit_rows(query_key_ref[1, rows[c], at])
+    grams = {p: (dot(ks[p], ks[p], NT), dot(qs[p], ks[p], NT)) for p in ks}
+    state_of, value_of, right_of = {}, {}, {}
+    betas, starts, ends = {}, {}, {}
+    for c, h in each:
+        before = start_ref[c, h]
         state = dot(before[:, :DK], state_in_ref[h]) + before[:, DK:].astype(F32)
-        state_of.append(state.astype(BF16))
-    for h in range(heads):
-        k = ks[h // repeat]
-        v = value_ref[:, h * DV : (h + 1) * DV]
-        seen = dot(k, state_of[h])
-        right_of.append(beta[:, h : h + 1] * (v - start[:, h : h + 1] * seen))
-    for h in range(heads):
-        value_of.append(dot(solve_ref[0, h], right_of[h]).astype(BF16))
-    decay_of, delta_value_of, delta_right_of = [], [], []
-    for h in range(heads):
-        decay = pair_decay(cum_col, cum_row, same, h)
-        decay_of.append(decay)
-        k = ks[h // repeat]
-        delta_out = delta_out_ref[:, h * DV : (h + 1) * DV]
-        carry = carry_ref[h].astype(BF16)
-        delta_value_of.append(
-            dot(decay * grams[h // repeat][1], delta_out, TN)
-            + dot(end[:, h : h + 1] * k, carry)
+        state_of[c, h] = state.astype(BF16)
+    for c, h in each:
+        beta, start, end = terms[c][0], terms[c][4], terms[c][5]
+        seen = dot(ks[c, h // repeat], state_of[c, h])
+        betas[c, h] = spread_column(beta, h)
+        starts[c, h] = spread_column(start, h)
+        ends[c, h] = spread_column(end, h)
+        right_of[c, h] = betas[c, h] * (value_ref[rows[c], cols[h]] - starts[c, h] * seen)
+    for c, h in each:
+        value_of[c, h] = dot(solve_ref[c, h], right_of[c, h]).astype(BF16)
+    decay_of, delta_value_of, delta_right_of = {}, {}, {}
+    for c, h in each:
+        decay_of[c, h] = pair_decay(terms[c][1], terms[c][2], terms[c][3], h)
+        delta_value_of[c, h] = dot(
+            decay_of[c, h] * grams[c, h // repeat][1], delta_out_ref[rows[c], cols[h]], TN
         )
-    for h in range(heads):
-        delta_right_of.append(dot(solve_ref[0, h], delta_value_of[h], TN))
-    sums = jnp.zeros((CHUNK, heads), F32)
-    logits = jnp.zeros((CHUNK, heads), F32)
-    tail = jnp.zeros((1, heads), F32)
-    lower_rows = []
-    for g in range(key_heads):
-        q, k = qs[g], ks[g]
-        key_gram, query_gram = grams[g]
-        delta_q = jnp.zeros((CHUNK, DK), F32)
-        delta_k = jnp.zeros((CHUNK, DK), F32)
-        for h in range(g * repeat, (g + 1) * repeat):
-            cols = slice(h * DV, (h + 1) * DV)
-            b, s, e = beta[:, h : h + 1], start[:, h : h + 1], end[:, h : h + 1]
-            delta_out = delta_out_ref[:, cols]
-            delta_right = delta_right_of[h]
-            delta_value_ref[:, cols] = (b * delta_right).astype(BF16)
-            pseudo = value_of[h]
-            both = jnp.concatenate([delta_out, delta_right.astype(BF16)], axis=0)
+    both_of, held_of, carry_of = {}, {}, {}
+    for c in reversed(range(spans)):
+        total = terms[c][6]
+        for h in range(heads):
+            carry_of[c, h] = carry_ref[h].astype(BF16)
+            delta_value_of[c, h] += dot(ends[c, h] * ks[c, h // repeat], carry_of[c, h])
+        for h in range(heads):
+            delta_right_of[c, h] = dot(solve_ref[c, h], delta_value_of[c, h], TN)
+        for h in range(heads):
+            q, k = qs[c, h // repeat], ks[c, h // repeat]
+            b, s = betas[c, h], starts[c, h]
+            delta_right = delta_right_of[c, h]
+            delta_value_ref[rows[c], cols[h]] = (b * delta_right).astype(BF16)
+            both_of[c, h] = jnp.concatenate(
+                [delta_out_ref[rows[c], cols[h]], delta_right.astype(BF16)], axis=0
+            )
             carry = carry_ref[h]
-            pairs = dot(both, pseudo, NT)
-            states = dot(both, state_of[h], NT)
-            decay = decay_of[h]
-            pair_q = decay * pairs[:CHUNK]
-            pair_k = jnp.where(strict, (-b) * decay * pairs[CHUNK:], 0.0)
-            cross = pair_q * query_gram + pair_k * key_gram
-            state_q = s * states[:CHUNK]
-            state_k = (b * s) * states[CHUNK:]
-            end_k = e * dot(pseudo, carry, NT)
-            delta_q += dot(pair_q, k) + state_q
-            delta_k += (
-                dot(pair_k, k)
-                + dot(
-                    jnp.concatenate([pair_q, pair_k], axis=0),
-                    jnp.concatenate([q, k], axis=0),
-                    TN,
+            held_of[c, h] = total[:, h : h + 1] * row_sum(
+                jnp.sum(state_of[c, h].astype(F32) * carry, axis=0, keepdims=True)
+            )
+            carry_ref[h] = total[:, h : h + 1] * carry + dot(
+                jnp.concatenate([s * q, (-b * s) * k], axis=0), both_of[c, h], TN
+            )
+    pairs_of = {p: dot(both_of[p], value_of[p], NT) for p in each}
+    states_of = {p: dot(both_of[p], state_of[p], NT) for p in each}
+    ends_of = {p: ends[p] * dot(value_of[p], carry_of[p], NT) for p in each}
+    pair_of, sum_of, tail_of, lower_of = {}, {}, {}, {}
+    for c, h in each:
+        q, k = qs[c, h // repeat], ks[c, h // repeat]
+        key_gram, query_gram = grams[c, h // repeat]
+        decay, b, s = decay_of[c, h], betas[c, h], starts[c, h]
+        pair_q = decay * pairs_of[c, h][:CHUNK]
+        pair_k = jnp.where(strict, (-b) * decay * pairs_of[c, h][CHUNK:], 0.0)
+        cross = jnp.where(strict, pair_q * query_gram + pair_k * key_gram, 0.0).astype(BF16)
+        pair_of[c, h] = (pair_q.astype(BF16), pair_k.astype(BF16))
+        state_q = s * states_of[c, h][:CHUNK]
+        state_k = (b * s) * states_of[c, h][CHUNK:]
+        states_of[c, h] = (state_q, ends_of[c, h] - state_k)
+        sum_of[c, h] = jnp.concatenate(
+            [cross, (state_q * q - state_k * k).astype(BF16)], axis=1
+        )
+        tail_of[c, h] = jnp.concatenate(
+            [ends_of[c, h] * k, delta_right_of[c, h] * value_of[c, h].astype(F32)], axis=1
+        ).astype(BF16)
+        lower_of[c, h] = jnp.sum(cross.astype(F32), axis=0, keepdims=True)
+    for c in range(spans):
+        for g in range(key_heads):
+            q, k = qs[c, g], ks[c, g]
+            both = jnp.concatenate([q, k], axis=0)
+            delta_q = jnp.zeros((CHUNK, DK), F32)
+            delta_k = jnp.zeros((CHUNK, DK), F32)
+            for h in range(g * repeat, (g + 1) * repeat):
+                pair_q, pair_k = pair_of[c, h]
+                delta_q += dot(pair_q, k) + states_of[c, h][0]
+                delta_k += (
+                    dot(pair_k, k)
+                    + dot(jnp.concatenate([pair_q, pair_k], axis=0), both, TN)
+                    + states_of[c, h][1]
                 )
-                + end_k
-                - state_k
-            )
-            ends = row_sum(end_k * k)
-            column = row_sum(cross + state_q * q - state_k * k) - ends
-            sums = jnp.where(lane == h, column, sums)
-            lower_rows.append(jnp.sum(cross, axis=0, keepdims=True))
-            held = total[:, h : h + 1] * jnp.sum(
-                state_of[h].astype(F32) * carry, axis=(0, 1), keepdims=True
-            )
-            tail = jnp.where(lane_one == h, held + jnp.sum(ends, axis=0, keepdims=True), tail)
-            logits = jnp.where(lane == h, row_sum(delta_right * pseudo.astype(F32)), logits)
-            carry_ref[h] = total[:, h : h + 1] * carry + dot(
-                jnp.concatenate([s * q, (-b * s) * k], axis=0), both, TN
-            )
-        delta_q = delta_q * QUERY_SCALE
-        unit = q * (1.0 / QUERY_SCALE)
-        delta_q = q_inv[g] * (delta_q - unit * row_sum(unit * delta_q))
-        delta_k = k_inv[g] * (delta_k - k * row_sum(k * delta_k))
-        delta_query_key_ref[:, g * DK : (g + 1) * DK] = delta_q.astype(BF16)
-        delta_query_key_ref[:, (key_heads + g) * DK : (key_heads + g + 1) * DK] = (
-            delta_k.astype(BF16)
-        )
-    upper = (row <= col).astype(F32)
-    reset_col = dot((row == col).astype(F32), resets, NT)[:, 0:1]
-    pad = -heads % 8
-    if pad:
-        lower_rows.append(jnp.zeros((pad, CHUNK), F32))
-    below = jnp.concatenate(lower_rows, axis=0)
-    delta_log = exact(upper, sums) - exact(upper, below, NT)[:, :heads] + tail
-    delta_log = jnp.where(reset_col == 0.0, delta_log, 0.0)
-    delta_decay = delta_log * (-scale_ref[...]) * sigmoid(decay_beta_ref[:, :heads])
-    delta_beta = logits * (1.0 - beta)
-    rest = jnp.zeros((CHUNK, LANES - 2 * heads), F32)
-    delta_query_key_ref[:, 2 * key_heads * DK :] = jnp.concatenate(
-        [delta_decay, delta_beta, rest], axis=1
-    ).astype(BF16)
+            delta_q = delta_q * QUERY_SCALE
+            unit = q * (1.0 / QUERY_SCALE)
+            delta_q = q_inv[c, g] * (delta_q - unit * row_sum(unit * delta_q))
+            delta_k = k_inv[c, g] * (delta_k - k * row_sum(k * delta_k))
+            at, after = g * DK, (key_heads + g) * DK
+            delta_query_key_ref[rows[c], at : at + DK] = delta_q.astype(BF16)
+            delta_query_key_ref[rows[c], after : after + DK] = delta_k.astype(BF16)
+    for c in range(spans):
+        beta, resets = terms[c][0], terms[c][7]
+        sums = jnp.zeros((CHUNK, 2 * heads), F32)
+        tails = jnp.zeros((CHUNK, 2 * heads), F32)
+        tail = jnp.zeros((1, heads), F32)
+        for h in range(heads):
+            sums += dot(sum_of[c, h], lane == h)
+            tails += dot(tail_of[c, h], lane == h + heads * half)
+            tail = jnp.where(lane_one == h, held_of[c, h], tail)
+        below = [lower_of[c, h] for h in range(heads)]
+        if heads % 8:
+            below.append(jnp.zeros((-heads % 8, CHUNK), F32))
+        below = exact(upper, jnp.concatenate(below, axis=0), NT)[:, :heads]
+        ends_sum = tails[:, :heads]
+        tail = tail + jnp.sum(ends_sum, axis=0, keepdims=True)
+        delta_log = exact(upper, sums[:, :heads] - ends_sum) - below + tail
+        reset_col = dot(identity, resets, NT)[:, 0:1]
+        delta_log = jnp.where(reset_col == 0.0, delta_log, 0.0)
+        logits = decay_beta_ref[rows[c], :heads]
+        delta_decay = delta_log * (-scale_ref[...]) * sigmoid(logits)
+        delta_beta = tails[:, heads:] * (1.0 - beta)
+        rest = jnp.zeros((CHUNK, LANES - 2 * heads), F32)
+        delta_query_key_ref[rows[c], 2 * key_heads * DK :] = jnp.concatenate(
+            [delta_decay, delta_beta, rest], axis=1
+        ).astype(BF16)
 
 
 def chain_forward_kernel(totals_ref, states_ref):
@@ -400,23 +436,25 @@
 def run_forward(query_key, value, decay_beta, bias, scale, resets):
     tokens, heads = query_key.shape[1], bias.shape[1]
     chunks = tokens // CHUNK
+    spans = min(FORWARD_SPANS, chunks)
+    step = spans * CHUNK
     key_width, value_width = query_key.shape[2], heads * DV
     return pl.pallas_call(
         forward_kernel,
-        grid=(chunks,),
+        grid=(chunks // spans,),
         in_specs=[
-            pl.BlockSpec((2, CHUNK, key_width), lambda c: (0, c, 0)),
-            pl.BlockSpec((CHUNK, value_width), lambda c: (c, 0)),
-            pl.BlockSpec((CHUNK, 2 * heads), lambda c: (c, 0)),
+            pl.BlockSpec((2, step, key_width), lambda c: (0, c, 0)),
+            pl.BlockSpec((step, value_width), lambda c: (c, 0)),
+            pl.BlockSpec((step, 2 * heads), lambda c: (c, 0)),
             whole((1, heads)),
             whole((1, heads)),
-            pl.BlockSpec((1, 1, CHUNK), lambda c: (c, 0, 0)),
+            pl.BlockSpec((spans, 1, CHUNK), lambda c: (c, 0, 0)),
         ],
         out_specs=[
-            pl.BlockSpec((1, heads, CHUNK, CHUNK), lambda c: (c, 0, 0, 0)),
-            pl.BlockSpec((1, heads, DK, DK + DV), lambda c: (c, 0, 0, 0)),
-            pl.BlockSpec((CHUNK, value_width), lambda c: (c, 0)),
-            pl.BlockSpec((CHUNK, value_width), lambda c: (c, 0)),
+            pl.BlockSpec((spans, heads, CHUNK, CHUNK), lambda c: (c, 0, 0, 0)),
+            pl.BlockSpec((spans, heads, DK, DK + DV), lambda c: (c, 0, 0, 0)),
+            pl.BlockSpec((step, value_width), lambda c: (c, 0)),
+            pl.BlockSpec((step, value_width), lambda c: (c, 0)),
             whole((heads, DK, DK + DV)),
         ],
         out_shape=[
@@ -468,27 +506,29 @@
 ):
     tokens, heads = query_key.shape[1], bias.shape[1]
     chunks = tokens // CHUNK
+    spans = min(BACKWARD_SPANS, chunks)
+    step = spans * CHUNK
     key_width, value_width = query_key.shape[2], heads * DV
-    last = chunks - 1
+    last = chunks // spans - 1
     return pl.pallas_call(
         backward_kernel,
-        grid=(chunks,),
+        grid=(chunks // spans,),
         in_specs=[
-            pl.BlockSpec((2, CHUNK, key_width), lambda c: (0, last - c, 0)),
-            pl.BlockSpec((CHUNK, value_width), lambda c: (last - c, 0)),
-            pl.BlockSpec((CHUNK, 2 * heads), lambda c: (last - c, 0)),
+            pl.BlockSpec((2, step, key_width), lambda c: (0, last - c, 0)),
+            pl.BlockSpec((step, value_width), lambda c: (last - c, 0)),
+            pl.BlockSpec((step, 2 * heads), lambda c: (last - c, 0)),
             whole((1, heads)),
             whole((1, heads)),
-            pl.BlockSpec((1, 1, CHUNK), lambda c: (last - c, 0, 0)),
-            pl.BlockSpec((1, heads, CHUNK, CHUNK), lambda c: (last - c, 0, 0, 0)),
-            pl.BlockSpec((1, heads, DK, DK + DV), lambda c: (last - c, 0, 0, 0)),
+            pl.BlockSpec((spans, 1, CHUNK), lambda c: (last - c, 0, 0)),
+            pl.BlockSpec((spans, heads, CHUNK, CHUNK), lambda c: (last - c, 0, 0, 0)),
+            pl.BlockSpec((spans, heads, DK, DK + DV), lambda c: (last - c, 0, 0, 0)),
             whole((heads, DK, DV)),
-            pl.BlockSpec((CHUNK, value_width), lambda c: (last - c, 0)),
+            pl.BlockSpec((step, value_width), lambda c: (last - c, 0)),
             whole((heads, DK, DV)),
         ],
         out_specs=[
-            pl.BlockSpec((CHUNK, 2 * key_width + LANES), lambda c: (last - c, 0)),
-            pl.BlockSpec((CHUNK, value_width), lambda c: (last - c, 0)),
+            pl.BlockSpec((step, 2 * key_width + LANES), lambda c: (last - c, 0)),
+            pl.BlockSpec((step, value_width), lambda c: (last - c, 0)),
         ],
         out_shape=[
             jax.ShapeDtypeStruct((tokens, 2 * key_width + LANES), BF16),
@@ -671,17 +711,17 @@
     return target_y * 4 + target_x * 2 + core
 
 
-def send_kernel(place_ref, left_a_ref, a_ref, left_b_ref, b_ref, a_out_ref, b_out_ref):
-    a_out_ref[...] = dot(left_a_ref[...], a_ref[...], TN).astype(BF16)
-    b_out_ref[...] = dot(left_b_ref[...], b_ref[...], TN).astype(BF16)
-
-
-def keep_kernel(
-    place_ref, left_a_ref, a_ref, left_b_ref, b_ref, a_arrived_ref, b_arrived_ref, *out_refs
-):
+def send_kernel(place_ref, left_a_ref, a_ref, left_b_ref, b_ref, out_ref):
+    width = a_ref.shape[1]
+    out_ref[:, :width] = dot(left_a_ref[...], a_ref[...], TN).astype(BF16)
+    out_ref[:, width:] = dot(left_b_ref[...], b_ref[...], TN).astype(BF16)
+
+
+def keep_kernel(place_ref, left_a_ref, a_ref, left_b_ref, b_ref, arrived_ref, *out_refs):
     step = pl.program_id(0)
-    a = dot(left_a_ref[...], a_ref[...], TN) + a_arrived_ref[...].astype(F32)
-    b = dot(left_b_ref[...], b_ref[...], TN) + b_arrived_ref[...].astype(F32)
+    width = a_ref.shape[1]
+    a = dot(left_a_ref[...], a_ref[...], TN) + arrived_ref[:, :width].astype(F32)
+    b = dot(left_b_ref[...], b_ref[...], TN) + arrived_ref[:, width:].astype(F32)
     for i in range(4):
 
         @pl.when(step == i)
@@ -703,27 +743,23 @@
 
 
 def halving_start(place, left_a, a, left_b, b):
-    rows = left_a.shape[1] // 8
+    rows, width = left_a.shape[1] // 8, a.shape[1] + b.shape[1]
     return pl.pallas_call(
         send_kernel,
         grid_spec=pltpu.PrefetchScalarGridSpec(
             num_scalar_prefetch=1,
             grid=(4,),
             in_specs=pair_specs(left_a, a, left_b, b, 1),
-            out_specs=[
-                pl.BlockSpec((rows, delta.shape[1]), lambda i, place: (i, 0)) for delta in (a, b)
-            ],
+            out_specs=pl.BlockSpec((rows, width), lambda i, place: (i, 0)),
         ),
-        out_shape=[
-            jax.ShapeDtypeStruct((4 * rows, delta.shape[1]), BF16) for delta in (a, b)
-        ],
+        out_shape=jax.ShapeDtypeStruct((4 * rows, width), BF16),
         compiler_params=PARAMS,
         interpret=INTERPRET,
         name="send_rows",
     )(place, left_a, a, left_b, b)
 
 
-def halving_keep(place, left_a, a, left_b, b, a_arrived, b_arrived):
+def halving_keep(place, left_a, a, left_b, b, arrived):
     rows = left_a.shape[1] // 8
     return pl.pallas_call(
         keep_kernel,
@@ -731,7 +767,7 @@
             num_scalar_prefetch=1,
             grid=(4,),
             in_specs=pair_specs(left_a, a, left_b, b, 0)
-            + [pl.BlockSpec((rows, delta.shape[1]), lambda i, place: (i, 0)) for delta in (a, b)],
+            + [pl.BlockSpec((rows, arrived.shape[1]), lambda i, place: (i, 0))],
             out_specs=[
                 pl.BlockSpec((rows, delta.shape[1]), lambda i, place: (0, 0))
                 for delta in (a, b)
@@ -746,7 +782,7 @@
         compiler_params=PARAMS,
         interpret=INTERPRET,
         name="keep_rows",
-    )(place, left_a, a, left_b, b, a_arrived, b_arrived)
+    )(place, left_a, a, left_b, b, arrived)
 
 
 def summed(a, b):
@@ -758,9 +794,12 @@
     return exchange(a[0], 2), exchange(b[0], 4), exchange(a[1], 2), exchange(b[2], 4)
 
 
-def halving_last(pieces, arrived):
-    a, b = pieces[:4], pieces[4:]
-    return exchange(summed(a[2], arrived[0]), 4), exchange(summed(b[1], arrived[1]), 2)
+def halving_onward(pieces, arrived):
+    return summed(pieces[2], arrived[0]), summed(pieces[5], arrived[1])
+
+
+def halving_last(onward):
+    return exchange(onward[0], 4), exchange(onward[1], 2)
 
 
 def halving_sum(pieces, arrived, last):
@@ -818,9 +857,7 @@
     if cubic:
         place = lax.axis_index("ctx").astype(jnp.int32).reshape(1)
         early = (place, inputs, delta_gate, grad_mixed, hidden)
-        sent = halving_start(*early)
-        arrived = [exchange(part, 1) for part in sent]
-        early_pieces = halving_keep(*early, *arrived)
+        early_pieces = halving_keep(*early, exchange(halving_start(*early), 1))
         finals, early_pieces = together(finals, early_pieces)
         early_arrived = halving_cross(early_pieces)
     delta_final = gather_parts(finals, heads)
@@ -839,8 +876,10 @@
     )
     if cubic:
         late = (place, inputs, delta_value, inputs, delta_query_key)
-        sent = halving_start(*late)
-        arrived = [exchange(part, 1) for part in sent]
+        arrived = exchange(halving_start(*late), 1)
+        early_onward = halving_onward(early_pieces, early_arrived)
+        delta_gate, early_onward = together(delta_gate, early_onward)
+        early_last = halving_last(early_onward)
     grad_rows = run_input_gradient(
         delta_query_key,
         delta_value,
@@ -853,11 +892,9 @@
         grad_rows, arrived = together(grad_rows, arrived)
     grad_inputs = scatter(grad_rows, "head", 1)
     if cubic:
-        late_pieces = halving_keep(*late, *arrived)
-        late_pieces, early_arrived = together(late_pieces, early_arrived)
+        late_pieces = halving_keep(*late, arrived)
         late_arrived = halving_cross(late_pieces)
-        early_last = halving_last(early_pieces, early_arrived)
-        late_last = halving_last(late_pieces, late_arrived)
+        late_last = halving_last(halving_onward(late_pieces, late_arrived))
         grad_gate, grad_out = halving_sum(early_pieces, early_arrived, early_last)
         grad_out = grad_out.T
         grad_value, packed = halving_sum(late_pieces, late_arrived, late_last)

time: 236 us -> 230 us (0.975)
  waiting for transfers between devices: 45.1 us -> 56.8 us
  Pallas kernels: 106 us -> 95 us
  other arithmetic: 11.2 us -> 8.18 us
  starting transfers between devices: 32.9 us -> 30 us
    pallas_call x2, Pallas kernels: 41.5 us -> 29.9 us  [the longest x1 16.9 us: run_backward(): pl.pallas_call(backward_kernel, grid=(chunks // spans,), in_specs=[pl.Blo...]
    ppermute x16 -> x14, waiting for transfers between devices: 40.8 us -> 51.7 us  [exchange(): return lax.ppermute(array, 'ctx', [(i, i ^ distance) for i in devices])]
    ppermute x16 -> x14, starting transfers between devices: 16.3 us -> 13.4 us  [exchange(): return lax.ppermute(array, 'ctx', [(i, i ^ distance) for i in devices])]
    unnamed x37 -> x35, local copies, waits for them, and re-layouts: 6.92 us -> 5.74 us
  transfers between devices with their start and end apart: 22 -> 20, of which waited for: 7 -> 10; matrix products, arithmetic and copies ran while one was open for 13% -> 12% of each run, Pallas kernels for 30% -> 14%
where the time goes in v4:
time: 230 us; the launch traced here: 229 us
  Pallas kernels  95 us (41%)
  waiting for transfers between devices  56.8 us (25%)
  starting transfers between devices  30 us (13%)
  matrix products  18.3 us (8%)
  between operations  14.2 us (6%)
  other arithmetic  8.18 us (4%)
  local copies, waits for them, and re-layouts  6.09 us (3%)
    ppermute x14, waiting for transfers between devices, exchange(): return lax.ppermute(array, 'ctx', [(i, i ^ distance) for i in devices])  51.7 us
    dot_general x3, matrix products, product(): return jnp.einsum(spec, a, b, preferred_element_type=F32)  18.3 us
    pallas_call x2, Pallas kernels, halving_keep(): pl.pallas_call(keep_kernel, grid_spec=pltpu.PrefetchScalarGridSpec(num_sc...  17.1 us
    pallas_call x1, Pallas kernels, run_backward(): pl.pallas_call(backward_kernel, grid=(chunks // spans,), in_specs=[pl.Blo...  16.9 us
    all_to_all x4, starting transfers between devices, swap(): return lax.all_to_all(parts, 'ctx', split_axis=0, concat_axis=0, tiled=True)  16.1 us
    pallas_call x2, Pallas kernels, halving_start(): pl.pallas_call(send_kernel, grid_spec=pltpu.PrefetchScalarGridSpec(num_sc...  13.6 us
    ppermute x14, starting transfers between devices, exchange(): return lax.ppermute(array, 'ctx', [(i, i ^ distance) for i in devices])  13.4 us
    pallas_call x1, Pallas kernels, run_forward(): pl.pallas_call(forward_kernel, grid=(chunks // spans,), in_specs=[pl.Bloc...  13 us
  transfers between devices with their start and end apart: 20, of which 10 were waited for; matrix products, arithmetic and copies ran while one was open for 12% of the time, Pallas kernels for 14%

profile of v4, /device:TPU:0, one launch (start us, length us, event | category | flops | bytes accessed | tf_op | source)
XLA Modules:
  0.0 228.6 jit_solution(2773160118018774901)
XLA Ops:
  7.2 9.9 %projection.1 = (f32[2,512,512]{2,1,0:T(8,128)}, f32[512,1024]{1,0:T(8,128)}, f32[512,16]{1,0:T(8,128)}) custom-call(bf16[512,2048]{1,0:T(8,128)(2,1)} %left_b_ref.7, bf16[2,2048,512]{2,1,0:T(8,128)(2,1)} %query_key_weight_ref.3, bf16[2,2048,1024]{2,1,0:T(8,128)(2,1)} %value_gate_weight_ref.1, bf16[2,8,2048]{2,1,0:T(8,128)(2,1)} %bitcast.36), custom_call_target="tpu_custom_call" | custom-call | tf_op jit(solution)/shard_map/projection/pallas_call | solution.py:624
  17.1 13.0 %forward_blocks.1 = (bf16[4,8,128,128]{3,2,1,0:T(8,128)(2,1)}, bf16[4,8,128,256]{3,2,1,0:T(8,128)(2,1)}, bf16[512,1024]{1,0:T(8,128)(2,1)}, f32[512,1024]{1,0:T(8,128)}, bf16[8,128,256]{2,1,0:T(8,128)(2,1)}) custom-call(f32[2,512,512]{2,1,0:T(8,128)} %get-tuple-element.56.query_key_ref, f32[512,1024]{1,0:T(8,128)} %get-tuple-element.57.value_ref, ...), custom_call_target="tpu_custom_call" | custom-call | tf_op jit(solution)/shard_map/forward_blocks/pallas_call | solution.py:442
  30.1 5.2 %all-to-all-start = ((bf16[8,1,128,256]{3,2,1,0:T(8,128)(2,1)}), bf16[8,1,128,256]{3,2,1,0:T(8,128)(2,1)S(1)}, u32[]{:S(2)}, u32[]{:S(2)}) async-start(bf16[8,1,128,256]{3,2,1,0:T(8,128)(2,1)} %bitcast.35), calls=%async_computation | async-start | bytes 1048576 | tf_op jit(solution)/shard_map/all_to_all | solution.py:563
  35.3 5.9 %fusion.gate_ref = f32[512,1024]{1,0:T(8,128)} fusion(bf16[512,2048]{1,0:T(8,128)(2,1)S(1)} %copy-done, bf16[2,2048,1024]{2,1,0:T(8,128)(2,1)} %value_gate_weight_ref.1), kind=kOutput, calls=%fused_computation | convolution fusion | flops 2147483648 | bytes 8388608 | tf_op jit(solution)/shard_map/td,df->tf/dot_general | solution.py:593
  41.1 3.9 %all-to-all-done.totals_ref = bf16[8,1,128,256]{3,2,1,0:T(8,128)(2,1)S(1)} async-done(((bf16[8,1,128,256]{3,2,1,0:T(8,128)(2,1)}), bf16[8,1,128,256]{3,2,1,0:T(8,128)(2,1)S(1)}, u32[]{:S(2)}, u32[]{:S(2)}) %all-to-all-start) | async-done | bytes 524320 | tf_op jit(solution)/shard_map/all_to_all | solution.py:563
  45.8 2.8 %chain_forward.1 = bf16[8,1,128,128]{3,2,1,0:T(8,128)(2,1)} custom-call(bf16[8,1,128,256]{3,2,1,0:T(8,128)(2,1)} %copy-done.1), custom_call_target="tpu_custom_call" | custom-call | tf_op jit(solution)/shard_map/chain_forward/pallas_call | solution.py:575
  48.6 3.6 %all-to-all-start.1 = ((bf16[8,1,128,128]{3,2,1,0:T(8,128)(2,1)}), bf16[8,1,128,128]{3,2,1,0:T(8,128)(2,1)S(1)}, u32[]{:S(2)}, u32[]{:S(2)}) async-start(bf16[8,1,128,128]{3,2,1,0:T(8,128)(2,1)} %chain_forward.1), calls=%async_computation.1 | async-start | bytes 524288 | tf_op jit(solution)/shard_map/all_to_all | solution.py:563
  52.2 6.6 %fusion.3.delta_ref = f32[512,1024]{1,0:T(8,128)} fusion(bf16[512,2048]{1,0:T(8,128)(2,1)} %left_b_ref.5, bf16[1024,2048]{1,0:T(8,128)(2,1)} %param.17), kind=kOutput, calls=%fused_computation.19 | convolution fusion | flops 2147483648 | bytes 8388608 | tf_op jit(solution)/shard_map/td,fd->tf/dot_general | solution.py:593
  59.6 6.8 %gated_norm.1 = (bf16[512,1024]{1,0:T(8,128)(2,1)}, bf16[512,1024]{1,0:T(8,128)(2,1)}, bf16[512,1024]{1,0:T(8,128)(2,1)}, bf16[8,128,128]{2,1,0:T(8,128)(2,1)}) custom-call(f32[512,1024]{1,0:T(8,128)} %get-tuple-element.59.local_ref, bf16[512,1024]{1,0:T(8,128)(2,1)} %get-tuple-element.60.map_ref, f32[512,1024]{1,0:T(8,128)} %fusion.gate_ref, ...), custom_call_target="tpu_custom_call" | custom-call | tf_op jit(solution)/shard_map/gated_norm/pallas_call | solution.py:479
  66.5 6.7 %send_rows.2 = bf16[1024,2048]{1,0:T(8,128)(2,1)} custom-call(s32[1]{0:T(128)} %bitcast.9.place_ref, bf16[512,2048]{1,0:T(8,128)(2,1)} %left_b_ref.7, bf16[512,1024]{1,0:T(8,128)(2,1)} %get-tuple-element.89.a_ref.delta_gate_ref, bf16[512,2048]{1,0:T(8,128)(2,1)} %left_b_ref.5, bf16[512,1024]{1,0:T(8,128)(2,1)} %get-tuple-element.67.b_ref), custom_call_target="tpu_custom_call" | custom-call | tf_op jit(solution)/shard_map/send_rows/pallas_call | solution.py:747
  73.2 3.9 %all-to-all-start.2 = ((bf16[8,1,128,128]{3,2,1,0:T(8,128)(2,1)}), bf16[8,1,128,128]{3,2,1,0:T(8,128)(2,1)S(1)}, u32[]{:S(2)}, u32[]{:S(2)}) async-start(bf16[8,1,128,128]{3,2,1,0:T(8,128)(2,1)} %bitcast.8), calls=%async_computation.2 | async-start | bytes 524288 | tf_op jit(solution)/shard_map/all_to_all | solution.py:563
  77.1 5.8 %convolution_convert_fusion = bf16[512,2048]{1,0:T(8,128)(2,1)} fusion(bf16[512,1024]{1,0:T(8,128)(2,1)S(1)} %copy-done.2, bf16[1024,2048]{1,0:T(8,128)(2,1)} %param.17), kind=kOutput, calls=%fused_computation.3 | convolution fusion | flops 2148532224 | bytes 7340032 | tf_op jit(solution)/shard_map/tf,fd->td/dot_general | solution.py:593
  84.8 2.9 %chain_backward.1 = bf16[8,1,128,128]{3,2,1,0:T(8,128)(2,1)} custom-call(bf16[8,1,128,256]{3,2,1,0:T(8,128)(2,1)} %copy-done.1, bf16[8,1,128,128]{3,2,1,0:T(8,128)(2,1)} %copy-done.5), custom_call_target="tpu_custom_call" | custom-call | tf_op jit(solution)/shard_map/chain_backward/pallas_call | solution.py:584
  87.7 3.4 %all-to-all-start.3 = ((bf16[8,1,128,128]{3,2,1,0:T(8,128)(2,1)}), bf16[8,1,128,128]{3,2,1,0:T(8,128)(2,1)S(1)}, u32[]{:S(2)}, u32[]{:S(2)}) async-start(bf16[8,1,128,128]{3,2,1,0:T(8,128)(2,1)} %chain_backward.1), calls=%async_computation.4 | async-start | bytes 524288 | tf_op jit(solution)/shard_map/all_to_all | solution.py:563
  91.4 8.4 %keep_rows.2 = (bf16[256,1024]{1,0:T(8,128)(2,1)}, bf16[256,1024]{1,0:T(8,128)(2,1)}, bf16[256,1024]{1,0:T(8,128)(2,1)}, bf16[256,1024]{1,0:T(8,128)(2,1)}, bf16...) custom-call(s32[1]{0:T(128)} %bitcast.9.place_ref, ...), custom_call_target="tpu_custom_call" | custom-call | tf_op jit(solution)/shard_map/keep_rows/pallas_call | solution.py:764
  100.5 16.9 %backward_blocks.1 = (bf16[512,1152]{1,0:T(8,128)(2,1)}, bf16[512,1024]{1,0:T(8,128)(2,1)}) custom-call(f32[2,512,512]{2,1,0:T(8,128)} %get-tuple-element.56.query_key_ref, f32[512,1024]{1,0:T(8,128)} %get-tuple-element.57.value_ref, f32[512,16]{1,0:T(8,128)} %get-tuple-element.58.decay_beta_ref, f32[1,8]{1,0:T(1,128)} %bitcast.41, f32[1,8]{1,0:T(1,128)} %bitcast.43, ...), custom_call_target="tpu_custom_call" | custom-call | tf_op jit(solution)/shard_map/backward_blocks/pallas_call | solution.py:513
  117.4 6.9 %send_rows.3 = bf16[1024,2176]{1,0:T(8,128)(2,1)} custom-call(s32[1]{0:T(128)} %bitcast.9.place_ref, bf16[512,2048]{1,0:T(8,128)(2,1)} %left_b_ref.7, bf16[512,1024]{1,0:T(8,128)(2,1)} %get-tuple-element.84.delta_value_ref.a_ref, bf16[512,2048]{1,0:T(8,128)(2,1)} %left_b_ref.7, bf16[512,1152]{1,0:T(8,128)(2,1)} %get-tuple-element.83.delta_query_key_ref.b_ref), custom_call_target="tpu_custom_call" | custom-call | tf_op jit(solution)/shard_map/send_rows/pallas_call | solution.py:747
  125.4 1.7 collective-permute-start.1
  127.1 1.5 collective-permute-start.2
  128.6 10.8 %collective-permute-done.1 = bf16[256,1024]{1,0:T(8,128)(2,1)S(1)} collective-permute-done((bf16[256,1024]{1,0:T(8,128)(2,1)S(1)}, bf16[256,1024]{1,0:T(8,128)(2,1)S(1)}, u32[]{:S(2)}, u32[]{:S(2)}) %collective-permute-start.1) | collective-permute-done | bytes 524320 | tf_op jit(solution)/shard_map/ppermute | solution.py:703
  141.0 11.8 %input_gradient.1 = bf16[512,2048]{1,0:T(8,128)(2,1)} custom-call(bf16[512,1152]{1,0:T(8,128)(2,1)} %get-tuple-element.83.delta_query_key_ref.b_ref, bf16[512,1024]{1,0:T(8,128)(2,1)} %get-tuple-element.84.delta_value_ref.a_ref, bf16[512,1024]{1,0:T(8,128)(2,1)} %get-tuple-element.89.a_ref.delta_gate_ref, bf16[2,2048,512]{2,1,0:T(8,128)(2,1)} %query_key_weight_ref.3, ...), custom_call_target="tpu_custom_call" | custom-call | tf_op jit(solution)/shard_map/input_gradient/pallas_call | solution.py:678
  154.4 1.5 collective-permute-start.11
  155.9 8.7 %keep_rows.3 = (bf16[256,1024]{1,0:T(8,128)(2,1)}, bf16[256,1024]{1,0:T(8,128)(2,1)}, bf16[256,1024]{1,0:T(8,128)(2,1)}, bf16[256,1024]{1,0:T(8,128)(2,1)}, bf16...) custom-call(s32[1]{0:T(128)} %bitcast.9.place_ref, ...), custom_call_target="tpu_custom_call" | custom-call | tf_op jit(solution)/shard_map/keep_rows/pallas_call | solution.py:764
  164.7 1.5 collective-permute-start.8
  166.7 1.4 collective-permute-start.12
  169.0 1.5 collective-permute-start.7
  170.5 9.2 %collective-permute-done.8 = bf16[256,1024]{1,0:T(8,128)(2,1)S(1)} collective-permute-done((bf16[256,1024]{1,0:T(8,128)(2,1)}, bf16[256,1024]{1,0:T(8,128)(2,1)S(1)}, u32[]{:S(2)}, u32[]{:S(2)}) %collective-permute-start.8) | collective-permute-done | bytes 524320 | tf_op jit(solution)/shard_map/ppermute | solution.py:703
  183.3 10.5 %collective-permute-done.12 = bf16[256,1024]{1,0:T(8,128)(2,1)S(1)} collective-permute-done((bf16[256,1024]{1,0:T(8,128)(2,1)S(1)}, bf16[256,1024]{1,0:T(8,128)(2,1)S(1)}, u32[]{:S(2)}, u32[]{:S(2)}) %collective-permute-start.12) | collective-permute-done | bytes 524320 | tf_op jit(solution)/shard_map/ppermute | solution.py:703
  196.0 6.3 %collective-permute-done.7 = bf16[256,1024]{1,0:T(8,128)(2,1)} collective-permute-done((bf16[256,1024]{1,0:T(8,128)(2,1)}, bf16[256,1024]{1,0:T(8,128)(2,1)}, u32[]{:S(2)}, u32[]{:S(2)}) %collective-permute-start.7) | collective-permute-done | bytes 524320 | tf_op jit(solution)/shard_map/ppermute | solution.py:703
  202.3 12.9 %collective-permute-done.9 = bf16[256,1024]{1,0:T(8,128)(2,1)} collective-permute-done((bf16[256,1024]{1,0:T(8,128)(2,1)}, bf16[256,1024]{1,0:T(8,128)(2,1)}, u32[]{:S(2)}, u32[]{:S(2)}) %collective-permute-start.9) | collective-permute-done | bytes 524320 | tf_op jit(solution)/shard_map/ppermute | solution.py:703
  215.2 1.6 add_bitcast_fusion.2
  216.9 1.5 pad_maximum_fusion
  (74 shorter events, 19.2 us)
Async XLA Ops:
  17.1 18.2 %copy-start = (bf16[512,2048]{1,0:T(8,128)(2,1)S(1)}, bf16[512,2048]{1,0:T(8,128)(2,1)}, u32[]{:S(2)}) copy-start(bf16[512,2048]{1,0:T(8,128)(2,1)} %left_b_ref.7) | copy-start | bytes 6291460
  30.1 14.9 %all-to-all-start = ((bf16[8,1,128,256]{3,2,1,0:T(8,128)(2,1)}), bf16[8,1,128,256]{3,2,1,0:T(8,128)(2,1)S(1)}, u32[]{:S(2)}, u32[]{:S(2)}) async-start(bf16[8,1,128,256]{3,2,1,0:T(8,128)(2,1)} %bitcast.35), calls=%async_computation | async-start | bytes 1048576 | tf_op jit(solution)/shard_map/all_to_all | solution.py:563
  48.6 10.3 %all-to-all-start.1 = ((bf16[8,1,128,128]{3,2,1,0:T(8,128)(2,1)}), bf16[8,1,128,128]{3,2,1,0:T(8,128)(2,1)S(1)}, u32[]{:S(2)}, u32[]{:S(2)}) async-start(bf16[8,1,128,128]{3,2,1,0:T(8,128)(2,1)} %chain_forward.1), calls=%async_computation.1 | async-start | bytes 524288 | tf_op jit(solution)/shard_map/all_to_all | solution.py:563
  66.4 10.7 %copy-start.2 = (bf16[512,1024]{1,0:T(8,128)(2,1)S(1)}, bf16[512,1024]{1,0:T(8,128)(2,1)}, u32[]{:S(2)}) copy-start(bf16[512,1024]{1,0:T(8,128)(2,1)} %get-tuple-element.67.b_ref) | copy-start | bytes 3145732
  73.1 18.3 %collective-permute-start = (bf16[1024,2048]{1,0:T(8,128)(2,1)}, bf16[1024,2048]{1,0:T(8,128)(2,1)}, u32[]{:S(2)}, u32[]{:S(2)}) collective-permute-start(bf16[1024,2048]{1,0:T(8,128)(2,1)} %send_rows.2), channel_id=1, source_target_pairs={{0,4},{4,0},{8,12},{12,8},{16,20},{20,16},{24,28},{28,24},{1,5},{5... | collective-permute-start | bytes 12582920 | tf_op jit(solution)/shard_map/ppermute | solution.py:703
  73.2 10.8 %all-to-all-start.2 = ((bf16[8,1,128,128]{3,2,1,0:T(8,128)(2,1)}), bf16[8,1,128,128]{3,2,1,0:T(8,128)(2,1)S(1)}, u32[]{:S(2)}, u32[]{:S(2)}) async-start(bf16[8,1,128,128]{3,2,1,0:T(8,128)(2,1)} %bitcast.8), calls=%async_computation.2 | async-start | bytes 524288 | tf_op jit(solution)/shard_map/all_to_all | solution.py:563
  87.7 12.1 %all-to-all-start.3 = ((bf16[8,1,128,128]{3,2,1,0:T(8,128)(2,1)}), bf16[8,1,128,128]{3,2,1,0:T(8,128)(2,1)S(1)}, u32[]{:S(2)}, u32[]{:S(2)}) async-start(bf16[8,1,128,128]{3,2,1,0:T(8,128)(2,1)} %chain_backward.1), calls=%async_computation.4 | async-start | bytes 524288 | tf_op jit(solution)/shard_map/all_to_all | solution.py:563
  91.1 130.7 %reduce-scatter.3.cloned.1.call-start = ((), (), s32[]{:S(2)}) async-start(), calls=%async_computation.6 | async-start | bytes 2621440 | tf_op jit(solution)/shard_map/reduce_scatter | solution.py:813
  124.4 2.7 %copy-start.15 = (bf16[256,1024]{1,0:T(8,128)(2,1)S(1)}, bf16[256,1024]{1,0:T(8,128)(2,1)}, u32[]{:S(2)}) copy-start(bf16[256,1024]{1,0:T(8,128)(2,1)} %get-tuple-element.88) | copy-start | bytes 1572868
  124.4 15.0 %copy-start.11 = (bf16[256,1024]{1,0:T(8,128)(2,1)S(1)}, bf16[256,1024]{1,0:T(8,128)(2,1)}, u32[]{:S(2)}) copy-start(bf16[256,1024]{1,0:T(8,128)(2,1)} %get-tuple-element.85) | copy-start | bytes 1572868
  124.4 16.4 %copy-start.10 = (bf16[256,1024]{1,0:T(8,128)(2,1)S(1)}, bf16[256,1024]{1,0:T(8,128)(2,1)}, u32[]{:S(2)}) copy-start(bf16[256,1024]{1,0:T(8,128)(2,1)} %get-tuple-element.87) | copy-start | bytes 1572868
  124.4 28.4 %collective-permute-start.3 = (bf16[1024,2176]{1,0:T(8,128)(2,1)}, bf16[1024,2176]{1,0:T(8,128)(2,1)}, u32[]{:S(2)}, u32[]{:S(2)}) collective-permute-start(bf16[1024,2176]{1,0:T(8,128)(2,1)} %send_rows.3), channel_id=1, source_target_pairs={{0,4},{4,0},{8,12},{12,8},{16,20},{20,16},{24,28},{28,24},{1,5},{5... | collective-permute-start | bytes 13369352 | tf_op jit(solution)/shard_map/ppermute | solution.py:703
  124.6 97.2 %reduce-scatter.5.cloned.1.call-start = ((), (), s32[]{:S(2)}) async-start(), calls=%async_computation.7 | async-start | bytes 2621440 | tf_op jit(solution)/shard_map/reduce_scatter | solution.py:813
  125.4 14.0 %collective-permute-start.1 = (bf16[256,1024]{1,0:T(8,128)(2,1)S(1)}, bf16[256,1024]{1,0:T(8,128)(2,1)S(1)}, u32[]{:S(2)}, u32[]{:S(2)}) collective-permute-start(bf16[256,1024]{1,0:T(8,128)(2,1)S(1)} %copy-done.16), channel_id=1, source_target_pairs={{0,8},{4,12},{8,0},{12,4},{16,24},{20,28},{24,16},{28,20},{1,9},{5... | collective-permute-start | bytes 1572872 | tf_op jit(solution)/shard_map/ppermute | solution.py:703
  127.1 13.7 %collective-permute-start.2 = (bf16[256,1024]{1,0:T(8,128)(2,1)S(1)}, bf16[256,1024]{1,0:T(8,128)(2,1)S(1)}, u32[]{:S(2)}, u32[]{:S(2)}) collective-permute-start(bf16[256,1024]{1,0:T(8,128)(2,1)S(1)} %copy-done.15), channel_id=1, source_target_pairs={{0,16},{4,20},{8,24},{12,28},{16,0},{20,4},{24,8},{28,12},{1,17},{... | collective-permute-start | bytes 1572872 | tf_op jit(solution)/shard_map/ppermute | solution.py:703
  152.8 1.1 copy-start.14
  153.9 12.9 %copy-start.13 = (bf16[256,1024]{1,0:T(8,128)(2,1)S(1)}, bf16[256,1024]{1,0:T(8,128)(2,1)}, u32[]{:S(2)}) copy-start(bf16[256,1024]{1,0:T(8,128)(2,1)} %get-tuple-element.104) | copy-start | bytes 1572868
  153.9 14.9 %copy-start.9 = (bf16[256,1024]{1,0:T(8,128)(2,1)S(1)}, bf16[256,1024]{1,0:T(8,128)(2,1)}, u32[]{:S(2)}) copy-start(bf16[256,1024]{1,0:T(8,128)(2,1)} %get-tuple-element.100) | copy-start | bytes 1572868
  153.9 14.3 %collective-permute-start.10 = (bf16[256,1024]{1,0:T(8,128)(2,1)S(1)}, bf16[256,1024]{1,0:T(8,128)(2,1)S(1)}, u32[]{:S(2)}, u32[]{:S(2)}) collective-permute-start(bf16[256,1024]{1,0:T(8,128)(2,1)S(1)} %copy-done.14), channel_id=1, source_target_pairs={{0,8},{4,12},{8,0},{12,4},{16,24},{20,28},{24,16},{28,20},{1,9},{5... | collective-permute-start | bytes 1572872 | tf_op jit(solution)/shard_map/ppermute | solution.py:703
  154.4 14.3 %collective-permute-start.11 = (bf16[256,1024]{1,0:T(8,128)(2,1)S(1)}, bf16[256,1024]{1,0:T(8,128)(2,1)S(1)}, u32[]{:S(2)}, u32[]{:S(2)}) collective-permute-start(bf16[256,1024]{1,0:T(8,128)(2,1)S(1)} %add_convert_fusion.3), channel_id=1, source_target_pairs={{0,16},{4,20},{8,24},{12,28},{16,0},{20,4},{24,8},{28,12},{1,17},{... | collective-permute-start | bytes 1572872 | tf_op jit(solution)/shard_map/ppermute | solution.py:703
  164.7 16.2 %copy-start.12 = (bf16[256,1024]{1,0:T(8,128)(2,1)S(1)}, bf16[256,1024]{1,0:T(8,128)(2,1)}, u32[]{:S(2)}) copy-start(bf16[256,1024]{1,0:T(8,128)(2,1)} %get-tuple-element.98) | copy-start | bytes 1572868
  164.7 15.1 %collective-permute-start.8 = (bf16[256,1024]{1,0:T(8,128)(2,1)}, bf16[256,1024]{1,0:T(8,128)(2,1)S(1)}, u32[]{:S(2)}, u32[]{:S(2)}) collective-permute-start(bf16[256,1024]{1,0:T(8,128)(2,1)} %get-tuple-element.99), channel_id=1, source_target_pairs={{0,8},{4,12},{8,0},{12,4},{16,24},{20,28},{24,16},{28,20},{1,9},{5... | collective-permute-start | bytes 1572872 | tf_op jit(solution)/shard_map/ppermute | solution.py:703
  166.1 17.1 %copy-start.6 = (bf16[256,1152]{1,0:T(8,128)(2,1)S(1)}, bf16[256,1152]{1,0:T(8,128)(2,1)}, u32[]{:S(2)}) copy-start(bf16[256,1152]{1,0:T(8,128)(2,1)} %get-tuple-element.94) | copy-start | bytes 1769476
  166.1 16.5 %collective-permute-start.5 = (bf16[256,1152]{1,0:T(8,128)(2,1)}, bf16[256,1152]{1,0:T(8,128)(2,1)S(1)}, u32[]{:S(2)}, u32[]{:S(2)}) collective-permute-start(bf16[256,1152]{1,0:T(8,128)(2,1)} %get-tuple-element.95), channel_id=1, source_target_pairs={{0,16},{4,20},{8,24},{12,28},{16,0},{20,4},{24,8},{28,12},{1,17},{... | collective-permute-start | bytes 1769480 | tf_op jit(solution)/shard_map/ppermute | solution.py:703
  166.7 27.1 %collective-permute-start.12 = (bf16[256,1024]{1,0:T(8,128)(2,1)S(1)}, bf16[256,1024]{1,0:T(8,128)(2,1)S(1)}, u32[]{:S(2)}, u32[]{:S(2)}) collective-permute-start(bf16[256,1024]{1,0:T(8,128)(2,1)S(1)} %copy-done.13), channel_id=1, source_target_pairs={{0,16},{4,20},{8,24},{12,28},{16,0},{20,4},{24,8},{28,12},{1,17},{... | collective-permute-start | bytes 1572872 | tf_op jit(solution)/shard_map/ppermute | solution.py:703
  168.2 26.3 %collective-permute-start.13 = (bf16[256,1024]{1,0:T(8,128)(2,1)S(1)}, bf16[256,1024]{1,0:T(8,128)(2,1)S(1)}, u32[]{:S(2)}, u32[]{:S(2)}) collective-permute-start(bf16[256,1024]{1,0:T(8,128)(2,1)S(1)} %add_convert_fusion.2), channel_id=1, source_target_pairs={{0,8},{4,12},{8,0},{12,4},{16,24},{20,28},{24,16},{28,20},{1,9},{5... | collective-permute-start | bytes 1572872 | tf_op jit(solution)/shard_map/ppermute | solution.py:703
  169.0 25.4 %copy-start.8 = (bf16[256,1024]{1,0:T(8,128)(2,1)S(1)}, bf16[256,1024]{1,0:T(8,128)(2,1)}, u32[]{:S(2)}) copy-start(bf16[256,1024]{1,0:T(8,128)(2,1)} %get-tuple-element.103) | copy-start | bytes 1572868
  169.0 33.3 %collective-permute-start.7 = (bf16[256,1024]{1,0:T(8,128)(2,1)}, bf16[256,1024]{1,0:T(8,128)(2,1)}, u32[]{:S(2)}, u32[]{:S(2)}) collective-permute-start(bf16[256,1024]{1,0:T(8,128)(2,1)} %get-tuple-element.97), channel_id=1, source_target_pairs={{0,8},{4,12},{8,0},{12,4},{16,24},{20,28},{24,16},{28,20},{1,9},{5... | collective-permute-start | bytes 1572872 | tf_op jit(solution)/shard_map/ppermute | solution.py:703
  179.7 38.7 %collective-permute-start.4 = (bf16[256,1152]{1,0:T(8,128)(2,1)}, bf16[256,1152]{1,0:T(8,128)(2,1)S(1)}, u32[]{:S(2)}, u32[]{:S(2)}) collective-permute-start(bf16[256,1152]{1,0:T(8,128)(2,1)} %get-tuple-element.93), channel_id=1, source_target_pairs={{0,16},{4,20},{8,24},{12,28},{16,0},{20,4},{24,8},{28,12},{1,17},{... | collective-permute-start | bytes 1769480 | tf_op jit(solution)/shard_map/ppermute | solution.py:703
  182.6 32.6 %collective-permute-start.9 = (bf16[256,1024]{1,0:T(8,128)(2,1)}, bf16[256,1024]{1,0:T(8,128)(2,1)}, u32[]{:S(2)}, u32[]{:S(2)}) collective-permute-start(bf16[256,1024]{1,0:T(8,128)(2,1)} %add_convert_fusion.1), channel_id=1, source_target_pairs={{0,16},{4,20},{8,24},{12,28},{16,0},{20,4},{24,8},{28,12},{1,17},{... | collective-permute-start | bytes 1572872 | tf_op jit(solution)/shard_map/ppermute | solution.py:703
  193.8 24.6 %collective-permute-start.6 = (bf16[256,1152]{1,0:T(8,128)(2,1)S(1)}, bf16[256,1152]{1,0:T(8,128)(2,1)}, u32[]{:S(2)}, u32[]{:S(2)}) collective-permute-start(bf16[256,1152]{1,0:T(8,128)(2,1)S(1)} %add_convert_fusion), channel_id=1, source_target_pairs={{0,8},{4,12},{8,0},{12,4},{16,24},{20,28},{24,16},{28,20},{1,9},{5... | collective-permute-start | bytes 1769480 | tf_op jit(solution)/shard_map/ppermute | solution.py:703
  216.9 1.5 copy-start.7
  (5 other events, 3.9 us)
Sparse Core Ops, SparseCore 0:
  124.8 45.2 reduce-scatter.2
  173.0 43.1 reduce-scatter.4

commit v5 on v4

--- a/solution.py
+++ b/solution.py
@@ -429,6 +429,14 @@
 INTERPRET = False
 
 
+def cost(microseconds):
+    return pl.CostEstimate(
+        flops=int(microseconds * 1e9),
+        bytes_accessed=int(microseconds * 3.6e6),
+        transcendentals=0,
+    )
+
+
 def whole(shape):
     return pl.BlockSpec(shape, lambda c: (0,) * len(shape))
 
@@ -467,6 +475,7 @@
         scratch_shapes=[pltpu.VMEM((heads, DK, DK + DV), F32)],
         compiler_params=PARAMS,
         interpret=INTERPRET,
+        cost_estimate=cost(13),
         name="forward_blocks",
     )(query_key, value, decay_beta, bias, scale, resets)
 
@@ -497,6 +506,7 @@
         scratch_shapes=[pltpu.VMEM((heads, DK, DV), F32)],
         compiler_params=PARAMS,
         interpret=INTERPRET,
+        cost_estimate=cost(7),
         name="gated_norm",
     )(local, reach, gate, delta_hidden, state_in, gain)
 
@@ -537,6 +547,7 @@
         scratch_shapes=[pltpu.VMEM((heads, DK, DV), F32)],
         compiler_params=PARAMS,
         interpret=INTERPRET,
+        cost_estimate=cost(17),
         name="backward_blocks",
     )(query_key, value, decay_beta, bias, scale, resets, solve, starts, state_in, delta_out, final)
 
@@ -576,6 +587,7 @@
         chain_forward_kernel,
         out_shape=jax.ShapeDtypeStruct((*held.shape[:3], held.shape[3] - DK), BF16),
         interpret=INTERPRET,
+        cost_estimate=cost(3),
         name="chain_forward",
     )(held)
 
@@ -585,6 +597,7 @@
         chain_backward_kernel,
         out_shape=jax.ShapeDtypeStruct(deltas.shape, BF16),
         interpret=INTERPRET,
+        cost_estimate=cost(3),
         name="chain_backward",
     )(held, deltas)
 
@@ -642,6 +655,7 @@
         ],
         compiler_params=PARAMS,
         interpret=INTERPRET,
+        cost_estimate=cost(10),
         name="projection",
     )(inputs, query_key_weight, value_gate_weight, decay_beta_weight)
 
@@ -653,7 +667,8 @@
     query_key_weight_ref,
     value_gate_weight_ref,
     decay_beta_weight_ref,
-    out_ref,
+    first_ref,
+    second_ref,
 ):
     width = query_key_weight_ref.shape[2]
     heads = decay_beta_weight_ref.shape[1]
@@ -663,7 +678,10 @@
     total += dot(delta_value_ref[...], value_gate_weight_ref[0], NT)
     total += dot(delta_query_key_ref[:, : 2 * width], keys, NT)
     total += dot(small, rows_of(decay_beta_weight_ref))
-    out_ref[...] = total.astype(BF16)
+    total = total.astype(BF16)
+    cut = first_ref.shape[0]
+    first_ref[...] = total[:cut]
+    second_ref[...] = total[cut:]
 
 
 def run_input_gradient(
@@ -686,10 +704,11 @@
             weight(value_gate_weight),
             pl.BlockSpec((2, decay_beta_weight.shape[1], cut), lambda j: (0, 0, j)),
         ],
-        out_specs=pl.BlockSpec((tokens, cut), lambda j: (0, j)),
-        out_shape=jax.ShapeDtypeStruct((tokens, model), BF16),
+        out_specs=[pl.BlockSpec((tokens // 2, cut), lambda j: (0, j))] * 2,
+        out_shape=[jax.ShapeDtypeStruct((tokens // 2, model), BF16)] * 2,
         compiler_params=PARAMS,
         interpret=INTERPRET,
+        cost_estimate=cost(11),
         name="input_gradient",
     )(delta_query_key, delta_value, delta_gate, query_key_weight, value_gate_weight, decay_beta_weight)
 
@@ -755,6 +774,7 @@
         out_shape=jax.ShapeDtypeStruct((4 * rows, width), BF16),
         compiler_params=PARAMS,
         interpret=INTERPRET,
+        cost_estimate=cost(6),
         name="send_rows",
     )(place, left_a, a, left_b, b)
 
@@ -781,6 +801,7 @@
         ],
         compiler_params=PARAMS,
         interpret=INTERPRET,
+        cost_estimate=cost(8),
         name="keep_rows",
     )(place, left_a, a, left_b, b, arrived)
 
@@ -790,8 +811,11 @@
 
 
 def halving_cross(pieces):
-    a, b = pieces[:4], pieces[4:]
-    return exchange(a[0], 2), exchange(b[0], 4), exchange(a[1], 2), exchange(b[2], 4)
+    return exchange(pieces[0], 2), exchange(pieces[4], 4)
+
+
+def halving_stay(pieces):
+    return exchange(pieces[1], 2), exchange(pieces[6], 4)
 
 
 def halving_onward(pieces, arrived):
@@ -806,7 +830,35 @@
     def total(own, near, far):
         return own.astype(F32) + near.astype(F32) + far.astype(F32)
 
-    return total(pieces[3], arrived[2], last[0]), total(pieces[7], arrived[3], last[1])
+    return total(pieces[3], arrived[0], last[0]), total(pieces[7], arrived[1], last[1])
+
+
+def line_hop(step, partial, received):
+    devices = lax.axis_size("head")
+    place = lax.axis_index("head")
+
+    def send(block, arrived, route):
+        part = line_block(partial, jnp.clip(block, 0, devices - 1))
+        if arrived is not None:
+            part = summed(part, arrived)
+        return lax.ppermute(part, "head", route)
+
+    up = [(i, i + 1) for i in range(step)]
+    down = [(i, i - 1) for i in range(devices - step, devices)]
+    return (
+        send(devices - step + place, received[0], up),
+        send(place - devices + step, received[1], down),
+    )
+
+
+def line_block(partial, block):
+    width = partial.shape[1] // lax.axis_size("head")
+    return lax.dynamic_slice_in_dim(partial, block * width, width, 1)
+
+
+def line_sum(partial, received):
+    own = line_block(partial, lax.axis_index("head")).astype(F32)
+    return (own + received[0].astype(F32) + received[1].astype(F32)).astype(BF16)
 
 
 def scatter(partial, axis, dimension):
@@ -852,13 +904,20 @@
     deltas = swap(spread(delta_state, lax.axis_size("ctx")))
     partial_out = product("tf,fd->td", hidden, out_weight).astype(BF16)
     deltas, partial_out = together(deltas, partial_out)
-    mixed = scatter(partial_out, "head", 1)
+    line = cubic and lax.axis_size("head") == 4
+    if line:
+        hop = line_hop(1, partial_out, (None, None))
+    else:
+        mixed = scatter(partial_out, "head", 1)
     finals = swap(run_chain_backward(held, deltas))
     if cubic:
         place = lax.axis_index("ctx").astype(jnp.int32).reshape(1)
         early = (place, inputs, delta_gate, grad_mixed, hidden)
         early_pieces = halving_keep(*early, exchange(halving_start(*early), 1))
         finals, early_pieces = together(finals, early_pieces)
+        if line:
+            finals, hop = together(finals, hop)
+            hop = line_hop(2, partial_out, hop)
         early_arrived = halving_cross(early_pieces)
     delta_final = gather_parts(finals, heads)
     delta_query_key, delta_value = run_backward(
@@ -875,11 +934,16 @@
         delta_final,
     )
     if cubic:
+        delta_value, early_arrived, early_pieces = together(
+            delta_value, early_arrived, early_pieces
+        )
+        if line:
+            delta_value, hop = together(delta_value, hop)
+            hop = line_hop(3, partial_out, hop)
+        early_last = halving_last(halving_onward(early_pieces, early_arrived))
+        early_stay = halving_stay(early_pieces)
         late = (place, inputs, delta_value, inputs, delta_query_key)
         arrived = exchange(halving_start(*late), 1)
-        early_onward = halving_onward(early_pieces, early_arrived)
-        delta_gate, early_onward = together(delta_gate, early_onward)
-        early_last = halving_last(early_onward)
     grad_rows = run_input_gradient(
         delta_query_key,
         delta_value,
@@ -889,15 +953,20 @@
         small_weight,
     )
     if cubic:
-        grad_rows, arrived = together(grad_rows, arrived)
-    grad_inputs = scatter(grad_rows, "head", 1)
+        grad_rows, arrived, early_last = together(grad_rows, arrived, early_last)
+        if line:
+            arrived, hop = together(arrived, hop)
+            mixed = line_sum(partial_out, hop)
+    grad_inputs = jnp.concatenate([scatter(part, "head", 1) for part in grad_rows], axis=0)
     if cubic:
         late_pieces = halving_keep(*late, arrived)
+        late_pieces, early_stay = together(late_pieces, early_stay)
         late_arrived = halving_cross(late_pieces)
+        late_stay = halving_stay(late_pieces)
         late_last = halving_last(halving_onward(late_pieces, late_arrived))
-        grad_gate, grad_out = halving_sum(early_pieces, early_arrived, early_last)
+        grad_gate, grad_out = halving_sum(early_pieces, early_stay, early_last)
         grad_out = grad_out.T
-        grad_value, packed = halving_sum(late_pieces, late_arrived, late_last)
+        grad_value, packed = halving_sum(late_pieces, late_stay, late_last)
     else:
         grad_gate = scatter(product("td,tf->df", inputs, delta_gate), "ctx", 0).astype(F32)
         grad_out = scatter(product("tf,td->fd", hidden, grad_mixed), "ctx", 1).astype(F32)

time: 230 us -> 256 us (1.11)
  starting transfers between devices: 30 us -> 46.2 us
  other arithmetic: 8.18 us -> 16.2 us
  waiting for transfers between devices: 56.8 us -> 60.5 us
    ppermute x0 -> x6, waiting for transfers between devices: none -> 28.7 us  [send(): return lax.ppermute(part, 'head', route)]
    ppermute x14, waiting for transfers between devices: 51.7 us -> 26 us  [exchange(): return lax.ppermute(array, 'ctx', [(i, i ^ distance) for i in devices])]
    ppermute x0 -> x6, starting transfers between devices: none -> 16.4 us  [send(): return lax.ppermute(part, 'head', route)]
    convert_element_type x4 -> x6, other arithmetic: 1.51 us -> 5.62 us  [summed(): return (a.astype(F32) + b.astype(F32)).astype(BF16)]
    unnamed x35 -> x39, local copies, waits for them, and re-layouts: 5.74 us -> 3.58 us
  transfers between devices with their start and end apart: 20 -> 26, of which waited for: 10 -> 11; matrix products, arithmetic and copies ran while one was open for 12% -> 13% of each run, Pallas kernels for 14% -> 19%
where the time goes in v5:
time: 256 us; the launch traced here: 255 us
  Pallas kernels  94.8 us (37%)
  waiting for transfers between devices  60.5 us (24%)
  starting transfers between devices  46.2 us (18%)
  matrix products  17.6 us (7%)
  other arithmetic  16.2 us (6%)
  between operations  14.4 us (6%)
  local copies, waits for them, and re-layouts  4.83 us (2%)
    ppermute x6, waiting for transfers between devices, send(): return lax.ppermute(part, 'head', route)  28.7 us
    ppermute x14, waiting for transfers between devices, exchange(): return lax.ppermute(array, 'ctx', [(i, i ^ distance) for i in devices])  26 us
    dot_general x3, matrix products, product(): return jnp.einsum(spec, a, b, preferred_element_type=F32)  17.6 us
    pallas_call x2, Pallas kernels, halving_keep(): pl.pallas_call(keep_kernel, grid_spec=pltpu.PrefetchScalarGridSpec(num_sc...  17.3 us
    pallas_call x1, Pallas kernels, run_backward(): pl.pallas_call(backward_kernel, grid=(chunks // spans,), in_specs=[pl.Blo...  16.9 us
    ppermute x6, starting transfers between devices, send(): return lax.ppermute(part, 'head', route)  16.4 us
    all_to_all x4, starting transfers between devices, swap(): return lax.all_to_all(parts, 'ctx', split_axis=0, concat_axis=0, tiled=True)  16.1 us
    pallas_call x2, Pallas kernels, halving_start(): pl.pallas_call(send_kernel, grid_spec=pltpu.PrefetchScalarGridSpec(num_sc...  13.8 us
  transfers between devices with their start and end apart: 26, of which 11 were waited for; matrix products, arithmetic and copies ran while one was open for 13% of the time, Pallas kernels for 19%

profile of v5, /device:TPU:0, one launch (start us, length us, event | category | flops | bytes accessed | tf_op | source)
XLA Modules:
  0.0 254.5 jit_solution(16525342595821046386)
XLA Ops:
  7.2 9.9 %projection.1 = (f32[2,512,512]{2,1,0:T(8,128)}, f32[512,1024]{1,0:T(8,128)}, f32[512,16]{1,0:T(8,128)}) custom-call(bf16[512,2048]{1,0:T(8,128)(2,1)} %left_b_ref.7, bf16[2,2048,512]{2,1,0:T(8,128)(2,1)} %query_key_weight_ref.3, bf16[2,2048,1024]{2,1,0:T(8,128)(2,1)} %value_gate_weight_ref.1, bf16[2,8,2048]{2,1,0:T(8,128)(2,1)} %bitcast.36), custom_call_target="tpu_custom_call" | custom-call | flops 10000000000 | bytes 36000000 | tf_op jit(solution)/shard_map/projection/pallas_call | solution.py:637
  17.1 12.8 %forward_blocks.1 = (bf16[4,8,128,128]{3,2,1,0:T(8,128)(2,1)}, bf16[4,8,128,256]{3,2,1,0:T(8,128)(2,1)}, bf16[512,1024]{1,0:T(8,128)(2,1)}, f32[512,1024]{1,0:T(8,128)}, bf16[8,128,256]{2,1,0:T(8,128)(2,1)}) custom-call(f32[2,512,512]{2,1,0:T(8,128)} %get-tuple-element.86.query_key_ref, f32[512,1024]{1,0:T(8,128)} %get-tuple-element.87.value_ref, ...), custom_call_target="tpu_custom_call" | custom-call | flops 12999999488 | bytes 46800000 | tf_op jit(solution)/shard_map/forward_blocks/pallas_call | solution.py:450
  29.9 5.2 %all-to-all-start = ((bf16[8,1,128,256]{3,2,1,0:T(8,128)(2,1)}), bf16[8,1,128,256]{3,2,1,0:T(8,128)(2,1)S(1)}, u32[]{:S(2)}, u32[]{:S(2)}) async-start(bf16[8,1,128,256]{3,2,1,0:T(8,128)(2,1)} %bitcast.32), calls=%async_computation | async-start | bytes 1048576 | tf_op jit(solution)/shard_map/all_to_all | solution.py:574
  35.1 6.5 %fusion.gate_ref = f32[512,1024]{1,0:T(8,128)} fusion(bf16[512,2048]{1,0:T(8,128)(2,1)} %left_b_ref.7, bf16[2,2048,1024]{2,1,0:T(8,128)(2,1)} %value_gate_weight_ref.1), kind=kOutput, calls=%fused_computation | convolution fusion | flops 2147483648 | bytes 8388608 | tf_op jit(solution)/shard_map/td,df->tf/dot_general | solution.py:606
  41.6 3.2 %all-to-all-done.totals_ref = bf16[8,1,128,256]{3,2,1,0:T(8,128)(2,1)S(1)} async-done(((bf16[8,1,128,256]{3,2,1,0:T(8,128)(2,1)}), bf16[8,1,128,256]{3,2,1,0:T(8,128)(2,1)S(1)}, u32[]{:S(2)}, u32[]{:S(2)}) %all-to-all-start) | async-done | bytes 524320 | tf_op jit(solution)/shard_map/all_to_all | solution.py:574
  45.6 2.8 %chain_forward.1 = bf16[8,1,128,128]{3,2,1,0:T(8,128)(2,1)} custom-call(bf16[8,1,128,256]{3,2,1,0:T(8,128)(2,1)} %copy-done.12), custom_call_target="tpu_custom_call" | custom-call | flops 3000000000 | bytes 10800000 | tf_op jit(solution)/shard_map/chain_forward/pallas_call | solution.py:586
  48.4 3.6 %all-to-all-start.1 = ((bf16[8,1,128,128]{3,2,1,0:T(8,128)(2,1)}), bf16[8,1,128,128]{3,2,1,0:T(8,128)(2,1)S(1)}, u32[]{:S(2)}, u32[]{:S(2)}) async-start(bf16[8,1,128,128]{3,2,1,0:T(8,128)(2,1)} %chain_forward.1), calls=%async_computation.1 | async-start | bytes 524288 | tf_op jit(solution)/shard_map/all_to_all | solution.py:574
  52.0 6.5 %fusion.3.delta_ref = f32[512,1024]{1,0:T(8,128)} fusion(bf16[512,2048]{1,0:T(8,128)(2,1)} %left_b_ref.5, bf16[1024,2048]{1,0:T(8,128)(2,1)} %param.17), kind=kOutput, calls=%fused_computation.27 | convolution fusion | flops 2147483648 | bytes 8388608 | tf_op jit(solution)/shard_map/td,fd->tf/dot_general | solution.py:606
  59.4 6.8 %gated_norm.1 = (bf16[512,1024]{1,0:T(8,128)(2,1)}, bf16[512,1024]{1,0:T(8,128)(2,1)}, bf16[512,1024]{1,0:T(8,128)(2,1)}, bf16[8,128,128]{2,1,0:T(8,128)(2,1)}) custom-call(f32[512,1024]{1,0:T(8,128)} %get-tuple-element.89.local_ref, bf16[512,1024]{1,0:T(8,128)(2,1)} %get-tuple-element.90.map_ref, f32[512,1024]{1,0:T(8,128)} %fusion.gate_ref, ...), custom_call_target="tpu_custom_call" | custom-call | flops 7000000000 | bytes 25200000 | tf_op jit(solution)/shard_map/gated_norm/pallas_call | solution.py:488
  66.3 6.7 %send_rows.2 = bf16[1024,2048]{1,0:T(8,128)(2,1)} custom-call(s32[1]{0:T(128)} %bitcast.9.place_ref, bf16[512,2048]{1,0:T(8,128)(2,1)} %left_b_ref.7, bf16[512,1024]{1,0:T(8,128)(2,1)} %get-tuple-element.103.a_ref.delta_gate_ref, bf16[512,2048]{1,0:T(8,128)(2,1)} %left_b_ref.5, bf16[512,1024]{1,0:T(8,128)(2,1)} %get-tuple-element.97.b_ref), custom_call_target="tpu_custom_call" | custom-call | flops 6000000000 | bytes 21600000 | tf_op jit(solution)/shard_map/send_rows/pallas_call | solution.py:766
  73.0 3.9 %all-to-all-start.2 = ((bf16[8,1,128,128]{3,2,1,0:T(8,128)(2,1)}), bf16[8,1,128,128]{3,2,1,0:T(8,128)(2,1)S(1)}, u32[]{:S(2)}, u32[]{:S(2)}) async-start(bf16[8,1,128,128]{3,2,1,0:T(8,128)(2,1)} %bitcast.8), calls=%async_computation.2 | async-start | bytes 524288 | tf_op jit(solution)/shard_map/all_to_all | solution.py:574
  76.9 4.5 %convolution_convert_fusion = bf16[512,2048]{1,0:T(8,128)(2,1)S(1)} fusion(bf16[512,1024]{1,0:T(8,128)(2,1)S(1)} %copy-done.18, bf16[1024,2048]{1,0:T(8,128)(2,1)} %param.17), kind=kOutput, calls=%fused_computation.3 | convolution fusion | flops 2148532224 | bytes 7340032 | tf_op jit(solution)/shard_map/tf,fd->td/dot_general | solution.py:606
  81.5 2.4 all-to-all-done.2.deltas_ref
  84.6 2.9 %chain_backward.1 = bf16[8,1,128,128]{3,2,1,0:T(8,128)(2,1)} custom-call(bf16[8,1,128,256]{3,2,1,0:T(8,128)(2,1)} %copy-done.12, bf16[8,1,128,128]{3,2,1,0:T(8,128)(2,1)} %copy-done.15), custom_call_target="tpu_custom_call" | custom-call | flops 3000000000 | bytes 10800000 | tf_op jit(solution)/shard_map/chain_backward/pallas_call | solution.py:596
  87.5 3.4 %all-to-all-start.3 = ((bf16[8,1,128,128]{3,2,1,0:T(8,128)(2,1)}), bf16[8,1,128,128]{3,2,1,0:T(8,128)(2,1)S(1)}, u32[]{:S(2)}, u32[]{:S(2)}) async-start(bf16[8,1,128,128]{3,2,1,0:T(8,128)(2,1)} %chain_backward.1), calls=%async_computation.3 | async-start | bytes 524288 | tf_op jit(solution)/shard_map/all_to_all | solution.py:574
  91.9 3.5 %collective-permute-start.1 = (bf16[512,512]{1,0:T(8,128)(2,1)}, bf16[512,512]{1,0:T(8,128)(2,1)S(1)}, u32[]{:S(2)}, u32[]{:S(2)}) collective-permute-start(bf16[512,512]{1,0:T(8,128)(2,1)} %get-tuple-element.183), channel_id=1, source_target_pairs={{0,1},{4,5},{8,9},{12,13},{16,17},{20,21},{24,25},{28,29}} | collective-permute-start | bytes 1572872 | tf_op jit(solution)/shard_map/ppermute | solution.py:844
  96.8 8.4 %keep_rows.2 = (bf16[256,1024]{1,0:T(8,128)(2,1)}, bf16[256,1024]{1,0:T(8,128)(2,1)}, bf16[256,1024]{1,0:T(8,128)(2,1)}, bf16[256,1024]{1,0:T(8,128)(2,1)}, bf16...) custom-call(s32[1]{0:T(128)} %bitcast.9.place_ref, ...), custom_call_target="tpu_custom_call" | custom-call | flops 8000000000 | bytes 28800000 | tf_op jit(solution)/shard_map/keep_rows/pallas_call | solution.py:784
  105.2 2.1 collective-permute-done.1
  108.8 4.3 %collective-permute-start.5 = (bf16[512,512]{1,0:T(8,128)(2,1)S(1)}, bf16[512,512]{1,0:T(8,128)(2,1)S(1)}, u32[]{:S(2)}, u32[]{:S(2)}) collective-permute-start(bf16[512,512]{1,0:T(8,128)(2,1)S(1)} %get-tuple-element.181), channel_id=1, source_target_pairs={{0,1},{1,2},{4,5},{5,6},{8,9},{9,10},{12,13},{13,14},{16,17},{17,1... | collective-permute-start | bytes 1572872 | tf_op jit(solution)/shard_map/ppermute | solution.py:844
  114.0 1.7 collective-permute-start.3
  117.3 16.9 %backward_blocks.1 = (bf16[512,1152]{1,0:T(8,128)(2,1)}, bf16[512,1024]{1,0:T(8,128)(2,1)}) custom-call(f32[2,512,512]{2,1,0:T(8,128)} %get-tuple-element.86.query_key_ref, f32[512,1024]{1,0:T(8,128)} %get-tuple-element.87.value_ref, f32[512,16]{1,0:T(8,128)} %get-tuple-element.88.decay_beta_ref, f32[1,8]{1,0:T(1,128)} %bitcast.42, f32[1,8]{1,0:T(1,128)} %bitcast.44, ...), custom_call_target="tpu_custom_call" | custom-call | flops 16999999488 | bytes 61200000 | tf_op jit(solution)/shard_map/backward_blocks/pallas_call | solution.py:523
  134.2 7.1 %send_rows.3 = bf16[1024,2176]{1,0:T(8,128)(2,1)} custom-call(s32[1]{0:T(128)} %bitcast.9.place_ref, bf16[512,2048]{1,0:T(8,128)(2,1)} %left_b_ref.7, bf16[512,1024]{1,0:T(8,128)(2,1)} %get-tuple-element.127.delta_value_ref.a_ref, bf16[512,2048]{1,0:T(8,128)(2,1)} %left_b_ref.7, bf16[512,1152]{1,0:T(8,128)(2,1)} %get-tuple-element.114.delta_query_key_ref.b_ref), custom_call_target="tpu_custom_call" | custom-call | flops 6000000000 | bytes 21600000 | tf_op jit(solution)/shard_map/send_rows/pallas_call | solution.py:766
  142.7 11.6 %input_gradient.1 = (bf16[256,2048]{1,0:T(8,128)(2,1)}, bf16[256,2048]{1,0:T(8,128)(2,1)}) custom-call(bf16[512,1152]{1,0:T(8,128)(2,1)} %get-tuple-element.114.delta_query_key_ref.b_ref, bf16[512,1024]{1,0:T(8,128)(2,1)} %get-tuple-element.127.delta_value_ref.a_ref, bf16[512,1024]{1,0:T(8,128)(2,1)} %get-tuple-element.103.a_ref.delta_gate_ref, ...), custom_call_target="tpu_custom_call" | custom-call | flops 11000000512 | bytes 39600000 | tf_op jit(solution)/shard_map/input_gradient/pallas_call | solution.py:696
  158.0 4.6 %collective-permute-start.10 = (bf16[512,512]{1,0:T(8,128)(2,1)}, bf16[512,512]{1,0:T(8,128)(2,1)S(1)}, u32[]{:S(2)}, u32[]{:S(2)}) collective-permute-start(bf16[512,512]{1,0:T(8,128)(2,1)} %get-tuple-element.179), channel_id=1, source_target_pairs={{0,1},{1,2},{2,3},{4,5},{5,6},{6,7},{8,9},{9,10},{10,11},{12,13},{... | collective-permute-start | bytes 1572872 | tf_op jit(solution)/shard_map/ppermute | solution.py:844
  166.3 18.5 %collective-permute-done.10 = bf16[512,512]{1,0:T(8,128)(2,1)S(1)} collective-permute-done((bf16[512,512]{1,0:T(8,128)(2,1)}, bf16[512,512]{1,0:T(8,128)(2,1)S(1)}, u32[]{:S(2)}, u32[]{:S(2)}) %collective-permute-start.10) | collective-permute-done | bytes 524320 | tf_op jit(solution)/shard_map/ppermute | solution.py:844
  184.8 8.1 %collective-permute-done.11 = bf16[512,512]{1,0:T(8,128)(2,1)S(1)} collective-permute-done((bf16[512,512]{1,0:T(8,128)(2,1)}, bf16[512,512]{1,0:T(8,128)(2,1)S(1)}, u32[]{:S(2)}, u32[]{:S(2)}) %collective-permute-start.11) | collective-permute-done | bytes 524320 | tf_op jit(solution)/shard_map/ppermute | solution.py:844
  192.9 8.9 %keep_rows.3 = (bf16[256,1024]{1,0:T(8,128)(2,1)}, bf16[256,1024]{1,0:T(8,128)(2,1)}, bf16[256,1024]{1,0:T(8,128)(2,1)}, bf16[256,1024]{1,0:T(8,128)(2,1)}, bf16...) custom-call(s32[1]{0:T(128)} %bitcast.9.place_ref, ...), custom_call_target="tpu_custom_call" | custom-call | flops 8000000000 | bytes 28800000 | tf_op jit(solution)/shard_map/keep_rows/pallas_call | solution.py:784
  201.9 2.2 collective-permute-start.15
  211.2 8.1 %collective-permute-done.18 = bf16[256,1024]{1,0:T(8,128)(2,1)} collective-permute-done((bf16[256,1024]{1,0:T(8,128)(2,1)}, bf16[256,1024]{1,0:T(8,128)(2,1)}, u32[]{:S(2)}, u32[]{:S(2)}) %collective-permute-start.18) | collective-permute-done | bytes 524320 | tf_op jit(solution)/shard_map/ppermute | solution.py:722
  225.1 5.4 %collective-permute-done.17 = bf16[256,1024]{1,0:T(8,128)(2,1)} collective-permute-done((bf16[256,1024]{1,0:T(8,128)(2,1)}, bf16[256,1024]{1,0:T(8,128)(2,1)}, u32[]{:S(2)}, u32[]{:S(2)}) %collective-permute-start.17) | collective-permute-done | bytes 524320 | tf_op jit(solution)/shard_map/ppermute | solution.py:722
  230.5 10.2 %collective-permute-done.19 = bf16[256,1024]{1,0:T(8,128)(2,1)S(1)} collective-permute-done((bf16[256,1024]{1,0:T(8,128)(2,1)S(1)}, bf16[256,1024]{1,0:T(8,128)(2,1)S(1)}, u32[]{:S(2)}, u32[]{:S(2)}) %collective-permute-start.19) | collective-permute-done | bytes 524320 | tf_op jit(solution)/shard_map/ppermute | solution.py:722
  245.8 1.9 pad_maximum_fusion.2
  (95 shorter events, 35.3 us)
Async XLA Ops:
  29.9 14.9 %all-to-all-start = ((bf16[8,1,128,256]{3,2,1,0:T(8,128)(2,1)}), bf16[8,1,128,256]{3,2,1,0:T(8,128)(2,1)S(1)}, u32[]{:S(2)}, u32[]{:S(2)}) async-start(bf16[8,1,128,256]{3,2,1,0:T(8,128)(2,1)} %bitcast.32), calls=%async_computation | async-start | bytes 1048576 | tf_op jit(solution)/shard_map/all_to_all | solution.py:574
  48.4 10.3 %all-to-all-start.1 = ((bf16[8,1,128,128]{3,2,1,0:T(8,128)(2,1)}), bf16[8,1,128,128]{3,2,1,0:T(8,128)(2,1)S(1)}, u32[]{:S(2)}, u32[]{:S(2)}) async-start(bf16[8,1,128,128]{3,2,1,0:T(8,128)(2,1)} %chain_forward.1), calls=%async_computation.1 | async-start | bytes 524288 | tf_op jit(solution)/shard_map/all_to_all | solution.py:574
  73.0 23.9 %collective-permute-start = (bf16[1024,2048]{1,0:T(8,128)(2,1)}, bf16[1024,2048]{1,0:T(8,128)(2,1)}, u32[]{:S(2)}, u32[]{:S(2)}) collective-permute-start(bf16[1024,2048]{1,0:T(8,128)(2,1)} %send_rows.2), channel_id=1, source_target_pairs={{0,4},{4,0},{8,12},{12,8},{16,20},{20,16},{24,28},{28,24},{1,5},{5... | collective-permute-start | bytes 12582920 | tf_op jit(solution)/shard_map/ppermute | solution.py:722
  73.0 10.8 %all-to-all-start.2 = ((bf16[8,1,128,128]{3,2,1,0:T(8,128)(2,1)}), bf16[8,1,128,128]{3,2,1,0:T(8,128)(2,1)S(1)}, u32[]{:S(2)}, u32[]{:S(2)}) async-start(bf16[8,1,128,128]{3,2,1,0:T(8,128)(2,1)} %bitcast.8), calls=%async_computation.2 | async-start | bytes 524288 | tf_op jit(solution)/shard_map/all_to_all | solution.py:574
  87.5 17.7 %all-to-all-start.3 = ((bf16[8,1,128,128]{3,2,1,0:T(8,128)(2,1)}), bf16[8,1,128,128]{3,2,1,0:T(8,128)(2,1)S(1)}, u32[]{:S(2)}, u32[]{:S(2)}) async-start(bf16[8,1,128,128]{3,2,1,0:T(8,128)(2,1)} %chain_backward.1), calls=%async_computation.3 | async-start | bytes 524288 | tf_op jit(solution)/shard_map/all_to_all | solution.py:574
  90.9 154.9 %reduce-scatter.3.cloned.1.call-start = ((), (), s32[]{:S(2)}) async-start(), calls=%async_computation.6 | async-start | bytes 1310720 | tf_op jit(solution)/shard_map/reduce_scatter | solution.py:865
  91.9 15.5 %collective-permute-start.1 = (bf16[512,512]{1,0:T(8,128)(2,1)}, bf16[512,512]{1,0:T(8,128)(2,1)S(1)}, u32[]{:S(2)}, u32[]{:S(2)}) collective-permute-start(bf16[512,512]{1,0:T(8,128)(2,1)} %get-tuple-element.183), channel_id=1, source_target_pairs={{0,1},{4,5},{8,9},{12,13},{16,17},{20,21},{24,25},{28,29}} | collective-permute-start | bytes 1572872 | tf_op jit(solution)/shard_map/ppermute | solution.py:844
  95.4 12.0 %collective-permute-start.2 = (bf16[512,512]{1,0:T(8,128)(2,1)S(1)}, bf16[512,512]{1,0:T(8,128)(2,1)}, u32[]{:S(2)}, u32[]{:S(2)}) collective-permute-start(bf16[512,512]{1,0:T(8,128)(2,1)S(1)} %get-tuple-element.182), channel_id=1, source_target_pairs={{3,2},{7,6},{11,10},{15,14},{19,18},{23,22},{27,26},{31,30}} | collective-permute-start | bytes 1572872 | tf_op jit(solution)/shard_map/ppermute | solution.py:844
  105.2 12.1 %copy-start.14 = (bf16[8,1,128,128]{3,2,1,0:T(8,128)(2,1)}, bf16[8,1,128,128]{3,2,1,0:T(8,128)(2,1)S(1)}, u32[]{:S(2)}) copy-start(bf16[8,1,128,128]{3,2,1,0:T(8,128)(2,1)S(1)} %all-to-all-done.3) | copy-start | bytes 786436
  108.8 25.4 %collective-permute-start.5 = (bf16[512,512]{1,0:T(8,128)(2,1)S(1)}, bf16[512,512]{1,0:T(8,128)(2,1)S(1)}, u32[]{:S(2)}, u32[]{:S(2)}) collective-permute-start(bf16[512,512]{1,0:T(8,128)(2,1)S(1)} %get-tuple-element.181), channel_id=1, source_target_pairs={{0,1},{1,2},{4,5},{5,6},{8,9},{9,10},{12,13},{13,14},{16,17},{17,1... | collective-permute-start | bytes 1572872 | tf_op jit(solution)/shard_map/ppermute | solution.py:844
  113.1 21.1 %collective-permute-start.6 = (bf16[512,512]{1,0:T(8,128)(2,1)S(1)}, bf16[512,512]{1,0:T(8,128)(2,1)S(1)}, u32[]{:S(2)}, u32[]{:S(2)}) collective-permute-start(bf16[512,512]{1,0:T(8,128)(2,1)S(1)} %get-tuple-element.180), channel_id=1, source_target_pairs={{2,1},{3,2},{6,5},{7,6},{10,9},{11,10},{14,13},{15,14},{18,17},{19... | collective-permute-start | bytes 1572872 | tf_op jit(solution)/shard_map/ppermute | solution.py:844
  114.0 20.1 %collective-permute-start.3 = (bf16[256,1024]{1,0:T(8,128)(2,1)S(1)}, bf16[256,1024]{1,0:T(8,128)(2,1)S(1)}, u32[]{:S(2)}, u32[]{:S(2)}) collective-permute-start(bf16[256,1024]{1,0:T(8,128)(2,1)S(1)} %copy-done.17), channel_id=1, source_target_pairs={{0,8},{4,12},{8,0},{12,4},{16,24},{20,28},{24,16},{28,20},{1,9},{5... | collective-permute-start | bytes 1572872 | tf_op jit(solution)/shard_map/ppermute | solution.py:722
  115.8 18.4 %collective-permute-start.4 = (bf16[256,1024]{1,0:T(8,128)(2,1)S(1)}, bf16[256,1024]{1,0:T(8,128)(2,1)S(1)}, u32[]{:S(2)}, u32[]{:S(2)}) collective-permute-start(bf16[256,1024]{1,0:T(8,128)(2,1)S(1)} %copy-done.16), channel_id=1, source_target_pairs={{0,16},{4,20},{8,24},{12,28},{16,0},{20,4},{24,8},{28,12},{1,17},{... | collective-permute-start | bytes 1572872 | tf_op jit(solution)/shard_map/ppermute | solution.py:722
  141.3 15.2 %collective-permute-start.7 = (bf16[1024,2176]{1,0:T(8,128)(2,1)}, bf16[1024,2176]{1,0:T(8,128)(2,1)}, u32[]{:S(2)}, u32[]{:S(2)}) collective-permute-start(bf16[1024,2176]{1,0:T(8,128)(2,1)} %send_rows.3), channel_id=1, source_target_pairs={{0,4},{4,0},{8,12},{12,8},{16,20},{20,16},{24,28},{28,24},{1,5},{5... | collective-permute-start | bytes 13369352 | tf_op jit(solution)/shard_map/ppermute | solution.py:722
  141.5 14.5 %collective-permute-start.9 = (bf16[256,1024]{1,0:T(8,128)(2,1)S(1)}, bf16[256,1024]{1,0:T(8,128)(2,1)}, u32[]{:S(2)}, u32[]{:S(2)}) collective-permute-start(bf16[256,1024]{1,0:T(8,128)(2,1)S(1)} %add_convert_fusion.5), channel_id=1, source_target_pairs={{0,8},{4,12},{8,0},{12,4},{16,24},{20,28},{24,16},{28,20},{1,9},{5... | collective-permute-start | bytes 1572872 | tf_op jit(solution)/shard_map/ppermute | solution.py:722
  142.3 14.2 %collective-permute-start.8 = (bf16[256,1024]{1,0:T(8,128)(2,1)S(1)}, bf16[256,1024]{1,0:T(8,128)(2,1)}, u32[]{:S(2)}, u32[]{:S(2)}) collective-permute-start(bf16[256,1024]{1,0:T(8,128)(2,1)S(1)} %add_convert_fusion.6), channel_id=1, source_target_pairs={{0,16},{4,20},{8,24},{12,28},{16,0},{20,4},{24,8},{28,12},{1,17},{... | collective-permute-start | bytes 1572872 | tf_op jit(solution)/shard_map/ppermute | solution.py:722
  156.6 89.3 %reduce-scatter.5.cloned.1.call-start = ((), (), s32[]{:S(2)}) async-start(), calls=%async_computation.7 | async-start | bytes 1310720 | tf_op jit(solution)/shard_map/reduce_scatter | solution.py:865
  158.0 26.8 %collective-permute-start.10 = (bf16[512,512]{1,0:T(8,128)(2,1)}, bf16[512,512]{1,0:T(8,128)(2,1)S(1)}, u32[]{:S(2)}, u32[]{:S(2)}) collective-permute-start(bf16[512,512]{1,0:T(8,128)(2,1)} %get-tuple-element.179), channel_id=1, source_target_pairs={{0,1},{1,2},{2,3},{4,5},{5,6},{6,7},{8,9},{9,10},{10,11},{12,13},{... | collective-permute-start | bytes 1572872 | tf_op jit(solution)/shard_map/ppermute | solution.py:844
  162.7 30.2 %collective-permute-start.11 = (bf16[512,512]{1,0:T(8,128)(2,1)}, bf16[512,512]{1,0:T(8,128)(2,1)S(1)}, u32[]{:S(2)}, u32[]{:S(2)}) collective-permute-start(bf16[512,512]{1,0:T(8,128)(2,1)} %get-tuple-element.178), channel_id=1, source_target_pairs={{1,0},{2,1},{3,2},{5,4},{6,5},{7,6},{9,8},{10,9},{11,10},{13,12},{... | collective-permute-start | bytes 1572872 | tf_op jit(solution)/shard_map/ppermute | solution.py:844
  164.2 41.4 %copy-start.2 = (bf16[256,1024]{1,0:T(8,128)(2,1)S(1)}, bf16[256,1024]{1,0:T(8,128)(2,1)}, u32[]{:S(2)}) copy-start(bf16[256,1024]{1,0:T(8,128)(2,1)} %get-tuple-element.163) | copy-start | bytes 1572868
  164.2 37.6 %collective-permute-start.12 = (bf16[256,1024]{1,0:T(8,128)(2,1)}, bf16[256,1024]{1,0:T(8,128)(2,1)S(1)}, u32[]{:S(2)}, u32[]{:S(2)}) collective-permute-start(bf16[256,1024]{1,0:T(8,128)(2,1)} %get-tuple-element.150), channel_id=1, source_target_pairs={{0,8},{4,12},{8,0},{12,4},{16,24},{20,28},{24,16},{28,20},{1,9},{5... | collective-permute-start | bytes 1572872 | tf_op jit(solution)/shard_map/ppermute | solution.py:722
  165.8 36.1 %collective-permute-start.13 = (bf16[256,1024]{1,0:T(8,128)(2,1)}, bf16[256,1024]{1,0:T(8,128)(2,1)S(1)}, u32[]{:S(2)}, u32[]{:S(2)}) collective-permute-start(bf16[256,1024]{1,0:T(8,128)(2,1)} %get-tuple-element.151), channel_id=1, source_target_pairs={{0,16},{4,20},{8,24},{12,28},{16,0},{20,4},{24,8},{28,12},{1,17},{... | collective-permute-start | bytes 1572872 | tf_op jit(solution)/shard_map/ppermute | solution.py:722
  184.8 17.0 %copy-start.3 = (bf16[512,512]{1,0:T(8,128)(2,1)}, bf16[512,512]{1,0:T(8,128)(2,1)S(1)}, u32[]{:S(2)}) copy-start(bf16[512,512]{1,0:T(8,128)(2,1)S(1)} %collective-permute-done.10) | copy-start | bytes 1572868
  201.9 19.5 %collective-permute-start.15 = (bf16[256,1152]{1,0:T(8,128)(2,1)}, bf16[256,1152]{1,0:T(8,128)(2,1)}, u32[]{:S(2)}, u32[]{:S(2)}) collective-permute-start(bf16[256,1152]{1,0:T(8,128)(2,1)} %get-tuple-element.155), channel_id=1, source_target_pairs={{0,16},{4,20},{8,24},{12,28},{16,0},{20,4},{24,8},{28,12},{1,17},{... | collective-permute-start | bytes 1769480 | tf_op jit(solution)/shard_map/ppermute | solution.py:722
  204.1 15.2 %collective-permute-start.18 = (bf16[256,1024]{1,0:T(8,128)(2,1)}, bf16[256,1024]{1,0:T(8,128)(2,1)}, u32[]{:S(2)}, u32[]{:S(2)}) collective-permute-start(bf16[256,1024]{1,0:T(8,128)(2,1)} %get-tuple-element.159), channel_id=1, source_target_pairs={{0,8},{4,12},{8,0},{12,4},{16,24},{20,28},{24,16},{28,20},{1,9},{5... | collective-permute-start | bytes 1572872 | tf_op jit(solution)/shard_map/ppermute | solution.py:722
  208.2 35.4 %collective-permute-start.14 = (bf16[256,1152]{1,0:T(8,128)(2,1)}, bf16[256,1152]{1,0:T(8,128)(2,1)S(1)}, u32[]{:S(2)}, u32[]{:S(2)}) collective-permute-start(bf16[256,1152]{1,0:T(8,128)(2,1)} %get-tuple-element.153), channel_id=1, source_target_pairs={{0,16},{4,20},{8,24},{12,28},{16,0},{20,4},{24,8},{28,12},{1,17},{... | collective-permute-start | bytes 1769480 | tf_op jit(solution)/shard_map/ppermute | solution.py:722
  208.9 21.6 %collective-permute-start.17 = (bf16[256,1024]{1,0:T(8,128)(2,1)}, bf16[256,1024]{1,0:T(8,128)(2,1)}, u32[]{:S(2)}, u32[]{:S(2)}) collective-permute-start(bf16[256,1024]{1,0:T(8,128)(2,1)} %get-tuple-element.157), channel_id=1, source_target_pairs={{0,8},{4,12},{8,0},{12,4},{16,24},{20,28},{24,16},{28,20},{1,9},{5... | collective-permute-start | bytes 1572872 | tf_op jit(solution)/shard_map/ppermute | solution.py:722
  211.2 12.9 %copy-start.4 = (bf16[512,512]{1,0:T(8,128)(2,1)S(1)}, bf16[512,512]{1,0:T(8,128)(2,1)}, u32[]{:S(2)}) copy-start(bf16[512,512]{1,0:T(8,128)(2,1)} %copy-done.3) | copy-start | bytes 1572868
  211.2 12.9 %copy-start.6 = (bf16[512,512]{1,0:T(8,128)(2,1)S(1)}, bf16[512,512]{1,0:T(8,128)(2,1)}, u32[]{:S(2)}) copy-start(bf16[512,512]{1,0:T(8,128)(2,1)} %copy-done.5) | copy-start | bytes 1572868
  220.5 20.2 %copy-start.8 = (bf16[256,1024]{1,0:T(8,128)(2,1)S(1)}, bf16[256,1024]{1,0:T(8,128)(2,1)}, u32[]{:S(2)}) copy-start(bf16[256,1024]{1,0:T(8,128)(2,1)} %get-tuple-element.156) | copy-start | bytes 1572868
  220.5 20.2 %collective-permute-start.19 = (bf16[256,1024]{1,0:T(8,128)(2,1)S(1)}, bf16[256,1024]{1,0:T(8,128)(2,1)S(1)}, u32[]{:S(2)}, u32[]{:S(2)}) collective-permute-start(bf16[256,1024]{1,0:T(8,128)(2,1)S(1)} %add_convert_fusion.1), channel_id=1, source_target_pairs={{0,16},{4,20},{8,24},{12,28},{16,0},{20,4},{24,8},{28,12},{1,17},{... | collective-permute-start | bytes 1572872 | tf_op jit(solution)/shard_map/ppermute | solution.py:722
  222.6 21.0 %collective-permute-start.16 = (bf16[256,1152]{1,0:T(8,128)(2,1)S(1)}, bf16[256,1152]{1,0:T(8,128)(2,1)S(1)}, u32[]{:S(2)}, u32[]{:S(2)}) collective-permute-start(bf16[256,1152]{1,0:T(8,128)(2,1)S(1)} %add_convert_fusion), channel_id=1, source_target_pairs={{0,8},{4,12},{8,0},{12,4},{16,24},{20,28},{24,16},{28,20},{1,9},{5... | collective-permute-start | bytes 1769480 | tf_op jit(solution)/shard_map/ppermute | solution.py:722
  (13 other events, 82.9 us)
Sparse Core Ops, SparseCore 0:
  156.7 39.7 reduce-scatter.2
  209.6 26.7 reduce-scatter.4

commit v6 on v4

--- a/solution.py
+++ b/solution.py
@@ -711,17 +711,17 @@
     return target_y * 4 + target_x * 2 + core
 
 
-def send_kernel(place_ref, left_a_ref, a_ref, left_b_ref, b_ref, out_ref):
-    width = a_ref.shape[1]
-    out_ref[:, :width] = dot(left_a_ref[...], a_ref[...], TN).astype(BF16)
-    out_ref[:, width:] = dot(left_b_ref[...], b_ref[...], TN).astype(BF16)
-
-
-def keep_kernel(place_ref, left_a_ref, a_ref, left_b_ref, b_ref, arrived_ref, *out_refs):
+def send_kernel(place_ref, left_a_ref, a_ref, left_b_ref, b_ref, a_out_ref, b_out_ref):
+    a_out_ref[...] = dot(left_a_ref[...], a_ref[...], TN).astype(BF16)
+    b_out_ref[...] = dot(left_b_ref[...], b_ref[...], TN).astype(BF16)
+
+
+def keep_kernel(
+    place_ref, left_a_ref, a_ref, left_b_ref, b_ref, a_arrived_ref, b_arrived_ref, *out_refs
+):
     step = pl.program_id(0)
-    width = a_ref.shape[1]
-    a = dot(left_a_ref[...], a_ref[...], TN) + arrived_ref[:, :width].astype(F32)
-    b = dot(left_b_ref[...], b_ref[...], TN) + arrived_ref[:, width:].astype(F32)
+    a = dot(left_a_ref[...], a_ref[...], TN) + a_arrived_ref[...].astype(F32)
+    b = dot(left_b_ref[...], b_ref[...], TN) + b_arrived_ref[...].astype(F32)
     for i in range(4):
 
         @pl.when(step == i)
@@ -743,23 +743,27 @@
 
 
 def halving_start(place, left_a, a, left_b, b):
-    rows, width = left_a.shape[1] // 8, a.shape[1] + b.shape[1]
+    rows = left_a.shape[1] // 8
     return pl.pallas_call(
         send_kernel,
         grid_spec=pltpu.PrefetchScalarGridSpec(
             num_scalar_prefetch=1,
             grid=(4,),
             in_specs=pair_specs(left_a, a, left_b, b, 1),
-            out_specs=pl.BlockSpec((rows, width), lambda i, place: (i, 0)),
+            out_specs=[
+                pl.BlockSpec((rows, delta.shape[1]), lambda i, place: (i, 0)) for delta in (a, b)
+            ],
         ),
-        out_shape=jax.ShapeDtypeStruct((4 * rows, width), BF16),
+        out_shape=[
+            jax.ShapeDtypeStruct((4 * rows, delta.shape[1]), BF16) for delta in (a, b)
+        ],
         compiler_params=PARAMS,
         interpret=INTERPRET,
         name="send_rows",
     )(place, left_a, a, left_b, b)
 
 
-def halving_keep(place, left_a, a, left_b, b, arrived):
+def halving_keep(place, left_a, a, left_b, b, a_arrived, b_arrived):
     rows = left_a.shape[1] // 8
     return pl.pallas_call(
         keep_kernel,
@@ -767,7 +771,7 @@
             num_scalar_prefetch=1,
             grid=(4,),
             in_specs=pair_specs(left_a, a, left_b, b, 0)
-            + [pl.BlockSpec((rows, arrived.shape[1]), lambda i, place: (i, 0))],
+            + [pl.BlockSpec((rows, delta.shape[1]), lambda i, place: (i, 0)) for delta in (a, b)],
             out_specs=[
                 pl.BlockSpec((rows, delta.shape[1]), lambda i, place: (0, 0))
                 for delta in (a, b)
@@ -782,7 +786,7 @@
         compiler_params=PARAMS,
         interpret=INTERPRET,
         name="keep_rows",
-    )(place, left_a, a, left_b, b, arrived)
+    )(place, left_a, a, left_b, b, a_arrived, b_arrived)
 
 
 def summed(a, b):
@@ -790,23 +794,23 @@
 
 
 def halving_cross(pieces):
+    return exchange(pieces[0], 2), exchange(pieces[4], 4)
+
+
+def halving_stay(pieces):
+    return exchange(pieces[1], 2), exchange(pieces[6], 4)
+
+
+def halving_last(pieces, arrived):
     a, b = pieces[:4], pieces[4:]
-    return exchange(a[0], 2), exchange(b[0], 4), exchange(a[1], 2), exchange(b[2], 4)
-
-
-def halving_onward(pieces, arrived):
-    return summed(pieces[2], arrived[0]), summed(pieces[5], arrived[1])
-
-
-def halving_last(onward):
-    return exchange(onward[0], 4), exchange(onward[1], 2)
+    return exchange(summed(a[2], arrived[0]), 4), exchange(summed(b[1], arrived[1]), 2)
 
 
 def halving_sum(pieces, arrived, last):
     def total(own, near, far):
         return own.astype(F32) + near.astype(F32) + far.astype(F32)
 
-    return total(pieces[3], arrived[2], last[0]), total(pieces[7], arrived[3], last[1])
+    return total(pieces[3], arrived[0], last[0]), total(pieces[7], arrived[1], last[1])
 
 
 def scatter(partial, axis, dimension):
@@ -857,9 +861,12 @@
     if cubic:
         place = lax.axis_index("ctx").astype(jnp.int32).reshape(1)
         early = (place, inputs, delta_gate, grad_mixed, hidden)
-        early_pieces = halving_keep(*early, exchange(halving_start(*early), 1))
+        sent = halving_start(*early)
+        arrived = [exchange(part, 1) for part in sent]
+        early_pieces = halving_keep(*early, *arrived)
         finals, early_pieces = together(finals, early_pieces)
         early_arrived = halving_cross(early_pieces)
+        early_stay = halving_stay(early_pieces)
     delta_final = gather_parts(finals, heads)
     delta_query_key, delta_value = run_backward(
         query_key,
@@ -875,11 +882,12 @@
         delta_final,
     )
     if cubic:
+        delta_value, early_arrived = together(delta_value, early_arrived)
+        early_last = halving_last(early_pieces, early_arrived)
         late = (place, inputs, delta_value, inputs, delta_query_key)
-        arrived = exchange(halving_start(*late), 1)
-        early_onward = halving_onward(early_pieces, early_arrived)
-        delta_gate, early_onward = together(delta_gate, early_onward)
-        early_last = halving_last(early_onward)
+        sent = halving_start(*late)
+        sent, early_stay = together(sent, early_stay)
+        arrived = [exchange(part, 1) for part in sent]
     grad_rows = run_input_gradient(
         delta_query_key,
         delta_value,
@@ -889,15 +897,16 @@
         small_weight,
     )
     if cubic:
-        grad_rows, arrived = together(grad_rows, arrived)
+        grad_rows, arrived, early_last = together(grad_rows, arrived, early_last)
     grad_inputs = scatter(grad_rows, "head", 1)
     if cubic:
-        late_pieces = halving_keep(*late, arrived)
+        late_pieces = halving_keep(*late, *arrived)
         late_arrived = halving_cross(late_pieces)
-        late_last = halving_last(halving_onward(late_pieces, late_arrived))
-        grad_gate, grad_out = halving_sum(early_pieces, early_arrived, early_last)
+        late_stay = halving_stay(late_pieces)
+        late_last = halving_last(late_pieces, late_arrived)
+        grad_gate, grad_out = halving_sum(early_pieces, early_stay, early_last)
         grad_out = grad_out.T
-        grad_value, packed = halving_sum(late_pieces, late_arrived, late_last)
+        grad_value, packed = halving_sum(late_pieces, late_stay, late_last)
     else:
         grad_gate = scatter(product("td,tf->df", inputs, delta_gate), "ctx", 0).astype(F32)
         grad_out = scatter(product("tf,td->fd", hidden, grad_mixed), "ctx", 1).astype(F32)

time: 230 us -> 211 us (0.917)
  waiting for transfers between devices: 56.8 us -> 33.5 us
  other arithmetic: 8.18 us -> 10.8 us
    ppermute x14 -> x16, waiting for transfers between devices: 51.7 us -> 28.5 us  [exchange(): return lax.ppermute(array, 'ctx', [(i, i ^ distance) for i in devices])]
    ppermute x14 -> x16, starting transfers between devices: 13.4 us -> 14.9 us  [exchange(): return lax.ppermute(array, 'ctx', [(i, i ^ distance) for i in devices])]
    unnamed x35 -> x45, local copies, waits for them, and re-layouts: 5.74 us -> 7.17 us
  transfers between devices with their start and end apart: 20 -> 22, of which waited for: 10 -> 7; matrix products, arithmetic and copies ran while one was open for 12% -> 15% of each run, Pallas kernels for 14% -> 27%
where the time goes in v6:
time: 211 us; the launch traced here: 210 us
  Pallas kernels  94.7 us (45%)
  waiting for transfers between devices  33.5 us (16%)
  starting transfers between devices  31.1 us (15%)
  matrix products  18.4 us (9%)
  between operations  14.3 us (7%)
  other arithmetic  10.8 us (5%)
  local copies, waits for them, and re-layouts  7.52 us (4%)
    ppermute x16, waiting for transfers between devices, exchange(): return lax.ppermute(array, 'ctx', [(i, i ^ distance) for i in devices])  28.5 us
    dot_general x3, matrix products, product(): return jnp.einsum(spec, a, b, preferred_element_type=F32)  18.4 us
    pallas_call x2, Pallas kernels, halving_keep(): pl.pallas_call(keep_kernel, grid_spec=pltpu.PrefetchScalarGridSpec(num_sc...  17.6 us
    pallas_call x1, Pallas kernels, run_backward(): pl.pallas_call(backward_kernel, grid=(chunks // spans,), in_specs=[pl.Blo...  17 us
    all_to_all x4, starting transfers between devices, swap(): return lax.all_to_all(parts, 'ctx', split_axis=0, concat_axis=0, tiled=True)  16 us
    ppermute x16, starting transfers between devices, exchange(): return lax.ppermute(array, 'ctx', [(i, i ^ distance) for i in devices])  14.9 us
    pallas_call x1, Pallas kernels, run_forward(): pl.pallas_call(forward_kernel, grid=(chunks // spans,), in_specs=[pl.Bloc...  13 us
    pallas_call x2, Pallas kernels, halving_start(): pl.pallas_call(send_kernel, grid_spec=pltpu.PrefetchScalarGridSpec(num_sc...  12.9 us
  transfers between devices with their start and end apart: 22, of which 7 were waited for; matrix products, arithmetic and copies ran while one was open for 15% of the time, Pallas kernels for 27%

profile of v6, /device:TPU:0, one launch (start us, length us, event | category | flops | bytes accessed | tf_op | source)
XLA Modules:
  0.0 210.3 jit_solution(12097944890397186213)
XLA Ops:
  7.2 9.9 %projection.1 = (f32[2,512,512]{2,1,0:T(8,128)}, f32[512,1024]{1,0:T(8,128)}, f32[512,16]{1,0:T(8,128)}) custom-call(bf16[512,2048]{1,0:T(8,128)(2,1)} %left_b_ref.7, bf16[2,2048,512]{2,1,0:T(8,128)(2,1)} %query_key_weight_ref.3, bf16[2,2048,1024]{2,1,0:T(8,128)(2,1)} %value_gate_weight_ref.1, bf16[2,8,2048]{2,1,0:T(8,128)(2,1)} %bitcast.36), custom_call_target="tpu_custom_call" | custom-call | tf_op jit(solution)/shard_map/projection/pallas_call | solution.py:624
  17.1 13.0 %forward_blocks.1 = (bf16[4,8,128,128]{3,2,1,0:T(8,128)(2,1)}, bf16[4,8,128,256]{3,2,1,0:T(8,128)(2,1)}, bf16[512,1024]{1,0:T(8,128)(2,1)}, f32[512,1024]{1,0:T(8,128)}, bf16[8,128,256]{2,1,0:T(8,128)(2,1)}) custom-call(f32[2,512,512]{2,1,0:T(8,128)} %get-tuple-element.67.query_key_ref, f32[512,1024]{1,0:T(8,128)} %get-tuple-element.68.value_ref, ...), custom_call_target="tpu_custom_call" | custom-call | tf_op jit(solution)/shard_map/forward_blocks/pallas_call | solution.py:442
  30.1 5.2 %all-to-all-start = ((bf16[8,1,128,256]{3,2,1,0:T(8,128)(2,1)}), bf16[8,1,128,256]{3,2,1,0:T(8,128)(2,1)S(1)}, u32[]{:S(2)}, u32[]{:S(2)}) async-start(bf16[8,1,128,256]{3,2,1,0:T(8,128)(2,1)} %bitcast.35), calls=%async_computation | async-start | bytes 1048576 | tf_op jit(solution)/shard_map/all_to_all | solution.py:563
  35.3 6.0 %fusion.gate_ref = f32[512,1024]{1,0:T(8,128)} fusion(bf16[512,2048]{1,0:T(8,128)(2,1)S(1)} %copy-done, bf16[2,2048,1024]{2,1,0:T(8,128)(2,1)} %value_gate_weight_ref.1), kind=kOutput, calls=%fused_computation | convolution fusion | flops 2147483648 | bytes 8388608 | tf_op jit(solution)/shard_map/td,df->tf/dot_general | solution.py:593
  41.2 3.8 %all-to-all-done.totals_ref = bf16[8,1,128,256]{3,2,1,0:T(8,128)(2,1)S(1)} async-done(((bf16[8,1,128,256]{3,2,1,0:T(8,128)(2,1)}), bf16[8,1,128,256]{3,2,1,0:T(8,128)(2,1)S(1)}, u32[]{:S(2)}, u32[]{:S(2)}) %all-to-all-start) | async-done | bytes 524320 | tf_op jit(solution)/shard_map/all_to_all | solution.py:563
  45.8 2.8 %chain_forward.1 = bf16[8,1,128,128]{3,2,1,0:T(8,128)(2,1)} custom-call(bf16[8,1,128,256]{3,2,1,0:T(8,128)(2,1)} %copy-done.1), custom_call_target="tpu_custom_call" | custom-call | tf_op jit(solution)/shard_map/chain_forward/pallas_call | solution.py:575
  48.6 3.6 %all-to-all-start.1 = ((bf16[8,1,128,128]{3,2,1,0:T(8,128)(2,1)}), bf16[8,1,128,128]{3,2,1,0:T(8,128)(2,1)S(1)}, u32[]{:S(2)}, u32[]{:S(2)}) async-start(bf16[8,1,128,128]{3,2,1,0:T(8,128)(2,1)} %chain_forward.1), calls=%async_computation.1 | async-start | bytes 524288 | tf_op jit(solution)/shard_map/all_to_all | solution.py:563
  52.2 6.5 %fusion.3.delta_ref = f32[512,1024]{1,0:T(8,128)} fusion(bf16[512,2048]{1,0:T(8,128)(2,1)} %left_b_ref.5, bf16[1024,2048]{1,0:T(8,128)(2,1)} %param.17), kind=kOutput, calls=%fused_computation.19 | convolution fusion | flops 2147483648 | bytes 8388608 | tf_op jit(solution)/shard_map/td,fd->tf/dot_general | solution.py:593
  59.6 6.8 %gated_norm.1 = (bf16[512,1024]{1,0:T(8,128)(2,1)}, bf16[512,1024]{1,0:T(8,128)(2,1)}, bf16[512,1024]{1,0:T(8,128)(2,1)}, bf16[8,128,128]{2,1,0:T(8,128)(2,1)}) custom-call(f32[512,1024]{1,0:T(8,128)} %get-tuple-element.70.local_ref, bf16[512,1024]{1,0:T(8,128)(2,1)} %get-tuple-element.71.map_ref, f32[512,1024]{1,0:T(8,128)} %fusion.gate_ref, ...), custom_call_target="tpu_custom_call" | custom-call | tf_op jit(solution)/shard_map/gated_norm/pallas_call | solution.py:479
  66.5 6.2 %send_rows.2 = (bf16[1024,1024]{1,0:T(8,128)(2,1)}, bf16[1024,1024]{1,0:T(8,128)(2,1)}) custom-call(s32[1]{0:T(128)} %bitcast.9.place_ref, bf16[512,2048]{1,0:T(8,128)(2,1)} %left_b_ref.7, bf16[512,1024]{1,0:T(8,128)(2,1)} %get-tuple-element.84.a_ref.delta_gate_ref, bf16[512,2048]{1,0:T(8,128)(2,1)} %left_b_ref.5, bf16[512,1024]{1,0:T(8,128)(2,1)} %get-tuple-element.78.b_ref), custom_call_target="tpu_custom_call" | custom-call | tf_op jit(solution)/shard_map/send_rows/pallas_call | solution.py:747
  73.2 3.8 %all-to-all-start.2 = ((bf16[8,1,128,128]{3,2,1,0:T(8,128)(2,1)}), bf16[8,1,128,128]{3,2,1,0:T(8,128)(2,1)S(1)}, u32[]{:S(2)}, u32[]{:S(2)}) async-start(bf16[8,1,128,128]{3,2,1,0:T(8,128)(2,1)} %bitcast.38), calls=%async_computation.2 | async-start | bytes 524288 | tf_op jit(solution)/shard_map/all_to_all | solution.py:563
  77.0 5.9 %convolution_convert_fusion = bf16[512,2048]{1,0:T(8,128)(2,1)} fusion(bf16[512,1024]{1,0:T(8,128)(2,1)S(1)} %copy-done.2, bf16[1024,2048]{1,0:T(8,128)(2,1)} %param.17), kind=kOutput, calls=%fused_computation.3 | convolution fusion | flops 2148532224 | bytes 7340032 | tf_op jit(solution)/shard_map/tf,fd->td/dot_general | solution.py:593
  84.6 3.0 %chain_backward.1 = bf16[8,1,128,128]{3,2,1,0:T(8,128)(2,1)} custom-call(bf16[8,1,128,256]{3,2,1,0:T(8,128)(2,1)} %copy-done.1, bf16[8,1,128,128]{3,2,1,0:T(8,128)(2,1)} %copy-done.7), custom_call_target="tpu_custom_call" | custom-call | tf_op jit(solution)/shard_map/chain_backward/pallas_call | solution.py:584
  87.6 3.4 %all-to-all-start.3 = ((bf16[8,1,128,128]{3,2,1,0:T(8,128)(2,1)}), bf16[8,1,128,128]{3,2,1,0:T(8,128)(2,1)S(1)}, u32[]{:S(2)}, u32[]{:S(2)}) async-start(bf16[8,1,128,128]{3,2,1,0:T(8,128)(2,1)} %chain_backward.1), calls=%async_computation.4 | async-start | bytes 524288 | tf_op jit(solution)/shard_map/all_to_all | solution.py:563
  92.6 8.3 %keep_rows.2 = (bf16[256,1024]{1,0:T(8,128)(2,1)}, bf16[256,1024]{1,0:T(8,128)(2,1)}, bf16[256,1024]{1,0:T(8,128)(2,1)}, bf16[256,1024]{1,0:T(8,128)(2,1)}, bf16...) custom-call(s32[1]{0:T(128)} %bitcast.9.place_ref, ...), custom_call_target="tpu_custom_call" | custom-call | tf_op jit(solution)/shard_map/keep_rows/pallas_call | solution.py:768
  100.9 1.7 collective-permute-start.2
  102.6 1.5 collective-permute-start.3
  105.0 17.0 %backward_blocks.1 = (bf16[512,1152]{1,0:T(8,128)(2,1)}, bf16[512,1024]{1,0:T(8,128)(2,1)}) custom-call(f32[2,512,512]{2,1,0:T(8,128)} %get-tuple-element.67.query_key_ref, f32[512,1024]{1,0:T(8,128)} %get-tuple-element.68.value_ref, f32[512,16]{1,0:T(8,128)} %get-tuple-element.69.decay_beta_ref, f32[1,8]{1,0:T(1,128)} %bitcast.42, f32[1,8]{1,0:T(1,128)} %bitcast.44, ...), custom_call_target="tpu_custom_call" | custom-call | tf_op jit(solution)/shard_map/backward_blocks/pallas_call | solution.py:513
  122.1 6.7 %send_rows.3 = (bf16[1024,1024]{1,0:T(8,128)(2,1)}, bf16[1024,1152]{1,0:T(8,128)(2,1)}) custom-call(s32[1]{0:T(128)} %bitcast.9.place_ref, bf16[512,2048]{1,0:T(8,128)(2,1)} %left_b_ref.7, bf16[512,1024]{1,0:T(8,128)(2,1)} %get-tuple-element.100.delta_value_ref.a_ref, bf16[512,2048]{1,0:T(8,128)(2,1)} %left_b_ref.7, ...), custom_call_target="tpu_custom_call" | custom-call | tf_op jit(solution)/shard_map/send_rows/pallas_call | solution.py:747
  131.2 1.7 collective-permute-start.9
  133.9 1.5 collective-permute-start.8
  135.4 11.7 %input_gradient.1 = bf16[512,2048]{1,0:T(8,128)(2,1)} custom-call(bf16[512,1152]{1,0:T(8,128)(2,1)} %get-tuple-element.96.delta_query_key_ref.b_ref, bf16[512,1024]{1,0:T(8,128)(2,1)} %get-tuple-element.100.delta_value_ref.a_ref, bf16[512,1024]{1,0:T(8,128)(2,1)} %get-tuple-element.84.a_ref.delta_gate_ref, bf16[2,2048,512]{2,1,0:T(8,128)(2,1)} %query_key_weight_ref.3, ...), custom_call_target="tpu_custom_call" | custom-call | tf_op jit(solution)/shard_map/input_gradient/pallas_call | solution.py:678
  147.7 1.4 copy-done.4
  149.1 9.3 %keep_rows.3 = (bf16[256,1024]{1,0:T(8,128)(2,1)}, bf16[256,1024]{1,0:T(8,128)(2,1)}, bf16[256,1024]{1,0:T(8,128)(2,1)}, bf16[256,1024]{1,0:T(8,128)(2,1)}, bf16...) custom-call(s32[1]{0:T(128)} %bitcast.9.place_ref, ...), custom_call_target="tpu_custom_call" | custom-call | tf_op jit(solution)/shard_map/keep_rows/pallas_call | solution.py:768
  158.6 1.7 collective-permute-start.11
  160.3 1.8 collective-permute-start.13
  163.8 9.7 %collective-permute-done.14 = bf16[256,1024]{1,0:T(8,128)(2,1)S(1)} collective-permute-done((bf16[256,1024]{1,0:T(8,128)(2,1)}, bf16[256,1024]{1,0:T(8,128)(2,1)S(1)}, u32[]{:S(2)}, u32[]{:S(2)}) %collective-permute-start.14) | collective-permute-done | bytes 524320 | tf_op jit(solution)/shard_map/ppermute | solution.py:703
  174.5 1.6 collective-permute-start.15
  178.7 6.1 %collective-permute-done.13 = bf16[256,1024]{1,0:T(8,128)(2,1)} collective-permute-done((bf16[256,1024]{1,0:T(8,128)(2,1)}, bf16[256,1024]{1,0:T(8,128)(2,1)}, u32[]{:S(2)}, u32[]{:S(2)}) %collective-permute-start.13) | collective-permute-done | bytes 524320 | tf_op jit(solution)/shard_map/ppermute | solution.py:703
  184.8 12.1 %collective-permute-done.15 = bf16[256,1024]{1,0:T(8,128)(2,1)} collective-permute-done((bf16[256,1024]{1,0:T(8,128)(2,1)}, bf16[256,1024]{1,0:T(8,128)(2,1)}, u32[]{:S(2)}, u32[]{:S(2)}) %collective-permute-start.15) | collective-permute-done | bytes 524320 | tf_op jit(solution)/shard_map/ppermute | solution.py:703
  196.9 1.6 add_bitcast_fusion.2
  198.5 1.5 pad_maximum_fusion
  (88 shorter events, 19.4 us)
Async XLA Ops:
  17.1 18.2 %copy-start = (bf16[512,2048]{1,0:T(8,128)(2,1)S(1)}, bf16[512,2048]{1,0:T(8,128)(2,1)}, u32[]{:S(2)}) copy-start(bf16[512,2048]{1,0:T(8,128)(2,1)} %left_b_ref.7) | copy-start | bytes 6291460
  30.1 14.9 %all-to-all-start = ((bf16[8,1,128,256]{3,2,1,0:T(8,128)(2,1)}), bf16[8,1,128,256]{3,2,1,0:T(8,128)(2,1)S(1)}, u32[]{:S(2)}, u32[]{:S(2)}) async-start(bf16[8,1,128,256]{3,2,1,0:T(8,128)(2,1)} %bitcast.35), calls=%async_computation | async-start | bytes 1048576 | tf_op jit(solution)/shard_map/all_to_all | solution.py:563
  48.6 10.3 %all-to-all-start.1 = ((bf16[8,1,128,128]{3,2,1,0:T(8,128)(2,1)}), bf16[8,1,128,128]{3,2,1,0:T(8,128)(2,1)S(1)}, u32[]{:S(2)}, u32[]{:S(2)}) async-start(bf16[8,1,128,128]{3,2,1,0:T(8,128)(2,1)} %chain_forward.1), calls=%async_computation.1 | async-start | bytes 524288 | tf_op jit(solution)/shard_map/all_to_all | solution.py:563
  72.7 18.6 %collective-permute-start = (bf16[1024,1024]{1,0:T(8,128)(2,1)}, bf16[1024,1024]{1,0:T(8,128)(2,1)S(1)}, u32[]{:S(2)}, u32[]{:S(2)}) collective-permute-start(bf16[1024,1024]{1,0:T(8,128)(2,1)} %get-tuple-element.85), channel_id=1, source_target_pairs={{0,4},{4,0},{8,12},{12,8},{16,20},{20,16},{24,28},{28,24},{1,5},{5... | collective-permute-start | bytes 6291464 | tf_op jit(solution)/shard_map/ppermute | solution.py:703
  72.7 18.5 %collective-permute-start.1 = (bf16[1024,1024]{1,0:T(8,128)(2,1)}, bf16[1024,1024]{1,0:T(8,128)(2,1)}, u32[]{:S(2)}, u32[]{:S(2)}) collective-permute-start(bf16[1024,1024]{1,0:T(8,128)(2,1)} %get-tuple-element.86), channel_id=1, source_target_pairs={{0,4},{4,0},{8,12},{12,8},{16,20},{20,16},{24,28},{28,24},{1,5},{5... | collective-permute-start | bytes 6291464 | tf_op jit(solution)/shard_map/ppermute | solution.py:703
  73.2 10.7 %all-to-all-start.2 = ((bf16[8,1,128,128]{3,2,1,0:T(8,128)(2,1)}), bf16[8,1,128,128]{3,2,1,0:T(8,128)(2,1)S(1)}, u32[]{:S(2)}, u32[]{:S(2)}) async-start(bf16[8,1,128,128]{3,2,1,0:T(8,128)(2,1)} %bitcast.38), calls=%async_computation.2 | async-start | bytes 524288 | tf_op jit(solution)/shard_map/all_to_all | solution.py:563
  77.0 126.5 %reduce-scatter.3.cloned.1.call-start = ((), (), s32[]{:S(2)}) async-start(), calls=%async_computation.6 | async-start | bytes 2621440 | tf_op jit(solution)/shard_map/reduce_scatter | solution.py:817
  87.6 13.3 %all-to-all-start.3 = ((bf16[8,1,128,128]{3,2,1,0:T(8,128)(2,1)}), bf16[8,1,128,128]{3,2,1,0:T(8,128)(2,1)S(1)}, u32[]{:S(2)}, u32[]{:S(2)}) async-start(bf16[8,1,128,128]{3,2,1,0:T(8,128)(2,1)} %chain_backward.1), calls=%async_computation.4 | async-start | bytes 524288 | tf_op jit(solution)/shard_map/all_to_all | solution.py:563
  91.0 112.5 %reduce-scatter.5.cloned.1.call-start = ((), (), s32[]{:S(2)}) async-start(), calls=%async_computation.7 | async-start | bytes 2621440 | tf_op jit(solution)/shard_map/reduce_scatter | solution.py:817
  100.9 21.1 %collective-permute-start.2 = (bf16[256,1024]{1,0:T(8,128)(2,1)}, bf16[256,1024]{1,0:T(8,128)(2,1)S(1)}, u32[]{:S(2)}, u32[]{:S(2)}) collective-permute-start(bf16[256,1024]{1,0:T(8,128)(2,1)} %get-tuple-element.98), channel_id=1, source_target_pairs={{0,8},{4,12},{8,0},{12,4},{16,24},{20,28},{24,16},{28,20},{1,9},{5... | collective-permute-start | bytes 1572872 | tf_op jit(solution)/shard_map/ppermute | solution.py:703
  102.6 19.4 %collective-permute-start.3 = (bf16[256,1024]{1,0:T(8,128)(2,1)}, bf16[256,1024]{1,0:T(8,128)(2,1)S(1)}, u32[]{:S(2)}, u32[]{:S(2)}) collective-permute-start(bf16[256,1024]{1,0:T(8,128)(2,1)} %get-tuple-element.99), channel_id=1, source_target_pairs={{0,16},{4,20},{8,24},{12,28},{16,0},{20,4},{24,8},{28,12},{1,17},{... | collective-permute-start | bytes 1572872 | tf_op jit(solution)/shard_map/ppermute | solution.py:703
  104.1 24.6 %collective-permute-start.4 = (bf16[256,1024]{1,0:T(8,128)(2,1)}, bf16[256,1024]{1,0:T(8,128)(2,1)S(1)}, u32[]{:S(2)}, u32[]{:S(2)}) collective-permute-start(bf16[256,1024]{1,0:T(8,128)(2,1)} %get-tuple-element.103), channel_id=1, source_target_pairs={{0,8},{4,12},{8,0},{12,4},{16,24},{20,28},{24,16},{28,20},{1,9},{5... | collective-permute-start | bytes 1572872 | tf_op jit(solution)/shard_map/ppermute | solution.py:703
  104.7 24.1 %collective-permute-start.5 = (bf16[256,1024]{1,0:T(8,128)(2,1)}, bf16[256,1024]{1,0:T(8,128)(2,1)S(1)}, u32[]{:S(2)}, u32[]{:S(2)}) collective-permute-start(bf16[256,1024]{1,0:T(8,128)(2,1)} %get-tuple-element.104), channel_id=1, source_target_pairs={{0,16},{4,20},{8,24},{12,28},{16,0},{20,4},{24,8},{28,12},{1,17},{... | collective-permute-start | bytes 1572872 | tf_op jit(solution)/shard_map/ppermute | solution.py:703
  122.0 10.8 %copy-start.18 = (bf16[256,1024]{1,0:T(8,128)(2,1)S(1)}, bf16[256,1024]{1,0:T(8,128)(2,1)}, u32[]{:S(2)}) copy-start(bf16[256,1024]{1,0:T(8,128)(2,1)} %get-tuple-element.107) | copy-start | bytes 1572868
  129.7 17.9 %collective-permute-start.7 = (bf16[1024,1152]{1,0:T(8,128)(2,1)}, bf16[1024,1152]{1,0:T(8,128)(2,1)S(1)}, u32[]{:S(2)}, u32[]{:S(2)}) collective-permute-start(bf16[1024,1152]{1,0:T(8,128)(2,1)} %get-tuple-element.106), channel_id=1, source_target_pairs={{0,4},{4,0},{8,12},{12,8},{16,20},{20,16},{24,28},{28,24},{1,5},{5... | collective-permute-start | bytes 7077896 | tf_op jit(solution)/shard_map/ppermute | solution.py:703
  129.7 17.9 %collective-permute-start.6 = (bf16[1024,1024]{1,0:T(8,128)(2,1)}, bf16[1024,1024]{1,0:T(8,128)(2,1)}, u32[]{:S(2)}, u32[]{:S(2)}) collective-permute-start(bf16[1024,1024]{1,0:T(8,128)(2,1)} %get-tuple-element.105), channel_id=1, source_target_pairs={{0,4},{4,0},{8,12},{12,8},{16,20},{20,16},{24,28},{28,24},{1,5},{5... | collective-permute-start | bytes 6291464 | tf_op jit(solution)/shard_map/ppermute | solution.py:703
  131.2 15.9 %collective-permute-start.9 = (bf16[256,1024]{1,0:T(8,128)(2,1)}, bf16[256,1024]{1,0:T(8,128)(2,1)S(1)}, u32[]{:S(2)}, u32[]{:S(2)}) collective-permute-start(bf16[256,1024]{1,0:T(8,128)(2,1)} %add_convert_fusion.2), channel_id=1, source_target_pairs={{0,8},{4,12},{8,0},{12,4},{16,24},{20,28},{24,16},{28,20},{1,9},{5... | collective-permute-start | bytes 1572872 | tf_op jit(solution)/shard_map/ppermute | solution.py:703
  133.9 13.8 %collective-permute-start.8 = (bf16[256,1024]{1,0:T(8,128)(2,1)}, bf16[256,1024]{1,0:T(8,128)(2,1)S(1)}, u32[]{:S(2)}, u32[]{:S(2)}) collective-permute-start(bf16[256,1024]{1,0:T(8,128)(2,1)} %add_convert_fusion.3), channel_id=1, source_target_pairs={{0,16},{4,20},{8,24},{12,28},{16,0},{20,4},{24,8},{28,12},{1,17},{... | collective-permute-start | bytes 1572872 | tf_op jit(solution)/shard_map/ppermute | solution.py:703
  147.1 11.2 %copy-start.20 = (bf16[256,1024]{1,0:T(8,128)(2,1)}, bf16[256,1024]{1,0:T(8,128)(2,1)S(1)}, u32[]{:S(2)}) copy-start(bf16[256,1024]{1,0:T(8,128)(2,1)S(1)} %collective-permute-done.9) | copy-start | bytes 1572868
  149.1 13.4 %copy-start.13 = (bf16[256,1024]{1,0:T(8,128)(2,1)S(1)}, bf16[256,1024]{1,0:T(8,128)(2,1)}, u32[]{:S(2)}) copy-start(bf16[256,1024]{1,0:T(8,128)(2,1)} %get-tuple-element.125) | copy-start | bytes 1572868
  149.1 13.4 %copy-start.15 = (bf16[256,1024]{1,0:T(8,128)(2,1)S(1)}, bf16[256,1024]{1,0:T(8,128)(2,1)}, u32[]{:S(2)}) copy-start(bf16[256,1024]{1,0:T(8,128)(2,1)} %copy-done.14) | copy-start | bytes 1572868
  158.3 15.2 %copy-start.21 = (bf16[256,1024]{1,0:T(8,128)(2,1)S(1)}, bf16[256,1024]{1,0:T(8,128)(2,1)}, u32[]{:S(2)}) copy-start(bf16[256,1024]{1,0:T(8,128)(2,1)} %get-tuple-element.120) | copy-start | bytes 1572868
  158.3 15.1 %collective-permute-start.14 = (bf16[256,1024]{1,0:T(8,128)(2,1)}, bf16[256,1024]{1,0:T(8,128)(2,1)S(1)}, u32[]{:S(2)}, u32[]{:S(2)}) collective-permute-start(bf16[256,1024]{1,0:T(8,128)(2,1)} %get-tuple-element.121), channel_id=1, source_target_pairs={{0,8},{4,12},{8,0},{12,4},{16,24},{20,28},{24,16},{28,20},{1,9},{5... | collective-permute-start | bytes 1572872 | tf_op jit(solution)/shard_map/ppermute | solution.py:703
  158.6 17.5 %collective-permute-start.11 = (bf16[256,1152]{1,0:T(8,128)(2,1)}, bf16[256,1152]{1,0:T(8,128)(2,1)S(1)}, u32[]{:S(2)}, u32[]{:S(2)}) collective-permute-start(bf16[256,1152]{1,0:T(8,128)(2,1)} %get-tuple-element.117), channel_id=1, source_target_pairs={{0,16},{4,20},{8,24},{12,28},{16,0},{20,4},{24,8},{28,12},{1,17},{... | collective-permute-start | bytes 1769480 | tf_op jit(solution)/shard_map/ppermute | solution.py:703
  160.3 24.5 %collective-permute-start.13 = (bf16[256,1024]{1,0:T(8,128)(2,1)}, bf16[256,1024]{1,0:T(8,128)(2,1)}, u32[]{:S(2)}, u32[]{:S(2)}) collective-permute-start(bf16[256,1024]{1,0:T(8,128)(2,1)} %get-tuple-element.119), channel_id=1, source_target_pairs={{0,8},{4,12},{8,0},{12,4},{16,24},{20,28},{24,16},{28,20},{1,9},{5... | collective-permute-start | bytes 1572872 | tf_op jit(solution)/shard_map/ppermute | solution.py:703
  162.1 14.0 %copy-start.8 = (bf16[256,1152]{1,0:T(8,128)(2,1)S(1)}, bf16[256,1152]{1,0:T(8,128)(2,1)}, u32[]{:S(2)}) copy-start(bf16[256,1152]{1,0:T(8,128)(2,1)} %get-tuple-element.116) | copy-start | bytes 1769476
  162.1 38.0 %collective-permute-start.10 = (bf16[256,1152]{1,0:T(8,128)(2,1)}, bf16[256,1152]{1,0:T(8,128)(2,1)S(1)}, u32[]{:S(2)}, u32[]{:S(2)}) collective-permute-start(bf16[256,1152]{1,0:T(8,128)(2,1)} %get-tuple-element.115), channel_id=1, source_target_pairs={{0,16},{4,20},{8,24},{12,28},{16,0},{20,4},{24,8},{28,12},{1,17},{... | collective-permute-start | bytes 1769480 | tf_op jit(solution)/shard_map/ppermute | solution.py:703
  163.8 13.4 %copy-start.10 = (bf16[256,1024]{1,0:T(8,128)(2,1)S(1)}, bf16[256,1024]{1,0:T(8,128)(2,1)}, u32[]{:S(2)}) copy-start(bf16[256,1024]{1,0:T(8,128)(2,1)} %get-tuple-element.122) | copy-start | bytes 1572868
  163.8 13.3 %copy-start.12 = (bf16[256,1024]{1,0:T(8,128)(2,1)S(1)}, bf16[256,1024]{1,0:T(8,128)(2,1)}, u32[]{:S(2)}) copy-start(bf16[256,1024]{1,0:T(8,128)(2,1)} %copy-done.11) | copy-start | bytes 1572868
  163.8 13.3 %copy-start.17 = (bf16[256,1024]{1,0:T(8,128)(2,1)S(1)}, bf16[256,1024]{1,0:T(8,128)(2,1)}, u32[]{:S(2)}) copy-start(bf16[256,1024]{1,0:T(8,128)(2,1)} %copy-done.16) | copy-start | bytes 1572868
  174.5 22.4 %collective-permute-start.15 = (bf16[256,1024]{1,0:T(8,128)(2,1)}, bf16[256,1024]{1,0:T(8,128)(2,1)}, u32[]{:S(2)}, u32[]{:S(2)}) collective-permute-start(bf16[256,1024]{1,0:T(8,128)(2,1)} %add_convert_fusion.1), channel_id=1, source_target_pairs={{0,16},{4,20},{8,24},{12,28},{16,0},{20,4},{24,8},{28,12},{1,17},{... | collective-permute-start | bytes 1572872 | tf_op jit(solution)/shard_map/ppermute | solution.py:703
  176.2 23.8 %collective-permute-start.12 = (bf16[256,1152]{1,0:T(8,128)(2,1)S(1)}, bf16[256,1152]{1,0:T(8,128)(2,1)}, u32[]{:S(2)}, u32[]{:S(2)}) collective-permute-start(bf16[256,1152]{1,0:T(8,128)(2,1)S(1)} %add_convert_fusion), channel_id=1, source_target_pairs={{0,8},{4,12},{8,0},{12,4},{16,24},{20,28},{24,16},{28,20},{1,9},{5... | collective-permute-start | bytes 1769480 | tf_op jit(solution)/shard_map/ppermute | solution.py:703
  (12 other events, 41.8 us)
Sparse Core Ops, SparseCore 0:
  84.1 44.5 reduce-scatter.2
  147.8 44.0 reduce-scatter.4

commit v7 on v6

--- a/solution.py
+++ b/solution.py
@@ -206,8 +206,8 @@
     for h in range(heads):
         cols = slice(h * DV, (h + 1) * DV)
         out = outs[h]
-        gate = gate_ref[:, cols]
-        delta = delta_ref[:, cols]
+        gate = gate_ref[:, cols].astype(F32)
+        delta = delta_ref[:, cols].astype(F32)
         scale = lax.rsqrt(row_sum(out * out) * (1.0 / DV) + EPS)
         normed = out * scale
         share = sigmoid(gate)
@@ -806,11 +806,54 @@
     return exchange(summed(a[2], arrived[0]), 4), exchange(summed(b[1], arrived[1]), 2)
 
 
-def halving_sum(pieces, arrived, last):
-    def total(own, near, far):
-        return own.astype(F32) + near.astype(F32) + far.astype(F32)
-
-    return total(pieces[3], arrived[0], last[0]), total(pieces[7], arrived[1], last[1])
+def halving_terms(pieces, stay, last):
+    return (pieces[3], stay[0], last[0]), (pieces[7], stay[1], last[1])
+
+
+def finish_kernel(key_width, heads, *refs):
+    def total(*terms):
+        return sum(term[...].astype(F32) for term in terms)
+
+    query_key_ref, value_gate_ref, decay_beta_ref = refs[7:]
+    value_gate_ref[0] = total(*refs[0:2])
+    value_gate_ref[1] = total(*refs[2:5])
+    packed = total(*refs[5:7])
+    query_key_ref[0] = packed[:, :key_width]
+    query_key_ref[1] = packed[:, key_width : 2 * key_width]
+    small = packed[:, 2 * key_width :].T
+    decay_beta_ref[0] = small[:heads]
+    decay_beta_ref[1] = small[heads : 2 * heads]
+
+
+def run_finish(key_width, heads, value, gate, packed):
+    rows, width = value[0].shape
+    step = 128
+
+    def block(array):
+        return pl.BlockSpec((step, array.shape[1]), lambda i: (i, 0))
+
+    def pair(size):
+        return pl.BlockSpec((2, step, size), lambda i: (0, i, 0))
+
+    terms = [*value, *gate, *packed]
+    return pl.pallas_call(
+        functools.partial(finish_kernel, key_width, heads),
+        grid=(rows // step,),
+        in_specs=[block(term) for term in terms],
+        out_specs=[
+            pair(key_width),
+            pair(width),
+            pl.BlockSpec((2, heads, step), lambda i: (0, 0, i)),
+        ],
+        out_shape=[
+            jax.ShapeDtypeStruct((2, rows, key_width), F32),
+            jax.ShapeDtypeStruct((2, rows, width), F32),
+            jax.ShapeDtypeStruct((2, heads, rows), F32),
+        ],
+        compiler_params=PARAMS,
+        interpret=INTERPRET,
+        name="finish",
+    )(*terms)
 
 
 def scatter(partial, axis, dimension):
@@ -843,10 +886,10 @@
     )
 
     held = swap(spread_totals(totals))
-    gate = product("td,df->tf", inputs, value_gate_weight[1])
+    gate = product("td,df->tf", inputs, value_gate_weight[1]).astype(BF16)
     held, gate = together(held, gate)
     states = swap(run_chain_forward(held))
-    delta_hidden = product("td,fd->tf", grad_mixed, out_weight)
+    delta_hidden = product("td,fd->tf", grad_mixed, out_weight).astype(BF16)
     states, delta_hidden = together(states, delta_hidden)
     state_in = gather_parts(states, heads)
     hidden, delta_gate, delta_out, delta_state = run_output(
@@ -904,23 +947,25 @@
         late_arrived = halving_cross(late_pieces)
         late_stay = halving_stay(late_pieces)
         late_last = halving_last(late_pieces, late_arrived)
-        grad_gate, grad_out = halving_sum(early_pieces, early_stay, early_last)
-        grad_out = grad_out.T
-        grad_value, packed = halving_sum(late_pieces, late_stay, late_last)
+        gate_terms, out_terms = halving_terms(early_pieces, early_stay, early_last)
+        value_terms, packed_terms = halving_terms(late_pieces, late_stay, late_last)
+        value_terms = (value_terms[0].astype(F32) + value_terms[1].astype(F32), value_terms[2])
+        packed_terms = (packed_terms[0].astype(F32) + packed_terms[1].astype(F32), packed_terms[2])
+        grad_out = sum(term.astype(F32) for term in out_terms).T
+        grad_query_key, grad_value_gate, grad_decay_beta = run_finish(
+            key_width, heads, value_terms, gate_terms, packed_terms
+        )
+        grad_decay_beta = jnp.swapaxes(grad_decay_beta, 1, 2)
     else:
         grad_gate = scatter(product("td,tf->df", inputs, delta_gate), "ctx", 0).astype(F32)
         grad_out = scatter(product("tf,td->fd", hidden, grad_mixed), "ctx", 1).astype(F32)
         grad_value = scatter(product("td,tf->df", inputs, delta_value), "ctx", 0).astype(F32)
         packed = scatter(product("td,tf->df", inputs, delta_query_key), "ctx", 0).astype(F32)
-    rest = packed[:, 2 * key_width :]
-    return (
-        mixed,
-        grad_inputs,
-        jnp.stack([packed[:, :key_width], packed[:, key_width : 2 * key_width]]),
-        jnp.stack([grad_value, grad_gate]),
-        jnp.stack([rest[:, :heads], rest[:, heads : 2 * heads]]),
-        grad_out,
-    )
+        rest = packed[:, 2 * key_width :]
+        grad_query_key = jnp.stack([packed[:, :key_width], packed[:, key_width : 2 * key_width]])
+        grad_value_gate = jnp.stack([grad_value, grad_gate])
+        grad_decay_beta = jnp.stack([rest[:, :heads], rest[:, heads : 2 * heads]])
+    return (mixed, grad_inputs, grad_query_key, grad_value_gate, grad_decay_beta, grad_out)
 
 
 def solution(mesh):

time: 211 us -> 209 us (level)
  other arithmetic: 10.8 us -> 7.05 us
  Pallas kernels: 94.7 us -> 98.2 us
    another operation x5 -> x0, other arithmetic: 5.06 us -> none  [the longest x3 3.39 us: body(): jnp.stack([grad_value, grad_gate])]
    pallas_call x0 -> x1, Pallas kernels: none -> 3.81 us  [run_finish(): pl.pallas_call(functools.partial(finish_kernel, key_width, heads), grid=(...]
    unnamed x45 -> x43, local copies, waits for them, and re-layouts: 7.17 us -> 7.91 us
  transfers between devices with their start and end apart: 22 -> 22, of which waited for: 7 -> 8; matrix products, arithmetic and copies ran while one was open for 15% -> 12% of each run, Pallas kernels for 27% -> 29%
where the time goes in v7:
time: 209 us; the launch traced here: 208 us
  Pallas kernels  98.2 us (47%)
  waiting for transfers between devices  32.1 us (15%)
  starting transfers between devices  30.5 us (15%)
  matrix products  17.6 us (8%)
  between operations  14.3 us (7%)
  local copies, waits for them, and re-layouts  7.91 us (4%)
  other arithmetic  7.05 us (3%)
    ppermute x16, waiting for transfers between devices, exchange(): return lax.ppermute(array, 'ctx', [(i, i ^ distance) for i in devices])  26.4 us
    dot_general x3, matrix products, product(): return jnp.einsum(spec, a, b, preferred_element_type=F32)  17.6 us
    pallas_call x2, Pallas kernels, halving_keep(): pl.pallas_call(keep_kernel, grid_spec=pltpu.PrefetchScalarGridSpec(num_sc...  17.5 us
    pallas_call x1, Pallas kernels, run_backward(): pl.pallas_call(backward_kernel, grid=(chunks // spans,), in_specs=[pl.Blo...  17 us
    all_to_all x4, starting transfers between devices, swap(): return lax.all_to_all(parts, 'ctx', split_axis=0, concat_axis=0, tiled=True)  15.7 us
    ppermute x16, starting transfers between devices, exchange(): return lax.ppermute(array, 'ctx', [(i, i ^ distance) for i in devices])  14.6 us
    pallas_call x2, Pallas kernels, halving_start(): pl.pallas_call(send_kernel, grid_spec=pltpu.PrefetchScalarGridSpec(num_sc...  13 us
    pallas_call x1, Pallas kernels, run_forward(): pl.pallas_call(forward_kernel, grid=(chunks // spans,), in_specs=[pl.Bloc...  13 us
  transfers between devices with their start and end apart: 22, of which 8 were waited for; matrix products, arithmetic and copies ran while one was open for 12% of the time, Pallas kernels for 29%

profile of v7, /device:TPU:0, one launch (start us, length us, event | category | flops | bytes accessed | tf_op | source)
XLA Modules:
  0.0 207.8 jit_solution(12903376763976283602)
XLA Ops:
  7.2 9.9 %projection.1 = (f32[2,512,512]{2,1,0:T(8,128)}, f32[512,1024]{1,0:T(8,128)}, f32[512,16]{1,0:T(8,128)}) custom-call(bf16[512,2048]{1,0:T(8,128)(2,1)} %left_b_ref.7, bf16[2,2048,512]{2,1,0:T(8,128)(2,1)} %query_key_weight_ref.3, bf16[2,2048,1024]{2,1,0:T(8,128)(2,1)} %value_gate_weight_ref.1, bf16[2,8,2048]{2,1,0:T(8,128)(2,1)} %bitcast.27), custom_call_target="tpu_custom_call" | custom-call | tf_op jit(solution)/shard_map/projection/pallas_call | solution.py:624
  17.1 13.0 %forward_blocks.1 = (bf16[4,8,128,128]{3,2,1,0:T(8,128)(2,1)}, bf16[4,8,128,256]{3,2,1,0:T(8,128)(2,1)}, bf16[512,1024]{1,0:T(8,128)(2,1)}, f32[512,1024]{1,0:T(8,128)}, bf16[8,128,256]{2,1,0:T(8,128)(2,1)}) custom-call(f32[2,512,512]{2,1,0:T(8,128)} %get-tuple-element.70.query_key_ref, f32[512,1024]{1,0:T(8,128)} %get-tuple-element.71.value_ref, ...), custom_call_target="tpu_custom_call" | custom-call | tf_op jit(solution)/shard_map/forward_blocks/pallas_call | solution.py:442
  30.1 5.2 %all-to-all-start = ((bf16[8,1,128,256]{3,2,1,0:T(8,128)(2,1)}), bf16[8,1,128,256]{3,2,1,0:T(8,128)(2,1)S(1)}, u32[]{:S(2)}, u32[]{:S(2)}) async-start(bf16[8,1,128,256]{3,2,1,0:T(8,128)(2,1)} %bitcast.26), calls=%async_computation | async-start | bytes 1048576 | tf_op jit(solution)/shard_map/all_to_all | solution.py:563
  35.3 5.5 %fusion.3.gate_ref = bf16[512,1024]{1,0:T(8,128)(2,1)} fusion(bf16[512,2048]{1,0:T(8,128)(2,1)S(1)} %copy-done, bf16[2,2048,1024]{2,1,0:T(8,128)(2,1)} %value_gate_weight_ref.1), kind=kOutput, calls=%fused_computation.4 | convolution fusion | flops 2148007936 | bytes 7340032 | tf_op jit(solution)/shard_map/td,df->tf/dot_general | solution.py:593
  40.8 4.2 %all-to-all-done.totals_ref = bf16[8,1,128,256]{3,2,1,0:T(8,128)(2,1)S(1)} async-done(((bf16[8,1,128,256]{3,2,1,0:T(8,128)(2,1)}), bf16[8,1,128,256]{3,2,1,0:T(8,128)(2,1)S(1)}, u32[]{:S(2)}, u32[]{:S(2)}) %all-to-all-start) | async-done | bytes 524320 | tf_op jit(solution)/shard_map/all_to_all | solution.py:563
  45.8 2.8 %chain_forward.1 = bf16[8,1,128,128]{3,2,1,0:T(8,128)(2,1)} custom-call(bf16[8,1,128,256]{3,2,1,0:T(8,128)(2,1)} %copy-done.1), custom_call_target="tpu_custom_call" | custom-call | tf_op jit(solution)/shard_map/chain_forward/pallas_call | solution.py:575
  48.6 3.6 %all-to-all-start.1 = ((bf16[8,1,128,128]{3,2,1,0:T(8,128)(2,1)}), bf16[8,1,128,128]{3,2,1,0:T(8,128)(2,1)S(1)}, u32[]{:S(2)}, u32[]{:S(2)}) async-start(bf16[8,1,128,128]{3,2,1,0:T(8,128)(2,1)} %chain_forward.1), calls=%async_computation.1 | async-start | bytes 524288 | tf_op jit(solution)/shard_map/all_to_all | solution.py:563
  52.2 6.2 %convolution_convert_fusion.1.delta_ref = bf16[512,1024]{1,0:T(8,128)(2,1)} fusion(bf16[512,2048]{1,0:T(8,128)(2,1)} %left_b_ref.5, bf16[1024,2048]{1,0:T(8,128)(2,1)} %param.17), kind=kOutput, calls=%fused_computation.5 | convolution fusion | flops 2148007936 | bytes 7340032 | tf_op jit(solution)/shard_map/td,fd->tf/dot_general | solution.py:593
  59.6 6.5 %gated_norm.1 = (bf16[512,1024]{1,0:T(8,128)(2,1)}, bf16[512,1024]{1,0:T(8,128)(2,1)}, bf16[512,1024]{1,0:T(8,128)(2,1)}, bf16[8,128,128]{2,1,0:T(8,128)(2,1)}) custom-call(f32[512,1024]{1,0:T(8,128)} %get-tuple-element.73.local_ref, bf16[512,1024]{1,0:T(8,128)(2,1)} %get-tuple-element.74.map_ref, bf16[512,1024]{1,0:T(8,128)(2,1)} %fusion.3.gate_ref, ...), custom_call_target="tpu_custom_call" | custom-call | tf_op jit(solution)/shard_map/gated_norm/pallas_call | solution.py:479
  66.1 6.3 %send_rows.2 = (bf16[1024,1024]{1,0:T(8,128)(2,1)}, bf16[1024,1024]{1,0:T(8,128)(2,1)}) custom-call(s32[1]{0:T(128)} %bitcast.9.place_ref, bf16[512,2048]{1,0:T(8,128)(2,1)} %left_b_ref.7, bf16[512,1024]{1,0:T(8,128)(2,1)} %get-tuple-element.87.a_ref.delta_gate_ref, bf16[512,2048]{1,0:T(8,128)(2,1)} %left_b_ref.5, bf16[512,1024]{1,0:T(8,128)(2,1)} %get-tuple-element.81.b_ref), custom_call_target="tpu_custom_call" | custom-call | tf_op jit(solution)/shard_map/send_rows/pallas_call | solution.py:747
  72.9 3.5 %all-to-all-start.2 = ((bf16[8,1,128,128]{3,2,1,0:T(8,128)(2,1)}), bf16[8,1,128,128]{3,2,1,0:T(8,128)(2,1)S(1)}, u32[]{:S(2)}, u32[]{:S(2)}) async-start(bf16[8,1,128,128]{3,2,1,0:T(8,128)(2,1)} %bitcast.29), calls=%async_computation.2 | async-start | bytes 524288 | tf_op jit(solution)/shard_map/all_to_all | solution.py:563
  76.5 5.9 %convolution_convert_fusion = bf16[512,2048]{1,0:T(8,128)(2,1)} fusion(bf16[512,1024]{1,0:T(8,128)(2,1)S(1)} %copy-done.2, bf16[1024,2048]{1,0:T(8,128)(2,1)} %param.17), kind=kOutput, calls=%fused_computation.3 | convolution fusion | flops 2148532224 | bytes 7340032 | tf_op jit(solution)/shard_map/tf,fd->td/dot_general | solution.py:593
  84.0 2.9 %chain_backward.1 = bf16[8,1,128,128]{3,2,1,0:T(8,128)(2,1)} custom-call(bf16[8,1,128,256]{3,2,1,0:T(8,128)(2,1)} %copy-done.1, bf16[8,1,128,128]{3,2,1,0:T(8,128)(2,1)} %copy-done.7), custom_call_target="tpu_custom_call" | custom-call | tf_op jit(solution)/shard_map/chain_backward/pallas_call | solution.py:584
  87.0 3.4 %all-to-all-start.3 = ((bf16[8,1,128,128]{3,2,1,0:T(8,128)(2,1)}), bf16[8,1,128,128]{3,2,1,0:T(8,128)(2,1)S(1)}, u32[]{:S(2)}, u32[]{:S(2)}) async-start(bf16[8,1,128,128]{3,2,1,0:T(8,128)(2,1)} %chain_backward.1), calls=%async_computation.4 | async-start | bytes 524288 | tf_op jit(solution)/shard_map/all_to_all | solution.py:563
  92.0 8.3 %keep_rows.2 = (bf16[256,1024]{1,0:T(8,128)(2,1)}, bf16[256,1024]{1,0:T(8,128)(2,1)}, bf16[256,1024]{1,0:T(8,128)(2,1)}, bf16[256,1024]{1,0:T(8,128)(2,1)}, bf16...) custom-call(s32[1]{0:T(128)} %bitcast.9.place_ref, ...), custom_call_target="tpu_custom_call" | custom-call | tf_op jit(solution)/shard_map/keep_rows/pallas_call | solution.py:768
  100.3 1.7 collective-permute-start.2
  102.1 1.5 collective-permute-start.3
  104.5 17.0 %backward_blocks.1 = (bf16[512,1152]{1,0:T(8,128)(2,1)}, bf16[512,1024]{1,0:T(8,128)(2,1)}) custom-call(f32[2,512,512]{2,1,0:T(8,128)} %get-tuple-element.70.query_key_ref, f32[512,1024]{1,0:T(8,128)} %get-tuple-element.71.value_ref, f32[512,16]{1,0:T(8,128)} %get-tuple-element.72.decay_beta_ref, f32[1,8]{1,0:T(1,128)} %bitcast.33, f32[1,8]{1,0:T(1,128)} %bitcast.35, ...), custom_call_target="tpu_custom_call" | custom-call | tf_op jit(solution)/shard_map/backward_blocks/pallas_call | solution.py:513
  121.5 6.7 %send_rows.3 = (bf16[1024,1024]{1,0:T(8,128)(2,1)}, bf16[1024,1152]{1,0:T(8,128)(2,1)}) custom-call(s32[1]{0:T(128)} %bitcast.9.place_ref, bf16[512,2048]{1,0:T(8,128)(2,1)} %left_b_ref.7, bf16[512,1024]{1,0:T(8,128)(2,1)} %get-tuple-element.103.delta_value_ref.a_ref, bf16[512,2048]{1,0:T(8,128)(2,1)} %left_b_ref.7, ...), custom_call_target="tpu_custom_call" | custom-call | tf_op jit(solution)/shard_map/send_rows/pallas_call | solution.py:747
  129.8 1.6 collective-permute-start.9
  132.5 1.5 collective-permute-start.8
  133.9 11.7 %input_gradient.1 = bf16[512,2048]{1,0:T(8,128)(2,1)} custom-call(bf16[512,1152]{1,0:T(8,128)(2,1)} %get-tuple-element.99.delta_query_key_ref.b_ref, bf16[512,1024]{1,0:T(8,128)(2,1)} %get-tuple-element.103.delta_value_ref.a_ref, bf16[512,1024]{1,0:T(8,128)(2,1)} %get-tuple-element.87.a_ref.delta_gate_ref, bf16[2,2048,512]{2,1,0:T(8,128)(2,1)} %query_key_weight_ref.3, ...), custom_call_target="tpu_custom_call" | custom-call | tf_op jit(solution)/shard_map/input_gradient/pallas_call | solution.py:678
  146.3 1.4 copy-done.4
  147.7 9.2 %keep_rows.3 = (bf16[256,1024]{1,0:T(8,128)(2,1)}, bf16[256,1024]{1,0:T(8,128)(2,1)}, bf16[256,1024]{1,0:T(8,128)(2,1)}, bf16[256,1024]{1,0:T(8,128)(2,1)}, bf16...) custom-call(s32[1]{0:T(128)} %bitcast.9.place_ref, ...), custom_call_target="tpu_custom_call" | custom-call | tf_op jit(solution)/shard_map/keep_rows/pallas_call | solution.py:768
  157.2 1.7 collective-permute-start.14
  161.5 1.8 collective-permute-start.10
  163.7 8.5 %collective-permute-done.11 = bf16[256,1024]{1,0:T(8,128)(2,1)} collective-permute-done((bf16[256,1024]{1,0:T(8,128)(2,1)}, bf16[256,1024]{1,0:T(8,128)(2,1)}, u32[]{:S(2)}, u32[]{:S(2)}) %collective-permute-start.11) | collective-permute-done | bytes 524320 | tf_op jit(solution)/shard_map/ppermute | solution.py:703
  173.4 1.7 collective-permute-start.12
  175.7 7.6 %collective-permute-done.10 = bf16[256,1024]{1,0:T(8,128)(2,1)S(1)} collective-permute-done((bf16[256,1024]{1,0:T(8,128)(2,1)}, bf16[256,1024]{1,0:T(8,128)(2,1)S(1)}, u32[]{:S(2)}, u32[]{:S(2)}) %collective-permute-start.10) | collective-permute-done | bytes 524320 | tf_op jit(solution)/shard_map/ppermute | solution.py:703
  184.4 1.9 collective-permute-done.13
  187.6 7.8 %collective-permute-done.12.refs_1_ = bf16[256,1024]{1,0:T(8,128)(2,1)S(1)} collective-permute-done((bf16[256,1024]{1,0:T(8,128)(2,1)S(1)}, bf16[256,1024]{1,0:T(8,128)(2,1)S(1)}, u32[]{:S(2)}, u32[]{:S(2)}) %collective-permute-start.12) | collective-permute-done | bytes 524320 | tf_op jit(solution)/shard_map/ppermute | solution.py:703
  197.1 3.8 %finish.1 = (f32[2,256,512]{2,1,0:T(8,128)}, f32[2,256,1024]{2,1,0:T(8,128)}, f32[2,8,256]{2,1,0:T(8,128)}) custom-call(f32[256,1024]{1,0:T(8,128)} %convert_add_fusion.1.refs_0_, bf16[256,1024]{1,0:T(8,128)(2,1)} %copy-done.18, bf16[256,1024]{1,0:T(8,128)(2,1)} %get-tuple-element.121.refs_2_, bf16[256,1024]{1,0:T(8,128)(2,1)} %copy-done.11, ...), custom_call_target="tpu_custom_call" | custom-call | tf_op jit(solution)/shard_map/finish/pallas_call | solution.py:839
  (79 shorter events, 19.2 us)
Async XLA Ops:
  17.1 18.2 %copy-start = (bf16[512,2048]{1,0:T(8,128)(2,1)S(1)}, bf16[512,2048]{1,0:T(8,128)(2,1)}, u32[]{:S(2)}) copy-start(bf16[512,2048]{1,0:T(8,128)(2,1)} %left_b_ref.7) | copy-start | bytes 6291460
  30.1 14.9 %all-to-all-start = ((bf16[8,1,128,256]{3,2,1,0:T(8,128)(2,1)}), bf16[8,1,128,256]{3,2,1,0:T(8,128)(2,1)S(1)}, u32[]{:S(2)}, u32[]{:S(2)}) async-start(bf16[8,1,128,256]{3,2,1,0:T(8,128)(2,1)} %bitcast.26), calls=%async_computation | async-start | bytes 1048576 | tf_op jit(solution)/shard_map/all_to_all | solution.py:563
  48.6 10.3 %all-to-all-start.1 = ((bf16[8,1,128,128]{3,2,1,0:T(8,128)(2,1)}), bf16[8,1,128,128]{3,2,1,0:T(8,128)(2,1)S(1)}, u32[]{:S(2)}, u32[]{:S(2)}) async-start(bf16[8,1,128,128]{3,2,1,0:T(8,128)(2,1)} %chain_forward.1), calls=%async_computation.1 | async-start | bytes 524288 | tf_op jit(solution)/shard_map/all_to_all | solution.py:563
  66.1 10.3 %copy-start.2 = (bf16[512,1024]{1,0:T(8,128)(2,1)S(1)}, bf16[512,1024]{1,0:T(8,128)(2,1)}, u32[]{:S(2)}) copy-start(bf16[512,1024]{1,0:T(8,128)(2,1)} %get-tuple-element.81.b_ref) | copy-start | bytes 3145732
  72.4 18.3 %collective-permute-start = (bf16[1024,1024]{1,0:T(8,128)(2,1)}, bf16[1024,1024]{1,0:T(8,128)(2,1)S(1)}, u32[]{:S(2)}, u32[]{:S(2)}) collective-permute-start(bf16[1024,1024]{1,0:T(8,128)(2,1)} %get-tuple-element.88), channel_id=1, source_target_pairs={{0,4},{4,0},{8,12},{12,8},{16,20},{20,16},{24,28},{28,24},{1,5},{5... | collective-permute-start | bytes 6291464 | tf_op jit(solution)/shard_map/ppermute | solution.py:703
  72.4 18.3 %collective-permute-start.1 = (bf16[1024,1024]{1,0:T(8,128)(2,1)}, bf16[1024,1024]{1,0:T(8,128)(2,1)}, u32[]{:S(2)}, u32[]{:S(2)}) collective-permute-start(bf16[1024,1024]{1,0:T(8,128)(2,1)} %get-tuple-element.89), channel_id=1, source_target_pairs={{0,4},{4,0},{8,12},{12,8},{16,20},{20,16},{24,28},{28,24},{1,5},{5... | collective-permute-start | bytes 6291464 | tf_op jit(solution)/shard_map/ppermute | solution.py:703
  72.9 10.4 %all-to-all-start.2 = ((bf16[8,1,128,128]{3,2,1,0:T(8,128)(2,1)}), bf16[8,1,128,128]{3,2,1,0:T(8,128)(2,1)S(1)}, u32[]{:S(2)}, u32[]{:S(2)}) async-start(bf16[8,1,128,128]{3,2,1,0:T(8,128)(2,1)} %bitcast.29), calls=%async_computation.2 | async-start | bytes 524288 | tf_op jit(solution)/shard_map/all_to_all | solution.py:563
  76.4 124.5 %reduce-scatter.3.cloned.1.call-start = ((), (), s32[]{:S(2)}) async-start(), calls=%async_computation.6 | async-start | bytes 2621440 | tf_op jit(solution)/shard_map/reduce_scatter | solution.py:860
  87.0 13.4 %all-to-all-start.3 = ((bf16[8,1,128,128]{3,2,1,0:T(8,128)(2,1)}), bf16[8,1,128,128]{3,2,1,0:T(8,128)(2,1)S(1)}, u32[]{:S(2)}, u32[]{:S(2)}) async-start(bf16[8,1,128,128]{3,2,1,0:T(8,128)(2,1)} %chain_backward.1), calls=%async_computation.4 | async-start | bytes 524288 | tf_op jit(solution)/shard_map/all_to_all | solution.py:563
  90.4 110.5 %reduce-scatter.5.cloned.1.call-start = ((), (), s32[]{:S(2)}) async-start(), calls=%async_computation.7 | async-start | bytes 2621440 | tf_op jit(solution)/shard_map/reduce_scatter | solution.py:860
  100.3 21.1 %collective-permute-start.2 = (bf16[256,1024]{1,0:T(8,128)(2,1)}, bf16[256,1024]{1,0:T(8,128)(2,1)S(1)}, u32[]{:S(2)}, u32[]{:S(2)}) collective-permute-start(bf16[256,1024]{1,0:T(8,128)(2,1)} %get-tuple-element.101), channel_id=1, source_target_pairs={{0,8},{4,12},{8,0},{12,4},{16,24},{20,28},{24,16},{28,20},{1,9},{5... | collective-permute-start | bytes 1572872 | tf_op jit(solution)/shard_map/ppermute | solution.py:703
  102.1 19.4 %collective-permute-start.3 = (bf16[256,1024]{1,0:T(8,128)(2,1)}, bf16[256,1024]{1,0:T(8,128)(2,1)S(1)}, u32[]{:S(2)}, u32[]{:S(2)}) collective-permute-start(bf16[256,1024]{1,0:T(8,128)(2,1)} %get-tuple-element.102), channel_id=1, source_target_pairs={{0,16},{4,20},{8,24},{12,28},{16,0},{20,4},{24,8},{28,12},{1,17},{... | collective-permute-start | bytes 1572872 | tf_op jit(solution)/shard_map/ppermute | solution.py:703
  103.6 24.7 %collective-permute-start.4 = (bf16[256,1024]{1,0:T(8,128)(2,1)}, bf16[256,1024]{1,0:T(8,128)(2,1)S(1)}, u32[]{:S(2)}, u32[]{:S(2)}) collective-permute-start(bf16[256,1024]{1,0:T(8,128)(2,1)} %get-tuple-element.106), channel_id=1, source_target_pairs={{0,8},{4,12},{8,0},{12,4},{16,24},{20,28},{24,16},{28,20},{1,9},{5... | collective-permute-start | bytes 1572872 | tf_op jit(solution)/shard_map/ppermute | solution.py:703
  104.1 24.1 %collective-permute-start.5 = (bf16[256,1024]{1,0:T(8,128)(2,1)}, bf16[256,1024]{1,0:T(8,128)(2,1)S(1)}, u32[]{:S(2)}, u32[]{:S(2)}) collective-permute-start(bf16[256,1024]{1,0:T(8,128)(2,1)} %get-tuple-element.107), channel_id=1, source_target_pairs={{0,16},{4,20},{8,24},{12,28},{16,0},{20,4},{24,8},{28,12},{1,17},{... | collective-permute-start | bytes 1572872 | tf_op jit(solution)/shard_map/ppermute | solution.py:703
  128.2 17.5 %copy-start.11 = (bf16[256,1024]{1,0:T(8,128)(2,1)}, bf16[256,1024]{1,0:T(8,128)(2,1)S(1)}, u32[]{:S(2)}) copy-start(bf16[256,1024]{1,0:T(8,128)(2,1)S(1)} %collective-permute-done.4.refs_3_) | copy-start | bytes 1572868
  128.2 18.1 %collective-permute-start.7 = (bf16[1024,1152]{1,0:T(8,128)(2,1)}, bf16[1024,1152]{1,0:T(8,128)(2,1)S(1)}, u32[]{:S(2)}, u32[]{:S(2)}) collective-permute-start(bf16[1024,1152]{1,0:T(8,128)(2,1)} %get-tuple-element.109), channel_id=1, source_target_pairs={{0,4},{4,0},{8,12},{12,8},{16,20},{20,16},{24,28},{28,24},{1,5},{5... | collective-permute-start | bytes 7077896 | tf_op jit(solution)/shard_map/ppermute | solution.py:703
  128.3 18.0 %collective-permute-start.6 = (bf16[1024,1024]{1,0:T(8,128)(2,1)}, bf16[1024,1024]{1,0:T(8,128)(2,1)}, u32[]{:S(2)}, u32[]{:S(2)}) collective-permute-start(bf16[1024,1024]{1,0:T(8,128)(2,1)} %get-tuple-element.108), channel_id=1, source_target_pairs={{0,4},{4,0},{8,12},{12,8},{16,20},{20,16},{24,28},{28,24},{1,5},{5... | collective-permute-start | bytes 6291464 | tf_op jit(solution)/shard_map/ppermute | solution.py:703
  129.8 15.9 %collective-permute-start.9 = (bf16[256,1024]{1,0:T(8,128)(2,1)}, bf16[256,1024]{1,0:T(8,128)(2,1)}, u32[]{:S(2)}, u32[]{:S(2)}) collective-permute-start(bf16[256,1024]{1,0:T(8,128)(2,1)} %add_convert_fusion.2), channel_id=1, source_target_pairs={{0,8},{4,12},{8,0},{12,4},{16,24},{20,28},{24,16},{28,20},{1,9},{5... | collective-permute-start | bytes 1572872 | tf_op jit(solution)/shard_map/ppermute | solution.py:703
  132.5 13.8 %collective-permute-start.8 = (bf16[256,1024]{1,0:T(8,128)(2,1)}, bf16[256,1024]{1,0:T(8,128)(2,1)S(1)}, u32[]{:S(2)}, u32[]{:S(2)}) collective-permute-start(bf16[256,1024]{1,0:T(8,128)(2,1)} %add_convert_fusion.3), channel_id=1, source_target_pairs={{0,16},{4,20},{8,24},{12,28},{16,0},{20,4},{24,8},{28,12},{1,17},{... | collective-permute-start | bytes 1572872 | tf_op jit(solution)/shard_map/ppermute | solution.py:703
  146.3 10.6 %copy-start.13 = (bf16[256,1024]{1,0:T(8,128)(2,1)}, bf16[256,1024]{1,0:T(8,128)(2,1)S(1)}, u32[]{:S(2)}) copy-start(bf16[256,1024]{1,0:T(8,128)(2,1)S(1)} %collective-permute-done.8.refs_4_) | copy-start | bytes 1572868
  147.7 11.2 %copy-start.12 = (bf16[256,1024]{1,0:T(8,128)(2,1)S(1)}, bf16[256,1024]{1,0:T(8,128)(2,1)}, u32[]{:S(2)}) copy-start(bf16[256,1024]{1,0:T(8,128)(2,1)} %get-tuple-element.131) | copy-start | bytes 1572868
  147.7 11.2 %copy-start.15 = (bf16[256,1024]{1,0:T(8,128)(2,1)S(1)}, bf16[256,1024]{1,0:T(8,128)(2,1)}, u32[]{:S(2)}) copy-start(bf16[256,1024]{1,0:T(8,128)(2,1)} %copy-done.14) | copy-start | bytes 1572868
  156.9 15.2 %collective-permute-start.11 = (bf16[256,1024]{1,0:T(8,128)(2,1)}, bf16[256,1024]{1,0:T(8,128)(2,1)}, u32[]{:S(2)}, u32[]{:S(2)}) collective-permute-start(bf16[256,1024]{1,0:T(8,128)(2,1)} %get-tuple-element.120), channel_id=1, source_target_pairs={{0,8},{4,12},{8,0},{12,4},{16,24},{20,28},{24,16},{28,20},{1,9},{5... | collective-permute-start | bytes 1572872 | tf_op jit(solution)/shard_map/ppermute | solution.py:703
  157.2 15.0 %copy-start.19 = (bf16[256,1024]{1,0:T(8,128)(2,1)S(1)}, bf16[256,1024]{1,0:T(8,128)(2,1)}, u32[]{:S(2)}) copy-start(bf16[256,1024]{1,0:T(8,128)(2,1)} %get-tuple-element.119) | copy-start | bytes 1572868
  157.2 17.9 %collective-permute-start.14 = (bf16[256,1152]{1,0:T(8,128)(2,1)}, bf16[256,1152]{1,0:T(8,128)(2,1)S(1)}, u32[]{:S(2)}, u32[]{:S(2)}) collective-permute-start(bf16[256,1152]{1,0:T(8,128)(2,1)} %get-tuple-element.127), channel_id=1, source_target_pairs={{0,16},{4,20},{8,24},{12,28},{16,0},{20,4},{24,8},{28,12},{1,17},{... | collective-permute-start | bytes 1769480 | tf_op jit(solution)/shard_map/ppermute | solution.py:703
  160.2 14.9 %copy-start.9 = (bf16[256,1152]{1,0:T(8,128)(2,1)S(1)}, bf16[256,1152]{1,0:T(8,128)(2,1)}, u32[]{:S(2)}) copy-start(bf16[256,1152]{1,0:T(8,128)(2,1)} %get-tuple-element.126) | copy-start | bytes 1769476
  161.5 21.8 %copy-start.20 = (bf16[256,1024]{1,0:T(8,128)(2,1)S(1)}, bf16[256,1024]{1,0:T(8,128)(2,1)}, u32[]{:S(2)}) copy-start(bf16[256,1024]{1,0:T(8,128)(2,1)} %get-tuple-element.117) | copy-start | bytes 1572868
  161.5 21.8 %collective-permute-start.10 = (bf16[256,1024]{1,0:T(8,128)(2,1)}, bf16[256,1024]{1,0:T(8,128)(2,1)S(1)}, u32[]{:S(2)}, u32[]{:S(2)}) collective-permute-start(bf16[256,1024]{1,0:T(8,128)(2,1)} %get-tuple-element.118), channel_id=1, source_target_pairs={{0,8},{4,12},{8,0},{12,4},{16,24},{20,28},{24,16},{28,20},{1,9},{5... | collective-permute-start | bytes 1572872 | tf_op jit(solution)/shard_map/ppermute | solution.py:703
  163.3 23.1 %collective-permute-start.13 = (bf16[256,1152]{1,0:T(8,128)(2,1)}, bf16[256,1152]{1,0:T(8,128)(2,1)S(1)}, u32[]{:S(2)}, u32[]{:S(2)}) collective-permute-start(bf16[256,1152]{1,0:T(8,128)(2,1)} %get-tuple-element.125), channel_id=1, source_target_pairs={{0,16},{4,20},{8,24},{12,28},{16,0},{20,4},{24,8},{28,12},{1,17},{... | collective-permute-start | bytes 1769480 | tf_op jit(solution)/shard_map/ppermute | solution.py:703
  173.4 12.9 %copy-start.10 = (bf16[256,1152]{1,0:T(8,128)(2,1)S(1)}, bf16[256,1152]{1,0:T(8,128)(2,1)}, u32[]{:S(2)}) copy-start(bf16[256,1152]{1,0:T(8,128)(2,1)} %get-tuple-element.124) | copy-start | bytes 1769476
  173.4 21.9 %collective-permute-start.12 = (bf16[256,1024]{1,0:T(8,128)(2,1)S(1)}, bf16[256,1024]{1,0:T(8,128)(2,1)S(1)}, u32[]{:S(2)}, u32[]{:S(2)}) collective-permute-start(bf16[256,1024]{1,0:T(8,128)(2,1)S(1)} %add_convert_fusion.1), channel_id=1, source_target_pairs={{0,16},{4,20},{8,24},{12,28},{16,0},{20,4},{24,8},{28,12},{1,17},{... | collective-permute-start | bytes 1572872 | tf_op jit(solution)/shard_map/ppermute | solution.py:703
  175.2 20.1 %collective-permute-start.15 = (bf16[256,1152]{1,0:T(8,128)(2,1)S(1)}, bf16[256,1152]{1,0:T(8,128)(2,1)S(1)}, u32[]{:S(2)}, u32[]{:S(2)}) collective-permute-start(bf16[256,1152]{1,0:T(8,128)(2,1)S(1)} %add_convert_fusion), channel_id=1, source_target_pairs={{0,8},{4,12},{8,0},{12,4},{16,24},{20,28},{24,16},{28,20},{1,9},{5... | collective-permute-start | bytes 1769480 | tf_op jit(solution)/shard_map/ppermute | solution.py:703
  (11 other events, 31.3 us)
Sparse Core Ops, SparseCore 0:
  83.5 44.5 reduce-scatter.2
  146.5 44.0 reduce-scatter.4

commit v8 on v7

--- a/solution.py
+++ b/solution.py
@@ -716,10 +716,9 @@
     b_out_ref[...] = dot(left_b_ref[...], b_ref[...], TN).astype(BF16)
 
 
-def keep_kernel(
-    place_ref, left_a_ref, a_ref, left_b_ref, b_ref, a_arrived_ref, b_arrived_ref, *out_refs
+def keep_step(
+    step, left_a_ref, a_ref, left_b_ref, b_ref, a_arrived_ref, b_arrived_ref, *out_refs
 ):
-    step = pl.program_id(0)
     a = dot(left_a_ref[...], a_ref[...], TN) + a_arrived_ref[...].astype(F32)
     b = dot(left_b_ref[...], b_ref[...], TN) + b_arrived_ref[...].astype(F32)
     for i in range(4):
@@ -728,6 +727,10 @@
         def _():
             out_refs[i][...] = a.astype(BF16)
             out_refs[4 + i][...] = b.astype(BF16)
+
+
+def keep_kernel(place_ref, *refs):
+    keep_step(pl.program_id(0), *refs)
 
 
 def pair_specs(left_a, a, left_b, b, flip):
@@ -740,6 +743,44 @@
         return pl.BlockSpec(delta.shape, lambda i, place: (0, 0))
 
     return [rows(left_a), full(a), rows(left_b), full(b)]
+
+
+def send_and_sum_kernel(
+    place_ref, left_a_ref, a_ref, left_b_ref, b_ref, *refs
+):
+    sums, outs = refs[:4], refs[4:]
+    send_kernel(place_ref, left_a_ref, a_ref, left_b_ref, b_ref, outs[0], outs[1])
+    for i in range(2):
+        outs[2 + i][...] = summed(sums[2 * i][...], sums[2 * i + 1][...])
+
+
+def halving_start_and_sum(place, left_a, a, left_b, b, pieces, arrived):
+    rows = left_a.shape[1] // 8
+    terms = [pieces[2], arrived[0], pieces[5], arrived[1]]
+
+    def quarter(array):
+        return pl.BlockSpec((rows // 4, array.shape[1]), lambda i, place: (i, 0))
+
+    results = pl.pallas_call(
+        send_and_sum_kernel,
+        grid_spec=pltpu.PrefetchScalarGridSpec(
+            num_scalar_prefetch=1,
+            grid=(4,),
+            in_specs=pair_specs(left_a, a, left_b, b, 1) + [quarter(term) for term in terms],
+            out_specs=[
+                pl.BlockSpec((rows, delta.shape[1]), lambda i, place: (i, 0)) for delta in (a, b)
+            ]
+            + [quarter(terms[0]), quarter(terms[2])],
+        ),
+        out_shape=[
+            jax.ShapeDtypeStruct((4 * rows, delta.shape[1]), BF16) for delta in (a, b)
+        ]
+        + [jax.ShapeDtypeStruct(term.shape, BF16) for term in (terms[0], terms[2])],
+        compiler_params=PARAMS,
+        interpret=INTERPRET,
+        name="send_rows_and_sum",
+    )(place, left_a, a, left_b, b, *terms)
+    return results[:2], results[2:]
 
 
 def halving_start(place, left_a, a, left_b, b):
@@ -801,9 +842,12 @@
     return exchange(pieces[1], 2), exchange(pieces[6], 4)
 
 
-def halving_last(pieces, arrived):
-    a, b = pieces[:4], pieces[4:]
-    return exchange(summed(a[2], arrived[0]), 4), exchange(summed(b[1], arrived[1]), 2)
+def halving_onward(pieces, arrived):
+    return summed(pieces[2], arrived[0]), summed(pieces[5], arrived[1])
+
+
+def halving_last(onward):
+    return exchange(onward[0], 4), exchange(onward[1], 2)
 
 
 def halving_terms(pieces, stay, last):
@@ -854,6 +898,85 @@
         interpret=INTERPRET,
         name="finish",
     )(*terms)
+
+
+def gradient_and_keep_kernel(place_ref, *refs):
+    step = pl.program_id(0)
+    cuts = pl.num_programs(0) - 4
+    gradient_refs, keep_refs = refs[:6], refs[6:12]
+    out_ref, piece_refs = refs[12], refs[13:]
+
+    @pl.when(step < cuts)
+    def _():
+        input_gradient_kernel(*gradient_refs, out_ref)
+
+    @pl.when(step >= cuts)
+    def _():
+        keep_step(step - cuts, *keep_refs, *piece_refs)
+
+
+def run_gradient_and_keep(place, gradient_args, keep_args):
+    delta_query_key, delta_value, delta_gate, query_key_weight, value_gate_weight, small_weight = (
+        gradient_args
+    )
+    left_a, a, left_b, b, a_arrived, b_arrived = keep_args
+    tokens, model = delta_value.shape[0], query_key_weight.shape[1]
+    cut = 512
+    cuts = model // cut
+    rows = left_a.shape[1] // 8
+
+    def full(array):
+        return pl.BlockSpec(array.shape, lambda i, place: (0, 0))
+
+    def weight(array):
+        return pl.BlockSpec(
+            (2, cut, array.shape[2]), lambda i, place: (0, jnp.minimum(i, cuts - 1), 0)
+        )
+
+    def left(array):
+        return pl.BlockSpec(
+            (array.shape[0], rows),
+            lambda i, place: (0, block_of(jnp.maximum(i - cuts, 0), place[0], 0)),
+        )
+
+    def arrived(array):
+        return pl.BlockSpec((rows, array.shape[1]), lambda i, place: (jnp.maximum(i - cuts, 0), 0))
+
+    widths = [delta.shape[1] for delta in (a, b) for _ in range(4)]
+    results = pl.pallas_call(
+        gradient_and_keep_kernel,
+        grid_spec=pltpu.PrefetchScalarGridSpec(
+            num_scalar_prefetch=1,
+            grid=(cuts + 4,),
+            in_specs=[
+                full(delta_query_key),
+                full(delta_value),
+                full(delta_gate),
+                weight(query_key_weight),
+                weight(value_gate_weight),
+                pl.BlockSpec(
+                    (2, small_weight.shape[1], cut),
+                    lambda i, place: (0, 0, jnp.minimum(i, cuts - 1)),
+                ),
+                left(left_a),
+                full(a),
+                left(left_b),
+                full(b),
+                arrived(a_arrived),
+                arrived(b_arrived),
+            ],
+            out_specs=[
+                pl.BlockSpec((tokens, cut), lambda i, place: (0, jnp.minimum(i, cuts - 1)))
+            ]
+            + [pl.BlockSpec((rows, width), lambda i, place: (0, 0)) for width in widths],
+        ),
+        out_shape=[jax.ShapeDtypeStruct((tokens, model), BF16)]
+        + [jax.ShapeDtypeStruct((rows, width), BF16) for width in widths],
+        compiler_params=PARAMS,
+        interpret=INTERPRET,
+        name="input_gradient_and_keep",
+    )(place, *gradient_args, *keep_args)
+    return results[0], results[1:]
 
 
 def scatter(partial, axis, dimension):
@@ -924,14 +1047,7 @@
         delta_out,
         delta_final,
     )
-    if cubic:
-        delta_value, early_arrived = together(delta_value, early_arrived)
-        early_last = halving_last(early_pieces, early_arrived)
-        late = (place, inputs, delta_value, inputs, delta_query_key)
-        sent = halving_start(*late)
-        sent, early_stay = together(sent, early_stay)
-        arrived = [exchange(part, 1) for part in sent]
-    grad_rows = run_input_gradient(
+    gradient_args = (
         delta_query_key,
         delta_value,
         delta_gate,
@@ -940,13 +1056,20 @@
         small_weight,
     )
     if cubic:
-        grad_rows, arrived, early_last = together(grad_rows, arrived, early_last)
+        late = (inputs, delta_value, inputs, delta_query_key)
+        sent, early_onward = halving_start_and_sum(place, *late, early_pieces, early_arrived)
+        sent, early_stay = together(sent, early_stay)
+        arrived = [exchange(part, 1) for part in sent]
+        early_last = halving_last(early_onward)
+        grad_rows, late_pieces = run_gradient_and_keep(place, gradient_args, (*late, *arrived))
+        grad_rows, late_pieces, early_last = together(grad_rows, late_pieces, early_last)
+    else:
+        grad_rows = run_input_gradient(*gradient_args)
     grad_inputs = scatter(grad_rows, "head", 1)
     if cubic:
-        late_pieces = halving_keep(*late, *arrived)
         late_arrived = halving_cross(late_pieces)
         late_stay = halving_stay(late_pieces)
-        late_last = halving_last(late_pieces, late_arrived)
+        late_last = halving_last(halving_onward(late_pieces, late_arrived))
         gate_terms, out_terms = halving_terms(early_pieces, early_stay, early_last)
         value_terms, packed_terms = halving_terms(late_pieces, late_stay, late_last)
         value_terms = (value_terms[0].astype(F32) + value_terms[1].astype(F32), value_terms[2])

time: 209 us -> 217 us (1.038)
  waiting for transfers between devices: 32.1 us -> 36.8 us
  local copies, waits for them, and re-layouts: 7.91 us -> 11.7 us
    pallas_call x1 -> x2, Pallas kernels: 11.7 us -> 27.8 us  [the longest x1 20.7 us: run_gradient_and_keep(): pl.pallas_call(gradient_and_keep_kernel, grid_spec=pltpu.PrefetchScalarGr...]
    pallas_call x2 -> x1, Pallas kernels: 17.5 us -> 8.32 us  [halving_keep(): pl.pallas_call(keep_kernel, grid_spec=pltpu.PrefetchScalarGridSpec(num_sc...]
    pallas_call x2 -> x1, Pallas kernels: 13 us -> 6.27 us  [halving_start(): pl.pallas_call(send_kernel, grid_spec=pltpu.PrefetchScalarGridSpec(num_sc...]
    ppermute x16, waiting for transfers between devices: 26.4 us -> 31.1 us  [exchange(): return lax.ppermute(array, 'ctx', [(i, i ^ distance) for i in devices])]
    unnamed x43 -> x45, local copies, waits for them, and re-layouts: 7.91 us -> 11.7 us
  transfers between devices with their start and end apart: 22 -> 22, of which waited for: 8 -> 8; matrix products, arithmetic and copies ran while one was open for 12% -> 11% of each run, Pallas kernels for 29% -> 28%
where the time goes in v8:
time: 217 us; the launch traced here: 216 us
  Pallas kernels  98.3 us (45%)
  waiting for transfers between devices  36.8 us (17%)
  starting transfers between devices  31.5 us (15%)
  matrix products  17.6 us (8%)
  between operations  14.3 us (7%)
  local copies, waits for them, and re-layouts  11.7 us (5%)
  other arithmetic  5.18 us (2%)
    ppermute x16, waiting for transfers between devices, exchange(): return lax.ppermute(array, 'ctx', [(i, i ^ distance) for i in devices])  31.1 us
    pallas_call x1, Pallas kernels, run_gradient_and_keep(): pl.pallas_call(gradient_and_keep_kernel, grid_spec=pltpu.PrefetchScalarGr...  20.7 us
    dot_general x3, matrix products, product(): return jnp.einsum(spec, a, b, preferred_element_type=F32)  17.6 us
    pallas_call x1, Pallas kernels, run_backward(): pl.pallas_call(backward_kernel, grid=(chunks // spans,), in_specs=[pl.Blo...  17 us
    all_to_all x4, starting transfers between devices, swap(): return lax.all_to_all(parts, 'ctx', split_axis=0, concat_axis=0, tiled=True)  15.7 us
    ppermute x16, starting transfers between devices, exchange(): return lax.ppermute(array, 'ctx', [(i, i ^ distance) for i in devices])  15.6 us
    pallas_call x1, Pallas kernels, run_forward(): pl.pallas_call(forward_kernel, grid=(chunks // spans,), in_specs=[pl.Bloc...  13 us
    unnamed x45, local copies, waits for them, and re-layouts  11.7 us
  transfers between devices with their start and end apart: 22, of which 8 were waited for; matrix products, arithmetic and copies ran while one was open for 11% of the time, Pallas kernels for 28%

profile of v8, /device:TPU:0, one launch (start us, length us, event | category | flops | bytes accessed | tf_op | source)
XLA Modules:
  0.0 215.6 jit_solution(12125250453806172161)
XLA Ops:
  7.2 9.9 %projection.1 = (f32[2,512,512]{2,1,0:T(8,128)}, f32[512,1024]{1,0:T(8,128)}, f32[512,16]{1,0:T(8,128)}) custom-call(bf16[512,2048]{1,0:T(8,128)(2,1)} %refs_8_.1, bf16[2,2048,512]{2,1,0:T(8,128)(2,1)} %refs_3_.1, bf16[2,2048,1024]{2,1,0:T(8,128)(2,1)} %refs_4_.1, bf16[2,8,2048]{2,1,0:T(8,128)(2,1)} %bitcast.27), custom_call_target="tpu_custom_call" | custom-call | tf_op jit(solution)/shard_map/projection/pallas_call | solution.py:624
  17.1 13.0 %forward_blocks.1 = (bf16[4,8,128,128]{3,2,1,0:T(8,128)(2,1)}, bf16[4,8,128,256]{3,2,1,0:T(8,128)(2,1)}, bf16[512,1024]{1,0:T(8,128)(2,1)}, f32[512,1024]{1,0:T(8,128)}, bf16[8,128,256]{2,1,0:T(8,128)(2,1)}) custom-call(f32[2,512,512]{2,1,0:T(8,128)} %get-tuple-element.76.query_key_ref, f32[512,1024]{1,0:T(8,128)} %get-tuple-element.77.value_ref, ...), custom_call_target="tpu_custom_call" | custom-call | tf_op jit(solution)/shard_map/forward_blocks/pallas_call | solution.py:442
  30.1 5.2 %all-to-all-start = ((bf16[8,1,128,256]{3,2,1,0:T(8,128)(2,1)}), bf16[8,1,128,256]{3,2,1,0:T(8,128)(2,1)S(1)}, u32[]{:S(2)}, u32[]{:S(2)}) async-start(bf16[8,1,128,256]{3,2,1,0:T(8,128)(2,1)} %bitcast.26), calls=%async_computation | async-start | bytes 1048576 | tf_op jit(solution)/shard_map/all_to_all | solution.py:563
  35.2 5.5 %fusion.3.gate_ref = bf16[512,1024]{1,0:T(8,128)(2,1)} fusion(bf16[512,2048]{1,0:T(8,128)(2,1)S(1)} %copy-done, bf16[2,2048,1024]{2,1,0:T(8,128)(2,1)} %refs_4_.1), kind=kOutput, calls=%fused_computation.4 | convolution fusion | flops 2148007936 | bytes 7340032 | tf_op jit(solution)/shard_map/td,df->tf/dot_general | solution.py:593
  40.8 4.2 %all-to-all-done.totals_ref = bf16[8,1,128,256]{3,2,1,0:T(8,128)(2,1)S(1)} async-done(((bf16[8,1,128,256]{3,2,1,0:T(8,128)(2,1)}), bf16[8,1,128,256]{3,2,1,0:T(8,128)(2,1)S(1)}, u32[]{:S(2)}, u32[]{:S(2)}) %all-to-all-start) | async-done | bytes 524320 | tf_op jit(solution)/shard_map/all_to_all | solution.py:563
  45.8 2.8 %chain_forward.1 = bf16[8,1,128,128]{3,2,1,0:T(8,128)(2,1)} custom-call(bf16[8,1,128,256]{3,2,1,0:T(8,128)(2,1)} %copy-done.1), custom_call_target="tpu_custom_call" | custom-call | tf_op jit(solution)/shard_map/chain_forward/pallas_call | solution.py:575
  48.6 3.6 %all-to-all-start.1 = ((bf16[8,1,128,128]{3,2,1,0:T(8,128)(2,1)}), bf16[8,1,128,128]{3,2,1,0:T(8,128)(2,1)S(1)}, u32[]{:S(2)}, u32[]{:S(2)}) async-start(bf16[8,1,128,128]{3,2,1,0:T(8,128)(2,1)} %chain_forward.1), calls=%async_computation.1 | async-start | bytes 524288 | tf_op jit(solution)/shard_map/all_to_all | solution.py:563
  52.2 6.2 %convolution_convert_fusion.1.delta_ref = bf16[512,1024]{1,0:T(8,128)(2,1)} fusion(bf16[512,2048]{1,0:T(8,128)(2,1)} %refs_2_.1, bf16[1024,2048]{1,0:T(8,128)(2,1)} %param.17), kind=kOutput, calls=%fused_computation.5 | convolution fusion | flops 2148007936 | bytes 7340032 | tf_op jit(solution)/shard_map/td,fd->tf/dot_general | solution.py:593
  59.6 6.5 %gated_norm.1 = (bf16[512,1024]{1,0:T(8,128)(2,1)}, bf16[512,1024]{1,0:T(8,128)(2,1)}, bf16[512,1024]{1,0:T(8,128)(2,1)}, bf16[8,128,128]{2,1,0:T(8,128)(2,1)}) custom-call(f32[512,1024]{1,0:T(8,128)} %get-tuple-element.79.local_ref, bf16[512,1024]{1,0:T(8,128)(2,1)} %get-tuple-element.80.map_ref, bf16[512,1024]{1,0:T(8,128)(2,1)} %fusion.3.gate_ref, ...), custom_call_target="tpu_custom_call" | custom-call | tf_op jit(solution)/shard_map/gated_norm/pallas_call | solution.py:479
  66.1 6.3 %send_rows.1 = (bf16[1024,1024]{1,0:T(8,128)(2,1)}, bf16[1024,1024]{1,0:T(8,128)(2,1)}) custom-call(s32[1]{0:T(128)} %bitcast.9.place_ref, bf16[512,2048]{1,0:T(8,128)(2,1)} %refs_8_.1, bf16[512,1024]{1,0:T(8,128)(2,1)} %get-tuple-element.93.a_ref.refs_1_.refs_2_, bf16[512,2048]{1,0:T(8,128)(2,1)} %refs_2_.1, bf16[512,1024]{1,0:T(8,128)(2,1)} %get-tuple-element.87.b_ref.refs_3_), custom_call_target="tpu_custom_call" | custom-call | tf_op jit(solution)/shard_map/send_rows/pallas_call | solution.py:788
  72.9 3.5 %all-to-all-start.2 = ((bf16[8,1,128,128]{3,2,1,0:T(8,128)(2,1)}), bf16[8,1,128,128]{3,2,1,0:T(8,128)(2,1)S(1)}, u32[]{:S(2)}, u32[]{:S(2)}) async-start(bf16[8,1,128,128]{3,2,1,0:T(8,128)(2,1)} %bitcast.29), calls=%async_computation.2 | async-start | bytes 524288 | tf_op jit(solution)/shard_map/all_to_all | solution.py:563
  76.4 5.9 %convolution_convert_fusion = bf16[512,2048]{1,0:T(8,128)(2,1)} fusion(bf16[512,1024]{1,0:T(8,128)(2,1)S(1)} %copy-done.2, bf16[1024,2048]{1,0:T(8,128)(2,1)} %param.17), kind=kOutput, calls=%fused_computation.3 | convolution fusion | flops 2148532224 | bytes 7340032 | tf_op jit(solution)/shard_map/tf,fd->td/dot_general | solution.py:593
  84.0 3.0 %chain_backward.1 = bf16[8,1,128,128]{3,2,1,0:T(8,128)(2,1)} custom-call(bf16[8,1,128,256]{3,2,1,0:T(8,128)(2,1)} %copy-done.1, bf16[8,1,128,128]{3,2,1,0:T(8,128)(2,1)} %copy-done.8), custom_call_target="tpu_custom_call" | custom-call | tf_op jit(solution)/shard_map/chain_backward/pallas_call | solution.py:584
  87.0 3.4 %all-to-all-start.3 = ((bf16[8,1,128,128]{3,2,1,0:T(8,128)(2,1)}), bf16[8,1,128,128]{3,2,1,0:T(8,128)(2,1)S(1)}, u32[]{:S(2)}, u32[]{:S(2)}) async-start(bf16[8,1,128,128]{3,2,1,0:T(8,128)(2,1)} %chain_backward.1), calls=%async_computation.4 | async-start | bytes 524288 | tf_op jit(solution)/shard_map/all_to_all | solution.py:563
  92.0 8.3 %keep_rows.1 = (bf16[256,1024]{1,0:T(8,128)(2,1)}, bf16[256,1024]{1,0:T(8,128)(2,1)}, bf16[256,1024]{1,0:T(8,128)(2,1)}, bf16[256,1024]{1,0:T(8,128)(2,1)}, bf16...) custom-call(s32[1]{0:T(128)} %bitcast.9.place_ref, ...), custom_call_target="tpu_custom_call" | custom-call | tf_op jit(solution)/shard_map/keep_rows/pallas_call | solution.py:809
  100.3 1.7 collective-permute-start.2
  102.1 1.5 collective-permute-start.3
  104.5 17.0 %backward_blocks.1 = (bf16[512,1152]{1,0:T(8,128)(2,1)}, bf16[512,1024]{1,0:T(8,128)(2,1)}) custom-call(f32[2,512,512]{2,1,0:T(8,128)} %get-tuple-element.76.query_key_ref, f32[512,1024]{1,0:T(8,128)} %get-tuple-element.77.value_ref, f32[512,16]{1,0:T(8,128)} %get-tuple-element.78.decay_beta_ref, f32[1,8]{1,0:T(1,128)} %bitcast.33, f32[1,8]{1,0:T(1,128)} %bitcast.35, ...), custom_call_target="tpu_custom_call" | custom-call | tf_op jit(solution)/shard_map/backward_blocks/pallas_call | solution.py:513
  122.4 7.2 %send_rows_and_sum.1 = (bf16[1024,1024]{1,0:T(8,128)(2,1)}, bf16[1024,1152]{1,0:T(8,128)(2,1)}, bf16[256,1024]{1,0:T(8,128)(2,1)}, bf16[256,1024]{1,0:T(8,128)(2,1)}) custom-call(s32[1]{0:T(128)} %bitcast.9.place_ref, bf16[512,2048]{1,0:T(8,128)(2,1)} %refs_8_.1, bf16[512,1024]{1,0:T(8,128)(2,1)} %get-tuple-element.106.a_ref.refs_1_.refs_7_, ...), custom_call_target="tpu_custom_call" | custom-call | tf_op jit(solution)/shard_map/send_rows_and_sum/pallas_call | solution.py:764
  130.9 1.7 collective-permute-start.8
  132.6 1.5 collective-permute-start.9
  134.1 4.1 %collective-permute-done.6.refs_10_ = bf16[1024,1024]{1,0:T(8,128)(2,1)S(1)} collective-permute-done((bf16[1024,1024]{1,0:T(8,128)(2,1)}, bf16[1024,1024]{1,0:T(8,128)(2,1)S(1)}, u32[]{:S(2)}, u32[]{:S(2)}) %collective-permute-start.6) | collective-permute-done | bytes 2097184 | tf_op jit(solution)/shard_map/ppermute | solution.py:703
  140.9 20.7 %input_gradient_and_keep.1 = (bf16[512,2048]{1,0:T(8,128)(2,1)}, bf16[256,1024]{1,0:T(8,128)(2,1)}, bf16[256,1024]{1,0:T(8,128)(2,1)}, bf16[256,1024]{1,0:T(8,12...) custom-call(s32[1]{0:T(128)} %bitcast.9.place_ref, ...), custom_call_target="tpu_custom_call" | custom-call | tf_op jit(solution)/shard_map/input_gradient_and_keep/pallas_call | solution.py:946
  162.4 1.7 collective-permute-start.11
  164.1 1.4 collective-permute-start.14
  169.1 8.4 %collective-permute-done.11 = bf16[256,1024]{1,0:T(8,128)(2,1)} collective-permute-done((bf16[256,1024]{1,0:T(8,128)(2,1)}, bf16[256,1024]{1,0:T(8,128)(2,1)}, u32[]{:S(2)}, u32[]{:S(2)}) %collective-permute-start.11) | collective-permute-done | bytes 524320 | tf_op jit(solution)/shard_map/ppermute | solution.py:703
  178.9 1.7 collective-permute-start.12
  180.7 1.6 collective-permute-start.15
  182.3 6.3 %collective-permute-done.10 = bf16[256,1024]{1,0:T(8,128)(2,1)S(1)} collective-permute-done((bf16[256,1024]{1,0:T(8,128)(2,1)}, bf16[256,1024]{1,0:T(8,128)(2,1)S(1)}, u32[]{:S(2)}, u32[]{:S(2)}) %collective-permute-start.10) | collective-permute-done | bytes 524320 | tf_op jit(solution)/shard_map/ppermute | solution.py:703
  189.8 3.4 %collective-permute-done.13 = bf16[256,1152]{1,0:T(8,128)(2,1)S(1)} collective-permute-done((bf16[256,1152]{1,0:T(8,128)(2,1)}, bf16[256,1152]{1,0:T(8,128)(2,1)S(1)}, u32[]{:S(2)}, u32[]{:S(2)}) %collective-permute-start.13) | collective-permute-done | bytes 589856 | tf_op jit(solution)/shard_map/ppermute | solution.py:703
  194.4 8.9 %collective-permute-done.12.refs_1_ = bf16[256,1024]{1,0:T(8,128)(2,1)S(1)} collective-permute-done((bf16[256,1024]{1,0:T(8,128)(2,1)S(1)}, bf16[256,1024]{1,0:T(8,128)(2,1)S(1)}, u32[]{:S(2)}, u32[]{:S(2)}) %collective-permute-start.12) | collective-permute-done | bytes 524320 | tf_op jit(solution)/shard_map/ppermute | solution.py:703
  204.9 3.8 %finish.1 = (f32[2,256,512]{2,1,0:T(8,128)}, f32[2,256,1024]{2,1,0:T(8,128)}, f32[2,8,256]{2,1,0:T(8,128)}) custom-call(f32[256,1024]{1,0:T(8,128)} %convert_add_fusion.1.refs_0_, bf16[256,1024]{1,0:T(8,128)(2,1)} %copy-done.19, bf16[256,1024]{1,0:T(8,128)(2,1)} %get-tuple-element.133.refs_2_, bf16[256,1024]{1,0:T(8,128)(2,1)} %copy-done.12, ...), custom_call_target="tpu_custom_call" | custom-call | tf_op jit(solution)/shard_map/finish/pallas_call | solution.py:883
  (78 shorter events, 21.6 us)
Async XLA Ops:
  17.1 18.2 %copy-start = (bf16[512,2048]{1,0:T(8,128)(2,1)S(1)}, bf16[512,2048]{1,0:T(8,128)(2,1)}, u32[]{:S(2)}) copy-start(bf16[512,2048]{1,0:T(8,128)(2,1)} %refs_8_.1) | copy-start | bytes 6291460
  30.1 14.9 %all-to-all-start = ((bf16[8,1,128,256]{3,2,1,0:T(8,128)(2,1)}), bf16[8,1,128,256]{3,2,1,0:T(8,128)(2,1)S(1)}, u32[]{:S(2)}, u32[]{:S(2)}) async-start(bf16[8,1,128,256]{3,2,1,0:T(8,128)(2,1)} %bitcast.26), calls=%async_computation | async-start | bytes 1048576 | tf_op jit(solution)/shard_map/all_to_all | solution.py:563
  48.6 10.3 %all-to-all-start.1 = ((bf16[8,1,128,128]{3,2,1,0:T(8,128)(2,1)}), bf16[8,1,128,128]{3,2,1,0:T(8,128)(2,1)S(1)}, u32[]{:S(2)}, u32[]{:S(2)}) async-start(bf16[8,1,128,128]{3,2,1,0:T(8,128)(2,1)} %chain_forward.1), calls=%async_computation.1 | async-start | bytes 524288 | tf_op jit(solution)/shard_map/all_to_all | solution.py:563
  66.1 10.3 %copy-start.2 = (bf16[512,1024]{1,0:T(8,128)(2,1)S(1)}, bf16[512,1024]{1,0:T(8,128)(2,1)}, u32[]{:S(2)}) copy-start(bf16[512,1024]{1,0:T(8,128)(2,1)} %get-tuple-element.87.b_ref.refs_3_) | copy-start | bytes 3145732
  72.4 18.3 %collective-permute-start = (bf16[1024,1024]{1,0:T(8,128)(2,1)}, bf16[1024,1024]{1,0:T(8,128)(2,1)S(1)}, u32[]{:S(2)}, u32[]{:S(2)}) collective-permute-start(bf16[1024,1024]{1,0:T(8,128)(2,1)} %get-tuple-element.94), channel_id=1, source_target_pairs={{0,4},{4,0},{8,12},{12,8},{16,20},{20,16},{24,28},{28,24},{1,5},{5... | collective-permute-start | bytes 6291464 | tf_op jit(solution)/shard_map/ppermute | solution.py:703
  72.4 18.3 %collective-permute-start.1 = (bf16[1024,1024]{1,0:T(8,128)(2,1)}, bf16[1024,1024]{1,0:T(8,128)(2,1)}, u32[]{:S(2)}, u32[]{:S(2)}) collective-permute-start(bf16[1024,1024]{1,0:T(8,128)(2,1)} %get-tuple-element.95), channel_id=1, source_target_pairs={{0,4},{4,0},{8,12},{12,8},{16,20},{20,16},{24,28},{28,24},{1,5},{5... | collective-permute-start | bytes 6291464 | tf_op jit(solution)/shard_map/ppermute | solution.py:703
  72.9 10.4 %all-to-all-start.2 = ((bf16[8,1,128,128]{3,2,1,0:T(8,128)(2,1)}), bf16[8,1,128,128]{3,2,1,0:T(8,128)(2,1)S(1)}, u32[]{:S(2)}, u32[]{:S(2)}) async-start(bf16[8,1,128,128]{3,2,1,0:T(8,128)(2,1)} %bitcast.29), calls=%async_computation.2 | async-start | bytes 524288 | tf_op jit(solution)/shard_map/all_to_all | solution.py:563
  76.4 132.3 %reduce-scatter.3.cloned.1.call-start = ((), (), s32[]{:S(2)}) async-start(), calls=%async_computation.6 | async-start | bytes 2621440 | tf_op jit(solution)/shard_map/reduce_scatter | solution.py:983
  87.0 13.3 %all-to-all-start.3 = ((bf16[8,1,128,128]{3,2,1,0:T(8,128)(2,1)}), bf16[8,1,128,128]{3,2,1,0:T(8,128)(2,1)S(1)}, u32[]{:S(2)}, u32[]{:S(2)}) async-start(bf16[8,1,128,128]{3,2,1,0:T(8,128)(2,1)} %chain_backward.1), calls=%async_computation.4 | async-start | bytes 524288 | tf_op jit(solution)/shard_map/all_to_all | solution.py:563
  90.4 118.3 %reduce-scatter.5.cloned.1.call-start = ((), (), s32[]{:S(2)}) async-start(), calls=%async_computation.7 | async-start | bytes 2621440 | tf_op jit(solution)/shard_map/reduce_scatter | solution.py:983
  100.3 4.1 %copy-start.7 = (bf16[8,1,128,128]{3,2,1,0:T(8,128)(2,1)}, bf16[8,1,128,128]{3,2,1,0:T(8,128)(2,1)S(1)}, u32[]{:S(2)}) copy-start(bf16[8,1,128,128]{3,2,1,0:T(8,128)(2,1)S(1)} %all-to-all-done.3) | copy-start | bytes 786436
  100.3 21.1 %collective-permute-start.2 = (bf16[256,1024]{1,0:T(8,128)(2,1)}, bf16[256,1024]{1,0:T(8,128)(2,1)S(1)}, u32[]{:S(2)}, u32[]{:S(2)}) collective-permute-start(bf16[256,1024]{1,0:T(8,128)(2,1)} %get-tuple-element.108), channel_id=1, source_target_pairs={{0,8},{4,12},{8,0},{12,4},{16,24},{20,28},{24,16},{28,20},{1,9},{5... | collective-permute-start | bytes 1572872 | tf_op jit(solution)/shard_map/ppermute | solution.py:703
  102.1 19.4 %collective-permute-start.3 = (bf16[256,1024]{1,0:T(8,128)(2,1)}, bf16[256,1024]{1,0:T(8,128)(2,1)S(1)}, u32[]{:S(2)}, u32[]{:S(2)}) collective-permute-start(bf16[256,1024]{1,0:T(8,128)(2,1)} %get-tuple-element.110), channel_id=1, source_target_pairs={{0,16},{4,20},{8,24},{12,28},{16,0},{20,4},{24,8},{28,12},{1,17},{... | collective-permute-start | bytes 1572872 | tf_op jit(solution)/shard_map/ppermute | solution.py:703
  103.6 26.0 %collective-permute-start.4 = (bf16[256,1024]{1,0:T(8,128)(2,1)}, bf16[256,1024]{1,0:T(8,128)(2,1)S(1)}, u32[]{:S(2)}, u32[]{:S(2)}) collective-permute-start(bf16[256,1024]{1,0:T(8,128)(2,1)} %get-tuple-element.113), channel_id=1, source_target_pairs={{0,8},{4,12},{8,0},{12,4},{16,24},{20,28},{24,16},{28,20},{1,9},{5... | collective-permute-start | bytes 1572872 | tf_op jit(solution)/shard_map/ppermute | solution.py:703
  104.1 25.5 %collective-permute-start.5 = (bf16[256,1024]{1,0:T(8,128)(2,1)}, bf16[256,1024]{1,0:T(8,128)(2,1)S(1)}, u32[]{:S(2)}, u32[]{:S(2)}) collective-permute-start(bf16[256,1024]{1,0:T(8,128)(2,1)} %get-tuple-element.114), channel_id=1, source_target_pairs={{0,16},{4,20},{8,24},{12,28},{16,0},{20,4},{24,8},{28,12},{1,17},{... | collective-permute-start | bytes 1572872 | tf_op jit(solution)/shard_map/ppermute | solution.py:703
  129.6 32.0 %copy-start.12 = (bf16[256,1024]{1,0:T(8,128)(2,1)}, bf16[256,1024]{1,0:T(8,128)(2,1)S(1)}, u32[]{:S(2)}) copy-start(bf16[256,1024]{1,0:T(8,128)(2,1)S(1)} %collective-permute-done.4.refs_3_) | copy-start | bytes 1572868
  130.4 7.8 %collective-permute-start.7 = (bf16[1024,1152]{1,0:T(8,128)(2,1)}, bf16[1024,1152]{1,0:T(8,128)(2,1)S(1)}, u32[]{:S(2)}, u32[]{:S(2)}) collective-permute-start(bf16[1024,1152]{1,0:T(8,128)(2,1)} %get-tuple-element.116), channel_id=1, source_target_pairs={{0,4},{4,0},{8,12},{12,8},{16,20},{20,16},{24,28},{28,24},{1,5},{5... | collective-permute-start | bytes 7077896 | tf_op jit(solution)/shard_map/ppermute | solution.py:703
  130.4 7.7 %collective-permute-start.6 = (bf16[1024,1024]{1,0:T(8,128)(2,1)}, bf16[1024,1024]{1,0:T(8,128)(2,1)S(1)}, u32[]{:S(2)}, u32[]{:S(2)}) collective-permute-start(bf16[1024,1024]{1,0:T(8,128)(2,1)} %get-tuple-element.115), channel_id=1, source_target_pairs={{0,4},{4,0},{8,12},{12,8},{16,20},{20,16},{24,28},{28,24},{1,5},{5... | collective-permute-start | bytes 6291464 | tf_op jit(solution)/shard_map/ppermute | solution.py:703
  130.9 30.6 %collective-permute-start.8 = (bf16[256,1024]{1,0:T(8,128)(2,1)}, bf16[256,1024]{1,0:T(8,128)(2,1)S(1)}, u32[]{:S(2)}, u32[]{:S(2)}) collective-permute-start(bf16[256,1024]{1,0:T(8,128)(2,1)} %get-tuple-element.126), channel_id=1, source_target_pairs={{0,16},{4,20},{8,24},{12,28},{16,0},{20,4},{24,8},{28,12},{1,17},{... | collective-permute-start | bytes 1572872 | tf_op jit(solution)/shard_map/ppermute | solution.py:703
  132.6 29.0 %collective-permute-start.9 = (bf16[256,1024]{1,0:T(8,128)(2,1)}, bf16[256,1024]{1,0:T(8,128)(2,1)S(1)}, u32[]{:S(2)}, u32[]{:S(2)}) collective-permute-start(bf16[256,1024]{1,0:T(8,128)(2,1)} %get-tuple-element.127), channel_id=1, source_target_pairs={{0,8},{4,12},{8,0},{12,4},{16,24},{20,28},{24,16},{28,20},{1,9},{5... | collective-permute-start | bytes 1572872 | tf_op jit(solution)/shard_map/ppermute | solution.py:703
  161.6 4.0 %copy-start.13 = (bf16[256,1024]{1,0:T(8,128)(2,1)S(1)}, bf16[256,1024]{1,0:T(8,128)(2,1)}, u32[]{:S(2)}) copy-start(bf16[256,1024]{1,0:T(8,128)(2,1)} %get-tuple-element.143) | copy-start | bytes 1572868
  161.6 5.2 %copy-start.14 = (bf16[256,1024]{1,0:T(8,128)(2,1)}, bf16[256,1024]{1,0:T(8,128)(2,1)S(1)}, u32[]{:S(2)}) copy-start(bf16[256,1024]{1,0:T(8,128)(2,1)S(1)} %collective-permute-done.8.refs_4_) | copy-start | bytes 1572868
  161.6 3.9 %copy-start.16 = (bf16[256,1024]{1,0:T(8,128)(2,1)S(1)}, bf16[256,1024]{1,0:T(8,128)(2,1)}, u32[]{:S(2)}) copy-start(bf16[256,1024]{1,0:T(8,128)(2,1)} %copy-done.15) | copy-start | bytes 1572868
  162.4 15.1 %collective-permute-start.11 = (bf16[256,1024]{1,0:T(8,128)(2,1)}, bf16[256,1024]{1,0:T(8,128)(2,1)}, u32[]{:S(2)}, u32[]{:S(2)}) collective-permute-start(bf16[256,1024]{1,0:T(8,128)(2,1)} %get-tuple-element.132), channel_id=1, source_target_pairs={{0,8},{4,12},{8,0},{12,4},{16,24},{20,28},{24,16},{28,20},{1,9},{5... | collective-permute-start | bytes 1572872 | tf_op jit(solution)/shard_map/ppermute | solution.py:703
  164.1 16.5 %collective-permute-start.14 = (bf16[256,1152]{1,0:T(8,128)(2,1)}, bf16[256,1152]{1,0:T(8,128)(2,1)S(1)}, u32[]{:S(2)}, u32[]{:S(2)}) collective-permute-start(bf16[256,1152]{1,0:T(8,128)(2,1)} %get-tuple-element.139), channel_id=1, source_target_pairs={{0,16},{4,20},{8,24},{12,28},{16,0},{20,4},{24,8},{28,12},{1,17},{... | collective-permute-start | bytes 1769480 | tf_op jit(solution)/shard_map/ppermute | solution.py:703
  166.8 13.7 %copy-start.10 = (bf16[256,1152]{1,0:T(8,128)(2,1)S(1)}, bf16[256,1152]{1,0:T(8,128)(2,1)}, u32[]{:S(2)}) copy-start(bf16[256,1152]{1,0:T(8,128)(2,1)} %get-tuple-element.138) | copy-start | bytes 1769476
  168.2 20.5 %copy-start.21 = (bf16[256,1024]{1,0:T(8,128)(2,1)S(1)}, bf16[256,1024]{1,0:T(8,128)(2,1)}, u32[]{:S(2)}) copy-start(bf16[256,1024]{1,0:T(8,128)(2,1)} %get-tuple-element.129) | copy-start | bytes 1572868
  168.2 20.5 %collective-permute-start.10 = (bf16[256,1024]{1,0:T(8,128)(2,1)}, bf16[256,1024]{1,0:T(8,128)(2,1)S(1)}, u32[]{:S(2)}, u32[]{:S(2)}) collective-permute-start(bf16[256,1024]{1,0:T(8,128)(2,1)} %get-tuple-element.130), channel_id=1, source_target_pairs={{0,8},{4,12},{8,0},{12,4},{16,24},{20,28},{24,16},{28,20},{1,9},{5... | collective-permute-start | bytes 1572872 | tf_op jit(solution)/shard_map/ppermute | solution.py:703
  168.7 24.5 %collective-permute-start.13 = (bf16[256,1152]{1,0:T(8,128)(2,1)}, bf16[256,1152]{1,0:T(8,128)(2,1)S(1)}, u32[]{:S(2)}, u32[]{:S(2)}) collective-permute-start(bf16[256,1152]{1,0:T(8,128)(2,1)} %get-tuple-element.137), channel_id=1, source_target_pairs={{0,16},{4,20},{8,24},{12,28},{16,0},{20,4},{24,8},{28,12},{1,17},{... | collective-permute-start | bytes 1769480 | tf_op jit(solution)/shard_map/ppermute | solution.py:703
  178.9 14.3 %copy-start.11 = (bf16[256,1152]{1,0:T(8,128)(2,1)S(1)}, bf16[256,1152]{1,0:T(8,128)(2,1)}, u32[]{:S(2)}) copy-start(bf16[256,1152]{1,0:T(8,128)(2,1)} %get-tuple-element.136) | copy-start | bytes 1769476
  178.9 24.4 %collective-permute-start.12 = (bf16[256,1024]{1,0:T(8,128)(2,1)S(1)}, bf16[256,1024]{1,0:T(8,128)(2,1)S(1)}, u32[]{:S(2)}, u32[]{:S(2)}) collective-permute-start(bf16[256,1024]{1,0:T(8,128)(2,1)S(1)} %add_convert_fusion.1), channel_id=1, source_target_pairs={{0,16},{4,20},{8,24},{12,28},{16,0},{20,4},{24,8},{28,12},{1,17},{... | collective-permute-start | bytes 1572872 | tf_op jit(solution)/shard_map/ppermute | solution.py:703
  180.7 22.5 %collective-permute-start.15 = (bf16[256,1152]{1,0:T(8,128)(2,1)S(1)}, bf16[256,1152]{1,0:T(8,128)(2,1)S(1)}, u32[]{:S(2)}, u32[]{:S(2)}) collective-permute-start(bf16[256,1152]{1,0:T(8,128)(2,1)S(1)} %add_convert_fusion), channel_id=1, source_target_pairs={{0,8},{4,12},{8,0},{12,4},{16,24},{20,28},{24,16},{28,20},{1,9},{5... | collective-permute-start | bytes 1769480 | tf_op jit(solution)/shard_map/ppermute | solution.py:703
  (12 other events, 11.2 us)
Sparse Core Ops, SparseCore 0:
  83.5 44.5 reduce-scatter.2
  161.8 45.2 reduce-scatter.4

commit v9 on v7

--- a/solution.py
+++ b/solution.py
@@ -706,7 +706,7 @@
 def block_of(step, place, flip):
     x, y = (place // 2) % 2, place // 4
     core = lax.rem(place + flip, 2)
-    across_x, across_y = 1 - step // 2, 1 - lax.rem(step, 2)
+    across_x, across_y = 1 - step // 2, 1 - step % 2
     target_x, target_y = lax.rem(x + across_x, 2), lax.rem(y + across_y, 2)
     return target_y * 4 + target_x * 2 + core
 
@@ -716,21 +716,38 @@
     b_out_ref[...] = dot(left_b_ref[...], b_ref[...], TN).astype(BF16)
 
 
-def keep_kernel(
-    place_ref, left_a_ref, a_ref, left_b_ref, b_ref, a_arrived_ref, b_arrived_ref, *out_refs
-):
-    step = pl.program_id(0)
-    a = dot(left_a_ref[...], a_ref[...], TN) + a_arrived_ref[...].astype(F32)
-    b = dot(left_b_ref[...], b_ref[...], TN) + b_arrived_ref[...].astype(F32)
+def keep_kernel(place_ref, *refs):
+    lefts_a, a_ref, lefts_b, b_ref = refs[:4], refs[4], refs[5:9], refs[9]
+    a_arrived_ref, b_arrived_ref = refs[10:12]
+    out_refs = refs[12:]
+    rows = lefts_a[0].shape[1]
     for i in range(4):
-
-        @pl.when(step == i)
-        def _():
-            out_refs[i][...] = a.astype(BF16)
-            out_refs[4 + i][...] = b.astype(BF16)
+        at = slice(i * rows, (i + 1) * rows)
+        a = dot(lefts_a[i][...], a_ref[...], TN) + a_arrived_ref[at].astype(F32)
+        b = dot(lefts_b[i][...], b_ref[...], TN) + b_arrived_ref[at].astype(F32)
+        out_refs[i][...] = a.astype(BF16)
+        out_refs[4 + i][...] = b.astype(BF16)
+
+
+def at_start(array):
+    return pl.BlockSpec(array.shape, lambda i, place: (0, 0))
 
 
 def pair_specs(left_a, a, left_b, b, flip):
+    def rows(left, k):
+        return pl.BlockSpec(
+            (left.shape[0], left.shape[1] // 8), lambda i, place: (0, block_of(k, place[0], flip))
+        )
+
+    return [
+        *[rows(left_a, k) for k in range(4)],
+        at_start(a),
+        *[rows(left_b, k) for k in range(4)],
+        at_start(b),
+    ]
+
+
+def step_specs(left_a, a, left_b, b, flip):
     def rows(left):
         return pl.BlockSpec(
             (left.shape[0], left.shape[1] // 8), lambda i, place: (0, block_of(i, place[0], flip))
@@ -749,7 +766,7 @@
         grid_spec=pltpu.PrefetchScalarGridSpec(
             num_scalar_prefetch=1,
             grid=(4,),
-            in_specs=pair_specs(left_a, a, left_b, b, 1),
+            in_specs=step_specs(left_a, a, left_b, b, 1),
             out_specs=[
                 pl.BlockSpec((rows, delta.shape[1]), lambda i, place: (i, 0)) for delta in (a, b)
             ],
@@ -765,28 +782,23 @@
 
 def halving_keep(place, left_a, a, left_b, b, a_arrived, b_arrived):
     rows = left_a.shape[1] // 8
+    outs = [
+        jax.ShapeDtypeStruct((rows, delta.shape[1]), BF16) for delta in (a, b) for _ in range(4)
+    ]
     return pl.pallas_call(
         keep_kernel,
         grid_spec=pltpu.PrefetchScalarGridSpec(
             num_scalar_prefetch=1,
-            grid=(4,),
+            grid=(1,),
             in_specs=pair_specs(left_a, a, left_b, b, 0)
-            + [pl.BlockSpec((rows, delta.shape[1]), lambda i, place: (i, 0)) for delta in (a, b)],
-            out_specs=[
-                pl.BlockSpec((rows, delta.shape[1]), lambda i, place: (0, 0))
-                for delta in (a, b)
-                for _ in range(4)
-            ],
+            + [at_start(a_arrived), at_start(b_arrived)],
+            out_specs=[at_start(out) for out in outs],
         ),
-        out_shape=[
-            jax.ShapeDtypeStruct((rows, delta.shape[1]), BF16)
-            for delta in (a, b)
-            for _ in range(4)
-        ],
+        out_shape=outs,
         compiler_params=PARAMS,
         interpret=INTERPRET,
         name="keep_rows",
-    )(place, left_a, a, left_b, b, a_arrived, b_arrived)
+    )(place, *[left_a] * 4, a, *[left_b] * 4, b, a_arrived, b_arrived)
 
 
 def summed(a, b):

time: 209 us -> 206 us (0.986)
  Pallas kernels: 98.2 us -> 94.8 us
    pallas_call x2, Pallas kernels: 17.5 us -> 14.2 us  [halving_keep(): pl.pallas_call(keep_kernel, grid_spec=pltpu.PrefetchScalarGridSpec(num_sc...]
  transfers between devices with their start and end apart: 22 -> 22, of which waited for: 8 -> 8; matrix products, arithmetic and copies ran while one was open for 12% -> 13% of each run, Pallas kernels for 29% -> 28%
where the time goes in v9:
time: 206 us; the launch traced here: 205 us
  Pallas kernels  94.8 us (46%)
  waiting for transfers between devices  32.3 us (16%)
  starting transfers between devices  30.6 us (15%)
  matrix products  17.6 us (9%)
  between operations  14.3 us (7%)
  local copies, waits for them, and re-layouts  7.91 us (4%)
  other arithmetic  7.05 us (3%)
    ppermute x16, waiting for transfers between devices, exchange(): return lax.ppermute(array, 'ctx', [(i, i ^ distance) for i in devices])  26.5 us
    dot_general x3, matrix products, product(): return jnp.einsum(spec, a, b, preferred_element_type=F32)  17.6 us
    pallas_call x1, Pallas kernels, run_backward(): pl.pallas_call(backward_kernel, grid=(chunks // spans,), in_specs=[pl.Blo...  16.9 us
    all_to_all x4, starting transfers between devices, swap(): return lax.all_to_all(parts, 'ctx', split_axis=0, concat_axis=0, tiled=True)  15.7 us
    ppermute x16, starting transfers between devices, exchange(): return lax.ppermute(array, 'ctx', [(i, i ^ distance) for i in devices])  14.6 us
    pallas_call x2, Pallas kernels, halving_keep(): pl.pallas_call(keep_kernel, grid_spec=pltpu.PrefetchScalarGridSpec(num_sc...  14.2 us
    pallas_call x1, Pallas kernels, run_forward(): pl.pallas_call(forward_kernel, grid=(chunks // spans,), in_specs=[pl.Bloc...  13 us
    pallas_call x2, Pallas kernels, halving_start(): pl.pallas_call(send_kernel, grid_spec=pltpu.PrefetchScalarGridSpec(num_sc...  12.9 us
  transfers between devices with their start and end apart: 22, of which 8 were waited for; matrix products, arithmetic and copies ran while one was open for 13% of the time, Pallas kernels for 28%

profile of v9, /device:TPU:0, one launch (start us, length us, event | category | flops | bytes accessed | tf_op | source)
XLA Modules:
  0.0 204.5 jit_solution(14415791304984406312)
XLA Ops:
  7.2 9.9 %projection.1 = (f32[2,512,512]{2,1,0:T(8,128)}, f32[512,1024]{1,0:T(8,128)}, f32[512,16]{1,0:T(8,128)}) custom-call(bf16[512,2048]{1,0:T(8,128)(2,1)} %refs_8_.3, bf16[2,2048,512]{2,1,0:T(8,128)(2,1)} %query_key_weight_ref.3, bf16[2,2048,1024]{2,1,0:T(8,128)(2,1)} %value_gate_weight_ref.1, bf16[2,8,2048]{2,1,0:T(8,128)(2,1)} %bitcast.27), custom_call_target="tpu_custom_call" | custom-call | tf_op jit(solution)/shard_map/projection/pallas_call | solution.py:624
  17.1 13.0 %forward_blocks.1 = (bf16[4,8,128,128]{3,2,1,0:T(8,128)(2,1)}, bf16[4,8,128,256]{3,2,1,0:T(8,128)(2,1)}, bf16[512,1024]{1,0:T(8,128)(2,1)}, f32[512,1024]{1,0:T(8,128)}, bf16[8,128,256]{2,1,0:T(8,128)(2,1)}) custom-call(f32[2,512,512]{2,1,0:T(8,128)} %get-tuple-element.70.query_key_ref, f32[512,1024]{1,0:T(8,128)} %get-tuple-element.71.value_ref, ...), custom_call_target="tpu_custom_call" | custom-call | tf_op jit(solution)/shard_map/forward_blocks/pallas_call | solution.py:442
  30.1 5.2 %all-to-all-start = ((bf16[8,1,128,256]{3,2,1,0:T(8,128)(2,1)}), bf16[8,1,128,256]{3,2,1,0:T(8,128)(2,1)S(1)}, u32[]{:S(2)}, u32[]{:S(2)}) async-start(bf16[8,1,128,256]{3,2,1,0:T(8,128)(2,1)} %bitcast.26), calls=%async_computation | async-start | bytes 1048576 | tf_op jit(solution)/shard_map/all_to_all | solution.py:563
  35.3 5.5 %fusion.3.gate_ref = bf16[512,1024]{1,0:T(8,128)(2,1)} fusion(bf16[512,2048]{1,0:T(8,128)(2,1)S(1)} %copy-done, bf16[2,2048,1024]{2,1,0:T(8,128)(2,1)} %value_gate_weight_ref.1), kind=kOutput, calls=%fused_computation.4 | convolution fusion | flops 2148007936 | bytes 7340032 | tf_op jit(solution)/shard_map/td,df->tf/dot_general | solution.py:593
  40.8 4.2 %all-to-all-done.totals_ref = bf16[8,1,128,256]{3,2,1,0:T(8,128)(2,1)S(1)} async-done(((bf16[8,1,128,256]{3,2,1,0:T(8,128)(2,1)}), bf16[8,1,128,256]{3,2,1,0:T(8,128)(2,1)S(1)}, u32[]{:S(2)}, u32[]{:S(2)}) %all-to-all-start) | async-done | bytes 524320 | tf_op jit(solution)/shard_map/all_to_all | solution.py:563
  45.8 2.8 %chain_forward.1 = bf16[8,1,128,128]{3,2,1,0:T(8,128)(2,1)} custom-call(bf16[8,1,128,256]{3,2,1,0:T(8,128)(2,1)} %copy-done.1), custom_call_target="tpu_custom_call" | custom-call | tf_op jit(solution)/shard_map/chain_forward/pallas_call | solution.py:575
  48.6 3.6 %all-to-all-start.1 = ((bf16[8,1,128,128]{3,2,1,0:T(8,128)(2,1)}), bf16[8,1,128,128]{3,2,1,0:T(8,128)(2,1)S(1)}, u32[]{:S(2)}, u32[]{:S(2)}) async-start(bf16[8,1,128,128]{3,2,1,0:T(8,128)(2,1)} %chain_forward.1), calls=%async_computation.1 | async-start | bytes 524288 | tf_op jit(solution)/shard_map/all_to_all | solution.py:563
  52.2 6.2 %convolution_convert_fusion.1.delta_ref = bf16[512,1024]{1,0:T(8,128)(2,1)} fusion(bf16[512,2048]{1,0:T(8,128)(2,1)} %refs_8_.2, bf16[1024,2048]{1,0:T(8,128)(2,1)} %param.17), kind=kOutput, calls=%fused_computation.5 | convolution fusion | flops 2148007936 | bytes 7340032 | tf_op jit(solution)/shard_map/td,fd->tf/dot_general | solution.py:593
  59.6 6.5 %gated_norm.1 = (bf16[512,1024]{1,0:T(8,128)(2,1)}, bf16[512,1024]{1,0:T(8,128)(2,1)}, bf16[512,1024]{1,0:T(8,128)(2,1)}, bf16[8,128,128]{2,1,0:T(8,128)(2,1)}) custom-call(f32[512,1024]{1,0:T(8,128)} %get-tuple-element.73.local_ref, bf16[512,1024]{1,0:T(8,128)(2,1)} %get-tuple-element.74.map_ref, bf16[512,1024]{1,0:T(8,128)(2,1)} %fusion.3.gate_ref, ...), custom_call_target="tpu_custom_call" | custom-call | tf_op jit(solution)/shard_map/gated_norm/pallas_call | solution.py:479
  66.1 6.3 %send_rows.2 = (bf16[1024,1024]{1,0:T(8,128)(2,1)}, bf16[1024,1024]{1,0:T(8,128)(2,1)}) custom-call(s32[1]{0:T(128)} %bitcast.9.place_ref, bf16[512,2048]{1,0:T(8,128)(2,1)} %refs_8_.3, bf16[512,1024]{1,0:T(8,128)(2,1)} %get-tuple-element.87.a_ref.refs_4_.delta_gate_ref, bf16[512,2048]{1,0:T(8,128)(2,1)} %refs_8_.2, ...), custom_call_target="tpu_custom_call" | custom-call | tf_op jit(solution)/shard_map/send_rows/pallas_call | solution.py:764
  72.9 3.5 %all-to-all-start.2 = ((bf16[8,1,128,128]{3,2,1,0:T(8,128)(2,1)}), bf16[8,1,128,128]{3,2,1,0:T(8,128)(2,1)S(1)}, u32[]{:S(2)}, u32[]{:S(2)}) async-start(bf16[8,1,128,128]{3,2,1,0:T(8,128)(2,1)} %bitcast.29), calls=%async_computation.2 | async-start | bytes 524288 | tf_op jit(solution)/shard_map/all_to_all | solution.py:563
  76.5 5.9 %convolution_convert_fusion = bf16[512,2048]{1,0:T(8,128)(2,1)} fusion(bf16[512,1024]{1,0:T(8,128)(2,1)S(1)} %copy-done.2, bf16[1024,2048]{1,0:T(8,128)(2,1)} %param.17), kind=kOutput, calls=%fused_computation.3 | convolution fusion | flops 2148532224 | bytes 7340032 | tf_op jit(solution)/shard_map/tf,fd->td/dot_general | solution.py:593
  84.0 2.9 %chain_backward.1 = bf16[8,1,128,128]{3,2,1,0:T(8,128)(2,1)} custom-call(bf16[8,1,128,256]{3,2,1,0:T(8,128)(2,1)} %copy-done.1, bf16[8,1,128,128]{3,2,1,0:T(8,128)(2,1)} %copy-done.7), custom_call_target="tpu_custom_call" | custom-call | tf_op jit(solution)/shard_map/chain_backward/pallas_call | solution.py:584
  87.0 3.4 %all-to-all-start.3 = ((bf16[8,1,128,128]{3,2,1,0:T(8,128)(2,1)}), bf16[8,1,128,128]{3,2,1,0:T(8,128)(2,1)S(1)}, u32[]{:S(2)}, u32[]{:S(2)}) async-start(bf16[8,1,128,128]{3,2,1,0:T(8,128)(2,1)} %chain_backward.1), calls=%async_computation.4 | async-start | bytes 524288 | tf_op jit(solution)/shard_map/all_to_all | solution.py:563
  92.0 6.8 %keep_rows.2 = (bf16[256,1024]{1,0:T(8,128)(2,1)}, bf16[256,1024]{1,0:T(8,128)(2,1)}, bf16[256,1024]{1,0:T(8,128)(2,1)}, bf16[256,1024]{1,0:T(8,128)(2,1)}, bf16...) custom-call(s32[1]{0:T(128)} %bitcast.9.place_ref, ...), custom_call_target="tpu_custom_call" | custom-call | tf_op jit(solution)/shard_map/keep_rows/pallas_call | solution.py:788
  98.8 1.7 collective-permute-start.2
  100.5 1.5 collective-permute-start.3
  102.9 16.9 %backward_blocks.1 = (bf16[512,1152]{1,0:T(8,128)(2,1)}, bf16[512,1024]{1,0:T(8,128)(2,1)}) custom-call(f32[2,512,512]{2,1,0:T(8,128)} %get-tuple-element.70.query_key_ref, f32[512,1024]{1,0:T(8,128)} %get-tuple-element.71.value_ref, f32[512,16]{1,0:T(8,128)} %get-tuple-element.72.decay_beta_ref, f32[1,8]{1,0:T(1,128)} %bitcast.33, f32[1,8]{1,0:T(1,128)} %bitcast.35, ...), custom_call_target="tpu_custom_call" | custom-call | tf_op jit(solution)/shard_map/backward_blocks/pallas_call | solution.py:513
  119.9 6.7 %send_rows.3 = (bf16[1024,1024]{1,0:T(8,128)(2,1)}, bf16[1024,1152]{1,0:T(8,128)(2,1)}) custom-call(s32[1]{0:T(128)} %bitcast.9.place_ref, bf16[512,2048]{1,0:T(8,128)(2,1)} %refs_8_.3, bf16[512,1024]{1,0:T(8,128)(2,1)} %get-tuple-element.103.delta_value_ref.a_ref.refs_4_, bf16[512,2048]{1,0:T(8,128)(2,1)} %refs_8_.3, ...), custom_call_target="tpu_custom_call" | custom-call | tf_op jit(solution)/shard_map/send_rows/pallas_call | solution.py:764
  128.2 1.7 collective-permute-start.9
  130.8 1.5 collective-permute-start.8
  132.3 11.7 %input_gradient.1 = bf16[512,2048]{1,0:T(8,128)(2,1)} custom-call(bf16[512,1152]{1,0:T(8,128)(2,1)} %get-tuple-element.99.delta_query_key_ref.b_ref.refs_9_, bf16[512,1024]{1,0:T(8,128)(2,1)} %get-tuple-element.103.delta_value_ref.a_ref.refs_4_, bf16[512,1024]{1,0:T(8,128)(2,1)} %get-tuple-element.87.a_ref.refs_4_.delta_gate_ref, ...), custom_call_target="tpu_custom_call" | custom-call | tf_op jit(solution)/shard_map/input_gradient/pallas_call | solution.py:678
  144.7 1.4 copy-done.3
  146.1 7.4 %keep_rows.3 = (bf16[256,1024]{1,0:T(8,128)(2,1)}, bf16[256,1024]{1,0:T(8,128)(2,1)}, bf16[256,1024]{1,0:T(8,128)(2,1)}, bf16[256,1024]{1,0:T(8,128)(2,1)}, bf16...) custom-call(s32[1]{0:T(128)} %bitcast.9.place_ref, ...), custom_call_target="tpu_custom_call" | custom-call | tf_op jit(solution)/shard_map/keep_rows/pallas_call | solution.py:788
  154.0 1.7 collective-permute-start.14
  158.3 1.5 collective-permute-start.10
  160.3 8.5 %collective-permute-done.11 = bf16[256,1024]{1,0:T(8,128)(2,1)} collective-permute-done((bf16[256,1024]{1,0:T(8,128)(2,1)}, bf16[256,1024]{1,0:T(8,128)(2,1)}, u32[]{:S(2)}, u32[]{:S(2)}) %collective-permute-start.11) | collective-permute-done | bytes 524320 | tf_op jit(solution)/shard_map/ppermute | solution.py:703
  170.0 1.5 collective-permute-start.12
  172.3 7.6 %collective-permute-done.10 = bf16[256,1024]{1,0:T(8,128)(2,1)S(1)} collective-permute-done((bf16[256,1024]{1,0:T(8,128)(2,1)}, bf16[256,1024]{1,0:T(8,128)(2,1)S(1)}, u32[]{:S(2)}, u32[]{:S(2)}) %collective-permute-start.10) | collective-permute-done | bytes 524320 | tf_op jit(solution)/shard_map/ppermute | solution.py:703
  181.1 2.0 collective-permute-done.13
  184.3 7.8 %collective-permute-done.12.refs_1_ = bf16[256,1024]{1,0:T(8,128)(2,1)S(1)} collective-permute-done((bf16[256,1024]{1,0:T(8,128)(2,1)S(1)}, bf16[256,1024]{1,0:T(8,128)(2,1)S(1)}, u32[]{:S(2)}, u32[]{:S(2)}) %collective-permute-start.12) | collective-permute-done | bytes 524320 | tf_op jit(solution)/shard_map/ppermute | solution.py:703
  193.8 3.8 %finish.1 = (f32[2,256,512]{2,1,0:T(8,128)}, f32[2,256,1024]{2,1,0:T(8,128)}, f32[2,8,256]{2,1,0:T(8,128)}) custom-call(f32[256,1024]{1,0:T(8,128)} %convert_add_fusion.1.refs_0_, bf16[256,1024]{1,0:T(8,128)(2,1)} %copy-done.18, bf16[256,1024]{1,0:T(8,128)(2,1)} %get-tuple-element.121.refs_2_, bf16[256,1024]{1,0:T(8,128)(2,1)} %copy-done.11, ...), custom_call_target="tpu_custom_call" | custom-call | tf_op jit(solution)/shard_map/finish/pallas_call | solution.py:851
  (79 shorter events, 19.6 us)
Async XLA Ops:
  17.1 18.2 %copy-start = (bf16[512,2048]{1,0:T(8,128)(2,1)S(1)}, bf16[512,2048]{1,0:T(8,128)(2,1)}, u32[]{:S(2)}) copy-start(bf16[512,2048]{1,0:T(8,128)(2,1)} %refs_8_.3) | copy-start | bytes 6291460
  30.1 14.9 %all-to-all-start = ((bf16[8,1,128,256]{3,2,1,0:T(8,128)(2,1)}), bf16[8,1,128,256]{3,2,1,0:T(8,128)(2,1)S(1)}, u32[]{:S(2)}, u32[]{:S(2)}) async-start(bf16[8,1,128,256]{3,2,1,0:T(8,128)(2,1)} %bitcast.26), calls=%async_computation | async-start | bytes 1048576 | tf_op jit(solution)/shard_map/all_to_all | solution.py:563
  48.6 10.3 %all-to-all-start.1 = ((bf16[8,1,128,128]{3,2,1,0:T(8,128)(2,1)}), bf16[8,1,128,128]{3,2,1,0:T(8,128)(2,1)S(1)}, u32[]{:S(2)}, u32[]{:S(2)}) async-start(bf16[8,1,128,128]{3,2,1,0:T(8,128)(2,1)} %chain_forward.1), calls=%async_computation.1 | async-start | bytes 524288 | tf_op jit(solution)/shard_map/all_to_all | solution.py:563
  66.1 10.3 %copy-start.2 = (bf16[512,1024]{1,0:T(8,128)(2,1)S(1)}, bf16[512,1024]{1,0:T(8,128)(2,1)}, u32[]{:S(2)}) copy-start(bf16[512,1024]{1,0:T(8,128)(2,1)} %get-tuple-element.81.b_ref.refs_9_) | copy-start | bytes 3145732
  72.4 18.3 %collective-permute-start = (bf16[1024,1024]{1,0:T(8,128)(2,1)}, bf16[1024,1024]{1,0:T(8,128)(2,1)S(1)}, u32[]{:S(2)}, u32[]{:S(2)}) collective-permute-start(bf16[1024,1024]{1,0:T(8,128)(2,1)} %get-tuple-element.88), channel_id=1, source_target_pairs={{0,4},{4,0},{8,12},{12,8},{16,20},{20,16},{24,28},{28,24},{1,5},{5... | collective-permute-start | bytes 6291464 | tf_op jit(solution)/shard_map/ppermute | solution.py:703
  72.4 18.3 %collective-permute-start.1 = (bf16[1024,1024]{1,0:T(8,128)(2,1)}, bf16[1024,1024]{1,0:T(8,128)(2,1)}, u32[]{:S(2)}, u32[]{:S(2)}) collective-permute-start(bf16[1024,1024]{1,0:T(8,128)(2,1)} %get-tuple-element.89), channel_id=1, source_target_pairs={{0,4},{4,0},{8,12},{12,8},{16,20},{20,16},{24,28},{28,24},{1,5},{5... | collective-permute-start | bytes 6291464 | tf_op jit(solution)/shard_map/ppermute | solution.py:703
  72.9 10.4 %all-to-all-start.2 = ((bf16[8,1,128,128]{3,2,1,0:T(8,128)(2,1)}), bf16[8,1,128,128]{3,2,1,0:T(8,128)(2,1)S(1)}, u32[]{:S(2)}, u32[]{:S(2)}) async-start(bf16[8,1,128,128]{3,2,1,0:T(8,128)(2,1)} %bitcast.29), calls=%async_computation.2 | async-start | bytes 524288 | tf_op jit(solution)/shard_map/all_to_all | solution.py:563
  76.4 121.3 %reduce-scatter.3.cloned.1.call-start = ((), (), s32[]{:S(2)}) async-start(), calls=%async_computation.6 | async-start | bytes 2621440 | tf_op jit(solution)/shard_map/reduce_scatter | solution.py:872
  87.0 11.8 %all-to-all-start.3 = ((bf16[8,1,128,128]{3,2,1,0:T(8,128)(2,1)}), bf16[8,1,128,128]{3,2,1,0:T(8,128)(2,1)S(1)}, u32[]{:S(2)}, u32[]{:S(2)}) async-start(bf16[8,1,128,128]{3,2,1,0:T(8,128)(2,1)} %chain_backward.1), calls=%async_computation.4 | async-start | bytes 524288 | tf_op jit(solution)/shard_map/all_to_all | solution.py:563
  90.4 107.3 %reduce-scatter.5.cloned.1.call-start = ((), (), s32[]{:S(2)}) async-start(), calls=%async_computation.7 | async-start | bytes 2621440 | tf_op jit(solution)/shard_map/reduce_scatter | solution.py:872
  98.8 21.1 %collective-permute-start.2 = (bf16[256,1024]{1,0:T(8,128)(2,1)}, bf16[256,1024]{1,0:T(8,128)(2,1)S(1)}, u32[]{:S(2)}, u32[]{:S(2)}) collective-permute-start(bf16[256,1024]{1,0:T(8,128)(2,1)} %get-tuple-element.101), channel_id=1, source_target_pairs={{0,8},{4,12},{8,0},{12,4},{16,24},{20,28},{24,16},{28,20},{1,9},{5... | collective-permute-start | bytes 1572872 | tf_op jit(solution)/shard_map/ppermute | solution.py:703
  100.5 19.3 %collective-permute-start.3 = (bf16[256,1024]{1,0:T(8,128)(2,1)}, bf16[256,1024]{1,0:T(8,128)(2,1)S(1)}, u32[]{:S(2)}, u32[]{:S(2)}) collective-permute-start(bf16[256,1024]{1,0:T(8,128)(2,1)} %get-tuple-element.102), channel_id=1, source_target_pairs={{0,16},{4,20},{8,24},{12,28},{16,0},{20,4},{24,8},{28,12},{1,17},{... | collective-permute-start | bytes 1572872 | tf_op jit(solution)/shard_map/ppermute | solution.py:703
  102.0 24.6 %collective-permute-start.4 = (bf16[256,1024]{1,0:T(8,128)(2,1)}, bf16[256,1024]{1,0:T(8,128)(2,1)S(1)}, u32[]{:S(2)}, u32[]{:S(2)}) collective-permute-start(bf16[256,1024]{1,0:T(8,128)(2,1)} %get-tuple-element.106), channel_id=1, source_target_pairs={{0,8},{4,12},{8,0},{12,4},{16,24},{20,28},{24,16},{28,20},{1,9},{5... | collective-permute-start | bytes 1572872 | tf_op jit(solution)/shard_map/ppermute | solution.py:703
  102.6 24.0 %collective-permute-start.5 = (bf16[256,1024]{1,0:T(8,128)(2,1)}, bf16[256,1024]{1,0:T(8,128)(2,1)S(1)}, u32[]{:S(2)}, u32[]{:S(2)}) collective-permute-start(bf16[256,1024]{1,0:T(8,128)(2,1)} %get-tuple-element.107), channel_id=1, source_target_pairs={{0,16},{4,20},{8,24},{12,28},{16,0},{20,4},{24,8},{28,12},{1,17},{... | collective-permute-start | bytes 1572872 | tf_op jit(solution)/shard_map/ppermute | solution.py:703
  119.9 10.0 %copy-start.16 = (bf16[256,1024]{1,0:T(8,128)(2,1)S(1)}, bf16[256,1024]{1,0:T(8,128)(2,1)}, u32[]{:S(2)}) copy-start(bf16[256,1024]{1,0:T(8,128)(2,1)} %get-tuple-element.110) | copy-start | bytes 1572868
  126.6 17.5 %copy-start.11 = (bf16[256,1024]{1,0:T(8,128)(2,1)}, bf16[256,1024]{1,0:T(8,128)(2,1)S(1)}, u32[]{:S(2)}) copy-start(bf16[256,1024]{1,0:T(8,128)(2,1)S(1)} %collective-permute-done.4.refs_3_) | copy-start | bytes 1572868
  126.6 18.1 %collective-permute-start.7 = (bf16[1024,1152]{1,0:T(8,128)(2,1)}, bf16[1024,1152]{1,0:T(8,128)(2,1)S(1)}, u32[]{:S(2)}, u32[]{:S(2)}) collective-permute-start(bf16[1024,1152]{1,0:T(8,128)(2,1)} %get-tuple-element.109), channel_id=1, source_target_pairs={{0,4},{4,0},{8,12},{12,8},{16,20},{20,16},{24,28},{28,24},{1,5},{5... | collective-permute-start | bytes 7077896 | tf_op jit(solution)/shard_map/ppermute | solution.py:703
  126.7 18.0 %collective-permute-start.6 = (bf16[1024,1024]{1,0:T(8,128)(2,1)}, bf16[1024,1024]{1,0:T(8,128)(2,1)}, u32[]{:S(2)}, u32[]{:S(2)}) collective-permute-start(bf16[1024,1024]{1,0:T(8,128)(2,1)} %get-tuple-element.108), channel_id=1, source_target_pairs={{0,4},{4,0},{8,12},{12,8},{16,20},{20,16},{24,28},{28,24},{1,5},{5... | collective-permute-start | bytes 6291464 | tf_op jit(solution)/shard_map/ppermute | solution.py:703
  128.2 15.9 %collective-permute-start.9 = (bf16[256,1024]{1,0:T(8,128)(2,1)}, bf16[256,1024]{1,0:T(8,128)(2,1)}, u32[]{:S(2)}, u32[]{:S(2)}) collective-permute-start(bf16[256,1024]{1,0:T(8,128)(2,1)} %add_convert_fusion.2), channel_id=1, source_target_pairs={{0,8},{4,12},{8,0},{12,4},{16,24},{20,28},{24,16},{28,20},{1,9},{5... | collective-permute-start | bytes 1572872 | tf_op jit(solution)/shard_map/ppermute | solution.py:703
  130.8 13.8 %collective-permute-start.8 = (bf16[256,1024]{1,0:T(8,128)(2,1)}, bf16[256,1024]{1,0:T(8,128)(2,1)S(1)}, u32[]{:S(2)}, u32[]{:S(2)}) collective-permute-start(bf16[256,1024]{1,0:T(8,128)(2,1)} %add_convert_fusion.3), channel_id=1, source_target_pairs={{0,16},{4,20},{8,24},{12,28},{16,0},{20,4},{24,8},{28,12},{1,17},{... | collective-permute-start | bytes 1572872 | tf_op jit(solution)/shard_map/ppermute | solution.py:703
  146.1 9.5 %copy-start.12 = (bf16[256,1024]{1,0:T(8,128)(2,1)S(1)}, bf16[256,1024]{1,0:T(8,128)(2,1)}, u32[]{:S(2)}) copy-start(bf16[256,1024]{1,0:T(8,128)(2,1)} %get-tuple-element.131) | copy-start | bytes 1572868
  146.1 9.5 %copy-start.15 = (bf16[256,1024]{1,0:T(8,128)(2,1)S(1)}, bf16[256,1024]{1,0:T(8,128)(2,1)}, u32[]{:S(2)}) copy-start(bf16[256,1024]{1,0:T(8,128)(2,1)} %copy-done.14) | copy-start | bytes 1572868
  153.5 15.2 %collective-permute-start.11 = (bf16[256,1024]{1,0:T(8,128)(2,1)}, bf16[256,1024]{1,0:T(8,128)(2,1)}, u32[]{:S(2)}, u32[]{:S(2)}) collective-permute-start(bf16[256,1024]{1,0:T(8,128)(2,1)} %get-tuple-element.120), channel_id=1, source_target_pairs={{0,8},{4,12},{8,0},{12,4},{16,24},{20,28},{24,16},{28,20},{1,9},{5... | collective-permute-start | bytes 1572872 | tf_op jit(solution)/shard_map/ppermute | solution.py:703
  154.0 14.8 %copy-start.19 = (bf16[256,1024]{1,0:T(8,128)(2,1)S(1)}, bf16[256,1024]{1,0:T(8,128)(2,1)}, u32[]{:S(2)}) copy-start(bf16[256,1024]{1,0:T(8,128)(2,1)} %get-tuple-element.119) | copy-start | bytes 1572868
  154.0 17.6 %collective-permute-start.14 = (bf16[256,1152]{1,0:T(8,128)(2,1)}, bf16[256,1152]{1,0:T(8,128)(2,1)S(1)}, u32[]{:S(2)}, u32[]{:S(2)}) collective-permute-start(bf16[256,1152]{1,0:T(8,128)(2,1)} %get-tuple-element.127), channel_id=1, source_target_pairs={{0,16},{4,20},{8,24},{12,28},{16,0},{20,4},{24,8},{28,12},{1,17},{... | collective-permute-start | bytes 1769480 | tf_op jit(solution)/shard_map/ppermute | solution.py:703
  157.0 14.6 %copy-start.9 = (bf16[256,1152]{1,0:T(8,128)(2,1)S(1)}, bf16[256,1152]{1,0:T(8,128)(2,1)}, u32[]{:S(2)}) copy-start(bf16[256,1152]{1,0:T(8,128)(2,1)} %get-tuple-element.126) | copy-start | bytes 1769476
  158.3 21.6 %copy-start.20 = (bf16[256,1024]{1,0:T(8,128)(2,1)S(1)}, bf16[256,1024]{1,0:T(8,128)(2,1)}, u32[]{:S(2)}) copy-start(bf16[256,1024]{1,0:T(8,128)(2,1)} %get-tuple-element.117) | copy-start | bytes 1572868
  158.3 21.6 %collective-permute-start.10 = (bf16[256,1024]{1,0:T(8,128)(2,1)}, bf16[256,1024]{1,0:T(8,128)(2,1)S(1)}, u32[]{:S(2)}, u32[]{:S(2)}) collective-permute-start(bf16[256,1024]{1,0:T(8,128)(2,1)} %get-tuple-element.118), channel_id=1, source_target_pairs={{0,8},{4,12},{8,0},{12,4},{16,24},{20,28},{24,16},{28,20},{1,9},{5... | collective-permute-start | bytes 1572872 | tf_op jit(solution)/shard_map/ppermute | solution.py:703
  159.7 23.3 %collective-permute-start.13 = (bf16[256,1152]{1,0:T(8,128)(2,1)}, bf16[256,1152]{1,0:T(8,128)(2,1)S(1)}, u32[]{:S(2)}, u32[]{:S(2)}) collective-permute-start(bf16[256,1152]{1,0:T(8,128)(2,1)} %get-tuple-element.125), channel_id=1, source_target_pairs={{0,16},{4,20},{8,24},{12,28},{16,0},{20,4},{24,8},{28,12},{1,17},{... | collective-permute-start | bytes 1769480 | tf_op jit(solution)/shard_map/ppermute | solution.py:703
  170.0 13.1 %copy-start.10 = (bf16[256,1152]{1,0:T(8,128)(2,1)S(1)}, bf16[256,1152]{1,0:T(8,128)(2,1)}, u32[]{:S(2)}) copy-start(bf16[256,1152]{1,0:T(8,128)(2,1)} %get-tuple-element.124) | copy-start | bytes 1769476
  170.0 22.1 %collective-permute-start.12 = (bf16[256,1024]{1,0:T(8,128)(2,1)S(1)}, bf16[256,1024]{1,0:T(8,128)(2,1)S(1)}, u32[]{:S(2)}, u32[]{:S(2)}) collective-permute-start(bf16[256,1024]{1,0:T(8,128)(2,1)S(1)} %add_convert_fusion.1), channel_id=1, source_target_pairs={{0,16},{4,20},{8,24},{12,28},{16,0},{20,4},{24,8},{28,12},{1,17},{... | collective-permute-start | bytes 1572872 | tf_op jit(solution)/shard_map/ppermute | solution.py:703
  171.7 20.4 %collective-permute-start.15 = (bf16[256,1152]{1,0:T(8,128)(2,1)S(1)}, bf16[256,1152]{1,0:T(8,128)(2,1)S(1)}, u32[]{:S(2)}, u32[]{:S(2)}) collective-permute-start(bf16[256,1152]{1,0:T(8,128)(2,1)S(1)} %add_convert_fusion), channel_id=1, source_target_pairs={{0,8},{4,12},{8,0},{12,4},{16,24},{20,28},{24,16},{28,20},{1,9},{5... | collective-permute-start | bytes 1769480 | tf_op jit(solution)/shard_map/ppermute | solution.py:703
  (11 other events, 30.2 us)
Sparse Core Ops, SparseCore 0:
  83.5 44.5 reduce-scatter.2
  144.8 44.1 reduce-scatter.4

commit v10 on v9

--- a/solution.py
+++ b/solution.py
@@ -154,7 +154,7 @@
     weights = {}
     for c, h in each:
         k = keys[c, h // repeat]
-        v = value_ref[rows[c], h * DV : (h + 1) * DV]
+        v = value_ref[rows[c], h * DV : (h + 1) * DV].astype(F32)
         b = betas[c, h]
         right = jnp.concatenate([(b * starts[c, h]) * k, b * v], axis=1)
         weights[c, h] = dot(inverse[c, h], right)
@@ -173,7 +173,7 @@
             state = state_ref[h]
             out = dot(starts[c, h] * q, state) + dot(scores[c, h], values[h])
             map_ref[rows[c], h * DK : (h + 1) * DK] = out[:, :DK].astype(BF16)
-            local_ref[rows[c], h * DV : (h + 1) * DV] = out[:, DK:]
+            local_ref[rows[c], h * DV : (h + 1) * DV] = out[:, DK:].astype(BF16)
             state = total[:, h : h + 1] * state + dot(spread_column(end, h) * k, values[h], TN)
             state_ref[h] = state
             total_ref[h] = state.astype(BF16)
@@ -202,7 +202,7 @@
     outs, deltas = [], []
     for h in range(heads):
         cols = slice(h * DV, (h + 1) * DV)
-        outs.append(local_ref[:, cols] + dot(map_ref[:, cols], state_ref[h]))
+        outs.append(local_ref[:, cols].astype(F32) + dot(map_ref[:, cols], state_ref[h]))
     for h in range(heads):
         cols = slice(h * DV, (h + 1) * DV)
         out = outs[h]
@@ -289,7 +289,9 @@
         betas[c, h] = spread_column(beta, h)
         starts[c, h] = spread_column(start, h)
         ends[c, h] = spread_column(end, h)
-        right_of[c, h] = betas[c, h] * (value_ref[rows[c], cols[h]] - starts[c, h] * seen)
+        right_of[c, h] = betas[c, h] * (
+            value_ref[rows[c], cols[h]].astype(F32) - starts[c, h] * seen
+        )
     for c, h in each:
         value_of[c, h] = dot(solve_ref[c, h], right_of[c, h]).astype(BF16)
     decay_of, delta_value_of, delta_right_of = {}, {}, {}
@@ -461,7 +463,7 @@
             jax.ShapeDtypeStruct((chunks, heads, CHUNK, CHUNK), BF16),
             jax.ShapeDtypeStruct((chunks, heads, DK, DK + DV), BF16),
             jax.ShapeDtypeStruct((tokens, value_width), BF16),
-            jax.ShapeDtypeStruct((tokens, value_width), F32),
+            jax.ShapeDtypeStruct((tokens, value_width), BF16),
             jax.ShapeDtypeStruct((heads, DK, DK + DV), BF16),
         ],
         scratch_shapes=[pltpu.VMEM((heads, DK, DK + DV), F32)],
@@ -608,7 +610,7 @@
 ):
     inputs = inputs_ref[...]
     query_key_ref[0] = dot(inputs, query_key_weight_ref[0])
-    value_ref[...] = dot(inputs, value_weight_ref[0])
+    value_ref[...] = dot(inputs, value_weight_ref[0]).astype(BF16)
 
     @pl.when(pl.program_id(0) == 0)
     def _():
@@ -637,7 +639,7 @@
         ],
         out_shape=[
             jax.ShapeDtypeStruct((2, tokens, key_width), F32),
-            jax.ShapeDtypeStruct((tokens, value_width), F32),
+            jax.ShapeDtypeStruct((tokens, value_width), BF16),
             jax.ShapeDtypeStruct((tokens, 2 * heads), F32),
         ],
         compiler_params=PARAMS,

time: 206 us -> 205 us (level)
  no operation moved by 1% of the time
where the time goes in v10:
time: 205 us; the launch traced here: 204 us
  Pallas kernels  93.8 us (46%)
  waiting for transfers between devices  32.3 us (16%)
  starting transfers between devices  30.6 us (15%)
  matrix products  17.6 us (9%)
  between operations  14.3 us (7%)
  local copies, waits for them, and re-layouts  7.95 us (4%)
  other arithmetic  7.02 us (3%)
    ppermute x16, waiting for transfers between devices, exchange(): return lax.ppermute(array, 'ctx', [(i, i ^ distance) for i in devices])  26.5 us
    dot_general x3, matrix products, product(): return jnp.einsum(spec, a, b, preferred_element_type=F32)  17.6 us
    pallas_call x1, Pallas kernels, run_backward(): pl.pallas_call(backward_kernel, grid=(chunks // spans,), in_specs=[pl.Blo...  16.7 us
    all_to_all x4, starting transfers between devices, swap(): return lax.all_to_all(parts, 'ctx', split_axis=0, concat_axis=0, tiled=True)  15.6 us
    ppermute x16, starting transfers between devices, exchange(): return lax.ppermute(array, 'ctx', [(i, i ^ distance) for i in devices])  14.6 us
    pallas_call x2, Pallas kernels, halving_keep(): pl.pallas_call(keep_kernel, grid_spec=pltpu.PrefetchScalarGridSpec(num_sc...  14.2 us
    pallas_call x2, Pallas kernels, halving_start(): pl.pallas_call(send_kernel, grid_spec=pltpu.PrefetchScalarGridSpec(num_sc...  12.9 us
    pallas_call x1, Pallas kernels, run_forward(): pl.pallas_call(forward_kernel, grid=(chunks // spans,), in_specs=[pl.Bloc...  12.6 us
  transfers between devices with their start and end apart: 22, of which 8 were waited for; matrix products, arithmetic and copies ran while one was open for 13% of the time, Pallas kernels for 28%

profile of v10, /device:TPU:0, one launch (start us, length us, event | category | flops | bytes accessed | tf_op | source)
XLA Modules:
  0.0 203.5 jit_solution(4109041130691818076)
XLA Ops:
  7.2 9.7 %projection.1 = (f32[2,512,512]{2,1,0:T(8,128)}, bf16[512,1024]{1,0:T(8,128)(2,1)}, f32[512,16]{1,0:T(8,128)}) custom-call(bf16[512,2048]{1,0:T(8,128)(2,1)} %refs_8_.3, bf16[2,2048,512]{2,1,0:T(8,128)(2,1)} %query_key_weight_ref.3, bf16[2,2048,1024]{2,1,0:T(8,128)(2,1)} %value_gate_weight_ref.1, bf16[2,8,2048]{2,1,0:T(8,128)(2,1)} %bitcast.27), custom_call_target="tpu_custom_call" | custom-call | tf_op jit(solution)/shard_map/projection/pallas_call | solution.py:626
  16.9 12.6 %forward_blocks.1 = (bf16[4,8,128,128]{3,2,1,0:T(8,128)(2,1)}, bf16[4,8,128,256]{3,2,1,0:T(8,128)(2,1)}, bf16[512,1024]{1,0:T(8,128)(2,1)}, bf16[512,1024]{1,0:T(8,128)(2,1)}, bf16[8,128,256]{2,1,0:T(8,128)(2,1)}) custom-call(f32[2,512,512]{2,1,0:T(8,128)} %get-tuple-element.70.query_key_ref, bf16[512,1024]{1,0:T(8,128)(2,1)} %get-tuple-element.71.value_ref, ...), custom_call_target="tpu_custom_call" | custom-call | tf_op jit(solution)/shard_map/forward_blocks/pallas_call | solution.py:444
  29.6 5.2 %all-to-all-start = ((bf16[8,1,128,256]{3,2,1,0:T(8,128)(2,1)}), bf16[8,1,128,256]{3,2,1,0:T(8,128)(2,1)S(1)}, u32[]{:S(2)}, u32[]{:S(2)}) async-start(bf16[8,1,128,256]{3,2,1,0:T(8,128)(2,1)} %bitcast.26), calls=%async_computation | async-start | bytes 1048576 | tf_op jit(solution)/shard_map/all_to_all | solution.py:565
  34.7 5.5 %fusion.3.gate_ref = bf16[512,1024]{1,0:T(8,128)(2,1)} fusion(bf16[512,2048]{1,0:T(8,128)(2,1)S(1)} %copy-done, bf16[2,2048,1024]{2,1,0:T(8,128)(2,1)} %value_gate_weight_ref.1), kind=kOutput, calls=%fused_computation.4 | convolution fusion | flops 2148007936 | bytes 7340032 | tf_op jit(solution)/shard_map/td,df->tf/dot_general | solution.py:595
  40.2 4.2 %all-to-all-done.totals_ref = bf16[8,1,128,256]{3,2,1,0:T(8,128)(2,1)S(1)} async-done(((bf16[8,1,128,256]{3,2,1,0:T(8,128)(2,1)}), bf16[8,1,128,256]{3,2,1,0:T(8,128)(2,1)S(1)}, u32[]{:S(2)}, u32[]{:S(2)}) %all-to-all-start) | async-done | bytes 524320 | tf_op jit(solution)/shard_map/all_to_all | solution.py:565
  45.3 2.8 %chain_forward.1 = bf16[8,1,128,128]{3,2,1,0:T(8,128)(2,1)} custom-call(bf16[8,1,128,256]{3,2,1,0:T(8,128)(2,1)} %copy-done.1), custom_call_target="tpu_custom_call" | custom-call | tf_op jit(solution)/shard_map/chain_forward/pallas_call | solution.py:577
  48.1 3.6 %all-to-all-start.1 = ((bf16[8,1,128,128]{3,2,1,0:T(8,128)(2,1)}), bf16[8,1,128,128]{3,2,1,0:T(8,128)(2,1)S(1)}, u32[]{:S(2)}, u32[]{:S(2)}) async-start(bf16[8,1,128,128]{3,2,1,0:T(8,128)(2,1)} %chain_forward.1), calls=%async_computation.1 | async-start | bytes 524288 | tf_op jit(solution)/shard_map/all_to_all | solution.py:565
  51.7 6.2 %convolution_convert_fusion.1.delta_ref = bf16[512,1024]{1,0:T(8,128)(2,1)} fusion(bf16[512,2048]{1,0:T(8,128)(2,1)} %refs_8_.2, bf16[1024,2048]{1,0:T(8,128)(2,1)} %param.17), kind=kOutput, calls=%fused_computation.5 | convolution fusion | flops 2148007936 | bytes 7340032 | tf_op jit(solution)/shard_map/td,fd->tf/dot_general | solution.py:595
  59.1 6.3 %gated_norm.1 = (bf16[512,1024]{1,0:T(8,128)(2,1)}, bf16[512,1024]{1,0:T(8,128)(2,1)}, bf16[512,1024]{1,0:T(8,128)(2,1)}, bf16[8,128,128]{2,1,0:T(8,128)(2,1)}) custom-call(bf16[512,1024]{1,0:T(8,128)(2,1)} %get-tuple-element.73.local_ref, bf16[512,1024]{1,0:T(8,128)(2,1)} %get-tuple-element.74.map_ref, bf16[512,1024]{1,0:T(8,128)(2,1)} %fusion.3.gate_ref, ...), custom_call_target="tpu_custom_call" | custom-call | tf_op jit(solution)/shard_map/gated_norm/pallas_call | solution.py:481
  65.4 6.2 %send_rows.2 = (bf16[1024,1024]{1,0:T(8,128)(2,1)}, bf16[1024,1024]{1,0:T(8,128)(2,1)}) custom-call(s32[1]{0:T(128)} %bitcast.9.place_ref, bf16[512,2048]{1,0:T(8,128)(2,1)} %refs_8_.3, bf16[512,1024]{1,0:T(8,128)(2,1)} %get-tuple-element.87.a_ref.refs_4_.delta_gate_ref, bf16[512,2048]{1,0:T(8,128)(2,1)} %refs_8_.2, ...), custom_call_target="tpu_custom_call" | custom-call | tf_op jit(solution)/shard_map/send_rows/pallas_call | solution.py:766
  72.2 3.5 %all-to-all-start.2 = ((bf16[8,1,128,128]{3,2,1,0:T(8,128)(2,1)}), bf16[8,1,128,128]{3,2,1,0:T(8,128)(2,1)S(1)}, u32[]{:S(2)}, u32[]{:S(2)}) async-start(bf16[8,1,128,128]{3,2,1,0:T(8,128)(2,1)} %bitcast.29), calls=%async_computation.2 | async-start | bytes 524288 | tf_op jit(solution)/shard_map/all_to_all | solution.py:565
  75.7 5.9 %convolution_convert_fusion = bf16[512,2048]{1,0:T(8,128)(2,1)} fusion(bf16[512,1024]{1,0:T(8,128)(2,1)S(1)} %copy-done.2, bf16[1024,2048]{1,0:T(8,128)(2,1)} %param.17), kind=kOutput, calls=%fused_computation.3 | convolution fusion | flops 2148532224 | bytes 7340032 | tf_op jit(solution)/shard_map/tf,fd->td/dot_general | solution.py:595
  83.3 3.0 %chain_backward.1 = bf16[8,1,128,128]{3,2,1,0:T(8,128)(2,1)} custom-call(bf16[8,1,128,256]{3,2,1,0:T(8,128)(2,1)} %copy-done.1, bf16[8,1,128,128]{3,2,1,0:T(8,128)(2,1)} %copy-done.7), custom_call_target="tpu_custom_call" | custom-call | tf_op jit(solution)/shard_map/chain_backward/pallas_call | solution.py:586
  86.3 3.4 %all-to-all-start.3 = ((bf16[8,1,128,128]{3,2,1,0:T(8,128)(2,1)}), bf16[8,1,128,128]{3,2,1,0:T(8,128)(2,1)S(1)}, u32[]{:S(2)}, u32[]{:S(2)}) async-start(bf16[8,1,128,128]{3,2,1,0:T(8,128)(2,1)} %chain_backward.1), calls=%async_computation.4 | async-start | bytes 524288 | tf_op jit(solution)/shard_map/all_to_all | solution.py:565
  91.3 6.8 %keep_rows.2 = (bf16[256,1024]{1,0:T(8,128)(2,1)}, bf16[256,1024]{1,0:T(8,128)(2,1)}, bf16[256,1024]{1,0:T(8,128)(2,1)}, bf16[256,1024]{1,0:T(8,128)(2,1)}, bf16...) custom-call(s32[1]{0:T(128)} %bitcast.9.place_ref, ...), custom_call_target="tpu_custom_call" | custom-call | tf_op jit(solution)/shard_map/keep_rows/pallas_call | solution.py:790
  98.1 1.7 collective-permute-start.2
  99.9 1.5 collective-permute-start.3
  102.3 16.7 %backward_blocks.1 = (bf16[512,1152]{1,0:T(8,128)(2,1)}, bf16[512,1024]{1,0:T(8,128)(2,1)}) custom-call(f32[2,512,512]{2,1,0:T(8,128)} %get-tuple-element.70.query_key_ref, bf16[512,1024]{1,0:T(8,128)(2,1)} %get-tuple-element.71.value_ref, f32[512,16]{1,0:T(8,128)} %get-tuple-element.72.decay_beta_ref, f32[1,8]{1,0:T(1,128)} %bitcast.33, f32[1,8]{1,0:T(1,128)} %bitcast.35, ...), custom_call_target="tpu_custom_call" | custom-call | tf_op jit(solution)/shard_map/backward_blocks/pallas_call | solution.py:515
  119.0 6.7 %send_rows.3 = (bf16[1024,1024]{1,0:T(8,128)(2,1)}, bf16[1024,1152]{1,0:T(8,128)(2,1)}) custom-call(s32[1]{0:T(128)} %bitcast.9.place_ref, bf16[512,2048]{1,0:T(8,128)(2,1)} %refs_8_.3, bf16[512,1024]{1,0:T(8,128)(2,1)} %get-tuple-element.103.delta_value_ref.a_ref.refs_4_, bf16[512,2048]{1,0:T(8,128)(2,1)} %refs_8_.3, ...), custom_call_target="tpu_custom_call" | custom-call | tf_op jit(solution)/shard_map/send_rows/pallas_call | solution.py:766
  127.2 1.7 collective-permute-start.9
  129.9 1.5 collective-permute-start.8
  131.4 11.7 %input_gradient.1 = bf16[512,2048]{1,0:T(8,128)(2,1)} custom-call(bf16[512,1152]{1,0:T(8,128)(2,1)} %get-tuple-element.99.delta_query_key_ref.b_ref.refs_9_, bf16[512,1024]{1,0:T(8,128)(2,1)} %get-tuple-element.103.delta_value_ref.a_ref.refs_4_, bf16[512,1024]{1,0:T(8,128)(2,1)} %get-tuple-element.87.a_ref.refs_4_.delta_gate_ref, ...), custom_call_target="tpu_custom_call" | custom-call | tf_op jit(solution)/shard_map/input_gradient/pallas_call | solution.py:680
  143.8 1.4 copy-done.3
  145.2 7.4 %keep_rows.3 = (bf16[256,1024]{1,0:T(8,128)(2,1)}, bf16[256,1024]{1,0:T(8,128)(2,1)}, bf16[256,1024]{1,0:T(8,128)(2,1)}, bf16[256,1024]{1,0:T(8,128)(2,1)}, bf16...) custom-call(s32[1]{0:T(128)} %bitcast.9.place_ref, ...), custom_call_target="tpu_custom_call" | custom-call | tf_op jit(solution)/shard_map/keep_rows/pallas_call | solution.py:790
  153.0 1.7 collective-permute-start.14
  157.3 1.5 collective-permute-start.10
  159.4 8.5 %collective-permute-done.11 = bf16[256,1024]{1,0:T(8,128)(2,1)} collective-permute-done((bf16[256,1024]{1,0:T(8,128)(2,1)}, bf16[256,1024]{1,0:T(8,128)(2,1)}, u32[]{:S(2)}, u32[]{:S(2)}) %collective-permute-start.11) | collective-permute-done | bytes 524320 | tf_op jit(solution)/shard_map/ppermute | solution.py:705
  169.1 1.6 collective-permute-start.12
  171.4 7.6 %collective-permute-done.10 = bf16[256,1024]{1,0:T(8,128)(2,1)S(1)} collective-permute-done((bf16[256,1024]{1,0:T(8,128)(2,1)}, bf16[256,1024]{1,0:T(8,128)(2,1)S(1)}, u32[]{:S(2)}, u32[]{:S(2)}) %collective-permute-start.10) | collective-permute-done | bytes 524320 | tf_op jit(solution)/shard_map/ppermute | solution.py:705
  180.2 2.0 collective-permute-done.13
  183.4 7.8 %collective-permute-done.12.refs_1_ = bf16[256,1024]{1,0:T(8,128)(2,1)S(1)} collective-permute-done((bf16[256,1024]{1,0:T(8,128)(2,1)S(1)}, bf16[256,1024]{1,0:T(8,128)(2,1)S(1)}, u32[]{:S(2)}, u32[]{:S(2)}) %collective-permute-start.12) | collective-permute-done | bytes 524320 | tf_op jit(solution)/shard_map/ppermute | solution.py:705
  192.8 3.8 %finish.1 = (f32[2,256,512]{2,1,0:T(8,128)}, f32[2,256,1024]{2,1,0:T(8,128)}, f32[2,8,256]{2,1,0:T(8,128)}) custom-call(f32[256,1024]{1,0:T(8,128)} %convert_add_fusion.1.refs_0_, bf16[256,1024]{1,0:T(8,128)(2,1)} %copy-done.18, bf16[256,1024]{1,0:T(8,128)(2,1)} %get-tuple-element.121.refs_2_, bf16[256,1024]{1,0:T(8,128)(2,1)} %copy-done.11, ...), custom_call_target="tpu_custom_call" | custom-call | tf_op jit(solution)/shard_map/finish/pallas_call | solution.py:853
  (79 shorter events, 19.6 us)
Async XLA Ops:
  16.9 17.8 %copy-start = (bf16[512,2048]{1,0:T(8,128)(2,1)S(1)}, bf16[512,2048]{1,0:T(8,128)(2,1)}, u32[]{:S(2)}) copy-start(bf16[512,2048]{1,0:T(8,128)(2,1)} %refs_8_.3) | copy-start | bytes 6291460
  29.6 14.9 %all-to-all-start = ((bf16[8,1,128,256]{3,2,1,0:T(8,128)(2,1)}), bf16[8,1,128,256]{3,2,1,0:T(8,128)(2,1)S(1)}, u32[]{:S(2)}, u32[]{:S(2)}) async-start(bf16[8,1,128,256]{3,2,1,0:T(8,128)(2,1)} %bitcast.26), calls=%async_computation | async-start | bytes 1048576 | tf_op jit(solution)/shard_map/all_to_all | solution.py:565
  48.1 10.3 %all-to-all-start.1 = ((bf16[8,1,128,128]{3,2,1,0:T(8,128)(2,1)}), bf16[8,1,128,128]{3,2,1,0:T(8,128)(2,1)S(1)}, u32[]{:S(2)}, u32[]{:S(2)}) async-start(bf16[8,1,128,128]{3,2,1,0:T(8,128)(2,1)} %chain_forward.1), calls=%async_computation.1 | async-start | bytes 524288 | tf_op jit(solution)/shard_map/all_to_all | solution.py:565
  65.4 10.3 %copy-start.2 = (bf16[512,1024]{1,0:T(8,128)(2,1)S(1)}, bf16[512,1024]{1,0:T(8,128)(2,1)}, u32[]{:S(2)}) copy-start(bf16[512,1024]{1,0:T(8,128)(2,1)} %get-tuple-element.81.b_ref.refs_9_) | copy-start | bytes 3145732
  71.7 18.3 %collective-permute-start = (bf16[1024,1024]{1,0:T(8,128)(2,1)}, bf16[1024,1024]{1,0:T(8,128)(2,1)S(1)}, u32[]{:S(2)}, u32[]{:S(2)}) collective-permute-start(bf16[1024,1024]{1,0:T(8,128)(2,1)} %get-tuple-element.88), channel_id=1, source_target_pairs={{0,4},{4,0},{8,12},{12,8},{16,20},{20,16},{24,28},{28,24},{1,5},{5... | collective-permute-start | bytes 6291464 | tf_op jit(solution)/shard_map/ppermute | solution.py:705
  71.7 18.3 %collective-permute-start.1 = (bf16[1024,1024]{1,0:T(8,128)(2,1)}, bf16[1024,1024]{1,0:T(8,128)(2,1)}, u32[]{:S(2)}, u32[]{:S(2)}) collective-permute-start(bf16[1024,1024]{1,0:T(8,128)(2,1)} %get-tuple-element.89), channel_id=1, source_target_pairs={{0,4},{4,0},{8,12},{12,8},{16,20},{20,16},{24,28},{28,24},{1,5},{5... | collective-permute-start | bytes 6291464 | tf_op jit(solution)/shard_map/ppermute | solution.py:705
  72.2 10.4 %all-to-all-start.2 = ((bf16[8,1,128,128]{3,2,1,0:T(8,128)(2,1)}), bf16[8,1,128,128]{3,2,1,0:T(8,128)(2,1)S(1)}, u32[]{:S(2)}, u32[]{:S(2)}) async-start(bf16[8,1,128,128]{3,2,1,0:T(8,128)(2,1)} %bitcast.29), calls=%async_computation.2 | async-start | bytes 524288 | tf_op jit(solution)/shard_map/all_to_all | solution.py:565
  75.6 121.0 %reduce-scatter.3.cloned.1.call-start = ((), (), s32[]{:S(2)}) async-start(), calls=%async_computation.6 | async-start | bytes 2621440 | tf_op jit(solution)/shard_map/reduce_scatter | solution.py:874
  86.3 11.9 %all-to-all-start.3 = ((bf16[8,1,128,128]{3,2,1,0:T(8,128)(2,1)}), bf16[8,1,128,128]{3,2,1,0:T(8,128)(2,1)S(1)}, u32[]{:S(2)}, u32[]{:S(2)}) async-start(bf16[8,1,128,128]{3,2,1,0:T(8,128)(2,1)} %chain_backward.1), calls=%async_computation.4 | async-start | bytes 524288 | tf_op jit(solution)/shard_map/all_to_all | solution.py:565
  89.7 107.0 %reduce-scatter.5.cloned.1.call-start = ((), (), s32[]{:S(2)}) async-start(), calls=%async_computation.7 | async-start | bytes 2621440 | tf_op jit(solution)/shard_map/reduce_scatter | solution.py:874
  98.1 20.8 %collective-permute-start.2 = (bf16[256,1024]{1,0:T(8,128)(2,1)}, bf16[256,1024]{1,0:T(8,128)(2,1)S(1)}, u32[]{:S(2)}, u32[]{:S(2)}) collective-permute-start(bf16[256,1024]{1,0:T(8,128)(2,1)} %get-tuple-element.101), channel_id=1, source_target_pairs={{0,8},{4,12},{8,0},{12,4},{16,24},{20,28},{24,16},{28,20},{1,9},{5... | collective-permute-start | bytes 1572872 | tf_op jit(solution)/shard_map/ppermute | solution.py:705
  99.9 19.1 %collective-permute-start.3 = (bf16[256,1024]{1,0:T(8,128)(2,1)}, bf16[256,1024]{1,0:T(8,128)(2,1)S(1)}, u32[]{:S(2)}, u32[]{:S(2)}) collective-permute-start(bf16[256,1024]{1,0:T(8,128)(2,1)} %get-tuple-element.102), channel_id=1, source_target_pairs={{0,16},{4,20},{8,24},{12,28},{16,0},{20,4},{24,8},{28,12},{1,17},{... | collective-permute-start | bytes 1572872 | tf_op jit(solution)/shard_map/ppermute | solution.py:705
  101.4 24.3 %collective-permute-start.4 = (bf16[256,1024]{1,0:T(8,128)(2,1)}, bf16[256,1024]{1,0:T(8,128)(2,1)S(1)}, u32[]{:S(2)}, u32[]{:S(2)}) collective-permute-start(bf16[256,1024]{1,0:T(8,128)(2,1)} %get-tuple-element.106), channel_id=1, source_target_pairs={{0,8},{4,12},{8,0},{12,4},{16,24},{20,28},{24,16},{28,20},{1,9},{5... | collective-permute-start | bytes 1572872 | tf_op jit(solution)/shard_map/ppermute | solution.py:705
  101.9 23.8 %collective-permute-start.5 = (bf16[256,1024]{1,0:T(8,128)(2,1)}, bf16[256,1024]{1,0:T(8,128)(2,1)S(1)}, u32[]{:S(2)}, u32[]{:S(2)}) collective-permute-start(bf16[256,1024]{1,0:T(8,128)(2,1)} %get-tuple-element.107), channel_id=1, source_target_pairs={{0,16},{4,20},{8,24},{12,28},{16,0},{20,4},{24,8},{28,12},{1,17},{... | collective-permute-start | bytes 1572872 | tf_op jit(solution)/shard_map/ppermute | solution.py:705
  119.0 9.9 %copy-start.16 = (bf16[256,1024]{1,0:T(8,128)(2,1)S(1)}, bf16[256,1024]{1,0:T(8,128)(2,1)}, u32[]{:S(2)}) copy-start(bf16[256,1024]{1,0:T(8,128)(2,1)} %get-tuple-element.110) | copy-start | bytes 1572868
  125.6 17.5 %copy-start.11 = (bf16[256,1024]{1,0:T(8,128)(2,1)}, bf16[256,1024]{1,0:T(8,128)(2,1)S(1)}, u32[]{:S(2)}) copy-start(bf16[256,1024]{1,0:T(8,128)(2,1)S(1)} %collective-permute-done.4.refs_3_) | copy-start | bytes 1572868
  125.7 18.1 %collective-permute-start.7 = (bf16[1024,1152]{1,0:T(8,128)(2,1)}, bf16[1024,1152]{1,0:T(8,128)(2,1)S(1)}, u32[]{:S(2)}, u32[]{:S(2)}) collective-permute-start(bf16[1024,1152]{1,0:T(8,128)(2,1)} %get-tuple-element.109), channel_id=1, source_target_pairs={{0,4},{4,0},{8,12},{12,8},{16,20},{20,16},{24,28},{28,24},{1,5},{5... | collective-permute-start | bytes 7077896 | tf_op jit(solution)/shard_map/ppermute | solution.py:705
  125.8 18.0 %collective-permute-start.6 = (bf16[1024,1024]{1,0:T(8,128)(2,1)}, bf16[1024,1024]{1,0:T(8,128)(2,1)}, u32[]{:S(2)}, u32[]{:S(2)}) collective-permute-start(bf16[1024,1024]{1,0:T(8,128)(2,1)} %get-tuple-element.108), channel_id=1, source_target_pairs={{0,4},{4,0},{8,12},{12,8},{16,20},{20,16},{24,28},{28,24},{1,5},{5... | collective-permute-start | bytes 6291464 | tf_op jit(solution)/shard_map/ppermute | solution.py:705
  127.2 15.9 %collective-permute-start.9 = (bf16[256,1024]{1,0:T(8,128)(2,1)}, bf16[256,1024]{1,0:T(8,128)(2,1)}, u32[]{:S(2)}, u32[]{:S(2)}) collective-permute-start(bf16[256,1024]{1,0:T(8,128)(2,1)} %add_convert_fusion.2), channel_id=1, source_target_pairs={{0,8},{4,12},{8,0},{12,4},{16,24},{20,28},{24,16},{28,20},{1,9},{5... | collective-permute-start | bytes 1572872 | tf_op jit(solution)/shard_map/ppermute | solution.py:705
  129.9 13.8 %collective-permute-start.8 = (bf16[256,1024]{1,0:T(8,128)(2,1)}, bf16[256,1024]{1,0:T(8,128)(2,1)S(1)}, u32[]{:S(2)}, u32[]{:S(2)}) collective-permute-start(bf16[256,1024]{1,0:T(8,128)(2,1)} %add_convert_fusion.3), channel_id=1, source_target_pairs={{0,16},{4,20},{8,24},{12,28},{16,0},{20,4},{24,8},{28,12},{1,17},{... | collective-permute-start | bytes 1572872 | tf_op jit(solution)/shard_map/ppermute | solution.py:705
  145.2 9.5 %copy-start.12 = (bf16[256,1024]{1,0:T(8,128)(2,1)S(1)}, bf16[256,1024]{1,0:T(8,128)(2,1)}, u32[]{:S(2)}) copy-start(bf16[256,1024]{1,0:T(8,128)(2,1)} %get-tuple-element.131) | copy-start | bytes 1572868
  145.2 9.5 %copy-start.15 = (bf16[256,1024]{1,0:T(8,128)(2,1)S(1)}, bf16[256,1024]{1,0:T(8,128)(2,1)}, u32[]{:S(2)}) copy-start(bf16[256,1024]{1,0:T(8,128)(2,1)} %copy-done.14) | copy-start | bytes 1572868
  152.6 15.2 %collective-permute-start.11 = (bf16[256,1024]{1,0:T(8,128)(2,1)}, bf16[256,1024]{1,0:T(8,128)(2,1)}, u32[]{:S(2)}, u32[]{:S(2)}) collective-permute-start(bf16[256,1024]{1,0:T(8,128)(2,1)} %get-tuple-element.120), channel_id=1, source_target_pairs={{0,8},{4,12},{8,0},{12,4},{16,24},{20,28},{24,16},{28,20},{1,9},{5... | collective-permute-start | bytes 1572872 | tf_op jit(solution)/shard_map/ppermute | solution.py:705
  153.0 14.8 %copy-start.19 = (bf16[256,1024]{1,0:T(8,128)(2,1)S(1)}, bf16[256,1024]{1,0:T(8,128)(2,1)}, u32[]{:S(2)}) copy-start(bf16[256,1024]{1,0:T(8,128)(2,1)} %get-tuple-element.119) | copy-start | bytes 1572868
  153.0 17.6 %collective-permute-start.14 = (bf16[256,1152]{1,0:T(8,128)(2,1)}, bf16[256,1152]{1,0:T(8,128)(2,1)S(1)}, u32[]{:S(2)}, u32[]{:S(2)}) collective-permute-start(bf16[256,1152]{1,0:T(8,128)(2,1)} %get-tuple-element.127), channel_id=1, source_target_pairs={{0,16},{4,20},{8,24},{12,28},{16,0},{20,4},{24,8},{28,12},{1,17},{... | collective-permute-start | bytes 1769480 | tf_op jit(solution)/shard_map/ppermute | solution.py:705
  156.0 14.7 %copy-start.9 = (bf16[256,1152]{1,0:T(8,128)(2,1)S(1)}, bf16[256,1152]{1,0:T(8,128)(2,1)}, u32[]{:S(2)}) copy-start(bf16[256,1152]{1,0:T(8,128)(2,1)} %get-tuple-element.126) | copy-start | bytes 1769476
  157.3 21.6 %copy-start.20 = (bf16[256,1024]{1,0:T(8,128)(2,1)S(1)}, bf16[256,1024]{1,0:T(8,128)(2,1)}, u32[]{:S(2)}) copy-start(bf16[256,1024]{1,0:T(8,128)(2,1)} %get-tuple-element.117) | copy-start | bytes 1572868
  157.3 21.6 %collective-permute-start.10 = (bf16[256,1024]{1,0:T(8,128)(2,1)}, bf16[256,1024]{1,0:T(8,128)(2,1)S(1)}, u32[]{:S(2)}, u32[]{:S(2)}) collective-permute-start(bf16[256,1024]{1,0:T(8,128)(2,1)} %get-tuple-element.118), channel_id=1, source_target_pairs={{0,8},{4,12},{8,0},{12,4},{16,24},{20,28},{24,16},{28,20},{1,9},{5... | collective-permute-start | bytes 1572872 | tf_op jit(solution)/shard_map/ppermute | solution.py:705
  158.8 23.3 %collective-permute-start.13 = (bf16[256,1152]{1,0:T(8,128)(2,1)}, bf16[256,1152]{1,0:T(8,128)(2,1)S(1)}, u32[]{:S(2)}, u32[]{:S(2)}) collective-permute-start(bf16[256,1152]{1,0:T(8,128)(2,1)} %get-tuple-element.125), channel_id=1, source_target_pairs={{0,16},{4,20},{8,24},{12,28},{16,0},{20,4},{24,8},{28,12},{1,17},{... | collective-permute-start | bytes 1769480 | tf_op jit(solution)/shard_map/ppermute | solution.py:705
  169.1 13.1 %copy-start.10 = (bf16[256,1152]{1,0:T(8,128)(2,1)S(1)}, bf16[256,1152]{1,0:T(8,128)(2,1)}, u32[]{:S(2)}) copy-start(bf16[256,1152]{1,0:T(8,128)(2,1)} %get-tuple-element.124) | copy-start | bytes 1769476
  169.1 22.1 %collective-permute-start.12 = (bf16[256,1024]{1,0:T(8,128)(2,1)S(1)}, bf16[256,1024]{1,0:T(8,128)(2,1)S(1)}, u32[]{:S(2)}, u32[]{:S(2)}) collective-permute-start(bf16[256,1024]{1,0:T(8,128)(2,1)S(1)} %add_convert_fusion.1), channel_id=1, source_target_pairs={{0,16},{4,20},{8,24},{12,28},{16,0},{20,4},{24,8},{28,12},{1,17},{... | collective-permute-start | bytes 1572872 | tf_op jit(solution)/shard_map/ppermute | solution.py:705
  170.8 20.4 %collective-permute-start.15 = (bf16[256,1152]{1,0:T(8,128)(2,1)S(1)}, bf16[256,1152]{1,0:T(8,128)(2,1)S(1)}, u32[]{:S(2)}, u32[]{:S(2)}) collective-permute-start(bf16[256,1152]{1,0:T(8,128)(2,1)S(1)} %add_convert_fusion), channel_id=1, source_target_pairs={{0,8},{4,12},{8,0},{12,4},{16,24},{20,28},{24,16},{28,20},{1,9},{5... | collective-permute-start | bytes 1769480 | tf_op jit(solution)/shard_map/ppermute | solution.py:705
  (11 other events, 30.2 us)
Sparse Core Ops, SparseCore 0:
  82.7 44.5 reduce-scatter.2
  143.9 44.1 reduce-scatter.4
